TPU v7x, 32 devices: a whole 2x2x4 slice. The times are simulated.
32 devices in a mesh: row: 4 (over y, x), col: 8 (over z, core).
Axes of the slice: x: 2, y: 2, z: 4, core: 2. Of those that a mesh axis runs over, the one named last changes fastest.
Arguments:
- source: float32 [256, 64, 128], P(('row', 'col')), may hold values from -6 to 6
- blocks: float32 [8192, 64, 64], P(('row', 'col')), may hold values from -0.15625 to 0.15625
- row_index: int32 [8192], P(('row', 'col')), may hold values from 0 to 63
- col_index: int32 [8192], P(('row', 'col')), may hold values from 0 to 31
- live_count: int32 [32], P(('row', 'col')), may hold values from 64 to 256, as said below
Outputs:
- irradiance: float32 [256, 64, 128], P(('row', 'col'))
Inputs may be any that keep to these rules, and one draw needn't show every extreme that they name: `live_count`: slots of a device beyond its live count are padding; some device has all 256 slots live.
All inputs are finite; a program needn't handle non-finite values.
Results may differ from a plain program's by a relative error of at most 0.0003.
Values sent between devices are 32-bit elements; how exact they have to be, the bound alone decides.
No kernel may reach another device: no remote copies, remote signals or barrier semaphores. Data moves between devices by JAX's collectives and lax.ppermute only.
A program may use at most 128 MiB of HBM per device.

v0:
```python
import jax
import jax.numpy as jnp
from jax import lax
from jax.sharding import PartitionSpec as P

ITERS = 2


def local_transfer(blocks, gathered, row_ids, col_index, group_rows):
    picked = jnp.take(gathered, col_index, axis=0)
    products = jnp.einsum("nij,njl->nil", blocks, picked, precision=lax.Precision.HIGHEST)
    summed = jax.ops.segment_sum(products, row_ids, num_segments=group_rows + 1)
    return summed[:group_rows]


def body(source, blocks, row_index, col_index, live_count):
    bricks_here = source.shape[0]
    group_rows = bricks_here * lax.axis_size("col")
    live_total = live_count[0]
    slot_ids = jnp.arange(blocks.shape[0], dtype=jnp.int32)
    row_ids = jnp.where(slot_ids < live_total, row_index, group_rows)
    field = source
    for bounce in range(ITERS):
        gathered = lax.all_gather(field, "row", axis=0, tiled=True)
        partial_value = local_transfer(blocks, gathered, row_ids, col_index, group_rows)
        owned = lax.psum_scatter(partial_value, "col", scatter_dimension=0, tiled=True)
        field = source + owned
    return field


def solution(mesh):
    in_specs = (
        P(("row", "col"), None, None),
        P(("row", "col"), None, None),
        P(("row", "col")),
        P(("row", "col")),
        P(("row", "col")),
    )
    out_specs = P(("row", "col"), None, None)
    return jax.shard_map(body, mesh=mesh, in_specs=in_specs, out_specs=out_specs, check_vma=False)
```

profile of v0, /device:TPU:0, one launch (start us, length us, event | category | flops | bytes accessed | tf_op | source)
XLA Modules:
  0.0 242.3 jit_solution(12168630809915848849)
XLA Ops:
  6.5 0.0 copy-start.1
  6.5 0.0 copy-start.2
  6.5 0.0 all-gather.3.cloned.1.call-start
  6.5 0.7 all-gather.3.cloned.1.call-update
  7.3 0.0 reduce-scatter.3.cloned.1.call-start
  7.3 9.2 %copy.7 = f32[256,64,64]{2,1,0:T(8,128)} copy(f32[256,64,64]{0,2,1:T(8,128)} %param.8) | data formatting | bytes 8388608 | tf_op args[1]
  17.1 0.0 copy-done.1
  17.2 0.0 copy-done.2
  17.2 21.4 %all-gather.3.cloned.1.call-done = f32[32,64,128]{2,1,0:T(8,128)} async-done(((f32[8,64,128]{2,1,0:T(8,128)}), f32[32,64,128]{2,1,0:T(8,128)}) %all-gather.3.cloned.1.call-update) | async-done | bytes 1048592 | tf_op jit(solution)/shard_map/all_gather | solution.py:24
  38.6 5.5 %gather_fusion = f32[256,64,128]{2,1,0:T(8,128)} fusion(f32[32,64,128]{2,1,0:T(8,128)} %all-gather.3.cloned.1.call-done, s32[1024]{0:T(1024)S(1)} %pad_clamp_fusion), kind=kCustom, calls=%fused_computation.clone | custom fusion | bytes 16778240 | tf_op jit(solution)/shard_map/jit(_take)/gather | solution.py:10
  44.1 14.7 %fusion.8 = f32[256,64,128]{2,1,0:T(8,128)} fusion(f32[256,64,64]{2,1,0:T(8,128)} %copy.7, f32[256,64,128]{2,1,0:T(8,128)} %gather_fusion, pred[256]{0:T(512)(128)(4,1)S(1)} %compare_and_fusion), kind=kOutput, calls=%fused_computation.12 | convolution fusion | flops 1612709888 | bytes 20971776 | tf_op jit(solution)/shard_map/nij,njl->nil/dot_general | solution.py:11
  58.8 0.2 broadcast.6.clone
  59.0 0.0 copy-start
  59.1 26.1 %scatter_fusion = f32[65,64,128]{2,1,0:T(8,128)S(1)} fusion(f32[65,64,128]{2,1,0:T(8,128)S(1)} %broadcast.6.clone, s32[256]{0:T(256)S(1)} %compare_select_fusion.1, f32[256,64,128]{2,1,0:T(8,128)} %fusion.8), kind=kCustom, calls=%fused_computation.2 | custom fusion | flops 2097152 | bytes 25166848 | tf_op jit(solution)/shard_map/scatter-add | solution.py:12
  85.2 1.5 slice.12
  86.7 0.0 reduce-scatter.3.cloned.1.call-update
  86.7 0.0 all-gather.5.cloned.1.call-start
  86.8 36.0 %reduce-scatter.3.cloned.1.call-done = f32[8,64,128]{2,1,0:T(8,128)} async-done(((f32[64,64,128]{2,1,0:T(8,128)}), f32[8,64,128]{2,1,0:T(8,128)}) %reduce-scatter.3.cloned.1.call-update) | async-done | bytes 262160 | tf_op jit(solution)/shard_map/reduce_scatter | solution.py:26
  122.7 0.0 copy-done
  122.7 1.7 add.20
  124.4 0.0 all-gather.5.cloned.1.call-update
  124.4 0.2 reduce-scatter.5.cloned.1.call-start
  124.7 25.2 %all-gather.5.cloned.1.call-done = f32[32,64,128]{2,1,0:T(8,128)} async-done(((f32[8,64,128]{2,1,0:T(8,128)}), f32[32,64,128]{2,1,0:T(8,128)}) %all-gather.5.cloned.1.call-update) | async-done | bytes 1048592 | tf_op jit(solution)/shard_map/all_gather | solution.py:24
  149.9 5.5 %gather_fusion.1 = f32[256,64,128]{2,1,0:T(8,128)} fusion(f32[32,64,128]{2,1,0:T(8,128)} %all-gather.5.cloned.1.call-done, s32[1024]{0:T(1024)S(1)} %pad_clamp_fusion), kind=kCustom, calls=%fused_computation.1.clone | custom fusion | bytes 16778240 | tf_op jit(solution)/shard_map/jit(_take)/gather | solution.py:10
  155.5 14.7 %fusion.11 = f32[256,64,128]{2,1,0:T(8,128)} fusion(f32[256,64,64]{2,1,0:T(8,128)} %copy.7, f32[256,64,128]{2,1,0:T(8,128)} %gather_fusion.1, pred[256]{0:T(512)(128)(4,1)S(1)} %compare_and_fusion), kind=kOutput, calls=%fused_computation.13 | convolution fusion | flops 1612709888 | bytes 20971776 | tf_op jit(solution)/shard_map/nij,njl->nil/dot_general | solution.py:11
  170.1 0.2 broadcast.6
  170.4 26.2 %scatter_fusion.1 = f32[65,64,128]{2,1,0:T(8,128)S(1)} fusion(f32[65,64,128]{2,1,0:T(8,128)S(1)} %broadcast.6, s32[256]{0:T(256)S(1)} %compare_select_fusion.1, f32[256,64,128]{2,1,0:T(8,128)} %fusion.11), kind=kCustom, calls=%fused_computation.3 | custom fusion | flops 2097152 | bytes 25166848 | tf_op jit(solution)/shard_map/scatter-add | solution.py:12
  196.6 1.5 slice.13
  198.0 0.0 reduce-scatter.5.cloned.1.call-update
  198.0 36.0 %reduce-scatter.5.cloned.1.call-done = f32[8,64,128]{2,1,0:T(8,128)} async-done(((f32[64,64,128]{2,1,0:T(8,128)}), f32[8,64,128]{2,1,0:T(8,128)}) %reduce-scatter.5.cloned.1.call-update) | async-done | bytes 262160 | tf_op jit(solution)/shard_map/reduce_scatter | solution.py:26
  234.1 1.7 add.21
  (4 shorter events, 0.0 us)
Async XLA Ops:
  6.5 10.6 %copy-start.1 = (s32[256]{0:T(256)S(1)}, s32[256]{0:T(256)}, u32[]{:S(2)}) copy-start(s32[256]{0:T(256)} %param.10) | copy-start | bytes 3076
  6.5 10.6 %copy-start.2 = (s32[256]{0:T(256)S(1)}, s32[256]{0:T(256)}, u32[]{:S(2)}) copy-start(s32[256]{0:T(256)} %param.9) | copy-start | bytes 3076
  6.5 32.0 %all-gather.3.cloned.1.call-start = ((), (), s32[]{:S(2)}) async-start(), calls=%async_computation.2 | async-start | bytes 1310720 | tf_op jit(solution)/shard_map/all_gather | solution.py:24
  7.3 115.5 %reduce-scatter.3.cloned.1.call-start = ((), (), s32[]{:S(2)}) async-start(), calls=%async_computation.3 | async-start | bytes 2359296 | tf_op jit(solution)/shard_map/reduce_scatter | solution.py:26
  59.0 63.7 %copy-start = (f32[8,64,128]{2,1,0:T(8,128)S(1)}, f32[8,64,128]{2,1,0:T(8,128)}, u32[]{:S(2)}) copy-start(f32[8,64,128]{2,1,0:T(8,128)} %param.7) | copy-start | bytes 786436
  86.7 63.2 %all-gather.5.cloned.1.call-start = ((), (), s32[]{:S(2)}) async-start(), calls=%async_computation.4 | async-start | bytes 1310720 | tf_op jit(solution)/shard_map/all_gather | solution.py:24
  124.4 109.6 %reduce-scatter.5.cloned.1.call-start = ((), (), s32[]{:S(2)}) async-start(), calls=%async_computation.5 | async-start | bytes 2359296 | tf_op jit(solution)/shard_map/reduce_scatter | solution.py:26
Sparse Core Ops, SparseCore 0:
  9.2 29.3 all-gather.2
  86.8 35.8 reduce-scatter.2
  124.6 25.2 all-gather.4
  198.2 35.8 reduce-scatter.4
where the time goes:
time: 244 us; the launch traced here: 242 us
  waiting for transfers between devices  119 us (49%)
  other arithmetic  55.7 us (23%)
  matrix products  29.4 us (12%)
  local copies, waits for them, and re-layouts  23.7 us (10%)
  between operations  13.9 us (6%)
    reduce_scatter x2, waiting for transfers between devices, body(): lax.psum_scatter(partial_value, 'col', scatter_dimension=0, tiled=True)  72 us
    scatter-add x2, other arithmetic, local_transfer(): summed = jax.ops.segment_sum(products, row_ids, num_segments=group_rows + 1)  52.3 us
    all_gather x2, waiting for transfers between devices, body(): gathered = lax.all_gather(field, 'row', axis=0, tiled=True)  46.6 us
    dot_general x2, matrix products, local_transfer(): jnp.einsum('nij,njl->nil', blocks, picked, precision=lax.Precision.HIGHEST)  29.4 us
    gather x2, local copies, waits for them, and re-layouts, local_transfer(): picked = jnp.take(gathered, col_index, axis=0)  11.1 us
    unnamed x7, local copies, waits for them, and re-layouts  9.18 us
  transfers between devices with their start and end apart: 4, of which 4 were waited for; matrix products, arithmetic and copies ran while one was open for 4% of the time, Pallas kernels for 0%

commit v1 on v0

v1 whole, which is shorter than its diff:
```python
import functools

import jax
import jax.numpy as jnp
from jax import lax
from jax.experimental import pallas as pl
from jax.experimental.pallas import tpu as pltpu
from jax.sharding import PartitionSpec as P

ITERS = 2
HALVES = 2
GROUP = 32
BF16 = jnp.bfloat16
F32 = jnp.float32


def split_parts(value):
    high = value.astype(BF16)
    low = (value - high.astype(F32)).astype(BF16)
    return high, low


def prepare_kernel(b_ref, o_ref, t_ref):
    cells, _, slots = b_ref.shape
    width = min(128, slots)

    def turn(i, carry):
        for c in range(slots // width):
            value = b_ref[i, :, pl.ds(c * width, width)]
            high = value.astype(BF16).astype(F32)
            t_ref[i, pl.ds(c * width, width), :] = jnp.concatenate([high, value - high], axis=0).T
        return carry

    lax.fori_loop(0, cells, turn, 0, unroll=4)

    def regroup(g, carry):
        first = pl.multiple_of(g * 8, 8)
        o_ref[pl.ds(first, 8)] = jnp.swapaxes(t_ref[:, pl.ds(first, 8), :], 0, 1).astype(BF16)
        return carry

    lax.fori_loop(0, slots // 8, regroup, 0)


def prepare(blocks):
    slots, cells, _ = blocks.shape
    whole = pl.BlockSpec(memory_space=pltpu.VMEM)
    return pl.pallas_call(
        prepare_kernel,
        in_specs=[whole],
        out_specs=whole,
        out_shape=jax.ShapeDtypeStruct((slots, cells, 2 * cells), BF16),
        scratch_shapes=[pltpu.VMEM((cells, slots, 2 * cells), F32)],
        compiler_params=pltpu.CompilerParams(vmem_limit_bytes=32 * 2**20),
        cost_estimate=pl.CostEstimate(flops=0, bytes_accessed=24 * 2**20, transcendentals=0),
        name="prepare",
    )(jnp.transpose(blocks, (1, 2, 0)))


def transfer_kernel(n_in, n_out, place_ref, sender_ref, live_ref, a_ref, *rest):
    x_refs, out_refs = rest[:n_in], rest[n_in : n_in + n_out]
    w_ref, acc_ref, sems = rest[n_in + n_out :]
    base = 0
    for x_ref in x_refs:

        def split_brick(c, carry, x_ref=x_ref, base=base):
            w_ref[base + c] = jnp.concatenate(split_parts(x_ref[c]), axis=0)
            return carry

        lax.fori_loop(0, x_ref.shape[0], split_brick, 0, unroll=4)
        base += x_ref.shape[0]

    def clear(c, carry):
        acc_ref[c] = jnp.zeros(acc_ref.shape[1:], F32)
        return carry

    lax.fori_loop(0, acc_ref.shape[0], clear, 0, unroll=5)
    cells = acc_ref.shape[1]

    def step(g, carry):
        results = []
        for u in range(GROUP):
            s = g * GROUP + u
            a = a_ref[s]
            w = w_ref[sender_ref[s]]
            high, low = w[:cells], w[cells:]
            results.append(
                jnp.dot(
                    jnp.concatenate([a, a], axis=1),
                    jnp.concatenate([high, high, low, low], axis=0),
                    preferred_element_type=F32,
                )
            )
        for u in range(GROUP):
            acc_ref[place_ref[g * GROUP + u]] += results[u]
        return carry

    lax.fori_loop(0, (live_ref[0] + GROUP - 1) // GROUP, step, 0)
    copies, base = [], 0
    for i, out_ref in enumerate(out_refs):
        copies.append(pltpu.make_async_copy(acc_ref.at[pl.ds(base, out_ref.shape[0])], out_ref, sems.at[i]))
        base += out_ref.shape[0]
    for copy in copies:
        copy.start()
    for copy in copies:
        copy.wait()


def transfer(place, sender, live, matrix, fields, out_bricks):
    cells, lights = fields[0].shape[1:]
    bricks = sum(f.shape[0] for f in fields)
    whole = pl.BlockSpec(memory_space=pltpu.VMEM)
    scalars = pl.BlockSpec(memory_space=pltpu.SMEM)
    rows = matrix.shape[0] * cells
    return pl.pallas_call(
        functools.partial(transfer_kernel, len(fields), len(out_bricks)),
        in_specs=[scalars] * 3 + [whole] * (1 + len(fields)),
        out_specs=[pl.BlockSpec(memory_space=pl.ANY)] * len(out_bricks),
        out_shape=[jax.ShapeDtypeStruct((n, cells, lights), F32) for n in out_bricks],
        scratch_shapes=[
            pltpu.VMEM((bricks, 2 * cells, lights), BF16),
            pltpu.VMEM((sum(out_bricks) + 1, cells, lights), F32),
            pltpu.SemaphoreType.DMA((len(out_bricks),)),
        ],
        compiler_params=pltpu.CompilerParams(vmem_limit_bytes=32 * 2**20),
        cost_estimate=pl.CostEstimate(flops=2 * rows * 4 * cells * lights, bytes_accessed=16 * 2**20, transcendentals=0),
        name="transfer",
    )(place, sender, live, matrix, *fields)


def places(row_index, live, bricks, n_col):
    pairs, half = n_col // 2, bricks // HALVES
    me = lax.axis_index("col")
    my_pair, my_side = me // 2, me % 2
    column, brick = row_index // bricks, row_index % bricks
    pair, side = column // 2, column % 2
    ahead = jnp.where(my_side == 0, pair - my_pair, my_pair - pair) % pairs
    carrier = jnp.where(pair > my_pair, 0, jnp.where(pair < my_pair, 1, my_side))
    within = (ahead * 2 + (side ^ carrier)) * half + brick % half
    place = (brick // half) * (pairs * 2 * half) + within
    slots = jnp.arange(row_index.shape[0], dtype=jnp.int32)
    return jnp.where(slots < live, place, bricks * n_col).astype(jnp.int32)


def body(source, blocks, row_index, col_index, live_count):
    bricks = source.shape[0]
    n_row, n_col = lax.axis_size("row"), lax.axis_size("col")
    pairs, half = n_col // 2, bricks // HALVES
    my_row, my_col = lax.axis_index("row"), lax.axis_index("col")
    live = live_count[0]

    swap = [(i, i ^ 1) for i in range(n_col)]
    ring = [(i, (i + 2 if i + 2 < n_col else n_col - 1) if i % 2 == 0 else (i - 2 if i > 2 else 0)) for i in range(n_col)]
    first_of_line = jnp.where(my_col % 2 == 0, my_col == 0, my_col == n_col - 1)

    place = places(row_index, live, bricks, n_col)
    from_row = col_index // bricks
    flips = n_row & (n_row - 1) == 0
    turn = from_row ^ my_row if flips else (from_row - my_row) % n_row
    sender = (turn * bricks + col_index % bricks).astype(jnp.int32)
    matrix = prepare(blocks)

    def gather(value):
        fields = [value]
        for k in range(1, n_row):
            fields.append(lax.ppermute(value, "row", [(i ^ k if flips else (i + k) % n_row, i) for i in range(n_row)]))
        return fields

    def scatter(own, sent):
        got = lax.ppermute(sent, "col", swap)
        block = 2 * half

        def both(distance):
            mine, other = half + (distance - 1) * block, half + (pairs - distance - 1) * block
            return sent[mine : mine + block] + got[other : other + block]

        total = both(pairs - 1) if pairs > 1 else None
        for distance in range(pairs - 1, 0, -1):
            came = jnp.where(first_of_line, 0.0, lax.ppermute(total, "col", ring))
            total = came if distance == 1 else came + both(distance - 1)
        out = own + got[:half]
        if total is not None:
            out = out + total[:half] + lax.ppermute(total[half:], "col", swap)
        return out

    field = source
    sizes = [half, (2 * pairs - 1) * half] * HALVES
    for bounce in range(ITERS):
        sums = transfer(place, sender, live_count, matrix, gather(field), sizes)
        parts = [scatter(sums[2 * h], sums[2 * h + 1]) for h in range(HALVES)]
        field = source + jnp.concatenate(parts, axis=0)
    return field


def solution(mesh):
    in_specs = (
        P(("row", "col"), None, None),
        P(("row", "col"), None, None),
        P(("row", "col")),
        P(("row", "col")),
        P(("row", "col")),
    )
    out_specs = P(("row", "col"), None, None)
    return jax.shard_map(body, mesh=mesh, in_specs=in_specs, out_specs=out_specs, check_vma=False)
```

time: 244 us -> 99 us (0.41)
  waiting for transfers between devices: 119 us -> 32.8 us
  other arithmetic: 55.7 us -> 7.18 us
  starting transfers between devices: 0.31 us -> 34.7 us
  matrix products: 29.4 us -> 0 us
  local copies, waits for them, and re-layouts: 23.7 us -> 7.37 us
  Pallas kernels: 0 us -> 15.9 us
  between operations: 13.9 us -> 0.89 us
    reduce_scatter x2 -> x0, waiting for transfers between devices: 72 us -> none  [body(): lax.psum_scatter(partial_value, 'col', scatter_dimension=0, tiled=True)]
    scatter-add x2 -> x0, other arithmetic: 52.3 us -> none  [local_transfer(): summed = jax.ops.segment_sum(products, row_ids, num_segments=group_rows + 1)]
    all_gather x2 -> x0, waiting for transfers between devices: 46.6 us -> none  [body(): gathered = lax.all_gather(field, 'row', axis=0, tiled=True)]
    ppermute x0 -> x26, starting transfers between devices: none -> 34.7 us  [the longest x12 25.2 us: scatter(): came = jnp.where(first_of_line, 0.0, lax.ppermute(total, 'col', ring))]
    ppermute x0 -> x26, waiting for transfers between devices: none -> 32.8 us  [the longest x12 14.4 us: scatter(): came = jnp.where(first_of_line, 0.0, lax.ppermute(total, 'col', ring))]
    dot_general x2 -> x0, matrix products: 29.4 us -> none  [local_transfer(): jnp.einsum('nij,njl->nil', blocks, picked, precision=lax.Precision.HIGHEST)]
    pallas_call x0 -> x3, Pallas kernels: none -> 15.9 us  [the longest x2 10.4 us: transfer(): pl.pallas_call(functools.partial(transfer_kernel, len(fields), len(out_br...]
    gather x2 -> x0, local copies, waits for them, and re-layouts: 11.1 us -> none  [local_transfer(): picked = jnp.take(gathered, col_index, axis=0)]
  transfers between devices with their start and end apart: 4 -> 26, of which waited for: 4 -> 18; matrix products, arithmetic and copies ran while one was open for 4% -> 6% of each run, Pallas kernels for 0% -> 6%
where the time goes in v1:
time: 99 us; the launch traced here: 98.8 us
  starting transfers between devices  34.7 us (35%)
  waiting for transfers between devices  32.8 us (33%)
  Pallas kernels  15.9 us (16%)
  local copies, waits for them, and re-layouts  7.37 us (7%)
  other arithmetic  7.18 us (7%)
    ppermute x12, starting transfers between devices, scatter(): came = jnp.where(first_of_line, 0.0, lax.ppermute(total, 'col', ring))  25.2 us
    ppermute x12, waiting for transfers between devices, scatter(): came = jnp.where(first_of_line, 0.0, lax.ppermute(total, 'col', ring))  14.4 us
    ppermute x6, waiting for transfers between devices, gather(): lax.ppermute(value, 'row', [(i ^ k if flips else (i + k) % n_row, i) for...  12.8 us
    pallas_call x2, Pallas kernels, transfer(): pl.pallas_call(functools.partial(transfer_kernel, len(fields), len(out_br...  10.4 us
    ppermute x6, starting transfers between devices, gather(): lax.ppermute(value, 'row', [(i ^ k if flips else (i + k) % n_row, i) for...  8.01 us
    unnamed x18, local copies, waits for them, and re-layouts  7.33 us
    pallas_call x1, Pallas kernels, prepare(): pl.pallas_call(prepare_kernel, in_specs=[whole], out_specs=whole, out_sha...  5.59 us
    add x8, other arithmetic, scatter(): total = came if distance == 1 else came + both(distance - 1)  4.21 us
  transfers between devices with their start and end apart: 26, of which 18 were waited for; matrix products, arithmetic and copies ran while one was open for 6% of the time, Pallas kernels for 6%

profile of v1, /device:TPU:0, one launch (start us, length us, event | category | flops | bytes accessed | tf_op | source)
XLA Modules:
  0.0 98.8 jit_solution(17360789017835417363)
XLA Ops:
  0.0 3.9 %collective-permute-start.2 = (f32[8,64,128]{2,1,0:T(8,128)}, f32[8,64,128]{2,1,0:T(8,128)S(1)}, u32[]{:S(2)}, u32[]{:S(2)}) collective-permute-start(f32[8,64,128]{2,1,0:T(8,128)} %rest_0_.1), channel_id=1, source_target_pairs={{24,0},{16,8},{8,16},{0,24},{25,1},{17,9},{9,17},{1,25},{26,2},{18... | collective-permute-start | bytes 786440 | tf_op jit(solution)/shard_map/ppermute | solution.py:165
  3.9 0.5 collective-permute-start.1
  5.1 2.2 %copy-done.3 = f32[256,64,64]{0,2,1:T(8,128)S(1)} copy-done((f32[256,64,64]{0,2,1:T(8,128)S(1)}, f32[256,64,64]{0,2,1:T(8,128)}, u32[]{:S(2)}) %copy-start.3) | copy-done | bytes 4194328
  7.3 5.6 %prepare.1.a_ref = bf16[256,64,128]{2,1,0:T(8,128)(2,1)S(1)} custom-call(f32[64,64,256]{2,1,0:T(8,128)S(1)} %bitcast.3), custom_call_target="tpu_custom_call" | custom-call | bytes 25165824 | tf_op jit(solution)/shard_map/prepare/pallas_call | solution.py:47
  12.9 2.0 %copy-done = bf16[256,64,128]{2,1,0:T(8,128)(2,1)} copy-done((bf16[256,64,128]{2,1,0:T(8,128)(2,1)}, bf16[256,64,128]{2,1,0:T(8,128)(2,1)S(1)}, u32[]{:S(2)}) %copy-start) | copy-done | bytes 4194328
  14.9 1.1 %collective-permute-done.1.rest_2_ = f32[8,64,128]{2,1,0:T(8,128)S(1)} collective-permute-done((f32[8,64,128]{2,1,0:T(8,128)}, f32[8,64,128]{2,1,0:T(8,128)S(1)}, u32[]{:S(2)}, u32[]{:S(2)}) %collective-permute-start.1) | collective-permute-done | bytes 262176 | tf_op jit(solution)/shard_map/ppermute | solution.py:165
  16.3 2.2 %copy-done.1 = bf16[256,64,128]{2,1,0:T(8,128)(2,1)S(1)} copy-done((bf16[256,64,128]{2,1,0:T(8,128)(2,1)S(1)}, bf16[256,64,128]{2,1,0:T(8,128)(2,1)}, u32[]{:S(2)}) %copy-start.1) | copy-done | bytes 4194328
  18.5 5.2 %transfer.2 = (f32[4,64,128]{2,1,0:T(8,128)S(1)}, f32[28,64,128]{2,1,0:T(8,128)S(1)}, f32[4,64,128]{2,1,0:T(8,128)S(1)}, f32[28,64,128]{2,1,0:T(8,128)S(1)}) custom-call(s32[256]{0:T(256)S(1)} %get-tuple-element.21.place_ref, s32[256]{0:T(256)S(1)} %get-tuple-element.22.sender_ref, s32[1]{0:T(128)} %copy.6.live_ref, bf16[256,64,128]{2,1,0:T(8,128)(2,1)S(1)} %copy-done.1, ...), custom_call_target="tpu_custom_call" | custom-call | flops 1073741824 | bytes 16777216 | tf_op jit(solution)/shard_map/transfer/pallas_call | solution.py:114
  23.8 0.5 collective-permute-start.8
  24.3 2.0 %collective-permute-done.3 = f32[28,64,128]{2,1,0:T(8,128)S(1)} collective-permute-done((f32[28,64,128]{2,1,0:T(8,128)S(1)}, f32[28,64,128]{2,1,0:T(8,128)S(1)}, u32[]{:S(2)}, u32[]{:S(2)}) %collective-permute-start.3) | collective-permute-done | bytes 917536 | tf_op jit(solution)/shard_map/ppermute | solution.py:169
  26.3 1.6 %collective-permute-start.4 = (f32[8,64,128]{2,1,0:T(8,128)S(1)}, f32[8,64,128]{2,1,0:T(8,128)S(1)}, u32[]{:S(2)}, u32[]{:S(2)}) collective-permute-start(f32[8,64,128]{2,1,0:T(8,128)S(1)} %slice_add_fusion.11), channel_id=1, source_target_pairs={{0,2},{1,0},{2,4},{3,1},{4,6},{5,3},{6,7},{7,5},{8,10},{9,8},{10,1... | collective-permute-start | bytes 786440 | tf_op jit(solution)/shard_map/ppermute | solution.py:178
  27.9 1.0 copy-done.5
  28.9 1.3 %collective-permute-start.9 = (f32[8,64,128]{2,1,0:T(8,128)S(1)}, f32[8,64,128]{2,1,0:T(8,128)S(1)}, u32[]{:S(2)}, u32[]{:S(2)}) collective-permute-start(f32[8,64,128]{2,1,0:T(8,128)S(1)} %slice_add_fusion.8), channel_id=1, source_target_pairs={{0,2},{1,0},{2,4},{3,1},{4,6},{5,3},{6,7},{7,5},{8,10},{9,8},{10,1... | collective-permute-start | bytes 786440 | tf_op jit(solution)/shard_map/ppermute | solution.py:178
  30.2 1.6 %collective-permute-done.4 = f32[8,64,128]{2,1,0:T(8,128)S(1)} collective-permute-done((f32[8,64,128]{2,1,0:T(8,128)S(1)}, f32[8,64,128]{2,1,0:T(8,128)S(1)}, u32[]{:S(2)}, u32[]{:S(2)}) %collective-permute-start.4) | collective-permute-done | bytes 262176 | tf_op jit(solution)/shard_map/ppermute | solution.py:178
  31.8 1.0 %fusion.7 = f32[8,64,128]{2,1,0:T(8,128)S(1)} fusion(f32[28,64,128]{2,1,0:T(8,128)} %copy-done.6, f32[28,64,128]{2,1,0:T(8,128)S(1)} %get-tuple-element.14, f32[8,64,128]{2,1,0:T(8,128)S(1)} %collective-permute-done.4, pred[]{:T(512)S(6)} %select_n.141), kind=kLoop, calls=%fused_computation.18 | loop fusion | flops 196608 | bytes 1048577 | tf_op jit(solution)/shard_map/add | solution.py:179
  32.8 2.5 %collective-permute-start.5 = (f32[8,64,128]{2,1,0:T(8,128)S(1)}, f32[8,64,128]{2,1,0:T(8,128)S(1)}, u32[]{:S(2)}, u32[]{:S(2)}) collective-permute-start(f32[8,64,128]{2,1,0:T(8,128)S(1)} %fusion.7), channel_id=1, source_target_pairs={{0,2},{1,0},{2,4},{3,1},{4,6},{5,3},{6,7},{7,5},{8,10},{9,8},{10,1... | collective-permute-start | bytes 786440 | tf_op jit(solution)/shard_map/ppermute | solution.py:178
  35.3 1.0 %fusion.5 = f32[8,64,128]{2,1,0:T(8,128)S(1)} fusion(f32[28,64,128]{2,1,0:T(8,128)} %copy-done.5, f32[28,64,128]{2,1,0:T(8,128)S(1)} %get-tuple-element.16, f32[8,64,128]{2,1,0:T(8,128)S(1)} %collective-permute-done.9, pred[]{:T(512)S(6)} %select_n.141), kind=kLoop, calls=%fused_computation.13 | loop fusion | flops 196608 | bytes 1048577 | tf_op jit(solution)/shard_map/add | solution.py:179
  36.3 1.8 %collective-permute-start.10 = (f32[8,64,128]{2,1,0:T(8,128)S(1)}, f32[8,64,128]{2,1,0:T(8,128)S(1)}, u32[]{:S(2)}, u32[]{:S(2)}) collective-permute-start(f32[8,64,128]{2,1,0:T(8,128)S(1)} %fusion.5), channel_id=1, source_target_pairs={{0,2},{1,0},{2,4},{3,1},{4,6},{5,3},{6,7},{7,5},{8,10},{9,8},{10,1... | collective-permute-start | bytes 786440 | tf_op jit(solution)/shard_map/ppermute | solution.py:178
  38.1 1.1 %collective-permute-done.5 = f32[8,64,128]{2,1,0:T(8,128)S(1)} collective-permute-done((f32[8,64,128]{2,1,0:T(8,128)S(1)}, f32[8,64,128]{2,1,0:T(8,128)S(1)}, u32[]{:S(2)}, u32[]{:S(2)}) %collective-permute-start.5) | collective-permute-done | bytes 262176 | tf_op jit(solution)/shard_map/ppermute | solution.py:178
  39.2 1.0 %fusion.6 = f32[8,64,128]{2,1,0:T(8,128)S(1)} fusion(f32[28,64,128]{2,1,0:T(8,128)} %copy-done.6, f32[28,64,128]{2,1,0:T(8,128)S(1)} %get-tuple-element.14, f32[8,64,128]{2,1,0:T(8,128)S(1)} %collective-permute-done.5, pred[]{:T(512)S(6)} %select_n.141), kind=kLoop, calls=%fused_computation.16 | loop fusion | flops 196608 | bytes 1048577 | tf_op jit(solution)/shard_map/add | solution.py:179
  40.2 2.5 %collective-permute-start.6 = (f32[8,64,128]{2,1,0:T(8,128)S(1)}, f32[8,64,128]{2,1,0:T(8,128)S(1)}, u32[]{:S(2)}, u32[]{:S(2)}) collective-permute-start(f32[8,64,128]{2,1,0:T(8,128)S(1)} %fusion.6), channel_id=1, source_target_pairs={{0,2},{1,0},{2,4},{3,1},{4,6},{5,3},{6,7},{7,5},{8,10},{9,8},{10,1... | collective-permute-start | bytes 786440 | tf_op jit(solution)/shard_map/ppermute | solution.py:178
  42.7 1.0 %fusion.4 = f32[8,64,128]{2,1,0:T(8,128)S(1)} fusion(f32[28,64,128]{2,1,0:T(8,128)} %copy-done.5, f32[28,64,128]{2,1,0:T(8,128)S(1)} %get-tuple-element.16, f32[8,64,128]{2,1,0:T(8,128)S(1)} %collective-permute-done.10, pred[]{:T(512)S(6)} %select_n.141), kind=kLoop, calls=%fused_computation.11 | loop fusion | flops 196608 | bytes 1048577 | tf_op jit(solution)/shard_map/add | solution.py:179
  43.7 1.8 %collective-permute-start.11 = (f32[8,64,128]{2,1,0:T(8,128)S(1)}, f32[8,64,128]{2,1,0:T(8,128)S(1)}, u32[]{:S(2)}, u32[]{:S(2)}) collective-permute-start(f32[8,64,128]{2,1,0:T(8,128)S(1)} %fusion.4), channel_id=1, source_target_pairs={{0,2},{1,0},{2,4},{3,1},{4,6},{5,3},{6,7},{7,5},{8,10},{9,8},{10,1... | collective-permute-start | bytes 786440 | tf_op jit(solution)/shard_map/ppermute | solution.py:178
  45.5 1.1 %collective-permute-done.6 = f32[8,64,128]{2,1,0:T(8,128)S(1)} collective-permute-done((f32[8,64,128]{2,1,0:T(8,128)S(1)}, f32[8,64,128]{2,1,0:T(8,128)S(1)}, u32[]{:S(2)}, u32[]{:S(2)}) %collective-permute-start.6) | collective-permute-done | bytes 262176 | tf_op jit(solution)/shard_map/ppermute | solution.py:178
  46.7 2.7 %collective-permute-done.11 = f32[8,64,128]{2,1,0:T(8,128)S(1)} collective-permute-done((f32[8,64,128]{2,1,0:T(8,128)S(1)}, f32[8,64,128]{2,1,0:T(8,128)S(1)}, u32[]{:S(2)}, u32[]{:S(2)}) %collective-permute-start.11) | collective-permute-done | bytes 262176 | tf_op jit(solution)/shard_map/ppermute | solution.py:178
  49.5 0.9 fusion.11
  50.5 0.4 collective-permute-done.12
  50.8 0.9 fusion.10
  51.8 1.7 %collective-permute-start.15 = (f32[8,64,128]{2,1,0:T(8,128)S(1)}, f32[8,64,128]{2,1,0:T(8,128)S(1)}, u32[]{:S(2)}, u32[]{:S(2)}) collective-permute-start(f32[8,64,128]{2,1,0:T(8,128)S(1)} %maximum_add_fusion.rest_0_), channel_id=1, source_target_pairs={{24,0},{16,8},{8,16},{0,24},{25,1},{17,9},{9,17},{1,25},{26,2},{18... | collective-permute-start | bytes 786440 | tf_op jit(solution)/shard_map/ppermute | solution.py:165
  53.5 0.4 collective-permute-start.14
  54.0 1.4 %collective-permute-start.13 = (f32[8,64,128]{2,1,0:T(8,128)S(1)}, f32[8,64,128]{2,1,0:T(8,128)S(1)}, u32[]{:S(2)}, u32[]{:S(2)}) collective-permute-start(f32[8,64,128]{2,1,0:T(8,128)S(1)} %maximum_add_fusion.rest_0_), channel_id=1, source_target_pairs={{8,0},{0,8},{24,16},{16,24},{9,1},{1,9},{25,17},{17,25},{10,2},{2,... | collective-permute-start | bytes 786440 | tf_op jit(solution)/shard_map/ppermute | solution.py:165
  55.4 6.6 %collective-permute-done.15.rest_3_ = f32[8,64,128]{2,1,0:T(8,128)S(1)} collective-permute-done((f32[8,64,128]{2,1,0:T(8,128)S(1)}, f32[8,64,128]{2,1,0:T(8,128)S(1)}, u32[]{:S(2)}, u32[]{:S(2)}) %collective-permute-start.15) | collective-permute-done | bytes 262176 | tf_op jit(solution)/shard_map/ppermute | solution.py:165
  62.0 4.8 %collective-permute-done.14.rest_2_ = f32[8,64,128]{2,1,0:T(8,128)S(1)} collective-permute-done((f32[8,64,128]{2,1,0:T(8,128)S(1)}, f32[8,64,128]{2,1,0:T(8,128)S(1)}, u32[]{:S(2)}, u32[]{:S(2)}) %collective-permute-start.14) | collective-permute-done | bytes 262176 | tf_op jit(solution)/shard_map/ppermute | solution.py:165
  66.8 5.2 %transfer.3 = (f32[4,64,128]{2,1,0:T(8,128)S(1)}, f32[28,64,128]{2,1,0:T(8,128)S(1)}, f32[4,64,128]{2,1,0:T(8,128)S(1)}, f32[28,64,128]{2,1,0:T(8,128)S(1)}) custom-call(s32[256]{0:T(256)S(1)} %get-tuple-element.21.place_ref, s32[256]{0:T(256)S(1)} %get-tuple-element.22.sender_ref, s32[1]{0:T(128)} %copy.6.live_ref, bf16[256,64,128]{2,1,0:T(8,128)(2,1)S(1)} %copy-done.2, ...), custom_call_target="tpu_custom_call" | custom-call | flops 1073741824 | bytes 16777216 | tf_op jit(solution)/shard_map/transfer/pallas_call | solution.py:114
  72.1 0.5 collective-permute-start.21
  72.5 2.0 %collective-permute-done.16 = f32[28,64,128]{2,1,0:T(8,128)S(1)} collective-permute-done((f32[28,64,128]{2,1,0:T(8,128)S(1)}, f32[28,64,128]{2,1,0:T(8,128)S(1)}, u32[]{:S(2)}, u32[]{:S(2)}) %collective-permute-start.16) | collective-permute-done | bytes 917536 | tf_op jit(solution)/shard_map/ppermute | solution.py:169
  74.5 2.5 %collective-permute-start.17 = (f32[8,64,128]{2,1,0:T(8,128)S(1)}, f32[8,64,128]{2,1,0:T(8,128)S(1)}, u32[]{:S(2)}, u32[]{:S(2)}) collective-permute-start(f32[8,64,128]{2,1,0:T(8,128)S(1)} %slice_add_fusion.5), channel_id=1, source_target_pairs={{0,2},{1,0},{2,4},{3,1},{4,6},{5,3},{6,7},{7,5},{8,10},{9,8},{10,1... | collective-permute-start | bytes 786440 | tf_op jit(solution)/shard_map/ppermute | solution.py:178
  77.1 1.3 %collective-permute-start.22 = (f32[8,64,128]{2,1,0:T(8,128)S(1)}, f32[8,64,128]{2,1,0:T(8,128)S(1)}, u32[]{:S(2)}, u32[]{:S(2)}) collective-permute-start(f32[8,64,128]{2,1,0:T(8,128)S(1)} %slice_add_fusion.2), channel_id=1, source_target_pairs={{0,2},{1,0},{2,4},{3,1},{4,6},{5,3},{6,7},{7,5},{8,10},{9,8},{10,1... | collective-permute-start | bytes 786440 | tf_op jit(solution)/shard_map/ppermute | solution.py:178
  78.4 2.6 %collective-permute-done.17 = f32[8,64,128]{2,1,0:T(8,128)S(1)} collective-permute-done((f32[8,64,128]{2,1,0:T(8,128)S(1)}, f32[8,64,128]{2,1,0:T(8,128)S(1)}, u32[]{:S(2)}, u32[]{:S(2)}) %collective-permute-start.17) | collective-permute-done | bytes 262176 | tf_op jit(solution)/shard_map/ppermute | solution.py:178
  81.0 2.5 %collective-permute-start.18 = (f32[8,64,128]{2,1,0:T(8,128)S(1)}, f32[8,64,128]{2,1,0:T(8,128)S(1)}, u32[]{:S(2)}, u32[]{:S(2)}) collective-permute-start(f32[8,64,128]{2,1,0:T(8,128)S(1)} %fusion.3), channel_id=1, source_target_pairs={{0,2},{1,0},{2,4},{3,1},{4,6},{5,3},{6,7},{7,5},{8,10},{9,8},{10,1... | collective-permute-start | bytes 786440 | tf_op jit(solution)/shard_map/ppermute | solution.py:178
  83.8 2.5 %collective-permute-start.23 = (f32[8,64,128]{2,1,0:T(8,128)S(1)}, f32[8,64,128]{2,1,0:T(8,128)S(1)}, u32[]{:S(2)}, u32[]{:S(2)}) collective-permute-start(f32[8,64,128]{2,1,0:T(8,128)S(1)} %fusion.1), channel_id=1, source_target_pairs={{0,2},{1,0},{2,4},{3,1},{4,6},{5,3},{6,7},{7,5},{8,10},{9,8},{10,1... | collective-permute-start | bytes 786440 | tf_op jit(solution)/shard_map/ppermute | solution.py:178
  86.3 1.1 %collective-permute-done.18 = f32[8,64,128]{2,1,0:T(8,128)S(1)} collective-permute-done((f32[8,64,128]{2,1,0:T(8,128)S(1)}, f32[8,64,128]{2,1,0:T(8,128)S(1)}, u32[]{:S(2)}, u32[]{:S(2)}) %collective-permute-start.18) | collective-permute-done | bytes 262176 | tf_op jit(solution)/shard_map/ppermute | solution.py:178
  87.4 2.5 %collective-permute-start.19 = (f32[8,64,128]{2,1,0:T(8,128)S(1)}, f32[8,64,128]{2,1,0:T(8,128)S(1)}, u32[]{:S(2)}, u32[]{:S(2)}) collective-permute-start(f32[8,64,128]{2,1,0:T(8,128)S(1)} %fusion.2), channel_id=1, source_target_pairs={{0,2},{1,0},{2,4},{3,1},{4,6},{5,3},{6,7},{7,5},{8,10},{9,8},{10,1... | collective-permute-start | bytes 786440 | tf_op jit(solution)/shard_map/ppermute | solution.py:178
  90.2 2.5 %collective-permute-start.24 = (f32[8,64,128]{2,1,0:T(8,128)S(1)}, f32[8,64,128]{2,1,0:T(8,128)S(1)}, u32[]{:S(2)}, u32[]{:S(2)}) collective-permute-start(f32[8,64,128]{2,1,0:T(8,128)S(1)} %fusion), channel_id=1, source_target_pairs={{0,2},{1,0},{2,4},{3,1},{4,6},{5,3},{6,7},{7,5},{8,10},{9,8},{10,1... | collective-permute-start | bytes 786440 | tf_op jit(solution)/shard_map/ppermute | solution.py:178
  92.7 1.1 %collective-permute-done.19 = f32[8,64,128]{2,1,0:T(8,128)S(1)} collective-permute-done((f32[8,64,128]{2,1,0:T(8,128)S(1)}, f32[8,64,128]{2,1,0:T(8,128)S(1)}, u32[]{:S(2)}, u32[]{:S(2)}) %collective-permute-start.19) | collective-permute-done | bytes 262176 | tf_op jit(solution)/shard_map/ppermute | solution.py:178
  93.9 2.7 %collective-permute-done.24 = f32[8,64,128]{2,1,0:T(8,128)S(1)} collective-permute-done((f32[8,64,128]{2,1,0:T(8,128)S(1)}, f32[8,64,128]{2,1,0:T(8,128)S(1)}, u32[]{:S(2)}, u32[]{:S(2)}) %collective-permute-start.24) | collective-permute-done | bytes 262176 | tf_op jit(solution)/shard_map/ppermute | solution.py:178
  96.8 1.3 %collective-permute-done.25 = f32[4,64,128]{2,1,0:T(8,128)S(1)} collective-permute-done((f32[4,64,128]{2,1,0:T(8,128)S(1)}, f32[4,64,128]{2,1,0:T(8,128)S(1)}, u32[]{:S(2)}, u32[]{:S(2)}) %collective-permute-start.25) | collective-permute-done | bytes 131104 | tf_op jit(solution)/shard_map/ppermute | solution.py:182
  98.1 0.7 maximum_add_fusion.1
  (52 shorter events, 1.9 us)
Async XLA Ops:
  0.0 14.9 %collective-permute-start.2 = (f32[8,64,128]{2,1,0:T(8,128)}, f32[8,64,128]{2,1,0:T(8,128)S(1)}, u32[]{:S(2)}, u32[]{:S(2)}) collective-permute-start(f32[8,64,128]{2,1,0:T(8,128)} %rest_0_.1), channel_id=1, source_target_pairs={{24,0},{16,8},{8,16},{0,24},{25,1},{17,9},{9,17},{1,25},{26,2},{18... | collective-permute-start | bytes 786440 | tf_op jit(solution)/shard_map/ppermute | solution.py:165
  3.9 12.1 %collective-permute-start.1 = (f32[8,64,128]{2,1,0:T(8,128)}, f32[8,64,128]{2,1,0:T(8,128)S(1)}, u32[]{:S(2)}, u32[]{:S(2)}) collective-permute-start(f32[8,64,128]{2,1,0:T(8,128)} %rest_0_.1), channel_id=1, source_target_pairs={{16,0},{24,8},{0,16},{8,24},{17,1},{25,9},{1,17},{9,25},{18,2},{26... | collective-permute-start | bytes 786440 | tf_op jit(solution)/shard_map/ppermute | solution.py:165
  4.4 11.9 %collective-permute-start = (f32[8,64,128]{2,1,0:T(8,128)}, f32[8,64,128]{2,1,0:T(8,128)S(1)}, u32[]{:S(2)}, u32[]{:S(2)}) collective-permute-start(f32[8,64,128]{2,1,0:T(8,128)} %rest_0_.1), channel_id=1, source_target_pairs={{8,0},{0,8},{24,16},{16,24},{9,1},{1,9},{25,17},{17,25},{10,2},{2,... | collective-permute-start | bytes 786440 | tf_op jit(solution)/shard_map/ppermute | solution.py:165
  5.1 2.2 %copy-start.3 = (f32[256,64,64]{0,2,1:T(8,128)S(1)}, f32[256,64,64]{0,2,1:T(8,128)}, u32[]{:S(2)}) copy-start(f32[256,64,64]{0,2,1:T(8,128)} %param.6) | copy-start | bytes 12582916
  7.3 7.6 %copy-start.7 = (s32[256]{0:T(256)S(1)}, s32[256]{0:T(256)}, u32[]{:S(2)}) copy-start(s32[256]{0:T(256)} %param.7) | copy-start | bytes 3076
  7.3 7.6 %copy-start.8 = (s32[256]{0:T(256)S(1)}, s32[256]{0:T(256)}, u32[]{:S(2)}) copy-start(s32[256]{0:T(256)} %param.8) | copy-start | bytes 3076
  7.3 9.0 %copy-start.4 = (f32[8,64,128]{2,1,0:T(8,128)S(1)}, f32[8,64,128]{2,1,0:T(8,128)}, u32[]{:S(2)}) copy-start(f32[8,64,128]{2,1,0:T(8,128)} %rest_0_.1) | copy-start | bytes 786436
  12.9 2.0 %copy-start = (bf16[256,64,128]{2,1,0:T(8,128)(2,1)}, bf16[256,64,128]{2,1,0:T(8,128)(2,1)S(1)}, u32[]{:S(2)}) copy-start(bf16[256,64,128]{2,1,0:T(8,128)(2,1)S(1)} %prepare.1.a_ref) | copy-start | bytes 12582916
  16.3 2.2 %copy-start.1 = (bf16[256,64,128]{2,1,0:T(8,128)(2,1)S(1)}, bf16[256,64,128]{2,1,0:T(8,128)(2,1)}, u32[]{:S(2)}) copy-start(bf16[256,64,128]{2,1,0:T(8,128)(2,1)} %copy-done) | copy-start | bytes 12582916
  23.7 2.5 %collective-permute-start.3 = (f32[28,64,128]{2,1,0:T(8,128)S(1)}, f32[28,64,128]{2,1,0:T(8,128)S(1)}, u32[]{:S(2)}, u32[]{:S(2)}) collective-permute-start(f32[28,64,128]{2,1,0:T(8,128)S(1)} %get-tuple-element.14), channel_id=1, source_target_pairs={{0,1},{1,0},{2,3},{3,2},{4,5},{5,4},{6,7},{7,6},{8,9},{9,8},{10,11... | collective-permute-start | bytes 2752520 | tf_op jit(solution)/shard_map/ppermute | solution.py:169
  23.8 4.1 %collective-permute-start.8 = (f32[28,64,128]{2,1,0:T(8,128)S(1)}, f32[28,64,128]{2,1,0:T(8,128)S(1)}, u32[]{:S(2)}, u32[]{:S(2)}) collective-permute-start(f32[28,64,128]{2,1,0:T(8,128)S(1)} %get-tuple-element.16), channel_id=1, source_target_pairs={{0,1},{1,0},{2,3},{3,2},{4,5},{5,4},{6,7},{7,6},{8,9},{9,8},{10,11... | collective-permute-start | bytes 2752520 | tf_op jit(solution)/shard_map/ppermute | solution.py:169
  26.2 2.7 %copy-start.6 = (f32[28,64,128]{2,1,0:T(8,128)}, f32[28,64,128]{2,1,0:T(8,128)S(1)}, u32[]{:S(2)}) copy-start(f32[28,64,128]{2,1,0:T(8,128)S(1)} %collective-permute-done.3) | copy-start | bytes 2752516
  26.3 5.5 %collective-permute-start.4 = (f32[8,64,128]{2,1,0:T(8,128)S(1)}, f32[8,64,128]{2,1,0:T(8,128)S(1)}, u32[]{:S(2)}, u32[]{:S(2)}) collective-permute-start(f32[8,64,128]{2,1,0:T(8,128)S(1)} %slice_add_fusion.11), channel_id=1, source_target_pairs={{0,2},{1,0},{2,4},{3,1},{4,6},{5,3},{6,7},{7,5},{8,10},{9,8},{10,1... | collective-permute-start | bytes 786440 | tf_op jit(solution)/shard_map/ppermute | solution.py:178
  27.9 1.0 copy-start.5
  28.9 6.4 %collective-permute-start.9 = (f32[8,64,128]{2,1,0:T(8,128)S(1)}, f32[8,64,128]{2,1,0:T(8,128)S(1)}, u32[]{:S(2)}, u32[]{:S(2)}) collective-permute-start(f32[8,64,128]{2,1,0:T(8,128)S(1)} %slice_add_fusion.8), channel_id=1, source_target_pairs={{0,2},{1,0},{2,4},{3,1},{4,6},{5,3},{6,7},{7,5},{8,10},{9,8},{10,1... | collective-permute-start | bytes 786440 | tf_op jit(solution)/shard_map/ppermute | solution.py:178
  30.2 36.6 %copy-start.2 = (bf16[256,64,128]{2,1,0:T(8,128)(2,1)S(1)}, bf16[256,64,128]{2,1,0:T(8,128)(2,1)}, u32[]{:S(2)}) copy-start(bf16[256,64,128]{2,1,0:T(8,128)(2,1)} %copy-done) | copy-start | bytes 12582916
  32.8 6.4 %collective-permute-start.5 = (f32[8,64,128]{2,1,0:T(8,128)S(1)}, f32[8,64,128]{2,1,0:T(8,128)S(1)}, u32[]{:S(2)}, u32[]{:S(2)}) collective-permute-start(f32[8,64,128]{2,1,0:T(8,128)S(1)} %fusion.7), channel_id=1, source_target_pairs={{0,2},{1,0},{2,4},{3,1},{4,6},{5,3},{6,7},{7,5},{8,10},{9,8},{10,1... | collective-permute-start | bytes 786440 | tf_op jit(solution)/shard_map/ppermute | solution.py:178
  36.3 6.4 %collective-permute-start.10 = (f32[8,64,128]{2,1,0:T(8,128)S(1)}, f32[8,64,128]{2,1,0:T(8,128)S(1)}, u32[]{:S(2)}, u32[]{:S(2)}) collective-permute-start(f32[8,64,128]{2,1,0:T(8,128)S(1)} %fusion.5), channel_id=1, source_target_pairs={{0,2},{1,0},{2,4},{3,1},{4,6},{5,3},{6,7},{7,5},{8,10},{9,8},{10,1... | collective-permute-start | bytes 786440 | tf_op jit(solution)/shard_map/ppermute | solution.py:178
  40.2 6.4 %collective-permute-start.6 = (f32[8,64,128]{2,1,0:T(8,128)S(1)}, f32[8,64,128]{2,1,0:T(8,128)S(1)}, u32[]{:S(2)}, u32[]{:S(2)}) collective-permute-start(f32[8,64,128]{2,1,0:T(8,128)S(1)} %fusion.6), channel_id=1, source_target_pairs={{0,2},{1,0},{2,4},{3,1},{4,6},{5,3},{6,7},{7,5},{8,10},{9,8},{10,1... | collective-permute-start | bytes 786440 | tf_op jit(solution)/shard_map/ppermute | solution.py:178
  43.7 5.7 %collective-permute-start.11 = (f32[8,64,128]{2,1,0:T(8,128)S(1)}, f32[8,64,128]{2,1,0:T(8,128)S(1)}, u32[]{:S(2)}, u32[]{:S(2)}) collective-permute-start(f32[8,64,128]{2,1,0:T(8,128)S(1)} %fusion.4), channel_id=1, source_target_pairs={{0,2},{1,0},{2,4},{3,1},{4,6},{5,3},{6,7},{7,5},{8,10},{9,8},{10,1... | collective-permute-start | bytes 786440 | tf_op jit(solution)/shard_map/ppermute | solution.py:178
  46.6 2.9 %collective-permute-start.7 = (f32[4,64,128]{2,1,0:T(8,128)S(1)}, f32[4,64,128]{2,1,0:T(8,128)S(1)}, u32[]{:S(2)}, u32[]{:S(2)}) collective-permute-start(f32[4,64,128]{2,1,0:T(8,128)S(1)} %slice.149), channel_id=1, source_target_pairs={{0,1},{1,0},{2,3},{3,2},{4,5},{5,4},{6,7},{7,6},{8,9},{9,8},{10,11... | collective-permute-start | bytes 393224 | tf_op jit(solution)/shard_map/ppermute | solution.py:182
  49.4 1.4 %collective-permute-start.12 = (f32[4,64,128]{2,1,0:T(8,128)S(1)}, f32[4,64,128]{2,1,0:T(8,128)S(1)}, u32[]{:S(2)}, u32[]{:S(2)}) collective-permute-start(f32[4,64,128]{2,1,0:T(8,128)S(1)} %slice.155), channel_id=1, source_target_pairs={{0,1},{1,0},{2,3},{3,2},{4,5},{5,4},{6,7},{7,6},{8,9},{9,8},{10,11... | collective-permute-start | bytes 393224 | tf_op jit(solution)/shard_map/ppermute | solution.py:182
  51.8 10.2 %collective-permute-start.15 = (f32[8,64,128]{2,1,0:T(8,128)S(1)}, f32[8,64,128]{2,1,0:T(8,128)S(1)}, u32[]{:S(2)}, u32[]{:S(2)}) collective-permute-start(f32[8,64,128]{2,1,0:T(8,128)S(1)} %maximum_add_fusion.rest_0_), channel_id=1, source_target_pairs={{24,0},{16,8},{8,16},{0,24},{25,1},{17,9},{9,17},{1,25},{26,2},{18... | collective-permute-start | bytes 786440 | tf_op jit(solution)/shard_map/ppermute | solution.py:165
  53.5 13.2 %collective-permute-start.14 = (f32[8,64,128]{2,1,0:T(8,128)S(1)}, f32[8,64,128]{2,1,0:T(8,128)S(1)}, u32[]{:S(2)}, u32[]{:S(2)}) collective-permute-start(f32[8,64,128]{2,1,0:T(8,128)S(1)} %maximum_add_fusion.rest_0_), channel_id=1, source_target_pairs={{16,0},{24,8},{0,16},{8,24},{17,1},{25,9},{1,17},{9,25},{18,2},{26... | collective-permute-start | bytes 786440 | tf_op jit(solution)/shard_map/ppermute | solution.py:165
  54.0 12.8 %collective-permute-start.13 = (f32[8,64,128]{2,1,0:T(8,128)S(1)}, f32[8,64,128]{2,1,0:T(8,128)S(1)}, u32[]{:S(2)}, u32[]{:S(2)}) collective-permute-start(f32[8,64,128]{2,1,0:T(8,128)S(1)} %maximum_add_fusion.rest_0_), channel_id=1, source_target_pairs={{8,0},{0,8},{24,16},{16,24},{9,1},{1,9},{25,17},{17,25},{10,2},{2,... | collective-permute-start | bytes 786440 | tf_op jit(solution)/shard_map/ppermute | solution.py:165
  72.0 2.5 %collective-permute-start.16 = (f32[28,64,128]{2,1,0:T(8,128)S(1)}, f32[28,64,128]{2,1,0:T(8,128)S(1)}, u32[]{:S(2)}, u32[]{:S(2)}) collective-permute-start(f32[28,64,128]{2,1,0:T(8,128)S(1)} %get-tuple-element.18), channel_id=1, source_target_pairs={{0,1},{1,0},{2,3},{3,2},{4,5},{5,4},{6,7},{7,6},{8,9},{9,8},{10,11... | collective-permute-start | bytes 2752520 | tf_op jit(solution)/shard_map/ppermute | solution.py:169
  72.1 5.0 %collective-permute-start.21 = (f32[28,64,128]{2,1,0:T(8,128)S(1)}, f32[28,64,128]{2,1,0:T(8,128)S(1)}, u32[]{:S(2)}, u32[]{:S(2)}) collective-permute-start(f32[28,64,128]{2,1,0:T(8,128)S(1)} %get-tuple-element.20), channel_id=1, source_target_pairs={{0,1},{1,0},{2,3},{3,2},{4,5},{5,4},{6,7},{7,6},{8,9},{9,8},{10,11... | collective-permute-start | bytes 2752520 | tf_op jit(solution)/shard_map/ppermute | solution.py:169
  74.5 6.4 %collective-permute-start.17 = (f32[8,64,128]{2,1,0:T(8,128)S(1)}, f32[8,64,128]{2,1,0:T(8,128)S(1)}, u32[]{:S(2)}, u32[]{:S(2)}) collective-permute-start(f32[8,64,128]{2,1,0:T(8,128)S(1)} %slice_add_fusion.5), channel_id=1, source_target_pairs={{0,2},{1,0},{2,4},{3,1},{4,6},{5,3},{6,7},{7,5},{8,10},{9,8},{10,1... | collective-permute-start | bytes 786440 | tf_op jit(solution)/shard_map/ppermute | solution.py:178
  77.1 6.7 %collective-permute-start.22 = (f32[8,64,128]{2,1,0:T(8,128)S(1)}, f32[8,64,128]{2,1,0:T(8,128)S(1)}, u32[]{:S(2)}, u32[]{:S(2)}) collective-permute-start(f32[8,64,128]{2,1,0:T(8,128)S(1)} %slice_add_fusion.2), channel_id=1, source_target_pairs={{0,2},{1,0},{2,4},{3,1},{4,6},{5,3},{6,7},{7,5},{8,10},{9,8},{10,1... | collective-permute-start | bytes 786440 | tf_op jit(solution)/shard_map/ppermute | solution.py:178
  81.0 6.4 %collective-permute-start.18 = (f32[8,64,128]{2,1,0:T(8,128)S(1)}, f32[8,64,128]{2,1,0:T(8,128)S(1)}, u32[]{:S(2)}, u32[]{:S(2)}) collective-permute-start(f32[8,64,128]{2,1,0:T(8,128)S(1)} %fusion.3), channel_id=1, source_target_pairs={{0,2},{1,0},{2,4},{3,1},{4,6},{5,3},{6,7},{7,5},{8,10},{9,8},{10,1... | collective-permute-start | bytes 786440 | tf_op jit(solution)/shard_map/ppermute | solution.py:178
  83.8 6.4 %collective-permute-start.23 = (f32[8,64,128]{2,1,0:T(8,128)S(1)}, f32[8,64,128]{2,1,0:T(8,128)S(1)}, u32[]{:S(2)}, u32[]{:S(2)}) collective-permute-start(f32[8,64,128]{2,1,0:T(8,128)S(1)} %fusion.1), channel_id=1, source_target_pairs={{0,2},{1,0},{2,4},{3,1},{4,6},{5,3},{6,7},{7,5},{8,10},{9,8},{10,1... | collective-permute-start | bytes 786440 | tf_op jit(solution)/shard_map/ppermute | solution.py:178
  87.4 6.4 %collective-permute-start.19 = (f32[8,64,128]{2,1,0:T(8,128)S(1)}, f32[8,64,128]{2,1,0:T(8,128)S(1)}, u32[]{:S(2)}, u32[]{:S(2)}) collective-permute-start(f32[8,64,128]{2,1,0:T(8,128)S(1)} %fusion.2), channel_id=1, source_target_pairs={{0,2},{1,0},{2,4},{3,1},{4,6},{5,3},{6,7},{7,5},{8,10},{9,8},{10,1... | collective-permute-start | bytes 786440 | tf_op jit(solution)/shard_map/ppermute | solution.py:178
  90.2 6.4 %collective-permute-start.24 = (f32[8,64,128]{2,1,0:T(8,128)S(1)}, f32[8,64,128]{2,1,0:T(8,128)S(1)}, u32[]{:S(2)}, u32[]{:S(2)}) collective-permute-start(f32[8,64,128]{2,1,0:T(8,128)S(1)} %fusion), channel_id=1, source_target_pairs={{0,2},{1,0},{2,4},{3,1},{4,6},{5,3},{6,7},{7,5},{8,10},{9,8},{10,1... | collective-permute-start | bytes 786440 | tf_op jit(solution)/shard_map/ppermute | solution.py:178
  93.9 2.9 %collective-permute-start.20 = (f32[4,64,128]{2,1,0:T(8,128)S(1)}, f32[4,64,128]{2,1,0:T(8,128)S(1)}, u32[]{:S(2)}, u32[]{:S(2)}) collective-permute-start(f32[4,64,128]{2,1,0:T(8,128)S(1)} %slice.161), channel_id=1, source_target_pairs={{0,1},{1,0},{2,3},{3,2},{4,5},{5,4},{6,7},{7,6},{8,9},{9,8},{10,11... | collective-permute-start | bytes 393224 | tf_op jit(solution)/shard_map/ppermute | solution.py:182
  96.7 1.4 %collective-permute-start.25 = (f32[4,64,128]{2,1,0:T(8,128)S(1)}, f32[4,64,128]{2,1,0:T(8,128)S(1)}, u32[]{:S(2)}, u32[]{:S(2)}) collective-permute-start(f32[4,64,128]{2,1,0:T(8,128)S(1)} %slice.167), channel_id=1, source_target_pairs={{0,1},{1,0},{2,3},{3,2},{4,5},{5,4},{6,7},{7,6},{8,9},{9,8},{10,11... | collective-permute-start | bytes 393224 | tf_op jit(solution)/shard_map/ppermute | solution.py:182

commit v2 on v0

v2 whole, which is shorter than its diff:
```python
import functools

import jax
import jax.numpy as jnp
from jax import lax
from jax.experimental import pallas as pl
from jax.experimental.pallas import tpu as pltpu
from jax.sharding import PartitionSpec as P

ITERS = 2
HALVES = 2
GROUP = 32
CHUNK = 16
PLAN_HEAD = 8
MIB = 2**20
SMALL = 2 * MIB
BF16 = jnp.bfloat16
F32 = jnp.float32


def split_parts(value):
    high = value.astype(BF16)
    low = (value - high.astype(F32)).astype(BF16)
    return high, low


def prepare_kernel(b_hbm, o_ref, b_ref, t_ref, sems):
    cells, _, slots = b_hbm.shape
    width = min(128, slots)
    rounds = cells // CHUNK
    copies = [
        pltpu.make_async_copy(b_hbm.at[pl.ds(r * CHUNK, CHUNK)], b_ref.at[pl.ds(r * CHUNK, CHUNK)], sems.at[r])
        for r in range(rounds)
    ]
    for copy in copies:
        copy.start()
    o_ref[slots] = jnp.zeros(o_ref.shape[1:], BF16)
    for r in range(rounds):
        copies[r].wait()

        def turn(i, carry, r=r):
            for c in range(slots // width):
                value = b_ref[r * CHUNK + i, :, pl.ds(c * width, width)]
                high = value.astype(BF16).astype(F32)
                t_ref[i, pl.ds(c * width, width), :] = jnp.concatenate([high, value - high], axis=0).T
            return carry

        lax.fori_loop(0, CHUNK, turn, 0, unroll=4)

        def regroup(g, carry, r=r):
            first = pl.multiple_of(g * 8, 8)
            o_ref[pl.ds(first, 8), pl.ds(r * CHUNK, CHUNK), :] = jnp.swapaxes(t_ref[:, pl.ds(first, 8), :], 0, 1).astype(BF16)
            return carry

        lax.fori_loop(0, slots // 8, regroup, 0, unroll=2)


def prepare(blocks):
    slots, cells, _ = blocks.shape
    return pl.pallas_call(
        prepare_kernel,
        in_specs=[pl.BlockSpec(memory_space=pltpu.HBM)],
        out_specs=pl.BlockSpec(memory_space=pltpu.VMEM),
        out_shape=jax.ShapeDtypeStruct((slots + 1, cells, 2 * cells), BF16),
        scratch_shapes=[
            pltpu.VMEM((cells, cells, slots), F32),
            pltpu.VMEM((CHUNK, slots, 2 * cells), F32),
            pltpu.SemaphoreType.DMA((cells // CHUNK,)),
        ],
        compiler_params=pltpu.CompilerParams(vmem_limit_bytes=14 * MIB),
        cost_estimate=pl.CostEstimate(flops=0, bytes_accessed=24 * MIB, transcendentals=0),
        name="prepare",
    )(pltpu.with_memory_space_constraint(jnp.transpose(blocks, (1, 2, 0)), pltpu.HBM))


def transfer_kernel(fields_at, jobs, n_before, plan_ref, a_ref, *rest):
    x_refs, rest = rest[: len(fields_at)], rest[len(fields_at) :]
    before_refs, out_refs, w_ref = rest[:n_before], rest[-1 - len(jobs) : -1], rest[-1]
    zero_slot, cells = a_ref.shape[0] - 1, a_ref.shape[1]
    length = (plan_ref.shape[0] - PLAN_HEAD) // 3
    for x_ref, at in zip(x_refs, fields_at):

        def split_brick(c, carry, x_ref=x_ref, at=at):
            w_ref[at + c] = jnp.concatenate(split_parts(x_ref[c]), axis=0)
            return carry

        lax.fori_loop(0, x_ref.shape[0], split_brick, 0, unroll=True)

    for n, ((begin, end), out_ref) in enumerate(zip(jobs, out_refs)):

        def clear(c, carry, n=n, out_ref=out_ref):
            out_ref[c] = before_refs[n][c] if n_before else jnp.zeros(out_ref.shape[1:], F32)
            return carry

        lax.fori_loop(0, out_ref.shape[0], clear, 0, unroll=4)
        first, last = plan_ref[begin], plan_ref[end]

        def step(g, carry, first=first, last=last, out_ref=out_ref):
            results, targets = [], []
            for u in range(GROUP):
                s = first + g * GROUP + u
                inside = s < last
                a = a_ref[jnp.where(inside, plan_ref[PLAN_HEAD + s], zero_slot)]
                w = w_ref[plan_ref[PLAN_HEAD + 2 * length + s]]
                targets.append(plan_ref[PLAN_HEAD + length + s])
                high, low = w[:cells], w[cells:]
                results.append(
                    jnp.dot(
                        jnp.concatenate([a, a], axis=1),
                        jnp.concatenate([high, high, low, low], axis=0),
                        preferred_element_type=F32,
                    )
                )
            for u in range(GROUP):
                out_ref[targets[u]] += results[u]
            return carry

        lax.fori_loop(0, (last - first + GROUP - 1) // GROUP, step, 0)


def transfer(plan, matrix, fields, fields_at, senders, jobs, before, out_bricks):
    cells, lights = fields[0].shape[1:]
    whole = pl.BlockSpec(memory_space=pltpu.VMEM)
    scratch = senders * 2 * cells * lights * 2
    rows = matrix.shape[0] * cells * sum(end - begin for begin, end in jobs) // HALVES**2
    return pl.pallas_call(
        functools.partial(transfer_kernel, fields_at, jobs, len(before)),
        in_specs=[pl.BlockSpec(memory_space=pltpu.SMEM)] + [whole] * (1 + len(fields) + len(before)),
        out_specs=[whole] * len(jobs),
        out_shape=[jax.ShapeDtypeStruct((out_bricks, cells, lights), F32)] * len(jobs),
        scratch_shapes=[pltpu.VMEM((senders, 2 * cells, lights), BF16)],
        compiler_params=pltpu.CompilerParams(vmem_limit_bytes=SMALL + scratch),
        cost_estimate=pl.CostEstimate(flops=2 * rows * 4 * cells * lights, bytes_accessed=8 * MIB, transcendentals=0),
        name="transfer",
    )(plan, matrix, *fields, *before)


def first_of_line():
    me, n = lax.axis_index("col"), lax.axis_size("col")
    return jnp.where(me % 2 == 0, me == 0, me == n - 1)


def small_call(kernel, out_bricks, name, *args, after=()):
    whole, anywhere = pl.BlockSpec(memory_space=pltpu.VMEM), pl.BlockSpec(memory_space=pl.ANY)
    shape = args[0].shape[1:]
    return pl.pallas_call(
        kernel,
        in_specs=[whole] * len(args) + [anywhere] * len(after),
        out_specs=[whole] * len(out_bricks),
        out_shape=[jax.ShapeDtypeStruct((n, *shape), F32) for n in out_bricks],
        compiler_params=pltpu.CompilerParams(vmem_limit_bytes=SMALL),
        cost_estimate=pl.CostEstimate(flops=0, bytes_accessed=MIB, transcendentals=0),
        name=name,
    )(*args, *after)


def block_of(distance):
    return {0: 1, 1: 0}.get(distance, distance)


def carry_kernel(mine, other, sums_ref, got_ref, *rest):
    came_refs, out_ref = rest[:-1], rest[-1]
    first = first_of_line()
    for c in range(out_ref.shape[0]):
        total = sums_ref[mine + c] + got_ref[other + c]
        if came_refs:
            total += jnp.where(first, 0.0, came_refs[0][c])
        out_ref[c] = total


def finish_kernel(n_halves, half_at, own, source_ref, *rest):
    out_ref = rest[-1]
    first = first_of_line()
    per = (len(rest) - 1) // n_halves
    for h in range(n_halves):
        sums_ref, got_ref, *ends = rest[h * per : (h + 1) * per]
        half = out_ref.shape[0] // n_halves
        for c in range(half):
            total = source_ref[(half_at + h) * half + c] + (sums_ref[own + c] + got_ref[half + c])
            if ends:
                total += jnp.where(first, 0.0, ends[0][c]) + ends[1][c]
            out_ref[h * half + c] = total


def cross_kernel(n_after, came_ref, *rest):
    out_ref = rest[n_after]
    half = out_ref.shape[0]
    first = first_of_line()
    for c in range(half):
        out_ref[c] = jnp.where(first, 0.0, came_ref[half + c])


def tail_kernel(value_ref, _, out_ref):
    out_ref[...] = value_ref[value_ref.shape[0] - out_ref.shape[0] :]


def make_plan(row_index, col_index, live, bricks, n_row, n_col, flips):
    pairs, half = n_col // 2, bricks // HALVES
    my_row, me = lax.axis_index("row"), lax.axis_index("col")
    my_pair, my_side = me // 2, me % 2
    column, brick = row_index // bricks, row_index % bricks
    pair, side = column // 2, column % 2
    ahead = jnp.where(my_side == 0, pair - my_pair, my_pair - pair) % pairs
    ahead = jnp.where(ahead < 2, 1 - ahead, ahead) if pairs > 1 else ahead
    carrier = jnp.where(pair > my_pair, 0, jnp.where(pair < my_pair, 1, my_side))
    place = (ahead * 2 + (side ^ carrier)) * half + brick % half

    from_row, from_brick = col_index // bricks, col_index % bricks
    turn = from_row ^ my_row if flips else (from_row - my_row) % n_row
    sender = turn * bricks + from_brick

    n = row_index.shape[0]
    slots = jnp.arange(n, dtype=jnp.int32)
    part = (brick // half) * HALVES + from_brick // half
    part = jnp.where(slots < live, part, HALVES**2)
    key = part * n + slots
    rank = jnp.sum(key[None, :] < key[:, None], axis=1, dtype=jnp.int32)
    chosen = rank[None, :] == jnp.arange(n + GROUP, dtype=jnp.int32)[:, None]

    def in_order(value):
        return jnp.sum(jnp.where(chosen, value[None, :], 0), axis=1, dtype=jnp.int32)

    bounds = jnp.arange(PLAN_HEAD, dtype=jnp.int32)
    starts = jnp.sum(part[None, :] < bounds[:, None], axis=1, dtype=jnp.int32)
    return jnp.concatenate([starts, in_order(slots), in_order(place), in_order(sender)])


def body(source, blocks, row_index, col_index, live_count):
    bricks = source.shape[0]
    n_row, n_col = lax.axis_size("row"), lax.axis_size("col")
    pairs, half = n_col // 2, bricks // HALVES
    block = 2 * half
    flips = n_row & (n_row - 1) == 0

    swap = [(i, i ^ 1) for i in range(n_col)]
    ring = [(i, (i + 2 if i + 2 < n_col else n_col - 1) if i % 2 == 0 else (i - 2 if i > 2 else 0)) for i in range(n_col)]
    def from_turn(value, k):
        return lax.ppermute(value, "row", [(i ^ k if flips else (i + k) % n_row, i) for i in range(n_row)])

    def gather(value, at, forward=None):
        if n_row != 4 or forward is None:
            fields = [value] + [from_turn(value, k) for k in range(1, n_row)]
            return fields, [k * bricks + at for k in range(n_row)]
        one, two = from_turn(value, 1), from_turn(value, 2)
        low, high = one[:forward], two[forward:]
        fields, places = [value, one, two], [at, bricks + at, 2 * bricks + at]
        if low.shape[0]:
            fields, places = fields + [from_turn(low, 2)], places + [3 * bricks + at]
        if high.shape[0]:
            fields, places = fields + [from_turn(high, 1)], places + [3 * bricks + at + forward]
        return fields, places

    own = block if pairs > 1 else 0

    def begin(sums):
        if pairs == 1:
            return [sums, lax.ppermute(sums, "col", swap)]
        lead = lax.ppermute(sums[:block], "col", swap)
        mine = block_of(pairs - 1) * block
        total = small_call(functools.partial(carry_kernel, mine, 0), (block,), "carry", sums, lead)[0]
        later = small_call(tail_kernel, (sums.shape[0] - block,), "tail", sums, after=(total,))[0]
        return [sums, lax.ppermute(later, "col", swap), total]

    def scatter(sums, rest, *total, after=()):
        for distance in range(pairs - 1, 0, -1):
            came = lax.ppermute(total[0], "col", ring)
            if distance == 1:
                kernel = functools.partial(cross_kernel, len(after))
                crossing = small_call(kernel, (half,), "cross", came, after=after)[0]
                return sums, rest, came, lax.ppermute(crossing, "col", swap)
            mine, other = block_of(distance - 1) * block, (block_of(pairs - distance + 1) - 1) * block
            kernel = functools.partial(carry_kernel, mine, other)
            total = small_call(kernel, (block,), "carry", sums, rest, came)
        return sums, rest

    def finish(parts, half_at):
        args = [a for p in parts for a in p]
        kernel = functools.partial(finish_kernel, len(parts), half_at, own)
        return small_call(kernel, (len(parts) * half,), "finish", source, *args)[0]

    plan = make_plan(row_index, col_index, live_count[0], bricks, n_row, n_col, flips)
    matrix = prepare(blocks)
    apply = functools.partial(transfer, plan, matrix)
    senders, out_bricks = n_row * bricks, half * n_col

    fields, at = gather(source, 0)
    sums = apply(fields, at, senders, ((0, 2), (2, 4)), (), out_bricks)
    for _ in range(ITERS - 1):
        chains = [begin(s) for s in sums]
        halves = []
        for h in range(HALVES):
            halves.append(finish([scatter(*chains[h], after=halves)], h))
        near, near_at = gather(halves[0], 0, half)
        far, far_at = gather(halves[1], half, 0)
        sums = apply(near, near_at, senders, ((0, 1), (2, 3)), (), out_bricks)
        sums = apply(far, far_at, senders, ((1, 2), (3, 4)), sums, out_bricks)
    chains = [begin(s) for s in sums]
    return finish([scatter(*chains[h]) for h in range(HALVES)], 0)


def solution(mesh):
    in_specs = (
        P(("row", "col"), None, None),
        P(("row", "col"), None, None),
        P(("row", "col")),
        P(("row", "col")),
        P(("row", "col")),
    )
    out_specs = P(("row", "col"), None, None)
    return jax.shard_map(body, mesh=mesh, in_specs=in_specs, out_specs=out_specs, check_vma=False)
```

time: 244 us -> 90.6 us (0.37)
  waiting for transfers between devices: 119 us -> 28.7 us
  other arithmetic: 55.7 us -> 1.38 us
  starting transfers between devices: 0.31 us -> 43.6 us
  matrix products: 29.4 us -> 0 us
  local copies, waits for them, and re-layouts: 23.7 us -> 0.08 us
  Pallas kernels: 0 us -> 15.3 us
  between operations: 13.9 us -> 0.91 us
    reduce_scatter x2 -> x0, waiting for transfers between devices: 72 us -> none  [body(): lax.psum_scatter(partial_value, 'col', scatter_dimension=0, tiled=True)]
    scatter-add x2 -> x0, other arithmetic: 52.3 us -> none  [local_transfer(): summed = jax.ops.segment_sum(products, row_ids, num_segments=group_rows + 1)]
    all_gather x2 -> x0, waiting for transfers between devices: 46.6 us -> none  [body(): gathered = lax.all_gather(field, 'row', axis=0, tiled=True)]
    ppermute x0 -> x33, starting transfers between devices: none -> 43.6 us  [the longest x12 30.6 us: scatter(): came = lax.ppermute(total[0], 'col', ring)]
    dot_general x2 -> x0, matrix products: 29.4 us -> none  [local_transfer(): jnp.einsum('nij,njl->nil', blocks, picked, precision=lax.Precision.HIGHEST)]
    ppermute x0 -> x33, waiting for transfers between devices: none -> 28.7 us  [the longest x12 12.6 us: scatter(): came = lax.ppermute(total[0], 'col', ring)]
    pallas_call x0 -> x27, Pallas kernels: none -> 15.3 us  [the longest x3 6.98 us: transfer(): pl.pallas_call(functools.partial(transfer_kernel, fields_at, jobs, len(be...]
    gather x2 -> x0, local copies, waits for them, and re-layouts: 11.1 us -> none  [local_transfer(): picked = jnp.take(gathered, col_index, axis=0)]
  transfers between devices with their start and end apart: 4 -> 33, of which waited for: 4 -> 23; matrix products, arithmetic and copies ran while one was open for 4% -> 2% of each run, Pallas kernels for 0% -> 11%
where the time goes in v2:
time: 90.6 us; the launch traced here: 90 us
  starting transfers between devices  43.6 us (48%)
  waiting for transfers between devices  28.7 us (32%)
  Pallas kernels  15.3 us (17%)
  other arithmetic  1.38 us (2%)
  between operations  0.91 us (1%)
    ppermute x12, starting transfers between devices, scatter(): came = lax.ppermute(total[0], 'col', ring)  30.6 us
    ppermute x12, waiting for transfers between devices, scatter(): came = lax.ppermute(total[0], 'col', ring)  12.6 us
    ppermute x9, waiting for transfers between devices, from_turn(): lax.ppermute(value, 'row', [(i ^ k if flips else (i + k) % n_row, i) for...  10.6 us
    ppermute x9, starting transfers between devices, from_turn(): lax.ppermute(value, 'row', [(i ^ k if flips else (i + k) % n_row, i) for...  8.84 us
    pallas_call x3, Pallas kernels, transfer(): pl.pallas_call(functools.partial(transfer_kernel, fields_at, jobs, len(be...  6.98 us
    pallas_call x1, Pallas kernels, prepare(): pl.pallas_call(prepare_kernel, in_specs=[pl.BlockSpec(memory_space=pltpu....  6.68 us
    ppermute x4, waiting for transfers between devices, scatter(): return (sums, rest, came, lax.ppermute(crossing, 'col', swap))  3.32 us
    ppermute x4, starting transfers between devices, begin(): lead = lax.ppermute(sums[:block], 'col', swap)  2.42 us
  transfers between devices with their start and end apart: 33, of which 23 were waited for; matrix products, arithmetic and copies ran while one was open for 2% of the time, Pallas kernels for 11%

profile of v2, /device:TPU:0, one launch (start us, length us, event | category | flops | bytes accessed | tf_op | source)
XLA Modules:
  0.0 90.0 jit_solution(6102886298882419749)
XLA Ops:
  0.0 3.9 %collective-permute-start.2 = (f32[8,64,128]{2,1,0:T(8,128)}, f32[8,64,128]{2,1,0:T(8,128)S(1)}, u32[]{:S(2)}, u32[]{:S(2)}) collective-permute-start(f32[8,64,128]{2,1,0:T(8,128)} %source_ref.5), channel_id=1, source_target_pairs={{24,0},{16,8},{8,16},{0,24},{25,1},{17,9},{9,17},{1,25},{26,2},{18... | collective-permute-start | bytes 786440 | tf_op jit(solution)/shard_map/ppermute | solution.py:238
  3.9 0.5 collective-permute-start.1
  5.1 0.7 iota_add_fusion
  6.2 6.7 %prepare.1.a_ref = bf16[257,64,128]{2,1,0:T(8,128)(2,1)S(1)} custom-call(f32[64,64,256]{2,1,0:T(8,128)} %bitcast.3), custom_call_target="tpu_custom_call" | custom-call | bytes 25165824 | tf_op jit(solution)/shard_map/prepare/pallas_call | solution.py:60
  13.2 2.8 %collective-permute-done.1.rest_2_ = f32[8,64,128]{2,1,0:T(8,128)S(1)} collective-permute-done((f32[8,64,128]{2,1,0:T(8,128)}, f32[8,64,128]{2,1,0:T(8,128)S(1)}, u32[]{:S(2)}, u32[]{:S(2)}) %collective-permute-start.1) | collective-permute-done | bytes 262176 | tf_op jit(solution)/shard_map/ppermute | solution.py:238
  16.0 0.3 collective-permute-done.rest_1_
  16.3 3.1 %transfer.3 = (f32[32,64,128]{2,1,0:T(8,128)S(1)}, f32[32,64,128]{2,1,0:T(8,128)S(1)}) custom-call(s32[872]{0:T(1024)S(1)} %pad_add_fusion.plan_ref, bf16[257,64,128]{2,1,0:T(8,128)(2,1)S(1)} %prepare.1.a_ref, f32[8,64,128]{2,1,0:T(8,128)S(1)} %copy-done, f32[8,64,128]{2,1,0:T(8,128)S(1)} %collective-permute-done.rest_1_, ...), custom_call_target="tpu_custom_call" | custom-call | flops 1077936128 | bytes 8388608 | tf_op jit(solution)/shard_map/transfer/pallas_call | solution.py:126
  19.5 1.1 %collective-permute-start.8 = (f32[8,64,128]{2,1,0:T(8,128)S(1)}, f32[8,64,128]{2,1,0:T(8,128)S(1)}, u32[]{:S(2)}, u32[]{:S(2)}) collective-permute-start(f32[8,64,128]{2,1,0:T(8,128)S(1)} %slice.13), channel_id=1, source_target_pairs={{0,1},{1,0},{2,3},{3,2},{4,5},{5,4},{6,7},{7,6},{8,9},{9,8},{10,11... | collective-permute-start | bytes 786440 | tf_op jit(solution)/shard_map/ppermute | solution.py:258
  20.7 1.1 %collective-permute-done.8.got_ref = f32[8,64,128]{2,1,0:T(8,128)S(1)} collective-permute-done((f32[8,64,128]{2,1,0:T(8,128)S(1)}, f32[8,64,128]{2,1,0:T(8,128)S(1)}, u32[]{:S(2)}, u32[]{:S(2)}) %collective-permute-start.8) | collective-permute-done | bytes 262176 | tf_op jit(solution)/shard_map/ppermute | solution.py:258
  21.8 0.4 collective-permute-start.9
  22.6 2.1 %collective-permute-start.10 = (f32[8,64,128]{2,1,0:T(8,128)S(1)}, f32[8,64,128]{2,1,0:T(8,128)S(1)}, u32[]{:S(2)}, u32[]{:S(2)}) collective-permute-start(f32[8,64,128]{2,1,0:T(8,128)S(1)} %carry.15._), channel_id=1, source_target_pairs={{0,2},{1,0},{2,4},{3,1},{4,6},{5,3},{6,7},{7,5},{8,10},{9,8},{10,1... | collective-permute-start | bytes 786440 | tf_op jit(solution)/shard_map/ppermute | solution.py:266
  24.8 2.0 %collective-permute-start.5 = (f32[8,64,128]{2,1,0:T(8,128)S(1)}, f32[8,64,128]{2,1,0:T(8,128)S(1)}, u32[]{:S(2)}, u32[]{:S(2)}) collective-permute-start(f32[8,64,128]{2,1,0:T(8,128)S(1)} %carry.12._), channel_id=1, source_target_pairs={{0,2},{1,0},{2,4},{3,1},{4,6},{5,3},{6,7},{7,5},{8,10},{9,8},{10,1... | collective-permute-start | bytes 786440 | tf_op jit(solution)/shard_map/ppermute | solution.py:266
  26.8 1.9 %collective-permute-done.10.rest_0_ = f32[8,64,128]{2,1,0:T(8,128)S(1)} collective-permute-done((f32[8,64,128]{2,1,0:T(8,128)S(1)}, f32[8,64,128]{2,1,0:T(8,128)S(1)}, u32[]{:S(2)}, u32[]{:S(2)}) %collective-permute-start.10) | collective-permute-done | bytes 262176 | tf_op jit(solution)/shard_map/ppermute | solution.py:266
  28.7 2.5 %collective-permute-start.11 = (f32[8,64,128]{2,1,0:T(8,128)S(1)}, f32[8,64,128]{2,1,0:T(8,128)S(1)}, u32[]{:S(2)}, u32[]{:S(2)}) collective-permute-start(f32[8,64,128]{2,1,0:T(8,128)S(1)} %carry.16), channel_id=1, source_target_pairs={{0,2},{1,0},{2,4},{3,1},{4,6},{5,3},{6,7},{7,5},{8,10},{9,8},{10,1... | collective-permute-start | bytes 786440 | tf_op jit(solution)/shard_map/ppermute | solution.py:266
  31.5 2.5 %collective-permute-start.6 = (f32[8,64,128]{2,1,0:T(8,128)S(1)}, f32[8,64,128]{2,1,0:T(8,128)S(1)}, u32[]{:S(2)}, u32[]{:S(2)}) collective-permute-start(f32[8,64,128]{2,1,0:T(8,128)S(1)} %carry.13), channel_id=1, source_target_pairs={{0,2},{1,0},{2,4},{3,1},{4,6},{5,3},{6,7},{7,5},{8,10},{9,8},{10,1... | collective-permute-start | bytes 786440 | tf_op jit(solution)/shard_map/ppermute | solution.py:266
  34.0 1.1 %collective-permute-done.11.rest_0_ = f32[8,64,128]{2,1,0:T(8,128)S(1)} collective-permute-done((f32[8,64,128]{2,1,0:T(8,128)S(1)}, f32[8,64,128]{2,1,0:T(8,128)S(1)}, u32[]{:S(2)}, u32[]{:S(2)}) %collective-permute-start.11) | collective-permute-done | bytes 262176 | tf_op jit(solution)/shard_map/ppermute | solution.py:266
  35.2 2.5 %collective-permute-start.12 = (f32[8,64,128]{2,1,0:T(8,128)S(1)}, f32[8,64,128]{2,1,0:T(8,128)S(1)}, u32[]{:S(2)}, u32[]{:S(2)}) collective-permute-start(f32[8,64,128]{2,1,0:T(8,128)S(1)} %carry.17), channel_id=1, source_target_pairs={{0,2},{1,0},{2,4},{3,1},{4,6},{5,3},{6,7},{7,5},{8,10},{9,8},{10,1... | collective-permute-start | bytes 786440 | tf_op jit(solution)/shard_map/ppermute | solution.py:266
  38.0 2.5 %collective-permute-start.7 = (f32[8,64,128]{2,1,0:T(8,128)S(1)}, f32[8,64,128]{2,1,0:T(8,128)S(1)}, u32[]{:S(2)}, u32[]{:S(2)}) collective-permute-start(f32[8,64,128]{2,1,0:T(8,128)S(1)} %carry.14), channel_id=1, source_target_pairs={{0,2},{1,0},{2,4},{3,1},{4,6},{5,3},{6,7},{7,5},{8,10},{9,8},{10,1... | collective-permute-start | bytes 786440 | tf_op jit(solution)/shard_map/ppermute | solution.py:266
  40.5 1.1 %collective-permute-done.12.came_ref.rest_2_ = f32[8,64,128]{2,1,0:T(8,128)S(1)} collective-permute-done((f32[8,64,128]{2,1,0:T(8,128)S(1)}, f32[8,64,128]{2,1,0:T(8,128)S(1)}, u32[]{:S(2)}, u32[]{:S(2)}) %collective-permute-start.12) | collective-permute-done | bytes 262176 | tf_op jit(solution)/shard_map/ppermute | solution.py:266
  41.7 1.3 %collective-permute-done.13.rest_3_ = f32[4,64,128]{2,1,0:T(8,128)S(1)} collective-permute-done((f32[4,64,128]{2,1,0:T(8,128)S(1)}, f32[4,64,128]{2,1,0:T(8,128)S(1)}, u32[]{:S(2)}, u32[]{:S(2)}) %collective-permute-start.13) | collective-permute-done | bytes 131104 | tf_op jit(solution)/shard_map/ppermute | solution.py:270
  43.0 1.3 %collective-permute-done.7.came_ref.rest_2_ = f32[8,64,128]{2,1,0:T(8,128)S(1)} collective-permute-done((f32[8,64,128]{2,1,0:T(8,128)S(1)}, f32[8,64,128]{2,1,0:T(8,128)S(1)}, u32[]{:S(2)}, u32[]{:S(2)}) %collective-permute-start.7) | collective-permute-done | bytes 262176 | tf_op jit(solution)/shard_map/ppermute | solution.py:266
  44.5 0.7 collective-permute-start.18
  45.2 0.7 collective-permute-done.14.rest_3_
  45.9 0.3 collective-permute-start.16
  46.2 1.8 %collective-permute-start.19 = (f32[4,64,128]{2,1,0:T(8,128)S(1)}, f32[4,64,128]{2,1,0:T(8,128)S(1)}, u32[]{:S(2)}, u32[]{:S(2)}) collective-permute-start(f32[4,64,128]{2,1,0:T(8,128)S(1)} %finish.3.rest_0_), channel_id=1, source_target_pairs={{16,0},{24,8},{0,16},{8,24},{17,1},{25,9},{1,17},{9,25},{18,2},{26... | collective-permute-start | bytes 393224 | tf_op jit(solution)/shard_map/ppermute | solution.py:238
  48.0 2.4 %collective-permute-done.18.rest_1_ = f32[4,64,128]{2,1,0:T(8,128)S(1)} collective-permute-done((f32[4,64,128]{2,1,0:T(8,128)S(1)}, f32[4,64,128]{2,1,0:T(8,128)S(1)}, u32[]{:S(2)}, u32[]{:S(2)}) %collective-permute-start.18) | collective-permute-done | bytes 131104 | tf_op jit(solution)/shard_map/ppermute | solution.py:238
  50.7 0.6 collective-permute-start.15
  51.3 1.0 %collective-permute-done.16.rest_2_ = f32[4,64,128]{2,1,0:T(8,128)S(1)} collective-permute-done((f32[4,64,128]{2,1,0:T(8,128)S(1)}, f32[4,64,128]{2,1,0:T(8,128)S(1)}, u32[]{:S(2)}, u32[]{:S(2)}) %collective-permute-start.16) | collective-permute-done | bytes 131104 | tf_op jit(solution)/shard_map/ppermute | solution.py:238
  52.3 0.8 collective-permute-start.17
  53.0 2.0 %collective-permute-done.19.rest_2_ = f32[4,64,128]{2,1,0:T(8,128)S(1)} collective-permute-done((f32[4,64,128]{2,1,0:T(8,128)S(1)}, f32[4,64,128]{2,1,0:T(8,128)S(1)}, u32[]{:S(2)}, u32[]{:S(2)}) %collective-permute-start.19) | collective-permute-done | bytes 131104 | tf_op jit(solution)/shard_map/ppermute | solution.py:238
  55.1 2.0 %collective-permute-done.20.rest_3_ = f32[4,64,128]{2,1,0:T(8,128)S(1)} collective-permute-done((f32[4,64,128]{2,1,0:T(8,128)S(1)}, f32[4,64,128]{2,1,0:T(8,128)S(1)}, u32[]{:S(2)}, u32[]{:S(2)}) %collective-permute-start.20) | collective-permute-done | bytes 131104 | tf_op jit(solution)/shard_map/ppermute | solution.py:238
  57.1 2.1 %transfer.4 = (f32[32,64,128]{2,1,0:T(8,128)S(1)}, f32[32,64,128]{2,1,0:T(8,128)S(1)}) custom-call(s32[872]{0:T(1024)S(1)} %pad_add_fusion.plan_ref, bf16[257,64,128]{2,1,0:T(8,128)(2,1)S(1)} %prepare.1.a_ref, f32[4,64,128]{2,1,0:T(8,128)S(1)} %finish.3.rest_0_, f32[4,64,128]{2,1,0:T(8,128)S(1)} %collective-permute-done.18.rest_1_, ...), custom_call_target="tpu_custom_call" | custom-call | flops 538968064 | bytes 8388608 | tf_op jit(solution)/shard_map/transfer/pallas_call | solution.py:126
  59.3 1.7 %transfer.5 = (f32[32,64,128]{2,1,0:T(8,128)S(1)}, f32[32,64,128]{2,1,0:T(8,128)S(1)}) custom-call(s32[872]{0:T(1024)S(1)} %pad_add_fusion.plan_ref, bf16[257,64,128]{2,1,0:T(8,128)(2,1)S(1)} %prepare.1.a_ref, f32[4,64,128]{2,1,0:T(8,128)S(1)} %finish.4.rest_0_, f32[4,64,128]{2,1,0:T(8,128)S(1)} %collective-permute-done.15.rest_1_, ...), custom_call_target="tpu_custom_call" | custom-call | flops 538968064 | bytes 8388608 | tf_op jit(solution)/shard_map/transfer/pallas_call | solution.py:126
  61.0 1.1 %collective-permute-start.27 = (f32[8,64,128]{2,1,0:T(8,128)S(1)}, f32[8,64,128]{2,1,0:T(8,128)S(1)}, u32[]{:S(2)}, u32[]{:S(2)}) collective-permute-start(f32[8,64,128]{2,1,0:T(8,128)S(1)} %slice.15), channel_id=1, source_target_pairs={{0,1},{1,0},{2,3},{3,2},{4,5},{5,4},{6,7},{7,6},{8,9},{9,8},{10,11... | collective-permute-start | bytes 786440 | tf_op jit(solution)/shard_map/ppermute | solution.py:258
  62.3 1.1 %collective-permute-done.27.got_ref = f32[8,64,128]{2,1,0:T(8,128)S(1)} collective-permute-done((f32[8,64,128]{2,1,0:T(8,128)S(1)}, f32[8,64,128]{2,1,0:T(8,128)S(1)}, u32[]{:S(2)}, u32[]{:S(2)}) %collective-permute-start.27) | collective-permute-done | bytes 262176 | tf_op jit(solution)/shard_map/ppermute | solution.py:258
  63.4 0.4 collective-permute-start.28
  64.2 3.9 %collective-permute-start.29 = (f32[8,64,128]{2,1,0:T(8,128)S(1)}, f32[8,64,128]{2,1,0:T(8,128)S(1)}, u32[]{:S(2)}, u32[]{:S(2)}) collective-permute-start(f32[8,64,128]{2,1,0:T(8,128)S(1)} %carry.21._), channel_id=1, source_target_pairs={{0,2},{1,0},{2,4},{3,1},{4,6},{5,3},{6,7},{7,5},{8,10},{9,8},{10,1... | collective-permute-start | bytes 786440 | tf_op jit(solution)/shard_map/ppermute | solution.py:266
  68.2 2.5 %collective-permute-start.23 = (f32[8,64,128]{2,1,0:T(8,128)S(1)}, f32[8,64,128]{2,1,0:T(8,128)S(1)}, u32[]{:S(2)}, u32[]{:S(2)}) collective-permute-start(f32[8,64,128]{2,1,0:T(8,128)S(1)} %carry.18._), channel_id=1, source_target_pairs={{0,2},{1,0},{2,4},{3,1},{4,6},{5,3},{6,7},{7,5},{8,10},{9,8},{10,1... | collective-permute-start | bytes 786440 | tf_op jit(solution)/shard_map/ppermute | solution.py:266
  70.6 1.4 %collective-permute-done.29.rest_0_ = f32[8,64,128]{2,1,0:T(8,128)S(1)} collective-permute-done((f32[8,64,128]{2,1,0:T(8,128)S(1)}, f32[8,64,128]{2,1,0:T(8,128)S(1)}, u32[]{:S(2)}, u32[]{:S(2)}) %collective-permute-start.29) | collective-permute-done | bytes 262176 | tf_op jit(solution)/shard_map/ppermute | solution.py:266
  72.1 2.5 %collective-permute-start.30 = (f32[8,64,128]{2,1,0:T(8,128)S(1)}, f32[8,64,128]{2,1,0:T(8,128)S(1)}, u32[]{:S(2)}, u32[]{:S(2)}) collective-permute-start(f32[8,64,128]{2,1,0:T(8,128)S(1)} %carry.22), channel_id=1, source_target_pairs={{0,2},{1,0},{2,4},{3,1},{4,6},{5,3},{6,7},{7,5},{8,10},{9,8},{10,1... | collective-permute-start | bytes 786440 | tf_op jit(solution)/shard_map/ppermute | solution.py:266
  74.9 2.5 %collective-permute-start.24 = (f32[8,64,128]{2,1,0:T(8,128)S(1)}, f32[8,64,128]{2,1,0:T(8,128)S(1)}, u32[]{:S(2)}, u32[]{:S(2)}) collective-permute-start(f32[8,64,128]{2,1,0:T(8,128)S(1)} %carry.19), channel_id=1, source_target_pairs={{0,2},{1,0},{2,4},{3,1},{4,6},{5,3},{6,7},{7,5},{8,10},{9,8},{10,1... | collective-permute-start | bytes 786440 | tf_op jit(solution)/shard_map/ppermute | solution.py:266
  77.4 1.1 %collective-permute-done.30.rest_0_ = f32[8,64,128]{2,1,0:T(8,128)S(1)} collective-permute-done((f32[8,64,128]{2,1,0:T(8,128)S(1)}, f32[8,64,128]{2,1,0:T(8,128)S(1)}, u32[]{:S(2)}, u32[]{:S(2)}) %collective-permute-start.30) | collective-permute-done | bytes 262176 | tf_op jit(solution)/shard_map/ppermute | solution.py:266
  78.6 2.5 %collective-permute-start.31 = (f32[8,64,128]{2,1,0:T(8,128)S(1)}, f32[8,64,128]{2,1,0:T(8,128)S(1)}, u32[]{:S(2)}, u32[]{:S(2)}) collective-permute-start(f32[8,64,128]{2,1,0:T(8,128)S(1)} %carry.23), channel_id=1, source_target_pairs={{0,2},{1,0},{2,4},{3,1},{4,6},{5,3},{6,7},{7,5},{8,10},{9,8},{10,1... | collective-permute-start | bytes 786440 | tf_op jit(solution)/shard_map/ppermute | solution.py:266
  81.4 2.5 %collective-permute-start.25 = (f32[8,64,128]{2,1,0:T(8,128)S(1)}, f32[8,64,128]{2,1,0:T(8,128)S(1)}, u32[]{:S(2)}, u32[]{:S(2)}) collective-permute-start(f32[8,64,128]{2,1,0:T(8,128)S(1)} %carry.20), channel_id=1, source_target_pairs={{0,2},{1,0},{2,4},{3,1},{4,6},{5,3},{6,7},{7,5},{8,10},{9,8},{10,1... | collective-permute-start | bytes 786440 | tf_op jit(solution)/shard_map/ppermute | solution.py:266
  83.9 1.1 %collective-permute-done.31.came_ref.rest_6_ = f32[8,64,128]{2,1,0:T(8,128)S(1)} collective-permute-done((f32[8,64,128]{2,1,0:T(8,128)S(1)}, f32[8,64,128]{2,1,0:T(8,128)S(1)}, u32[]{:S(2)}, u32[]{:S(2)}) %collective-permute-start.31) | collective-permute-done | bytes 262176 | tf_op jit(solution)/shard_map/ppermute | solution.py:266
  85.1 2.7 %collective-permute-done.25.came_ref.rest_2_ = f32[8,64,128]{2,1,0:T(8,128)S(1)} collective-permute-done((f32[8,64,128]{2,1,0:T(8,128)S(1)}, f32[8,64,128]{2,1,0:T(8,128)S(1)}, u32[]{:S(2)}, u32[]{:S(2)}) %collective-permute-start.25) | collective-permute-done | bytes 262176 | tf_op jit(solution)/shard_map/ppermute | solution.py:266
  87.9 1.3 %collective-permute-done.26.rest_3_ = f32[4,64,128]{2,1,0:T(8,128)S(1)} collective-permute-done((f32[4,64,128]{2,1,0:T(8,128)S(1)}, f32[4,64,128]{2,1,0:T(8,128)S(1)}, u32[]{:S(2)}, u32[]{:S(2)}) %collective-permute-start.26) | collective-permute-done | bytes 131104 | tf_op jit(solution)/shard_map/ppermute | solution.py:270
  89.2 0.8 finish.5
  (56 shorter events, 4.0 us)
Async XLA Ops:
  0.0 13.2 %collective-permute-start.2 = (f32[8,64,128]{2,1,0:T(8,128)}, f32[8,64,128]{2,1,0:T(8,128)S(1)}, u32[]{:S(2)}, u32[]{:S(2)}) collective-permute-start(f32[8,64,128]{2,1,0:T(8,128)} %source_ref.5), channel_id=1, source_target_pairs={{24,0},{16,8},{8,16},{0,24},{25,1},{17,9},{9,17},{1,25},{26,2},{18... | collective-permute-start | bytes 786440 | tf_op jit(solution)/shard_map/ppermute | solution.py:238
  3.9 12.1 %collective-permute-start.1 = (f32[8,64,128]{2,1,0:T(8,128)}, f32[8,64,128]{2,1,0:T(8,128)S(1)}, u32[]{:S(2)}, u32[]{:S(2)}) collective-permute-start(f32[8,64,128]{2,1,0:T(8,128)} %source_ref.5), channel_id=1, source_target_pairs={{16,0},{24,8},{0,16},{8,24},{17,1},{25,9},{1,17},{9,25},{18,2},{26... | collective-permute-start | bytes 786440 | tf_op jit(solution)/shard_map/ppermute | solution.py:238
  4.4 11.9 %collective-permute-start = (f32[8,64,128]{2,1,0:T(8,128)}, f32[8,64,128]{2,1,0:T(8,128)S(1)}, u32[]{:S(2)}, u32[]{:S(2)}) collective-permute-start(f32[8,64,128]{2,1,0:T(8,128)} %source_ref.5), channel_id=1, source_target_pairs={{8,0},{0,8},{24,16},{16,24},{9,1},{1,9},{25,17},{17,25},{10,2},{2,... | collective-permute-start | bytes 786440 | tf_op jit(solution)/shard_map/ppermute | solution.py:238
  6.1 10.2 %copy-start = (f32[8,64,128]{2,1,0:T(8,128)S(1)}, f32[8,64,128]{2,1,0:T(8,128)}, u32[]{:S(2)}) copy-start(f32[8,64,128]{2,1,0:T(8,128)} %source_ref.5) | copy-start | bytes 786436
  19.5 2.3 %collective-permute-start.8 = (f32[8,64,128]{2,1,0:T(8,128)S(1)}, f32[8,64,128]{2,1,0:T(8,128)S(1)}, u32[]{:S(2)}, u32[]{:S(2)}) collective-permute-start(f32[8,64,128]{2,1,0:T(8,128)S(1)} %slice.13), channel_id=1, source_target_pairs={{0,1},{1,0},{2,3},{3,2},{4,5},{5,4},{6,7},{7,6},{8,9},{9,8},{10,11... | collective-permute-start | bytes 786440 | tf_op jit(solution)/shard_map/ppermute | solution.py:258
  20.6 1.7 %collective-permute-start.3 = (f32[8,64,128]{2,1,0:T(8,128)S(1)}, f32[8,64,128]{2,1,0:T(8,128)S(1)}, u32[]{:S(2)}, u32[]{:S(2)}) collective-permute-start(f32[8,64,128]{2,1,0:T(8,128)S(1)} %slice.12), channel_id=1, source_target_pairs={{0,1},{1,0},{2,3},{3,2},{4,5},{5,4},{6,7},{7,6},{8,9},{9,8},{10,11... | collective-permute-start | bytes 786440 | tf_op jit(solution)/shard_map/ppermute | solution.py:258
  21.8 6.8 %collective-permute-start.9 = (f32[24,64,128]{2,1,0:T(8,128)S(1)}, f32[24,64,128]{2,1,0:T(8,128)S(1)}, u32[]{:S(2)}, u32[]{:S(2)}) collective-permute-start(f32[24,64,128]{2,1,0:T(8,128)S(1)} %tail.5), channel_id=1, source_target_pairs={{0,1},{1,0},{2,3},{3,2},{4,5},{5,4},{6,7},{7,6},{8,9},{9,8},{10,11... | collective-permute-start | bytes 2359304 | tf_op jit(solution)/shard_map/ppermute | solution.py:262
  22.4 9.1 %collective-permute-start.4 = (f32[24,64,128]{2,1,0:T(8,128)S(1)}, f32[24,64,128]{2,1,0:T(8,128)S(1)}, u32[]{:S(2)}, u32[]{:S(2)}) collective-permute-start(f32[24,64,128]{2,1,0:T(8,128)S(1)} %tail.4), channel_id=1, source_target_pairs={{0,1},{1,0},{2,3},{3,2},{4,5},{5,4},{6,7},{7,6},{8,9},{9,8},{10,11... | collective-permute-start | bytes 2359304 | tf_op jit(solution)/shard_map/ppermute | solution.py:262
  22.6 6.0 %collective-permute-start.10 = (f32[8,64,128]{2,1,0:T(8,128)S(1)}, f32[8,64,128]{2,1,0:T(8,128)S(1)}, u32[]{:S(2)}, u32[]{:S(2)}) collective-permute-start(f32[8,64,128]{2,1,0:T(8,128)S(1)} %carry.15._), channel_id=1, source_target_pairs={{0,2},{1,0},{2,4},{3,1},{4,6},{5,3},{6,7},{7,5},{8,10},{9,8},{10,1... | collective-permute-start | bytes 786440 | tf_op jit(solution)/shard_map/ppermute | solution.py:266
  24.8 6.7 %collective-permute-start.5 = (f32[8,64,128]{2,1,0:T(8,128)S(1)}, f32[8,64,128]{2,1,0:T(8,128)S(1)}, u32[]{:S(2)}, u32[]{:S(2)}) collective-permute-start(f32[8,64,128]{2,1,0:T(8,128)S(1)} %carry.12._), channel_id=1, source_target_pairs={{0,2},{1,0},{2,4},{3,1},{4,6},{5,3},{6,7},{7,5},{8,10},{9,8},{10,1... | collective-permute-start | bytes 786440 | tf_op jit(solution)/shard_map/ppermute | solution.py:266
  28.7 6.4 %collective-permute-start.11 = (f32[8,64,128]{2,1,0:T(8,128)S(1)}, f32[8,64,128]{2,1,0:T(8,128)S(1)}, u32[]{:S(2)}, u32[]{:S(2)}) collective-permute-start(f32[8,64,128]{2,1,0:T(8,128)S(1)} %carry.16), channel_id=1, source_target_pairs={{0,2},{1,0},{2,4},{3,1},{4,6},{5,3},{6,7},{7,5},{8,10},{9,8},{10,1... | collective-permute-start | bytes 786440 | tf_op jit(solution)/shard_map/ppermute | solution.py:266
  31.5 6.4 %collective-permute-start.6 = (f32[8,64,128]{2,1,0:T(8,128)S(1)}, f32[8,64,128]{2,1,0:T(8,128)S(1)}, u32[]{:S(2)}, u32[]{:S(2)}) collective-permute-start(f32[8,64,128]{2,1,0:T(8,128)S(1)} %carry.13), channel_id=1, source_target_pairs={{0,2},{1,0},{2,4},{3,1},{4,6},{5,3},{6,7},{7,5},{8,10},{9,8},{10,1... | collective-permute-start | bytes 786440 | tf_op jit(solution)/shard_map/ppermute | solution.py:266
  35.2 6.4 %collective-permute-start.12 = (f32[8,64,128]{2,1,0:T(8,128)S(1)}, f32[8,64,128]{2,1,0:T(8,128)S(1)}, u32[]{:S(2)}, u32[]{:S(2)}) collective-permute-start(f32[8,64,128]{2,1,0:T(8,128)S(1)} %carry.17), channel_id=1, source_target_pairs={{0,2},{1,0},{2,4},{3,1},{4,6},{5,3},{6,7},{7,5},{8,10},{9,8},{10,1... | collective-permute-start | bytes 786440 | tf_op jit(solution)/shard_map/ppermute | solution.py:266
  38.0 6.4 %collective-permute-start.7 = (f32[8,64,128]{2,1,0:T(8,128)S(1)}, f32[8,64,128]{2,1,0:T(8,128)S(1)}, u32[]{:S(2)}, u32[]{:S(2)}) collective-permute-start(f32[8,64,128]{2,1,0:T(8,128)S(1)} %carry.14), channel_id=1, source_target_pairs={{0,2},{1,0},{2,4},{3,1},{4,6},{5,3},{6,7},{7,5},{8,10},{9,8},{10,1... | collective-permute-start | bytes 786440 | tf_op jit(solution)/shard_map/ppermute | solution.py:266
  41.6 1.4 %collective-permute-start.13 = (f32[4,64,128]{2,1,0:T(8,128)S(1)}, f32[4,64,128]{2,1,0:T(8,128)S(1)}, u32[]{:S(2)}, u32[]{:S(2)}) collective-permute-start(f32[4,64,128]{2,1,0:T(8,128)S(1)} %cross.4), channel_id=1, source_target_pairs={{0,1},{1,0},{2,3},{3,2},{4,5},{5,4},{6,7},{7,6},{8,9},{9,8},{10,11... | collective-permute-start | bytes 393224 | tf_op jit(solution)/shard_map/ppermute | solution.py:270
  44.4 1.4 %collective-permute-start.14 = (f32[4,64,128]{2,1,0:T(8,128)S(1)}, f32[4,64,128]{2,1,0:T(8,128)S(1)}, u32[]{:S(2)}, u32[]{:S(2)}) collective-permute-start(f32[4,64,128]{2,1,0:T(8,128)S(1)} %cross.5), channel_id=1, source_target_pairs={{0,1},{1,0},{2,3},{3,2},{4,5},{5,4},{6,7},{7,6},{8,9},{9,8},{10,11... | collective-permute-start | bytes 393224 | tf_op jit(solution)/shard_map/ppermute | solution.py:270
  44.5 5.9 %collective-permute-start.18 = (f32[4,64,128]{2,1,0:T(8,128)S(1)}, f32[4,64,128]{2,1,0:T(8,128)S(1)}, u32[]{:S(2)}, u32[]{:S(2)}) collective-permute-start(f32[4,64,128]{2,1,0:T(8,128)S(1)} %finish.3.rest_0_), channel_id=1, source_target_pairs={{8,0},{0,8},{24,16},{16,24},{9,1},{1,9},{25,17},{17,25},{10,2},{2,... | collective-permute-start | bytes 393224 | tf_op jit(solution)/shard_map/ppermute | solution.py:238
  45.9 6.4 %collective-permute-start.16 = (f32[4,64,128]{2,1,0:T(8,128)S(1)}, f32[4,64,128]{2,1,0:T(8,128)S(1)}, u32[]{:S(2)}, u32[]{:S(2)}) collective-permute-start(f32[4,64,128]{2,1,0:T(8,128)S(1)} %finish.4.rest_0_), channel_id=1, source_target_pairs={{16,0},{24,8},{0,16},{8,24},{17,1},{25,9},{1,17},{9,25},{18,2},{26... | collective-permute-start | bytes 393224 | tf_op jit(solution)/shard_map/ppermute | solution.py:238
  46.2 8.9 %collective-permute-start.19 = (f32[4,64,128]{2,1,0:T(8,128)S(1)}, f32[4,64,128]{2,1,0:T(8,128)S(1)}, u32[]{:S(2)}, u32[]{:S(2)}) collective-permute-start(f32[4,64,128]{2,1,0:T(8,128)S(1)} %finish.3.rest_0_), channel_id=1, source_target_pairs={{16,0},{24,8},{0,16},{8,24},{17,1},{25,9},{1,17},{9,25},{18,2},{26... | collective-permute-start | bytes 393224 | tf_op jit(solution)/shard_map/ppermute | solution.py:238
  50.4 6.7 %collective-permute-start.20 = (f32[4,64,128]{2,1,0:T(8,128)S(1)}, f32[4,64,128]{2,1,0:T(8,128)S(1)}, u32[]{:S(2)}, u32[]{:S(2)}) collective-permute-start(f32[4,64,128]{2,1,0:T(8,128)S(1)} %collective-permute-done.18.rest_1_), channel_id=1, source_target_pairs={{16,0},{24,8},{0,16},{8,24},{17,1},{25,9},{1,17},{9,25},{18,2},{26... | collective-permute-start | bytes 393224 | tf_op jit(solution)/shard_map/ppermute | solution.py:238
  50.7 8.6 %collective-permute-start.15 = (f32[4,64,128]{2,1,0:T(8,128)S(1)}, f32[4,64,128]{2,1,0:T(8,128)S(1)}, u32[]{:S(2)}, u32[]{:S(2)}) collective-permute-start(f32[4,64,128]{2,1,0:T(8,128)S(1)} %finish.4.rest_0_), channel_id=1, source_target_pairs={{8,0},{0,8},{24,16},{16,24},{9,1},{1,9},{25,17},{17,25},{10,2},{2,... | collective-permute-start | bytes 393224 | tf_op jit(solution)/shard_map/ppermute | solution.py:238
  52.3 7.0 %collective-permute-start.17 = (f32[4,64,128]{2,1,0:T(8,128)S(1)}, f32[4,64,128]{2,1,0:T(8,128)S(1)}, u32[]{:S(2)}, u32[]{:S(2)}) collective-permute-start(f32[4,64,128]{2,1,0:T(8,128)S(1)} %collective-permute-done.16.rest_2_), channel_id=1, source_target_pairs={{8,0},{0,8},{24,16},{16,24},{9,1},{1,9},{25,17},{17,25},{10,2},{2,... | collective-permute-start | bytes 393224 | tf_op jit(solution)/shard_map/ppermute | solution.py:238
  61.0 2.3 %collective-permute-start.27 = (f32[8,64,128]{2,1,0:T(8,128)S(1)}, f32[8,64,128]{2,1,0:T(8,128)S(1)}, u32[]{:S(2)}, u32[]{:S(2)}) collective-permute-start(f32[8,64,128]{2,1,0:T(8,128)S(1)} %slice.15), channel_id=1, source_target_pairs={{0,1},{1,0},{2,3},{3,2},{4,5},{5,4},{6,7},{7,6},{8,9},{9,8},{10,11... | collective-permute-start | bytes 786440 | tf_op jit(solution)/shard_map/ppermute | solution.py:258
  62.2 1.7 %collective-permute-start.21 = (f32[8,64,128]{2,1,0:T(8,128)S(1)}, f32[8,64,128]{2,1,0:T(8,128)S(1)}, u32[]{:S(2)}, u32[]{:S(2)}) collective-permute-start(f32[8,64,128]{2,1,0:T(8,128)S(1)} %slice.14), channel_id=1, source_target_pairs={{0,1},{1,0},{2,3},{3,2},{4,5},{5,4},{6,7},{7,6},{8,9},{9,8},{10,11... | collective-permute-start | bytes 786440 | tf_op jit(solution)/shard_map/ppermute | solution.py:258
  63.4 8.6 %collective-permute-start.28 = (f32[24,64,128]{2,1,0:T(8,128)S(1)}, f32[24,64,128]{2,1,0:T(8,128)S(1)}, u32[]{:S(2)}, u32[]{:S(2)}) collective-permute-start(f32[24,64,128]{2,1,0:T(8,128)S(1)} %tail.7), channel_id=1, source_target_pairs={{0,1},{1,0},{2,3},{3,2},{4,5},{5,4},{6,7},{7,6},{8,9},{9,8},{10,11... | collective-permute-start | bytes 2359304 | tf_op jit(solution)/shard_map/ppermute | solution.py:262
  64.0 10.9 %collective-permute-start.22 = (f32[24,64,128]{2,1,0:T(8,128)S(1)}, f32[24,64,128]{2,1,0:T(8,128)S(1)}, u32[]{:S(2)}, u32[]{:S(2)}) collective-permute-start(f32[24,64,128]{2,1,0:T(8,128)S(1)} %tail.6), channel_id=1, source_target_pairs={{0,1},{1,0},{2,3},{3,2},{4,5},{5,4},{6,7},{7,6},{8,9},{9,8},{10,11... | collective-permute-start | bytes 2359304 | tf_op jit(solution)/shard_map/ppermute | solution.py:262
  64.2 7.8 %collective-permute-start.29 = (f32[8,64,128]{2,1,0:T(8,128)S(1)}, f32[8,64,128]{2,1,0:T(8,128)S(1)}, u32[]{:S(2)}, u32[]{:S(2)}) collective-permute-start(f32[8,64,128]{2,1,0:T(8,128)S(1)} %carry.21._), channel_id=1, source_target_pairs={{0,2},{1,0},{2,4},{3,1},{4,6},{5,3},{6,7},{7,5},{8,10},{9,8},{10,1... | collective-permute-start | bytes 786440 | tf_op jit(solution)/shard_map/ppermute | solution.py:266
  68.2 6.7 %collective-permute-start.23 = (f32[8,64,128]{2,1,0:T(8,128)S(1)}, f32[8,64,128]{2,1,0:T(8,128)S(1)}, u32[]{:S(2)}, u32[]{:S(2)}) collective-permute-start(f32[8,64,128]{2,1,0:T(8,128)S(1)} %carry.18._), channel_id=1, source_target_pairs={{0,2},{1,0},{2,4},{3,1},{4,6},{5,3},{6,7},{7,5},{8,10},{9,8},{10,1... | collective-permute-start | bytes 786440 | tf_op jit(solution)/shard_map/ppermute | solution.py:266
  72.1 6.4 %collective-permute-start.30 = (f32[8,64,128]{2,1,0:T(8,128)S(1)}, f32[8,64,128]{2,1,0:T(8,128)S(1)}, u32[]{:S(2)}, u32[]{:S(2)}) collective-permute-start(f32[8,64,128]{2,1,0:T(8,128)S(1)} %carry.22), channel_id=1, source_target_pairs={{0,2},{1,0},{2,4},{3,1},{4,6},{5,3},{6,7},{7,5},{8,10},{9,8},{10,1... | collective-permute-start | bytes 786440 | tf_op jit(solution)/shard_map/ppermute | solution.py:266
  74.9 6.4 %collective-permute-start.24 = (f32[8,64,128]{2,1,0:T(8,128)S(1)}, f32[8,64,128]{2,1,0:T(8,128)S(1)}, u32[]{:S(2)}, u32[]{:S(2)}) collective-permute-start(f32[8,64,128]{2,1,0:T(8,128)S(1)} %carry.19), channel_id=1, source_target_pairs={{0,2},{1,0},{2,4},{3,1},{4,6},{5,3},{6,7},{7,5},{8,10},{9,8},{10,1... | collective-permute-start | bytes 786440 | tf_op jit(solution)/shard_map/ppermute | solution.py:266
  78.6 6.4 %collective-permute-start.31 = (f32[8,64,128]{2,1,0:T(8,128)S(1)}, f32[8,64,128]{2,1,0:T(8,128)S(1)}, u32[]{:S(2)}, u32[]{:S(2)}) collective-permute-start(f32[8,64,128]{2,1,0:T(8,128)S(1)} %carry.23), channel_id=1, source_target_pairs={{0,2},{1,0},{2,4},{3,1},{4,6},{5,3},{6,7},{7,5},{8,10},{9,8},{10,1... | collective-permute-start | bytes 786440 | tf_op jit(solution)/shard_map/ppermute | solution.py:266
  81.4 6.4 %collective-permute-start.25 = (f32[8,64,128]{2,1,0:T(8,128)S(1)}, f32[8,64,128]{2,1,0:T(8,128)S(1)}, u32[]{:S(2)}, u32[]{:S(2)}) collective-permute-start(f32[8,64,128]{2,1,0:T(8,128)S(1)} %carry.20), channel_id=1, source_target_pairs={{0,2},{1,0},{2,4},{3,1},{4,6},{5,3},{6,7},{7,5},{8,10},{9,8},{10,1... | collective-permute-start | bytes 786440 | tf_op jit(solution)/shard_map/ppermute | solution.py:266
  85.0 2.9 %collective-permute-start.32 = (f32[4,64,128]{2,1,0:T(8,128)S(1)}, f32[4,64,128]{2,1,0:T(8,128)S(1)}, u32[]{:S(2)}, u32[]{:S(2)}) collective-permute-start(f32[4,64,128]{2,1,0:T(8,128)S(1)} %cross.7), channel_id=1, source_target_pairs={{0,1},{1,0},{2,3},{3,2},{4,5},{5,4},{6,7},{7,6},{8,9},{9,8},{10,11... | collective-permute-start | bytes 393224 | tf_op jit(solution)/shard_map/ppermute | solution.py:270
  87.8 1.4 %collective-permute-start.26 = (f32[4,64,128]{2,1,0:T(8,128)S(1)}, f32[4,64,128]{2,1,0:T(8,128)S(1)}, u32[]{:S(2)}, u32[]{:S(2)}) collective-permute-start(f32[4,64,128]{2,1,0:T(8,128)S(1)} %cross.6), channel_id=1, source_target_pairs={{0,1},{1,0},{2,3},{3,2},{4,5},{5,4},{6,7},{7,6},{8,9},{9,8},{10,11... | collective-permute-start | bytes 393224 | tf_op jit(solution)/shard_map/ppermute | solution.py:270

commit v3 on v2

v3 whole, which is shorter than its diff:
```python
import functools

import jax
import jax.numpy as jnp
from jax import lax
from jax.experimental import pallas as pl
from jax.experimental.pallas import tpu as pltpu
from jax.sharding import PartitionSpec as P

ITERS = 2
HALVES = 2
STAGES = 3
GROUP = 32
CHUNK = 16
PLAN_HEAD = 8
MIB = 2**20
SMALL = 2 * MIB
BF16 = jnp.bfloat16
F32 = jnp.float32


def split_parts(value):
    high = value.astype(BF16)
    low = (value - high.astype(F32)).astype(BF16)
    return high, low


def prepare_kernel(b_hbm, o_ref, b_ref, t_ref, sems):
    cells, _, slots = b_hbm.shape
    width = min(128, slots)
    rounds = cells // CHUNK
    copies = [
        pltpu.make_async_copy(b_hbm.at[pl.ds(r * CHUNK, CHUNK)], b_ref.at[pl.ds(r * CHUNK, CHUNK)], sems.at[r])
        for r in range(rounds)
    ]
    for copy in copies:
        copy.start()
    o_ref[slots] = jnp.zeros(o_ref.shape[1:], BF16)
    for r in range(rounds):
        copies[r].wait()

        def turn(i, carry, r=r):
            for c in range(slots // width):
                value = b_ref[r * CHUNK + i, :, pl.ds(c * width, width)]
                high = value.astype(BF16).astype(F32)
                t_ref[i, pl.ds(c * width, width), :] = jnp.concatenate([high, value - high], axis=0).T
            return carry

        lax.fori_loop(0, CHUNK, turn, 0, unroll=4)

        def regroup(g, carry, r=r):
            first = pl.multiple_of(g * 8, 8)
            o_ref[pl.ds(first, 8), pl.ds(r * CHUNK, CHUNK), :] = jnp.swapaxes(t_ref[:, pl.ds(first, 8), :], 0, 1).astype(BF16)
            return carry

        lax.fori_loop(0, slots // 8, regroup, 0, unroll=2)


def prepare(blocks):
    slots, cells, _ = blocks.shape
    return pl.pallas_call(
        prepare_kernel,
        in_specs=[pl.BlockSpec(memory_space=pltpu.HBM)],
        out_specs=pl.BlockSpec(memory_space=pltpu.VMEM),
        out_shape=jax.ShapeDtypeStruct((slots + 1, cells, 2 * cells), BF16),
        scratch_shapes=[
            pltpu.VMEM((cells, cells, slots), F32),
            pltpu.VMEM((CHUNK, slots, 2 * cells), F32),
            pltpu.SemaphoreType.DMA((cells // CHUNK,)),
        ],
        compiler_params=pltpu.CompilerParams(vmem_limit_bytes=14 * MIB),
        cost_estimate=pl.CostEstimate(flops=0, bytes_accessed=24 * MIB, transcendentals=0),
        name="prepare",
    )(pltpu.with_memory_space_constraint(jnp.transpose(blocks, (1, 2, 0)), pltpu.HBM))


def transfer_kernel(fields_at, begin, end, has_before, plan_ref, a_ref, *rest):
    x_refs, (out_ref, w_ref) = rest[: len(fields_at)], rest[-2:]
    zero_slot, cells = a_ref.shape[0] - 1, a_ref.shape[1]
    length = (plan_ref.shape[0] - PLAN_HEAD) // 3
    for x_ref, at in zip(x_refs, fields_at):

        def split_brick(c, carry, x_ref=x_ref, at=at):
            w_ref[at + c] = jnp.concatenate(split_parts(x_ref[c]), axis=0)
            return carry

        lax.fori_loop(0, x_ref.shape[0], split_brick, 0, unroll=True)

    def clear(c, carry):
        out_ref[c] = rest[-3][c] if has_before else jnp.zeros(out_ref.shape[1:], F32)
        return carry

    lax.fori_loop(0, out_ref.shape[0], clear, 0, unroll=4)
    first, last = plan_ref[begin], plan_ref[end]

    def step(g, carry, size, first):
        results, targets = [], []
        for u in range(size):
            s = first + g * size + u
            a = a_ref[jnp.where(s < last, plan_ref[PLAN_HEAD + s], zero_slot)]
            w = w_ref[jnp.where(s < last, plan_ref[PLAN_HEAD + 2 * length + s], fields_at[0])]
            targets.append(plan_ref[PLAN_HEAD + length + s])
            high, low = w[:cells], w[cells:]
            results.append(
                jnp.dot(
                    jnp.concatenate([a, a], axis=1),
                    jnp.concatenate([high, high, low, low], axis=0),
                    preferred_element_type=F32,
                )
            )
        for u in range(size):
            out_ref[targets[u]] += results[u]
        return carry

    large = (last - first + GROUP // 2 - 1) // GROUP
    lax.fori_loop(0, large, functools.partial(step, size=GROUP, first=first), 0)
    rest_first = first + large * GROUP
    small = jnp.where(rest_first < last, 1, 0)
    lax.fori_loop(0, small, functools.partial(step, size=GROUP // 2, first=rest_first), 0)


def transfer(plan, matrix, fields, fields_at, senders, begin, end, before, out_bricks):
    cells, lights = fields[0].shape[1:]
    whole = pl.BlockSpec(memory_space=pltpu.VMEM)
    scratch = senders * 2 * cells * lights * 2
    rows = matrix.shape[0] * cells * (end - begin) // STAGES
    return pl.pallas_call(
        functools.partial(transfer_kernel, fields_at, begin, end, len(before)),
        in_specs=[pl.BlockSpec(memory_space=pltpu.SMEM)] + [whole] * (1 + len(fields) + len(before)),
        out_specs=whole,
        out_shape=jax.ShapeDtypeStruct((out_bricks, cells, lights), F32),
        scratch_shapes=[pltpu.VMEM((senders, 2 * cells, lights), BF16)],
        compiler_params=pltpu.CompilerParams(vmem_limit_bytes=SMALL + scratch),
        cost_estimate=pl.CostEstimate(flops=2 * rows * 4 * cells * lights, bytes_accessed=8 * MIB, transcendentals=0),
        name="transfer",
    )(plan, matrix, *fields, *before)


def first_of_line():
    me, n = lax.axis_index("col"), lax.axis_size("col")
    return jnp.where(me % 2 == 0, me == 0, me == n - 1)


def small_call(kernel, out_bricks, name, *args, after=()):
    whole, anywhere = pl.BlockSpec(memory_space=pltpu.VMEM), pl.BlockSpec(memory_space=pl.ANY)
    shape = args[0].shape[1:]
    return pl.pallas_call(
        kernel,
        in_specs=[whole] * len(args) + [anywhere] * len(after),
        out_specs=[whole] * len(out_bricks),
        out_shape=[jax.ShapeDtypeStruct((n, *shape), F32) for n in out_bricks],
        compiler_params=pltpu.CompilerParams(vmem_limit_bytes=SMALL),
        cost_estimate=pl.CostEstimate(flops=0, bytes_accessed=MIB, transcendentals=0),
        name=name,
    )(*args, *after)


def block_of(distance):
    return {0: 1, 1: 0}.get(distance, distance)


def carry_kernel(mine, other, sums_ref, got_ref, *rest):
    came_refs, out_ref = rest[:-1], rest[-1]
    first = first_of_line()
    for c in range(out_ref.shape[0]):
        total = sums_ref[mine + c] + got_ref[other + c]
        if came_refs:
            total += jnp.where(first, 0.0, came_refs[0][c])
        out_ref[c] = total


def finish_kernel(n_halves, half_at, owns, source_ref, sums_ref, *rest):
    out_ref = rest[-1]
    first = first_of_line()
    per = (len(rest) - 1) // n_halves
    for h in range(n_halves):
        got_ref, *ends = rest[h * per : (h + 1) * per]
        half = out_ref.shape[0] // n_halves
        for c in range(half):
            total = source_ref[(half_at + h) * half + c] + (sums_ref[owns[half_at + h] + c] + got_ref[half + c])
            if ends:
                total += jnp.where(first, 0.0, ends[0][c]) + ends[1][c]
            out_ref[h * half + c] = total


def cross_kernel(came_ref, *rest):
    out_ref = rest[-1]
    half = out_ref.shape[0]
    first = first_of_line()
    for c in range(half):
        out_ref[c] = jnp.where(first, 0.0, came_ref[half + c])


def cut_kernel(at, value_ref, *rest):
    out_ref = rest[-1]
    out_ref[...] = value_ref[at : at + out_ref.shape[0]]


def make_plan(row_index, col_index, live, bricks, n_row, n_col, flips):
    pairs, half = n_col // 2, bricks // HALVES
    my_row, me = lax.axis_index("row"), lax.axis_index("col")
    my_pair, my_side = me // 2, me % 2
    column, brick = row_index // bricks, row_index % bricks
    pair, side = column // 2, column % 2
    ahead = jnp.where(my_side == 0, pair - my_pair, my_pair - pair) % pairs
    ahead = jnp.where(ahead < 2, 1 - ahead, ahead) if pairs > 1 else ahead
    carrier = jnp.where(pair > my_pair, 0, jnp.where(pair < my_pair, 1, my_side))
    place = ((brick // half * pairs + ahead) * 2 + (side ^ carrier)) * half + brick % half

    from_row, from_brick = col_index // bricks, col_index % bricks
    turn = from_row ^ my_row if flips else (from_row - my_row) % n_row
    sender = turn * bricks + from_brick

    n = row_index.shape[0]
    slots = jnp.arange(n, dtype=jnp.int32)
    part = jnp.where(turn == 0, 0, jnp.where(turn < n_row - 1, 1, 2))
    part = jnp.where(slots < live, part, STAGES)
    key = part * n + slots
    rank = jnp.sum(key[None, :] < key[:, None], axis=1, dtype=jnp.int32)
    chosen = rank[None, :] == jnp.arange(n + GROUP, dtype=jnp.int32)[:, None]

    def in_order(value):
        return jnp.sum(jnp.where(chosen, value[None, :], 0), axis=1, dtype=jnp.int32)

    bounds = jnp.arange(PLAN_HEAD, dtype=jnp.int32)
    starts = jnp.sum(part[None, :] < bounds[:, None], axis=1, dtype=jnp.int32)
    return jnp.concatenate([starts, in_order(slots), in_order(place), in_order(sender)])


def body(source, blocks, row_index, col_index, live_count):
    bricks = source.shape[0]
    n_row, n_col = lax.axis_size("row"), lax.axis_size("col")
    pairs, half = n_col // 2, bricks // HALVES
    block = 2 * half
    flips = n_row & (n_row - 1) == 0

    swap = [(i, i ^ 1) for i in range(n_col)]
    ring = [(i, (i + 2 if i + 2 < n_col else n_col - 1) if i % 2 == 0 else (i - 2 if i > 2 else 0)) for i in range(n_col)]
    def from_turn(value, k):
        return lax.ppermute(value, "row", [(i ^ k if flips else (i + k) % n_row, i) for i in range(n_row)])

    def gather(values, direct):
        return [[from_turn(v, k) for v in values] for k in range(1, n_row if direct else n_row - 1)]

    def cut(value, at, size, after):
        return small_call(functools.partial(cut_kernel, at), (size,), "cut", value, after=after)[0]

    def forward(value, k, *after):
        return from_turn(cut(value, 0, value.shape[0], after), k)

    def apply(turns, first, end, *before):
        fields = [f for pieces in turns.values() for f in pieces]
        at = [k * bricks + i * (bricks // len(pieces)) for k, pieces in turns.items() for i in range(len(pieces))]
        return transfer(plan, matrix, fields, at, n_row * bricks, first, end, before, bricks * n_col)

    in_half = half * n_col
    owns = [h * in_half + (block if pairs > 1 else 0) for h in range(HALVES)]

    def begin(sums, h):
        base = h * in_half
        if pairs == 1:
            return [base, lax.ppermute(sums[base : base + in_half], "col", swap)]
        lead = lax.ppermute(sums[base : base + block], "col", swap)
        mine = base + block_of(pairs - 1) * block
        total = small_call(functools.partial(carry_kernel, mine, 0), (block,), "carry", sums, lead)[0]
        later = cut(sums, base + block, in_half - block, (total,))
        return [base, lax.ppermute(later, "col", swap), total]

    def scatter(sums, base, rest, *total, after=()):
        for distance in range(pairs - 1, 0, -1):
            came = lax.ppermute(total[0], "col", ring)
            if distance == 1:
                crossing = small_call(cross_kernel, (half,), "cross", came, after=after)[0]
                return rest, came, lax.ppermute(crossing, "col", swap)
            mine, other = base + block_of(distance - 1) * block, (block_of(pairs - distance + 1) - 1) * block
            kernel = functools.partial(carry_kernel, mine, other)
            total = small_call(kernel, (block,), "carry", sums, rest, came)
        return (rest,)

    def finish(sums, parts, half_at):
        args = [a for p in parts for a in p]
        kernel = functools.partial(finish_kernel, len(parts), half_at, owns)
        return small_call(kernel, (len(parts) * half,), "finish", source, sums, *args)[0]

    plan = make_plan(row_index, col_index, live_count[0], bricks, n_row, n_col, flips)
    matrix = prepare(blocks)

    others = gather([source], True)
    sums = apply({0: [source]}, 0, 1)
    sums = apply(dict(enumerate(others, 1)), 1, STAGES, sums)
    for _ in range(ITERS - 1):
        chains = [begin(sums, h) for h in range(HALVES)]
        field = []
        for h in range(HALVES):
            field.append(finish(sums, [scatter(sums, *chains[h], after=field)], h))
        sums = apply({0: field}, 0, 1)
        if n_row == 4:
            one, two = gather(field, False)
            last = [forward(one[0], 2, two[0], sums), forward(two[1], 1, one[1])]
            sums = apply({1: one, 2: two}, 1, 2, sums)
            sums = apply({3: last}, 2, STAGES, sums)
        else:
            sums = apply(dict(enumerate(gather(field, True), 1)), 1, STAGES, sums)
    chains = [begin(sums, h) for h in range(HALVES)]
    return finish(sums, [scatter(sums, *c) for c in chains], 0)


def solution(mesh):
    in_specs = (
        P(("row", "col"), None, None),
        P(("row", "col"), None, None),
        P(("row", "col")),
        P(("row", "col")),
        P(("row", "col")),
    )
    out_specs = P(("row", "col"), None, None)
    return jax.shard_map(body, mesh=mesh, in_specs=in_specs, out_specs=out_specs, check_vma=False)
```

time: 90.6 us -> 87.4 us (0.965)
  starting transfers between devices: 43.6 us -> 37.5 us
  Pallas kernels: 15.3 us -> 17.8 us
    ppermute x12, starting transfers between devices: 30.6 us -> 25.7 us  [scatter(): came = lax.ppermute(total[0], 'col', ring)]
    pallas_call x3 -> x5, Pallas kernels: 6.98 us -> 9.4 us  [transfer(): pl.pallas_call(functools.partial(transfer_kernel, fields_at, begin, end,...]
    ppermute x12, waiting for transfers between devices: 12.6 us -> 14.8 us  [scatter(): came = lax.ppermute(total[0], 'col', ring)]
    ppermute x12, starting transfers between devices: 4.13 us -> 2.55 us  [the longest x4 1.14 us: begin(): lead = lax.ppermute(sums[base:base + block], 'col', swap)]
  transfers between devices with their start and end apart: 33 -> 33, of which waited for: 23 -> 23; matrix products, arithmetic and copies ran while one was open for 2% -> 2% of each run, Pallas kernels for 11% -> 15%
where the time goes in v3:
time: 87.4 us; the launch traced here: 87.2 us
  starting transfers between devices  37.5 us (43%)
  waiting for transfers between devices  29.5 us (34%)
  Pallas kernels  17.8 us (20%)
  other arithmetic  1.4 us (2%)
  between operations  0.95 us (1%)
    ppermute x12, starting transfers between devices, scatter(): came = lax.ppermute(total[0], 'col', ring)  25.7 us
    ppermute x12, waiting for transfers between devices, scatter(): came = lax.ppermute(total[0], 'col', ring)  14.8 us
    ppermute x9, waiting for transfers between devices, from_turn(): lax.ppermute(value, 'row', [(i ^ k if flips else (i + k) % n_row, i) for...  9.8 us
    pallas_call x5, Pallas kernels, transfer(): pl.pallas_call(functools.partial(transfer_kernel, fields_at, begin, end,...  9.4 us
    ppermute x9, starting transfers between devices, from_turn(): lax.ppermute(value, 'row', [(i ^ k if flips else (i + k) % n_row, i) for...  9.22 us
    pallas_call x1, Pallas kernels, prepare(): pl.pallas_call(prepare_kernel, in_specs=[pl.BlockSpec(memory_space=pltpu....  6.68 us
    ppermute x4, waiting for transfers between devices, scatter(): return (rest, came, lax.ppermute(crossing, 'col', swap))  2.66 us
    ppermute x4, waiting for transfers between devices, begin(): lead = lax.ppermute(sums[base:base + block], 'col', swap)  2.21 us
  transfers between devices with their start and end apart: 33, of which 23 were waited for; matrix products, arithmetic and copies ran while one was open for 2% of the time, Pallas kernels for 15%

profile of v3, /device:TPU:0, one launch (start us, length us, event | category | flops | bytes accessed | tf_op | source)
XLA Modules:
  0.0 87.2 jit_solution(6053571800315436566)
XLA Ops:
  0.0 2.9 %collective-permute-start = (f32[8,64,128]{2,1,0:T(8,128)}, f32[8,64,128]{2,1,0:T(8,128)S(1)}, u32[]{:S(2)}, u32[]{:S(2)}) collective-permute-start(f32[8,64,128]{2,1,0:T(8,128)} %source_ref.5), channel_id=1, source_target_pairs={{8,0},{0,8},{24,16},{16,24},{9,1},{1,9},{25,17},{17,25},{10,2},{2,... | collective-permute-start | bytes 786440 | tf_op jit(solution)/shard_map/ppermute | solution.py:240
  2.9 1.5 %collective-permute-start.1 = (f32[8,64,128]{2,1,0:T(8,128)}, f32[8,64,128]{2,1,0:T(8,128)S(1)}, u32[]{:S(2)}, u32[]{:S(2)}) collective-permute-start(f32[8,64,128]{2,1,0:T(8,128)} %source_ref.5), channel_id=1, source_target_pairs={{16,0},{24,8},{0,16},{8,24},{17,1},{25,9},{1,17},{9,25},{18,2},{26... | collective-permute-start | bytes 786440 | tf_op jit(solution)/shard_map/ppermute | solution.py:240
  5.1 0.7 fusion.4
  6.0 0.3 select_reduce_fusion.2
  6.3 6.7 %prepare.1.a_ref = bf16[257,64,128]{2,1,0:T(8,128)(2,1)S(1)} custom-call(f32[64,64,256]{2,1,0:T(8,128)} %bitcast.3), custom_call_target="tpu_custom_call" | custom-call | bytes 25165824 | tf_op jit(solution)/shard_map/prepare/pallas_call | solution.py:61
  13.2 1.5 %transfer.5.rest_3_ = f32[64,64,128]{2,1,0:T(8,128)S(1)} custom-call(s32[872]{0:T(1024)S(1)} %pad_add_fusion.plan_ref, bf16[257,64,128]{2,1,0:T(8,128)(2,1)S(1)} %prepare.1.a_ref, f32[8,64,128]{2,1,0:T(8,128)S(1)} %copy-done), custom_call_target="tpu_custom_call" | custom-call | flops 359268352 | bytes 8388608 | tf_op jit(solution)/shard_map/transfer/pallas_call | solution.py:127
  14.8 1.8 %collective-permute-done.1.rest_1_ = f32[8,64,128]{2,1,0:T(8,128)S(1)} collective-permute-done((f32[8,64,128]{2,1,0:T(8,128)}, f32[8,64,128]{2,1,0:T(8,128)S(1)}, u32[]{:S(2)}, u32[]{:S(2)}) %collective-permute-start.1) | collective-permute-done | bytes 262176 | tf_op jit(solution)/shard_map/ppermute | solution.py:240
  16.5 2.6 %transfer.6.sums_ref.value_ref = f32[64,64,128]{2,1,0:T(8,128)S(1)} custom-call(s32[872]{0:T(1024)S(1)} %pad_add_fusion.plan_ref, bf16[257,64,128]{2,1,0:T(8,128)(2,1)S(1)} %prepare.1.a_ref, f32[8,64,128]{2,1,0:T(8,128)S(1)} %collective-permute-done.rest_0_, f32[8,64,128]{2,1,0:T(8,128)S(1)} %collective-permute-done.1.rest_1_, ...), custom_call_target="tpu_custom_call" | custom-call | flops 718602240 | bytes 8388608 | tf_op jit(solution)/shard_map/transfer/pallas_call | solution.py:127
  19.3 0.5 collective-permute-start.11
  19.8 1.0 %collective-permute-done.3.got_ref = f32[8,64,128]{2,1,0:T(8,128)S(1)} collective-permute-done((f32[8,64,128]{2,1,0:T(8,128)S(1)}, f32[8,64,128]{2,1,0:T(8,128)S(1)}, u32[]{:S(2)}, u32[]{:S(2)}) %collective-permute-start.3) | collective-permute-done | bytes 262176 | tf_op jit(solution)/shard_map/ppermute | solution.py:263
  21.3 0.4 collective-permute-start.12
  21.6 1.2 %collective-permute-start.5 = (f32[8,64,128]{2,1,0:T(8,128)S(1)}, f32[8,64,128]{2,1,0:T(8,128)S(1)}, u32[]{:S(2)}, u32[]{:S(2)}) collective-permute-start(f32[8,64,128]{2,1,0:T(8,128)S(1)} %carry.12.rest_0_), channel_id=1, source_target_pairs={{0,2},{1,0},{2,4},{3,1},{4,6},{5,3},{6,7},{7,5},{8,10},{9,8},{10,1... | collective-permute-start | bytes 786440 | tf_op jit(solution)/shard_map/ppermute | solution.py:271
  22.9 1.1 %collective-permute-start.13 = (f32[8,64,128]{2,1,0:T(8,128)S(1)}, f32[8,64,128]{2,1,0:T(8,128)S(1)}, u32[]{:S(2)}, u32[]{:S(2)}) collective-permute-start(f32[8,64,128]{2,1,0:T(8,128)S(1)} %carry.15.rest_0_), channel_id=1, source_target_pairs={{0,2},{1,0},{2,4},{3,1},{4,6},{5,3},{6,7},{7,5},{8,10},{9,8},{10,1... | collective-permute-start | bytes 786440 | tf_op jit(solution)/shard_map/ppermute | solution.py:271
  23.9 2.8 %collective-permute-done.5.rest_0_ = f32[8,64,128]{2,1,0:T(8,128)S(1)} collective-permute-done((f32[8,64,128]{2,1,0:T(8,128)S(1)}, f32[8,64,128]{2,1,0:T(8,128)S(1)}, u32[]{:S(2)}, u32[]{:S(2)}) %collective-permute-start.5) | collective-permute-done | bytes 262176 | tf_op jit(solution)/shard_map/ppermute | solution.py:271
  26.8 2.5 %collective-permute-start.6 = (f32[8,64,128]{2,1,0:T(8,128)S(1)}, f32[8,64,128]{2,1,0:T(8,128)S(1)}, u32[]{:S(2)}, u32[]{:S(2)}) collective-permute-start(f32[8,64,128]{2,1,0:T(8,128)S(1)} %carry.13), channel_id=1, source_target_pairs={{0,2},{1,0},{2,4},{3,1},{4,6},{5,3},{6,7},{7,5},{8,10},{9,8},{10,1... | collective-permute-start | bytes 786440 | tf_op jit(solution)/shard_map/ppermute | solution.py:271
  29.6 2.5 %collective-permute-start.14 = (f32[8,64,128]{2,1,0:T(8,128)S(1)}, f32[8,64,128]{2,1,0:T(8,128)S(1)}, u32[]{:S(2)}, u32[]{:S(2)}) collective-permute-start(f32[8,64,128]{2,1,0:T(8,128)S(1)} %carry.16), channel_id=1, source_target_pairs={{0,2},{1,0},{2,4},{3,1},{4,6},{5,3},{6,7},{7,5},{8,10},{9,8},{10,1... | collective-permute-start | bytes 786440 | tf_op jit(solution)/shard_map/ppermute | solution.py:271
  32.1 1.1 %collective-permute-done.6.rest_0_ = f32[8,64,128]{2,1,0:T(8,128)S(1)} collective-permute-done((f32[8,64,128]{2,1,0:T(8,128)S(1)}, f32[8,64,128]{2,1,0:T(8,128)S(1)}, u32[]{:S(2)}, u32[]{:S(2)}) %collective-permute-start.6) | collective-permute-done | bytes 262176 | tf_op jit(solution)/shard_map/ppermute | solution.py:271
  33.3 2.5 %collective-permute-start.7 = (f32[8,64,128]{2,1,0:T(8,128)S(1)}, f32[8,64,128]{2,1,0:T(8,128)S(1)}, u32[]{:S(2)}, u32[]{:S(2)}) collective-permute-start(f32[8,64,128]{2,1,0:T(8,128)S(1)} %carry.14), channel_id=1, source_target_pairs={{0,2},{1,0},{2,4},{3,1},{4,6},{5,3},{6,7},{7,5},{8,10},{9,8},{10,1... | collective-permute-start | bytes 786440 | tf_op jit(solution)/shard_map/ppermute | solution.py:271
  36.1 2.5 %collective-permute-start.15 = (f32[8,64,128]{2,1,0:T(8,128)S(1)}, f32[8,64,128]{2,1,0:T(8,128)S(1)}, u32[]{:S(2)}, u32[]{:S(2)}) collective-permute-start(f32[8,64,128]{2,1,0:T(8,128)S(1)} %carry.17), channel_id=1, source_target_pairs={{0,2},{1,0},{2,4},{3,1},{4,6},{5,3},{6,7},{7,5},{8,10},{9,8},{10,1... | collective-permute-start | bytes 786440 | tf_op jit(solution)/shard_map/ppermute | solution.py:271
  38.6 1.1 %collective-permute-done.7.came_ref.rest_1_ = f32[8,64,128]{2,1,0:T(8,128)S(1)} collective-permute-done((f32[8,64,128]{2,1,0:T(8,128)S(1)}, f32[8,64,128]{2,1,0:T(8,128)S(1)}, u32[]{:S(2)}, u32[]{:S(2)}) %collective-permute-start.7) | collective-permute-done | bytes 262176 | tf_op jit(solution)/shard_map/ppermute | solution.py:271
  39.8 1.3 %collective-permute-done.8.rest_2_ = f32[4,64,128]{2,1,0:T(8,128)S(1)} collective-permute-done((f32[4,64,128]{2,1,0:T(8,128)S(1)}, f32[4,64,128]{2,1,0:T(8,128)S(1)}, u32[]{:S(2)}, u32[]{:S(2)}) %collective-permute-start.8) | collective-permute-done | bytes 131104 | tf_op jit(solution)/shard_map/ppermute | solution.py:274
  41.1 1.3 %collective-permute-done.15.came_ref.rest_1_ = f32[8,64,128]{2,1,0:T(8,128)S(1)} collective-permute-done((f32[8,64,128]{2,1,0:T(8,128)S(1)}, f32[8,64,128]{2,1,0:T(8,128)S(1)}, u32[]{:S(2)}, u32[]{:S(2)}) %collective-permute-start.15) | collective-permute-done | bytes 262176 | tf_op jit(solution)/shard_map/ppermute | solution.py:271
  42.6 2.4 %collective-permute-start.9 = (f32[4,64,128]{2,1,0:T(8,128)S(1)}, f32[4,64,128]{2,1,0:T(8,128)S(1)}, u32[]{:S(2)}, u32[]{:S(2)}) collective-permute-start(f32[4,64,128]{2,1,0:T(8,128)S(1)} %finish.3.rest_0_), channel_id=1, source_target_pairs={{8,0},{0,8},{24,16},{16,24},{9,1},{1,9},{25,17},{17,25},{10,2},{2,... | collective-permute-start | bytes 393224 | tf_op jit(solution)/shard_map/ppermute | solution.py:240
  45.1 2.0 %collective-permute-start.18 = (f32[4,64,128]{2,1,0:T(8,128)S(1)}, f32[4,64,128]{2,1,0:T(8,128)S(1)}, u32[]{:S(2)}, u32[]{:S(2)}) collective-permute-start(f32[4,64,128]{2,1,0:T(8,128)S(1)} %finish.4.rest_1_), channel_id=1, source_target_pairs={{16,0},{24,8},{0,16},{8,24},{17,1},{25,9},{1,17},{9,25},{18,2},{26... | collective-permute-start | bytes 393224 | tf_op jit(solution)/shard_map/ppermute | solution.py:240
  47.2 1.5 %transfer.7.rest_1_.rest_4_ = f32[64,64,128]{2,1,0:T(8,128)S(1)} custom-call(s32[872]{0:T(1024)S(1)} %pad_add_fusion.plan_ref, bf16[257,64,128]{2,1,0:T(8,128)(2,1)S(1)} %prepare.1.a_ref, f32[4,64,128]{2,1,0:T(8,128)S(1)} %finish.3.rest_0_, f32[4,64,128]{2,1,0:T(8,128)S(1)} %finish.4.rest_1_), custom_call_target="tpu_custom_call" | custom-call | flops 359268352 | bytes 8388608 | tf_op jit(solution)/shard_map/transfer/pallas_call | solution.py:127
  48.7 0.3 collective-permute-done.9.value_ref.rest_0_
  49.1 2.3 %collective-permute-done.10.rest_0_.rest_2_ = f32[4,64,128]{2,1,0:T(8,128)S(1)} collective-permute-done((f32[4,64,128]{2,1,0:T(8,128)S(1)}, f32[4,64,128]{2,1,0:T(8,128)S(1)}, u32[]{:S(2)}, u32[]{:S(2)}) %collective-permute-start.10) | collective-permute-done | bytes 131104 | tf_op jit(solution)/shard_map/ppermute | solution.py:240
  51.4 2.7 %collective-permute-done.18.value_ref.rest_3_ = f32[4,64,128]{2,1,0:T(8,128)S(1)} collective-permute-done((f32[4,64,128]{2,1,0:T(8,128)S(1)}, f32[4,64,128]{2,1,0:T(8,128)S(1)}, u32[]{:S(2)}, u32[]{:S(2)}) %collective-permute-start.18) | collective-permute-done | bytes 131104 | tf_op jit(solution)/shard_map/ppermute | solution.py:240
  54.2 2.2 %transfer.8.rest_2_ = f32[64,64,128]{2,1,0:T(8,128)S(1)} custom-call(s32[872]{0:T(1024)S(1)} %pad_add_fusion.plan_ref, bf16[257,64,128]{2,1,0:T(8,128)(2,1)S(1)} %prepare.1.a_ref, f32[4,64,128]{2,1,0:T(8,128)S(1)} %collective-permute-done.9.value_ref.rest_0_, f32[4,64,128]{2,1,0:T(8,128)S(1)} %collective-permute-done.19.rest_0_.rest_1_, ...), custom_call_target="tpu_custom_call" | custom-call | flops 359268352 | bytes 8388608 | tf_op jit(solution)/shard_map/transfer/pallas_call | solution.py:127
  56.4 2.8 %collective-permute-done.20.rest_1_ = f32[4,64,128]{2,1,0:T(8,128)S(1)} collective-permute-done((f32[4,64,128]{2,1,0:T(8,128)S(1)}, f32[4,64,128]{2,1,0:T(8,128)S(1)}, u32[]{:S(2)}, u32[]{:S(2)}) %collective-permute-start.20) | collective-permute-done | bytes 131104 | tf_op jit(solution)/shard_map/ppermute | solution.py:240
  59.2 1.5 %transfer.9.sums_ref.value_ref = f32[64,64,128]{2,1,0:T(8,128)S(1)} custom-call(s32[872]{0:T(1024)S(1)} %pad_add_fusion.plan_ref, bf16[257,64,128]{2,1,0:T(8,128)(2,1)S(1)} %prepare.1.a_ref, f32[4,64,128]{2,1,0:T(8,128)S(1)} %collective-permute-done.17.rest_0_, f32[4,64,128]{2,1,0:T(8,128)S(1)} %collective-permute-done.20.rest_1_, ...), custom_call_target="tpu_custom_call" | custom-call | flops 359268352 | bytes 8388608 | tf_op jit(solution)/shard_map/transfer/pallas_call | solution.py:127
  60.8 0.5 collective-permute-start.27
  61.3 1.0 %collective-permute-done.21.got_ref = f32[8,64,128]{2,1,0:T(8,128)S(1)} collective-permute-done((f32[8,64,128]{2,1,0:T(8,128)S(1)}, f32[8,64,128]{2,1,0:T(8,128)S(1)}, u32[]{:S(2)}, u32[]{:S(2)}) %collective-permute-start.21) | collective-permute-done | bytes 262176 | tf_op jit(solution)/shard_map/ppermute | solution.py:263
  62.8 0.4 collective-permute-start.28
  63.2 2.2 %collective-permute-start.23 = (f32[8,64,128]{2,1,0:T(8,128)S(1)}, f32[8,64,128]{2,1,0:T(8,128)S(1)}, u32[]{:S(2)}, u32[]{:S(2)}) collective-permute-start(f32[8,64,128]{2,1,0:T(8,128)S(1)} %carry.18.rest_0_), channel_id=1, source_target_pairs={{0,2},{1,0},{2,4},{3,1},{4,6},{5,3},{6,7},{7,5},{8,10},{9,8},{10,1... | collective-permute-start | bytes 786440 | tf_op jit(solution)/shard_map/ppermute | solution.py:271
  65.4 1.3 %collective-permute-start.29 = (f32[8,64,128]{2,1,0:T(8,128)S(1)}, f32[8,64,128]{2,1,0:T(8,128)S(1)}, u32[]{:S(2)}, u32[]{:S(2)}) collective-permute-start(f32[8,64,128]{2,1,0:T(8,128)S(1)} %carry.21.rest_0_), channel_id=1, source_target_pairs={{0,2},{1,0},{2,4},{3,1},{4,6},{5,3},{6,7},{7,5},{8,10},{9,8},{10,1... | collective-permute-start | bytes 786440 | tf_op jit(solution)/shard_map/ppermute | solution.py:271
  66.7 2.6 %collective-permute-done.23.rest_0_ = f32[8,64,128]{2,1,0:T(8,128)S(1)} collective-permute-done((f32[8,64,128]{2,1,0:T(8,128)S(1)}, f32[8,64,128]{2,1,0:T(8,128)S(1)}, u32[]{:S(2)}, u32[]{:S(2)}) %collective-permute-start.23) | collective-permute-done | bytes 262176 | tf_op jit(solution)/shard_map/ppermute | solution.py:271
  69.3 2.5 %collective-permute-start.24 = (f32[8,64,128]{2,1,0:T(8,128)S(1)}, f32[8,64,128]{2,1,0:T(8,128)S(1)}, u32[]{:S(2)}, u32[]{:S(2)}) collective-permute-start(f32[8,64,128]{2,1,0:T(8,128)S(1)} %carry.19), channel_id=1, source_target_pairs={{0,2},{1,0},{2,4},{3,1},{4,6},{5,3},{6,7},{7,5},{8,10},{9,8},{10,1... | collective-permute-start | bytes 786440 | tf_op jit(solution)/shard_map/ppermute | solution.py:271
  71.8 0.2 collective-permute-done.29.rest_0_
  72.1 2.5 %collective-permute-start.30 = (f32[8,64,128]{2,1,0:T(8,128)S(1)}, f32[8,64,128]{2,1,0:T(8,128)S(1)}, u32[]{:S(2)}, u32[]{:S(2)}) collective-permute-start(f32[8,64,128]{2,1,0:T(8,128)S(1)} %carry.22), channel_id=1, source_target_pairs={{0,2},{1,0},{2,4},{3,1},{4,6},{5,3},{6,7},{7,5},{8,10},{9,8},{10,1... | collective-permute-start | bytes 786440 | tf_op jit(solution)/shard_map/ppermute | solution.py:271
  74.6 1.1 %collective-permute-done.24.rest_0_ = f32[8,64,128]{2,1,0:T(8,128)S(1)} collective-permute-done((f32[8,64,128]{2,1,0:T(8,128)S(1)}, f32[8,64,128]{2,1,0:T(8,128)S(1)}, u32[]{:S(2)}, u32[]{:S(2)}) %collective-permute-start.24) | collective-permute-done | bytes 262176 | tf_op jit(solution)/shard_map/ppermute | solution.py:271
  75.8 2.5 %collective-permute-start.25 = (f32[8,64,128]{2,1,0:T(8,128)S(1)}, f32[8,64,128]{2,1,0:T(8,128)S(1)}, u32[]{:S(2)}, u32[]{:S(2)}) collective-permute-start(f32[8,64,128]{2,1,0:T(8,128)S(1)} %carry.20), channel_id=1, source_target_pairs={{0,2},{1,0},{2,4},{3,1},{4,6},{5,3},{6,7},{7,5},{8,10},{9,8},{10,1... | collective-permute-start | bytes 786440 | tf_op jit(solution)/shard_map/ppermute | solution.py:271
  78.3 0.3 collective-permute-done.30.rest_0_
  78.6 2.5 %collective-permute-start.31 = (f32[8,64,128]{2,1,0:T(8,128)S(1)}, f32[8,64,128]{2,1,0:T(8,128)S(1)}, u32[]{:S(2)}, u32[]{:S(2)}) collective-permute-start(f32[8,64,128]{2,1,0:T(8,128)S(1)} %carry.23), channel_id=1, source_target_pairs={{0,2},{1,0},{2,4},{3,1},{4,6},{5,3},{6,7},{7,5},{8,10},{9,8},{10,1... | collective-permute-start | bytes 786440 | tf_op jit(solution)/shard_map/ppermute | solution.py:271
  81.1 1.1 %collective-permute-done.25.came_ref.rest_1_ = f32[8,64,128]{2,1,0:T(8,128)S(1)} collective-permute-done((f32[8,64,128]{2,1,0:T(8,128)S(1)}, f32[8,64,128]{2,1,0:T(8,128)S(1)}, u32[]{:S(2)}, u32[]{:S(2)}) %collective-permute-start.25) | collective-permute-done | bytes 262176 | tf_op jit(solution)/shard_map/ppermute | solution.py:271
  82.3 2.7 %collective-permute-done.31.came_ref.rest_4_ = f32[8,64,128]{2,1,0:T(8,128)S(1)} collective-permute-done((f32[8,64,128]{2,1,0:T(8,128)S(1)}, f32[8,64,128]{2,1,0:T(8,128)S(1)}, u32[]{:S(2)}, u32[]{:S(2)}) %collective-permute-start.31) | collective-permute-done | bytes 262176 | tf_op jit(solution)/shard_map/ppermute | solution.py:271
  85.1 1.3 %collective-permute-done.32.rest_5_ = f32[4,64,128]{2,1,0:T(8,128)S(1)} collective-permute-done((f32[4,64,128]{2,1,0:T(8,128)S(1)}, f32[4,64,128]{2,1,0:T(8,128)S(1)}, u32[]{:S(2)}, u32[]{:S(2)}) %collective-permute-start.32) | collective-permute-done | bytes 131104 | tf_op jit(solution)/shard_map/ppermute | solution.py:274
  86.4 0.8 finish.5
  (59 shorter events, 3.3 us)
Async XLA Ops:
  0.0 14.8 %collective-permute-start = (f32[8,64,128]{2,1,0:T(8,128)}, f32[8,64,128]{2,1,0:T(8,128)S(1)}, u32[]{:S(2)}, u32[]{:S(2)}) collective-permute-start(f32[8,64,128]{2,1,0:T(8,128)} %source_ref.5), channel_id=1, source_target_pairs={{8,0},{0,8},{24,16},{16,24},{9,1},{1,9},{25,17},{17,25},{10,2},{2,... | collective-permute-start | bytes 786440 | tf_op jit(solution)/shard_map/ppermute | solution.py:240
  2.9 13.6 %collective-permute-start.1 = (f32[8,64,128]{2,1,0:T(8,128)}, f32[8,64,128]{2,1,0:T(8,128)S(1)}, u32[]{:S(2)}, u32[]{:S(2)}) collective-permute-start(f32[8,64,128]{2,1,0:T(8,128)} %source_ref.5), channel_id=1, source_target_pairs={{16,0},{24,8},{0,16},{8,24},{17,1},{25,9},{1,17},{9,25},{18,2},{26... | collective-permute-start | bytes 786440 | tf_op jit(solution)/shard_map/ppermute | solution.py:240
  4.5 12.1 %collective-permute-start.2 = (f32[8,64,128]{2,1,0:T(8,128)}, f32[8,64,128]{2,1,0:T(8,128)S(1)}, u32[]{:S(2)}, u32[]{:S(2)}) collective-permute-start(f32[8,64,128]{2,1,0:T(8,128)} %source_ref.5), channel_id=1, source_target_pairs={{24,0},{16,8},{8,16},{0,24},{25,1},{17,9},{9,17},{1,25},{26,2},{18... | collective-permute-start | bytes 786440 | tf_op jit(solution)/shard_map/ppermute | solution.py:240
  6.3 6.9 %copy-start = (f32[8,64,128]{2,1,0:T(8,128)S(1)}, f32[8,64,128]{2,1,0:T(8,128)}, u32[]{:S(2)}) copy-start(f32[8,64,128]{2,1,0:T(8,128)} %source_ref.5) | copy-start | bytes 786436
  19.2 1.6 %collective-permute-start.3 = (f32[8,64,128]{2,1,0:T(8,128)S(1)}, f32[8,64,128]{2,1,0:T(8,128)S(1)}, u32[]{:S(2)}, u32[]{:S(2)}) collective-permute-start(f32[8,64,128]{2,1,0:T(8,128)S(1)} %get-tuple-element.15), channel_id=1, source_target_pairs={{0,1},{1,0},{2,3},{3,2},{4,5},{5,4},{6,7},{7,6},{8,9},{9,8},{10,11... | collective-permute-start | bytes 786440 | tf_op jit(solution)/shard_map/ppermute | solution.py:263
  19.3 1.9 %collective-permute-start.11 = (f32[8,64,128]{2,1,0:T(8,128)S(1)}, f32[8,64,128]{2,1,0:T(8,128)S(1)}, u32[]{:S(2)}, u32[]{:S(2)}) collective-permute-start(f32[8,64,128]{2,1,0:T(8,128)S(1)} %get-tuple-element.14), channel_id=1, source_target_pairs={{0,1},{1,0},{2,3},{3,2},{4,5},{5,4},{6,7},{7,6},{8,9},{9,8},{10,11... | collective-permute-start | bytes 786440 | tf_op jit(solution)/shard_map/ppermute | solution.py:263
  20.9 5.8 %collective-permute-start.4 = (f32[24,64,128]{2,1,0:T(8,128)S(1)}, f32[24,64,128]{2,1,0:T(8,128)S(1)}, u32[]{:S(2)}, u32[]{:S(2)}) collective-permute-start(f32[24,64,128]{2,1,0:T(8,128)S(1)} %cut.6), channel_id=1, source_target_pairs={{0,1},{1,0},{2,3},{3,2},{4,5},{5,4},{6,7},{7,6},{8,9},{9,8},{10,11... | collective-permute-start | bytes 2359304 | tf_op jit(solution)/shard_map/ppermute | solution.py:267
  21.3 8.3 %collective-permute-start.12 = (f32[24,64,128]{2,1,0:T(8,128)S(1)}, f32[24,64,128]{2,1,0:T(8,128)S(1)}, u32[]{:S(2)}, u32[]{:S(2)}) collective-permute-start(f32[24,64,128]{2,1,0:T(8,128)S(1)} %cut.7), channel_id=1, source_target_pairs={{0,1},{1,0},{2,3},{3,2},{4,5},{5,4},{6,7},{7,6},{8,9},{9,8},{10,11... | collective-permute-start | bytes 2359304 | tf_op jit(solution)/shard_map/ppermute | solution.py:267
  21.6 5.1 %collective-permute-start.5 = (f32[8,64,128]{2,1,0:T(8,128)S(1)}, f32[8,64,128]{2,1,0:T(8,128)S(1)}, u32[]{:S(2)}, u32[]{:S(2)}) collective-permute-start(f32[8,64,128]{2,1,0:T(8,128)S(1)} %carry.12.rest_0_), channel_id=1, source_target_pairs={{0,2},{1,0},{2,4},{3,1},{4,6},{5,3},{6,7},{7,5},{8,10},{9,8},{10,1... | collective-permute-start | bytes 786440 | tf_op jit(solution)/shard_map/ppermute | solution.py:271
  22.9 6.7 %collective-permute-start.13 = (f32[8,64,128]{2,1,0:T(8,128)S(1)}, f32[8,64,128]{2,1,0:T(8,128)S(1)}, u32[]{:S(2)}, u32[]{:S(2)}) collective-permute-start(f32[8,64,128]{2,1,0:T(8,128)S(1)} %carry.15.rest_0_), channel_id=1, source_target_pairs={{0,2},{1,0},{2,4},{3,1},{4,6},{5,3},{6,7},{7,5},{8,10},{9,8},{10,1... | collective-permute-start | bytes 786440 | tf_op jit(solution)/shard_map/ppermute | solution.py:271
  26.8 6.4 %collective-permute-start.6 = (f32[8,64,128]{2,1,0:T(8,128)S(1)}, f32[8,64,128]{2,1,0:T(8,128)S(1)}, u32[]{:S(2)}, u32[]{:S(2)}) collective-permute-start(f32[8,64,128]{2,1,0:T(8,128)S(1)} %carry.13), channel_id=1, source_target_pairs={{0,2},{1,0},{2,4},{3,1},{4,6},{5,3},{6,7},{7,5},{8,10},{9,8},{10,1... | collective-permute-start | bytes 786440 | tf_op jit(solution)/shard_map/ppermute | solution.py:271
  29.6 6.4 %collective-permute-start.14 = (f32[8,64,128]{2,1,0:T(8,128)S(1)}, f32[8,64,128]{2,1,0:T(8,128)S(1)}, u32[]{:S(2)}, u32[]{:S(2)}) collective-permute-start(f32[8,64,128]{2,1,0:T(8,128)S(1)} %carry.16), channel_id=1, source_target_pairs={{0,2},{1,0},{2,4},{3,1},{4,6},{5,3},{6,7},{7,5},{8,10},{9,8},{10,1... | collective-permute-start | bytes 786440 | tf_op jit(solution)/shard_map/ppermute | solution.py:271
  33.3 6.4 %collective-permute-start.7 = (f32[8,64,128]{2,1,0:T(8,128)S(1)}, f32[8,64,128]{2,1,0:T(8,128)S(1)}, u32[]{:S(2)}, u32[]{:S(2)}) collective-permute-start(f32[8,64,128]{2,1,0:T(8,128)S(1)} %carry.14), channel_id=1, source_target_pairs={{0,2},{1,0},{2,4},{3,1},{4,6},{5,3},{6,7},{7,5},{8,10},{9,8},{10,1... | collective-permute-start | bytes 786440 | tf_op jit(solution)/shard_map/ppermute | solution.py:271
  36.1 6.4 %collective-permute-start.15 = (f32[8,64,128]{2,1,0:T(8,128)S(1)}, f32[8,64,128]{2,1,0:T(8,128)S(1)}, u32[]{:S(2)}, u32[]{:S(2)}) collective-permute-start(f32[8,64,128]{2,1,0:T(8,128)S(1)} %carry.17), channel_id=1, source_target_pairs={{0,2},{1,0},{2,4},{3,1},{4,6},{5,3},{6,7},{7,5},{8,10},{9,8},{10,1... | collective-permute-start | bytes 786440 | tf_op jit(solution)/shard_map/ppermute | solution.py:271
  39.7 1.4 %collective-permute-start.8 = (f32[4,64,128]{2,1,0:T(8,128)S(1)}, f32[4,64,128]{2,1,0:T(8,128)S(1)}, u32[]{:S(2)}, u32[]{:S(2)}) collective-permute-start(f32[4,64,128]{2,1,0:T(8,128)S(1)} %cross.4), channel_id=1, source_target_pairs={{0,1},{1,0},{2,3},{3,2},{4,5},{5,4},{6,7},{7,6},{8,9},{9,8},{10,11... | collective-permute-start | bytes 393224 | tf_op jit(solution)/shard_map/ppermute | solution.py:274
  42.5 2.6 %collective-permute-start.16 = (f32[4,64,128]{2,1,0:T(8,128)S(1)}, f32[4,64,128]{2,1,0:T(8,128)S(1)}, u32[]{:S(2)}, u32[]{:S(2)}) collective-permute-start(f32[4,64,128]{2,1,0:T(8,128)S(1)} %cross.5), channel_id=1, source_target_pairs={{0,1},{1,0},{2,3},{3,2},{4,5},{5,4},{6,7},{7,6},{8,9},{9,8},{10,11... | collective-permute-start | bytes 393224 | tf_op jit(solution)/shard_map/ppermute | solution.py:274
  42.6 6.5 %collective-permute-start.9 = (f32[4,64,128]{2,1,0:T(8,128)S(1)}, f32[4,64,128]{2,1,0:T(8,128)S(1)}, u32[]{:S(2)}, u32[]{:S(2)}) collective-permute-start(f32[4,64,128]{2,1,0:T(8,128)S(1)} %finish.3.rest_0_), channel_id=1, source_target_pairs={{8,0},{0,8},{24,16},{16,24},{9,1},{1,9},{25,17},{17,25},{10,2},{2,... | collective-permute-start | bytes 393224 | tf_op jit(solution)/shard_map/ppermute | solution.py:240
  45.0 6.3 %collective-permute-start.10 = (f32[4,64,128]{2,1,0:T(8,128)S(1)}, f32[4,64,128]{2,1,0:T(8,128)S(1)}, u32[]{:S(2)}, u32[]{:S(2)}) collective-permute-start(f32[4,64,128]{2,1,0:T(8,128)S(1)} %finish.3.rest_0_), channel_id=1, source_target_pairs={{16,0},{24,8},{0,16},{8,24},{17,1},{25,9},{1,17},{9,25},{18,2},{26... | collective-permute-start | bytes 393224 | tf_op jit(solution)/shard_map/ppermute | solution.py:240
  45.1 9.0 %collective-permute-start.18 = (f32[4,64,128]{2,1,0:T(8,128)S(1)}, f32[4,64,128]{2,1,0:T(8,128)S(1)}, u32[]{:S(2)}, u32[]{:S(2)}) collective-permute-start(f32[4,64,128]{2,1,0:T(8,128)S(1)} %finish.4.rest_1_), channel_id=1, source_target_pairs={{16,0},{24,8},{0,16},{8,24},{17,1},{25,9},{1,17},{9,25},{18,2},{26... | collective-permute-start | bytes 393224 | tf_op jit(solution)/shard_map/ppermute | solution.py:240
  47.1 7.0 %collective-permute-start.19 = (f32[4,64,128]{2,1,0:T(8,128)S(1)}, f32[4,64,128]{2,1,0:T(8,128)S(1)}, u32[]{:S(2)}, u32[]{:S(2)}) collective-permute-start(f32[4,64,128]{2,1,0:T(8,128)S(1)} %finish.4.rest_1_), channel_id=1, source_target_pairs={{8,0},{0,8},{24,16},{16,24},{9,1},{1,9},{25,17},{17,25},{10,2},{2,... | collective-permute-start | bytes 393224 | tf_op jit(solution)/shard_map/ppermute | solution.py:240
  51.3 5.1 %collective-permute-start.17 = (f32[4,64,128]{2,1,0:T(8,128)S(1)}, f32[4,64,128]{2,1,0:T(8,128)S(1)}, u32[]{:S(2)}, u32[]{:S(2)}) collective-permute-start(f32[4,64,128]{2,1,0:T(8,128)S(1)} %cut.8), channel_id=1, source_target_pairs={{16,0},{24,8},{0,16},{8,24},{17,1},{25,9},{1,17},{9,25},{18,2},{26... | collective-permute-start | bytes 393224 | tf_op jit(solution)/shard_map/ppermute | solution.py:240
  54.1 5.0 %collective-permute-start.20 = (f32[4,64,128]{2,1,0:T(8,128)S(1)}, f32[4,64,128]{2,1,0:T(8,128)S(1)}, u32[]{:S(2)}, u32[]{:S(2)}) collective-permute-start(f32[4,64,128]{2,1,0:T(8,128)S(1)} %cut.9), channel_id=1, source_target_pairs={{8,0},{0,8},{24,16},{16,24},{9,1},{1,9},{25,17},{17,25},{10,2},{2,... | collective-permute-start | bytes 393224 | tf_op jit(solution)/shard_map/ppermute | solution.py:240
  60.8 1.6 %collective-permute-start.21 = (f32[8,64,128]{2,1,0:T(8,128)S(1)}, f32[8,64,128]{2,1,0:T(8,128)S(1)}, u32[]{:S(2)}, u32[]{:S(2)}) collective-permute-start(f32[8,64,128]{2,1,0:T(8,128)S(1)} %get-tuple-element.13), channel_id=1, source_target_pairs={{0,1},{1,0},{2,3},{3,2},{4,5},{5,4},{6,7},{7,6},{8,9},{9,8},{10,11... | collective-permute-start | bytes 786440 | tf_op jit(solution)/shard_map/ppermute | solution.py:263
  60.8 1.9 %collective-permute-start.27 = (f32[8,64,128]{2,1,0:T(8,128)S(1)}, f32[8,64,128]{2,1,0:T(8,128)S(1)}, u32[]{:S(2)}, u32[]{:S(2)}) collective-permute-start(f32[8,64,128]{2,1,0:T(8,128)S(1)} %get-tuple-element.12), channel_id=1, source_target_pairs={{0,1},{1,0},{2,3},{3,2},{4,5},{5,4},{6,7},{7,6},{8,9},{9,8},{10,11... | collective-permute-start | bytes 786440 | tf_op jit(solution)/shard_map/ppermute | solution.py:263
  62.5 6.8 %collective-permute-start.22 = (f32[24,64,128]{2,1,0:T(8,128)S(1)}, f32[24,64,128]{2,1,0:T(8,128)S(1)}, u32[]{:S(2)}, u32[]{:S(2)}) collective-permute-start(f32[24,64,128]{2,1,0:T(8,128)S(1)} %cut.10), channel_id=1, source_target_pairs={{0,1},{1,0},{2,3},{3,2},{4,5},{5,4},{6,7},{7,6},{8,9},{9,8},{10,11... | collective-permute-start | bytes 2359304 | tf_op jit(solution)/shard_map/ppermute | solution.py:267
  62.8 9.3 %collective-permute-start.28 = (f32[24,64,128]{2,1,0:T(8,128)S(1)}, f32[24,64,128]{2,1,0:T(8,128)S(1)}, u32[]{:S(2)}, u32[]{:S(2)}) collective-permute-start(f32[24,64,128]{2,1,0:T(8,128)S(1)} %cut.11), channel_id=1, source_target_pairs={{0,1},{1,0},{2,3},{3,2},{4,5},{5,4},{6,7},{7,6},{8,9},{9,8},{10,11... | collective-permute-start | bytes 2359304 | tf_op jit(solution)/shard_map/ppermute | solution.py:267
  63.2 6.1 %collective-permute-start.23 = (f32[8,64,128]{2,1,0:T(8,128)S(1)}, f32[8,64,128]{2,1,0:T(8,128)S(1)}, u32[]{:S(2)}, u32[]{:S(2)}) collective-permute-start(f32[8,64,128]{2,1,0:T(8,128)S(1)} %carry.18.rest_0_), channel_id=1, source_target_pairs={{0,2},{1,0},{2,4},{3,1},{4,6},{5,3},{6,7},{7,5},{8,10},{9,8},{10,1... | collective-permute-start | bytes 786440 | tf_op jit(solution)/shard_map/ppermute | solution.py:271
  65.4 6.7 %collective-permute-start.29 = (f32[8,64,128]{2,1,0:T(8,128)S(1)}, f32[8,64,128]{2,1,0:T(8,128)S(1)}, u32[]{:S(2)}, u32[]{:S(2)}) collective-permute-start(f32[8,64,128]{2,1,0:T(8,128)S(1)} %carry.21.rest_0_), channel_id=1, source_target_pairs={{0,2},{1,0},{2,4},{3,1},{4,6},{5,3},{6,7},{7,5},{8,10},{9,8},{10,1... | collective-permute-start | bytes 786440 | tf_op jit(solution)/shard_map/ppermute | solution.py:271
  69.3 6.4 %collective-permute-start.24 = (f32[8,64,128]{2,1,0:T(8,128)S(1)}, f32[8,64,128]{2,1,0:T(8,128)S(1)}, u32[]{:S(2)}, u32[]{:S(2)}) collective-permute-start(f32[8,64,128]{2,1,0:T(8,128)S(1)} %carry.19), channel_id=1, source_target_pairs={{0,2},{1,0},{2,4},{3,1},{4,6},{5,3},{6,7},{7,5},{8,10},{9,8},{10,1... | collective-permute-start | bytes 786440 | tf_op jit(solution)/shard_map/ppermute | solution.py:271
  72.1 6.4 %collective-permute-start.30 = (f32[8,64,128]{2,1,0:T(8,128)S(1)}, f32[8,64,128]{2,1,0:T(8,128)S(1)}, u32[]{:S(2)}, u32[]{:S(2)}) collective-permute-start(f32[8,64,128]{2,1,0:T(8,128)S(1)} %carry.22), channel_id=1, source_target_pairs={{0,2},{1,0},{2,4},{3,1},{4,6},{5,3},{6,7},{7,5},{8,10},{9,8},{10,1... | collective-permute-start | bytes 786440 | tf_op jit(solution)/shard_map/ppermute | solution.py:271
  75.8 6.4 %collective-permute-start.25 = (f32[8,64,128]{2,1,0:T(8,128)S(1)}, f32[8,64,128]{2,1,0:T(8,128)S(1)}, u32[]{:S(2)}, u32[]{:S(2)}) collective-permute-start(f32[8,64,128]{2,1,0:T(8,128)S(1)} %carry.20), channel_id=1, source_target_pairs={{0,2},{1,0},{2,4},{3,1},{4,6},{5,3},{6,7},{7,5},{8,10},{9,8},{10,1... | collective-permute-start | bytes 786440 | tf_op jit(solution)/shard_map/ppermute | solution.py:271
  78.6 6.4 %collective-permute-start.31 = (f32[8,64,128]{2,1,0:T(8,128)S(1)}, f32[8,64,128]{2,1,0:T(8,128)S(1)}, u32[]{:S(2)}, u32[]{:S(2)}) collective-permute-start(f32[8,64,128]{2,1,0:T(8,128)S(1)} %carry.23), channel_id=1, source_target_pairs={{0,2},{1,0},{2,4},{3,1},{4,6},{5,3},{6,7},{7,5},{8,10},{9,8},{10,1... | collective-permute-start | bytes 786440 | tf_op jit(solution)/shard_map/ppermute | solution.py:271
  82.2 2.9 %collective-permute-start.26 = (f32[4,64,128]{2,1,0:T(8,128)S(1)}, f32[4,64,128]{2,1,0:T(8,128)S(1)}, u32[]{:S(2)}, u32[]{:S(2)}) collective-permute-start(f32[4,64,128]{2,1,0:T(8,128)S(1)} %cross.6), channel_id=1, source_target_pairs={{0,1},{1,0},{2,3},{3,2},{4,5},{5,4},{6,7},{7,6},{8,9},{9,8},{10,11... | collective-permute-start | bytes 393224 | tf_op jit(solution)/shard_map/ppermute | solution.py:274
  85.0 1.4 %collective-permute-start.32 = (f32[4,64,128]{2,1,0:T(8,128)S(1)}, f32[4,64,128]{2,1,0:T(8,128)S(1)}, u32[]{:S(2)}, u32[]{:S(2)}) collective-permute-start(f32[4,64,128]{2,1,0:T(8,128)S(1)} %cross.7), channel_id=1, source_target_pairs={{0,1},{1,0},{2,3},{3,2},{4,5},{5,4},{6,7},{7,6},{8,9},{9,8},{10,11... | collective-permute-start | bytes 393224 | tf_op jit(solution)/shard_map/ppermute | solution.py:274

commit v4 on v3

--- a/solution.py
+++ b/solution.py
@@ -27,33 +27,40 @@
 
 def prepare_kernel(b_hbm, o_ref, b_ref, t_ref, sems):
     cells, _, slots = b_hbm.shape
-    width = min(128, slots)
-    rounds = cells // CHUNK
-    copies = [
-        pltpu.make_async_copy(b_hbm.at[pl.ds(r * CHUNK, CHUNK)], b_ref.at[pl.ds(r * CHUNK, CHUNK)], sems.at[r])
-        for r in range(rounds)
-    ]
+    middle, width = cells // 2, min(128, slots)
+    copies = []
+    for r in range(middle // CHUNK):
+        for side in range(2):
+            rows = pl.ds(side * middle + r * CHUNK, CHUNK)
+            copies.append(pltpu.make_async_copy(b_hbm.at[rows], b_ref.at[rows], sems.at[2 * r + side]))
     for copy in copies:
         copy.start()
     o_ref[slots] = jnp.zeros(o_ref.shape[1:], BF16)
-    for r in range(rounds):
-        copies[r].wait()
+    for r in range(middle // CHUNK):
+        copies[2 * r].wait()
+        copies[2 * r + 1].wait()
 
         def turn(i, carry, r=r):
             for c in range(slots // width):
-                value = b_ref[r * CHUNK + i, :, pl.ds(c * width, width)]
-                high = value.astype(BF16).astype(F32)
-                t_ref[i, pl.ds(c * width, width), :] = jnp.concatenate([high, value - high], axis=0).T
+                first, second = [b_ref[side * middle + r * CHUNK + i, :, pl.ds(c * width, width)] for side in range(2)]
+                t_ref[i, pl.ds(c * width, width), :] = jnp.concatenate([first, second], axis=0).T
             return carry
 
-        lax.fori_loop(0, CHUNK, turn, 0, unroll=4)
+        lax.fori_loop(0, CHUNK, turn, 0, unroll=True)
 
         def regroup(g, carry, r=r):
             first = pl.multiple_of(g * 8, 8)
-            o_ref[pl.ds(first, 8), pl.ds(r * CHUNK, CHUNK), :] = jnp.swapaxes(t_ref[:, pl.ds(first, 8), :], 0, 1).astype(BF16)
+            value = jnp.swapaxes(t_ref[:, pl.ds(first, 8), :], 0, 1)
+            other = pltpu.roll(value, cells, 2)
+            left = lax.broadcasted_iota(jnp.int32, value.shape, 2) < cells
+            value_high, other_high = value.astype(BF16).astype(F32), other.astype(BF16).astype(F32)
+            upper = jnp.where(left, value_high, other - other_high)
+            lower = jnp.where(left, other_high, value - value_high)
+            o_ref[pl.ds(first, 8), pl.ds(r * CHUNK, CHUNK), :] = upper.astype(BF16)
+            o_ref[pl.ds(first, 8), pl.ds(middle + r * CHUNK, CHUNK), :] = lower.astype(BF16)
             return carry
 
-        lax.fori_loop(0, slots // 8, regroup, 0, unroll=2)
+        lax.fori_loop(0, slots // 8, regroup, 0, unroll=True)
 
 
 def prepare(blocks):
@@ -131,9 +138,27 @@
         out_shape=jax.ShapeDtypeStruct((out_bricks, cells, lights), F32),
         scratch_shapes=[pltpu.VMEM((senders, 2 * cells, lights), BF16)],
         compiler_params=pltpu.CompilerParams(vmem_limit_bytes=SMALL + scratch),
-        cost_estimate=pl.CostEstimate(flops=2 * rows * 4 * cells * lights, bytes_accessed=8 * MIB, transcendentals=0),
+        cost_estimate=pl.CostEstimate(flops=0, bytes_accessed=0, transcendentals=0),
         name="transfer",
-    )(plan, matrix, *fields, *before)
+    )(pltpu.with_memory_space_constraint(plan, pltpu.SMEM), matrix, *fields, *before)
+
+
+def keep_kernel(value_ref, out_ref, sem):
+    copy = pltpu.make_async_copy(value_ref, out_ref, sem)
+    copy.start()
+    copy.wait()
+
+
+def in_scalar_memory(value):
+    return pl.pallas_call(
+        keep_kernel,
+        in_specs=[pl.BlockSpec(memory_space=pltpu.VMEM)],
+        out_specs=pl.BlockSpec(memory_space=pltpu.SMEM),
+        out_shape=pltpu.SMEM(value.shape, value.dtype),
+        scratch_shapes=[pltpu.SemaphoreType.DMA],
+        compiler_params=pltpu.CompilerParams(vmem_limit_bytes=SMALL),
+        name="keep",
+    )(value)
 
 
 def first_of_line():
@@ -150,7 +175,7 @@
         out_specs=[whole] * len(out_bricks),
         out_shape=[jax.ShapeDtypeStruct((n, *shape), F32) for n in out_bricks],
         compiler_params=pltpu.CompilerParams(vmem_limit_bytes=SMALL),
-        cost_estimate=pl.CostEstimate(flops=0, bytes_accessed=MIB, transcendentals=0),
+        cost_estimate=pl.CostEstimate(flops=0, bytes_accessed=0, transcendentals=0),
         name=name,
     )(*args, *after)
 
@@ -185,8 +210,7 @@
 
 def cross_kernel(came_ref, *rest):
     out_ref = rest[-1]
-    half = out_ref.shape[0]
-    first = first_of_line()
+    half, first = out_ref.shape[0], first_of_line()
     for c in range(half):
         out_ref[c] = jnp.where(first, 0.0, came_ref[half + c])
 
@@ -236,6 +260,7 @@
 
     swap = [(i, i ^ 1) for i in range(n_col)]
     ring = [(i, (i + 2 if i + 2 < n_col else n_col - 1) if i % 2 == 0 else (i - 2 if i > 2 else 0)) for i in range(n_col)]
+
     def from_turn(value, k):
         return lax.ppermute(value, "row", [(i ^ k if flips else (i + k) % n_row, i) for i in range(n_row)])
 
@@ -259,40 +284,52 @@
     def begin(sums, h):
         base = h * in_half
         if pairs == 1:
-            return [base, lax.ppermute(sums[base : base + in_half], "col", swap)]
+            return base, None, lax.ppermute(sums[base : base + in_half], "col", swap)
         lead = lax.ppermute(sums[base : base + block], "col", swap)
         mine = base + block_of(pairs - 1) * block
         total = small_call(functools.partial(carry_kernel, mine, 0), (block,), "carry", sums, lead)[0]
         later = cut(sums, base + block, in_half - block, (total,))
-        return [base, lax.ppermute(later, "col", swap), total]
-
-    def scatter(sums, base, rest, *total, after=()):
-        for distance in range(pairs - 1, 0, -1):
-            came = lax.ppermute(total[0], "col", ring)
-            if distance == 1:
-                crossing = small_call(cross_kernel, (half,), "cross", came, after=after)[0]
-                return rest, came, lax.ppermute(crossing, "col", swap)
-            mine, other = base + block_of(distance - 1) * block, (block_of(pairs - distance + 1) - 1) * block
-            kernel = functools.partial(carry_kernel, mine, other)
-            total = small_call(kernel, (block,), "carry", sums, rest, came)
-        return (rest,)
-
-    def finish(sums, parts, half_at):
-        args = [a for p in parts for a in p]
+        return base, total, lax.ppermute(later, "col", swap)
+
+    def total_for(sums, base, rest, distance, came):
+        mine, other = base + block_of(distance) * block, (block_of(pairs - distance) - 1) * block
+        return small_call(functools.partial(carry_kernel, mine, other), (block,), "carry", sums, rest, came)[0]
+
+    def scatter(sums):
+        parts = []
+        for base, total, rest in [begin(sums, h) for h in range(HALVES)]:
+            parts.append([rest])
+            if pairs > 1:
+                came = lax.ppermute(total, "col", ring)
+                for distance in range(pairs - 2, 0, -1):
+                    came = lax.ppermute(total_for(sums, base, rest, distance, came), "col", ring)
+                parts[-1].append(came)
+        return parts
+
+    def finish(sums, parts, half_at, after=()):
+        args = []
+        for rest, *came in parts:
+            args += [rest, *came]
+            if came:
+                crossing = small_call(cross_kernel, (half,), "cross", *came, after=after)[0]
+                args.append(lax.ppermute(crossing, "col", swap))
         kernel = functools.partial(finish_kernel, len(parts), half_at, owns)
         return small_call(kernel, (len(parts) * half,), "finish", source, sums, *args)[0]
 
-    plan = make_plan(row_index, col_index, live_count[0], bricks, n_row, n_col, flips)
+    plan = in_scalar_memory(make_plan(row_index, col_index, live_count[0], bricks, n_row, n_col, flips))
     matrix = prepare(blocks)
 
-    others = gather([source], True)
-    sums = apply({0: [source]}, 0, 1)
-    sums = apply(dict(enumerate(others, 1)), 1, STAGES, sums)
+    if n_row == 4:
+        one, two = gather([source], False)
+        last = [forward(one[0][:half], 2, two[0], matrix), forward(two[0][half:], 1, one[0], matrix)]
+        sums = apply({0: [source], 1: one, 2: two}, 0, 2)
+        sums = apply({3: last}, 2, STAGES, sums)
+    else:
+        sums = apply(dict(enumerate([[source], *gather([source], True)])), 0, STAGES)
     for _ in range(ITERS - 1):
-        chains = [begin(sums, h) for h in range(HALVES)]
         field = []
-        for h in range(HALVES):
-            field.append(finish(sums, [scatter(sums, *chains[h], after=field)], h))
+        for h, part in enumerate(scatter(sums)):
+            field.append(finish(sums, [part], h, field))
         sums = apply({0: field}, 0, 1)
         if n_row == 4:
             one, two = gather(field, False)
@@ -301,8 +338,7 @@
             sums = apply({3: last}, 2, STAGES, sums)
         else:
             sums = apply(dict(enumerate(gather(field, True), 1)), 1, STAGES, sums)
-    chains = [begin(sums, h) for h in range(HALVES)]
-    return finish(sums, [scatter(sums, *c) for c in chains], 0)
+    return finish(sums, scatter(sums), 0)
 
 
 def solution(mesh):

time: 87.4 us -> 84.9 us (0.971)
  Pallas kernels: 17.8 us -> 13 us
  starting transfers between devices: 37.5 us -> 41.5 us
  waiting for transfers between devices: 29.5 us -> 27.9 us
    ppermute x9 -> x10, starting transfers between devices: 9.22 us -> 12.5 us  [from_turn(): lax.ppermute(value, 'row', [(i ^ k if flips else (i + k) % n_row, i) for...]
    pallas_call x5, Pallas kernels: 9.4 us -> 6.23 us  [transfer(): pl.pallas_call(functools.partial(transfer_kernel, fields_at, begin, end,...]
    pallas_call x1, Pallas kernels: 6.68 us -> 4.48 us  [prepare(): pl.pallas_call(prepare_kernel, in_specs=[pl.BlockSpec(memory_space=pltpu....]
    ppermute x9 -> x10, waiting for transfers between devices: 9.8 us -> 8.15 us  [from_turn(): lax.ppermute(value, 'row', [(i ^ k if flips else (i + k) % n_row, i) for...]
  transfers between devices with their start and end apart: 33 -> 34, of which waited for: 23 -> 25; matrix products, arithmetic and copies ran while one was open for 2% -> 2% of each run, Pallas kernels for 15% -> 12%
where the time goes in v4:
time: 84.9 us
  starting transfers between devices  41.5 us (49%)
  waiting for transfers between devices  27.9 us (33%)
  Pallas kernels  13 us (15%)
  other arithmetic  1.4 us (2%)
  between operations  1.01 us (1%)
    ppermute x8, starting transfers between devices, scatter(): lax.ppermute(total_for(sums, base, rest, distance, came), 'col', ring)  20 us
    ppermute x10, starting transfers between devices, from_turn(): lax.ppermute(value, 'row', [(i ^ k if flips else (i + k) % n_row, i) for...  12.5 us
    ppermute x8, waiting for transfers between devices, scatter(): lax.ppermute(total_for(sums, base, rest, distance, came), 'col', ring)  8.87 us
    ppermute x10, waiting for transfers between devices, from_turn(): lax.ppermute(value, 'row', [(i ^ k if flips else (i + k) % n_row, i) for...  8.15 us
    ppermute x4, starting transfers between devices, scatter(): came = lax.ppermute(total, 'col', ring)  6.56 us
    pallas_call x5, Pallas kernels, transfer(): pl.pallas_call(functools.partial(transfer_kernel, fields_at, begin, end,...  6.23 us
    ppermute x4, waiting for transfers between devices, scatter(): came = lax.ppermute(total, 'col', ring)  5.78 us
    pallas_call x1, Pallas kernels, prepare(): pl.pallas_call(prepare_kernel, in_specs=[pl.BlockSpec(memory_space=pltpu....  4.48 us
  transfers between devices with their start and end apart: 34, of which 25 were waited for; matrix products, arithmetic and copies ran while one was open for 2% of the time, Pallas kernels for 12%

profile of v4, /device:TPU:0, one launch (start us, length us, event | category | flops | bytes accessed | tf_op | source)
XLA Modules:
  0.0 84.9 jit_solution(10164017063230801607)
XLA Ops:
  0.0 2.9 %collective-permute-start = (f32[8,64,128]{2,1,0:T(8,128)}, f32[8,64,128]{2,1,0:T(8,128)S(1)}, u32[]{:S(2)}, u32[]{:S(2)}) collective-permute-start(f32[8,64,128]{2,1,0:T(8,128)} %source_ref.5), channel_id=1, source_target_pairs={{8,0},{0,8},{24,16},{16,24},{9,1},{1,9},{25,17},{17,25},{10,2},{2,... | collective-permute-start | bytes 786440 | tf_op jit(solution)/shard_map/ppermute | solution.py:265
  2.9 1.5 %collective-permute-start.1 = (f32[8,64,128]{2,1,0:T(8,128)}, f32[8,64,128]{2,1,0:T(8,128)S(1)}, u32[]{:S(2)}, u32[]{:S(2)}) collective-permute-start(f32[8,64,128]{2,1,0:T(8,128)} %source_ref.5), channel_id=1, source_target_pairs={{16,0},{24,8},{0,16},{8,24},{17,1},{25,9},{1,17},{9,25},{18,2},{26... | collective-permute-start | bytes 786440 | tf_op jit(solution)/shard_map/ppermute | solution.py:265
  5.1 0.7 fusion.4
  5.9 4.5 %prepare.1.rest_1_.a_ref = bf16[257,64,128]{2,1,0:T(8,128)(2,1)S(1)} custom-call(f32[64,64,256]{2,1,0:T(8,128)} %bitcast.3), custom_call_target="tpu_custom_call" | custom-call | bytes 25165824 | tf_op jit(solution)/shard_map/prepare/pallas_call | solution.py:68
  10.9 1.6 %collective-permute-start.2 = (f32[4,64,128]{2,1,0:T(8,128)S(1)}, f32[4,64,128]{2,1,0:T(8,128)S(1)}, u32[]{:S(2)}, u32[]{:S(2)}) collective-permute-start(f32[4,64,128]{2,1,0:T(8,128)S(1)} %cut.8), channel_id=1, source_target_pairs={{16,0},{24,8},{0,16},{8,24},{17,1},{25,9},{1,17},{9,25},{18,2},{26... | collective-permute-start | bytes 393224 | tf_op jit(solution)/shard_map/ppermute | solution.py:265
  12.6 0.6 collective-permute-start.3
  13.4 0.6 keep.1.plan_ref
  14.0 2.0 %transfer.5.rest_2_ = f32[64,64,128]{2,1,0:T(8,128)S(1)} custom-call(s32[872]{0:T(1024)S(4)} %keep.1.plan_ref, bf16[257,64,128]{2,1,0:T(8,128)(2,1)S(1)} %prepare.1.rest_1_.a_ref, f32[8,64,128]{2,1,0:T(8,128)S(1)} %copy-done, f32[8,64,128]{2,1,0:T(8,128)S(1)} %collective-permute-done.rest_0_.rest_1_, f32[8,64,128]{2,1,0:T(8,128)S(1)} %collective-permute-done.1.rest_0_.rest_2_), custom_call_target="tpu_custom_call" | custom-call | tf_op jit(solution)/shard_map/transfer/pallas_call | solution.py:134
  16.0 1.6 %collective-permute-done.3.rest_1_ = f32[4,64,128]{2,1,0:T(8,128)S(1)} collective-permute-done((f32[4,64,128]{2,1,0:T(8,128)S(1)}, f32[4,64,128]{2,1,0:T(8,128)S(1)}, u32[]{:S(2)}, u32[]{:S(2)}) %collective-permute-start.3) | collective-permute-done | bytes 131104 | tf_op jit(solution)/shard_map/ppermute | solution.py:265
  17.6 0.9 %transfer.6.sums_ref.value_ref = f32[64,64,128]{2,1,0:T(8,128)S(1)} custom-call(s32[872]{0:T(1024)S(4)} %keep.1.plan_ref, bf16[257,64,128]{2,1,0:T(8,128)(2,1)S(1)} %prepare.1.rest_1_.a_ref, f32[4,64,128]{2,1,0:T(8,128)S(1)} %collective-permute-done.2.rest_0_, f32[4,64,128]{2,1,0:T(8,128)S(1)} %collective-permute-done.3.rest_1_, ...), custom_call_target="tpu_custom_call" | custom-call | tf_op jit(solution)/shard_map/transfer/pallas_call | solution.py:134
  18.7 0.5 collective-permute-start.12
  19.2 1.0 %collective-permute-done.4.got_ref = f32[8,64,128]{2,1,0:T(8,128)S(1)} collective-permute-done((f32[8,64,128]{2,1,0:T(8,128)S(1)}, f32[8,64,128]{2,1,0:T(8,128)S(1)}, u32[]{:S(2)}, u32[]{:S(2)}) %collective-permute-start.4) | collective-permute-done | bytes 262176 | tf_op jit(solution)/shard_map/ppermute | solution.py:288
  21.0 1.6 %collective-permute-start.6 = (f32[8,64,128]{2,1,0:T(8,128)S(1)}, f32[8,64,128]{2,1,0:T(8,128)S(1)}, u32[]{:S(2)}, u32[]{:S(2)}) collective-permute-start(f32[8,64,128]{2,1,0:T(8,128)S(1)} %carry.12.rest_0_), channel_id=1, source_target_pairs={{0,2},{1,0},{2,4},{3,1},{4,6},{5,3},{6,7},{7,5},{8,10},{9,8},{10,1... | collective-permute-start | bytes 786440 | tf_op jit(solution)/shard_map/ppermute | solution.py:303
  22.6 1.6 %collective-permute-start.14 = (f32[8,64,128]{2,1,0:T(8,128)S(1)}, f32[8,64,128]{2,1,0:T(8,128)S(1)}, u32[]{:S(2)}, u32[]{:S(2)}) collective-permute-start(f32[8,64,128]{2,1,0:T(8,128)S(1)} %carry.15.rest_0_), channel_id=1, source_target_pairs={{0,2},{1,0},{2,4},{3,1},{4,6},{5,3},{6,7},{7,5},{8,10},{9,8},{10,1... | collective-permute-start | bytes 786440 | tf_op jit(solution)/shard_map/ppermute | solution.py:303
  24.2 2.3 %collective-permute-done.6.rest_0_ = f32[8,64,128]{2,1,0:T(8,128)S(1)} collective-permute-done((f32[8,64,128]{2,1,0:T(8,128)S(1)}, f32[8,64,128]{2,1,0:T(8,128)S(1)}, u32[]{:S(2)}, u32[]{:S(2)}) %collective-permute-start.6) | collective-permute-done | bytes 262176 | tf_op jit(solution)/shard_map/ppermute | solution.py:303
  26.6 2.5 %collective-permute-start.7 = (f32[8,64,128]{2,1,0:T(8,128)S(1)}, f32[8,64,128]{2,1,0:T(8,128)S(1)}, u32[]{:S(2)}, u32[]{:S(2)}) collective-permute-start(f32[8,64,128]{2,1,0:T(8,128)S(1)} %carry.13), channel_id=1, source_target_pairs={{0,2},{1,0},{2,4},{3,1},{4,6},{5,3},{6,7},{7,5},{8,10},{9,8},{10,1... | collective-permute-start | bytes 786440 | tf_op jit(solution)/shard_map/ppermute | solution.py:305
  29.4 2.5 %collective-permute-start.15 = (f32[8,64,128]{2,1,0:T(8,128)S(1)}, f32[8,64,128]{2,1,0:T(8,128)S(1)}, u32[]{:S(2)}, u32[]{:S(2)}) collective-permute-start(f32[8,64,128]{2,1,0:T(8,128)S(1)} %carry.16), channel_id=1, source_target_pairs={{0,2},{1,0},{2,4},{3,1},{4,6},{5,3},{6,7},{7,5},{8,10},{9,8},{10,1... | collective-permute-start | bytes 786440 | tf_op jit(solution)/shard_map/ppermute | solution.py:305
  31.9 1.1 %collective-permute-done.7.rest_0_ = f32[8,64,128]{2,1,0:T(8,128)S(1)} collective-permute-done((f32[8,64,128]{2,1,0:T(8,128)S(1)}, f32[8,64,128]{2,1,0:T(8,128)S(1)}, u32[]{:S(2)}, u32[]{:S(2)}) %collective-permute-start.7) | collective-permute-done | bytes 262176 | tf_op jit(solution)/shard_map/ppermute | solution.py:305
  33.0 2.5 %collective-permute-start.8 = (f32[8,64,128]{2,1,0:T(8,128)S(1)}, f32[8,64,128]{2,1,0:T(8,128)S(1)}, u32[]{:S(2)}, u32[]{:S(2)}) collective-permute-start(f32[8,64,128]{2,1,0:T(8,128)S(1)} %carry.14), channel_id=1, source_target_pairs={{0,2},{1,0},{2,4},{3,1},{4,6},{5,3},{6,7},{7,5},{8,10},{9,8},{10,1... | collective-permute-start | bytes 786440 | tf_op jit(solution)/shard_map/ppermute | solution.py:305
  35.8 2.5 %collective-permute-start.16 = (f32[8,64,128]{2,1,0:T(8,128)S(1)}, f32[8,64,128]{2,1,0:T(8,128)S(1)}, u32[]{:S(2)}, u32[]{:S(2)}) collective-permute-start(f32[8,64,128]{2,1,0:T(8,128)S(1)} %carry.17), channel_id=1, source_target_pairs={{0,2},{1,0},{2,4},{3,1},{4,6},{5,3},{6,7},{7,5},{8,10},{9,8},{10,1... | collective-permute-start | bytes 786440 | tf_op jit(solution)/shard_map/ppermute | solution.py:305
  38.3 1.1 %collective-permute-done.8.came_ref.rest_1_ = f32[8,64,128]{2,1,0:T(8,128)S(1)} collective-permute-done((f32[8,64,128]{2,1,0:T(8,128)S(1)}, f32[8,64,128]{2,1,0:T(8,128)S(1)}, u32[]{:S(2)}, u32[]{:S(2)}) %collective-permute-start.8) | collective-permute-done | bytes 262176 | tf_op jit(solution)/shard_map/ppermute | solution.py:305
  39.5 1.3 %collective-permute-done.9.rest_2_ = f32[4,64,128]{2,1,0:T(8,128)S(1)} collective-permute-done((f32[4,64,128]{2,1,0:T(8,128)S(1)}, f32[4,64,128]{2,1,0:T(8,128)S(1)}, u32[]{:S(2)}, u32[]{:S(2)}) %collective-permute-start.9) | collective-permute-done | bytes 131104 | tf_op jit(solution)/shard_map/ppermute | solution.py:315
  40.9 1.3 %collective-permute-done.16.came_ref.rest_1_ = f32[8,64,128]{2,1,0:T(8,128)S(1)} collective-permute-done((f32[8,64,128]{2,1,0:T(8,128)S(1)}, f32[8,64,128]{2,1,0:T(8,128)S(1)}, u32[]{:S(2)}, u32[]{:S(2)}) %collective-permute-start.16) | collective-permute-done | bytes 262176 | tf_op jit(solution)/shard_map/ppermute | solution.py:305
  42.3 0.7 collective-permute-start.10
  43.7 1.5 %collective-permute-start.19 = (f32[4,64,128]{2,1,0:T(8,128)S(1)}, f32[4,64,128]{2,1,0:T(8,128)S(1)}, u32[]{:S(2)}, u32[]{:S(2)}) collective-permute-start(f32[4,64,128]{2,1,0:T(8,128)S(1)} %finish.4.rest_1_), channel_id=1, source_target_pairs={{16,0},{24,8},{0,16},{8,24},{17,1},{25,9},{1,17},{9,25},{18,2},{26... | collective-permute-start | bytes 393224 | tf_op jit(solution)/shard_map/ppermute | solution.py:265
  45.2 1.3 %collective-permute-start.20 = (f32[4,64,128]{2,1,0:T(8,128)S(1)}, f32[4,64,128]{2,1,0:T(8,128)S(1)}, u32[]{:S(2)}, u32[]{:S(2)}) collective-permute-start(f32[4,64,128]{2,1,0:T(8,128)S(1)} %finish.4.rest_1_), channel_id=1, source_target_pairs={{8,0},{0,8},{24,16},{16,24},{9,1},{1,9},{25,17},{17,25},{10,2},{2,... | collective-permute-start | bytes 393224 | tf_op jit(solution)/shard_map/ppermute | solution.py:265
  46.5 0.9 %transfer.7.rest_1_.rest_4_ = f32[64,64,128]{2,1,0:T(8,128)S(1)} custom-call(s32[872]{0:T(1024)S(4)} %keep.1.plan_ref, bf16[257,64,128]{2,1,0:T(8,128)(2,1)S(1)} %prepare.1.rest_1_.a_ref, f32[4,64,128]{2,1,0:T(8,128)S(1)} %finish.3.rest_0_, f32[4,64,128]{2,1,0:T(8,128)S(1)} %finish.4.rest_1_), custom_call_target="tpu_custom_call" | custom-call | tf_op jit(solution)/shard_map/transfer/pallas_call | solution.py:134
  47.5 1.2 %collective-permute-done.10.value_ref.rest_0_ = f32[4,64,128]{2,1,0:T(8,128)S(1)} collective-permute-done((f32[4,64,128]{2,1,0:T(8,128)S(1)}, f32[4,64,128]{2,1,0:T(8,128)S(1)}, u32[]{:S(2)}, u32[]{:S(2)}) %collective-permute-start.10) | collective-permute-done | bytes 131104 | tf_op jit(solution)/shard_map/ppermute | solution.py:265
  48.7 0.7 collective-permute-done.11.rest_0_.rest_2_
  49.8 2.4 %collective-permute-done.19.value_ref.rest_3_ = f32[4,64,128]{2,1,0:T(8,128)S(1)} collective-permute-done((f32[4,64,128]{2,1,0:T(8,128)S(1)}, f32[4,64,128]{2,1,0:T(8,128)S(1)}, u32[]{:S(2)}, u32[]{:S(2)}) %collective-permute-start.19) | collective-permute-done | bytes 131104 | tf_op jit(solution)/shard_map/ppermute | solution.py:265
  52.2 1.4 %collective-permute-start.21 = (f32[4,64,128]{2,1,0:T(8,128)S(1)}, f32[4,64,128]{2,1,0:T(8,128)S(1)}, u32[]{:S(2)}, u32[]{:S(2)}) collective-permute-start(f32[4,64,128]{2,1,0:T(8,128)S(1)} %cut.13), channel_id=1, source_target_pairs={{8,0},{0,8},{24,16},{16,24},{9,1},{1,9},{25,17},{17,25},{10,2},{2,... | collective-permute-start | bytes 393224 | tf_op jit(solution)/shard_map/ppermute | solution.py:265
  53.6 1.4 %transfer.8.rest_2_ = f32[64,64,128]{2,1,0:T(8,128)S(1)} custom-call(s32[872]{0:T(1024)S(4)} %keep.1.plan_ref, bf16[257,64,128]{2,1,0:T(8,128)(2,1)S(1)} %prepare.1.rest_1_.a_ref, f32[4,64,128]{2,1,0:T(8,128)S(1)} %collective-permute-done.10.value_ref.rest_0_, f32[4,64,128]{2,1,0:T(8,128)S(1)} %collective-permute-done.20.rest_0_.rest_1_, ...), custom_call_target="tpu_custom_call" | custom-call | tf_op jit(solution)/shard_map/transfer/pallas_call | solution.py:134
  55.1 2.2 %collective-permute-done.21.rest_1_ = f32[4,64,128]{2,1,0:T(8,128)S(1)} collective-permute-done((f32[4,64,128]{2,1,0:T(8,128)S(1)}, f32[4,64,128]{2,1,0:T(8,128)S(1)}, u32[]{:S(2)}, u32[]{:S(2)}) %collective-permute-start.21) | collective-permute-done | bytes 131104 | tf_op jit(solution)/shard_map/ppermute | solution.py:265
  57.2 0.9 %transfer.9.sums_ref.value_ref = f32[64,64,128]{2,1,0:T(8,128)S(1)} custom-call(s32[872]{0:T(1024)S(4)} %keep.1.plan_ref, bf16[257,64,128]{2,1,0:T(8,128)(2,1)S(1)} %prepare.1.rest_1_.a_ref, f32[4,64,128]{2,1,0:T(8,128)S(1)} %collective-permute-done.18.rest_0_, f32[4,64,128]{2,1,0:T(8,128)S(1)} %collective-permute-done.21.rest_1_, ...), custom_call_target="tpu_custom_call" | custom-call | tf_op jit(solution)/shard_map/transfer/pallas_call | solution.py:134
  58.3 0.5 collective-permute-start.28
  58.8 1.0 %collective-permute-done.22.got_ref = f32[8,64,128]{2,1,0:T(8,128)S(1)} collective-permute-done((f32[8,64,128]{2,1,0:T(8,128)S(1)}, f32[8,64,128]{2,1,0:T(8,128)S(1)}, u32[]{:S(2)}, u32[]{:S(2)}) %collective-permute-start.22) | collective-permute-done | bytes 262176 | tf_op jit(solution)/shard_map/ppermute | solution.py:288
  60.7 2.5 %collective-permute-start.24 = (f32[8,64,128]{2,1,0:T(8,128)S(1)}, f32[8,64,128]{2,1,0:T(8,128)S(1)}, u32[]{:S(2)}, u32[]{:S(2)}) collective-permute-start(f32[8,64,128]{2,1,0:T(8,128)S(1)} %carry.18.rest_0_), channel_id=1, source_target_pairs={{0,2},{1,0},{2,4},{3,1},{4,6},{5,3},{6,7},{7,5},{8,10},{9,8},{10,1... | collective-permute-start | bytes 786440 | tf_op jit(solution)/shard_map/ppermute | solution.py:303
  63.1 0.9 %collective-permute-start.30 = (f32[8,64,128]{2,1,0:T(8,128)S(1)}, f32[8,64,128]{2,1,0:T(8,128)S(1)}, u32[]{:S(2)}, u32[]{:S(2)}) collective-permute-start(f32[8,64,128]{2,1,0:T(8,128)S(1)} %carry.21.rest_0_), channel_id=1, source_target_pairs={{0,2},{1,0},{2,4},{3,1},{4,6},{5,3},{6,7},{7,5},{8,10},{9,8},{10,1... | collective-permute-start | bytes 786440 | tf_op jit(solution)/shard_map/ppermute | solution.py:303
  64.1 3.0 %collective-permute-done.24.rest_0_ = f32[8,64,128]{2,1,0:T(8,128)S(1)} collective-permute-done((f32[8,64,128]{2,1,0:T(8,128)S(1)}, f32[8,64,128]{2,1,0:T(8,128)S(1)}, u32[]{:S(2)}, u32[]{:S(2)}) %collective-permute-start.24) | collective-permute-done | bytes 262176 | tf_op jit(solution)/shard_map/ppermute | solution.py:303
  67.1 2.5 %collective-permute-start.25 = (f32[8,64,128]{2,1,0:T(8,128)S(1)}, f32[8,64,128]{2,1,0:T(8,128)S(1)}, u32[]{:S(2)}, u32[]{:S(2)}) collective-permute-start(f32[8,64,128]{2,1,0:T(8,128)S(1)} %carry.19), channel_id=1, source_target_pairs={{0,2},{1,0},{2,4},{3,1},{4,6},{5,3},{6,7},{7,5},{8,10},{9,8},{10,1... | collective-permute-start | bytes 786440 | tf_op jit(solution)/shard_map/ppermute | solution.py:305
  69.9 2.5 %collective-permute-start.31 = (f32[8,64,128]{2,1,0:T(8,128)S(1)}, f32[8,64,128]{2,1,0:T(8,128)S(1)}, u32[]{:S(2)}, u32[]{:S(2)}) collective-permute-start(f32[8,64,128]{2,1,0:T(8,128)S(1)} %carry.22), channel_id=1, source_target_pairs={{0,2},{1,0},{2,4},{3,1},{4,6},{5,3},{6,7},{7,5},{8,10},{9,8},{10,1... | collective-permute-start | bytes 786440 | tf_op jit(solution)/shard_map/ppermute | solution.py:305
  72.4 1.1 %collective-permute-done.25.rest_0_ = f32[8,64,128]{2,1,0:T(8,128)S(1)} collective-permute-done((f32[8,64,128]{2,1,0:T(8,128)S(1)}, f32[8,64,128]{2,1,0:T(8,128)S(1)}, u32[]{:S(2)}, u32[]{:S(2)}) %collective-permute-start.25) | collective-permute-done | bytes 262176 | tf_op jit(solution)/shard_map/ppermute | solution.py:305
  73.5 2.5 %collective-permute-start.26 = (f32[8,64,128]{2,1,0:T(8,128)S(1)}, f32[8,64,128]{2,1,0:T(8,128)S(1)}, u32[]{:S(2)}, u32[]{:S(2)}) collective-permute-start(f32[8,64,128]{2,1,0:T(8,128)S(1)} %carry.20), channel_id=1, source_target_pairs={{0,2},{1,0},{2,4},{3,1},{4,6},{5,3},{6,7},{7,5},{8,10},{9,8},{10,1... | collective-permute-start | bytes 786440 | tf_op jit(solution)/shard_map/ppermute | solution.py:305
  76.4 2.5 %collective-permute-start.32 = (f32[8,64,128]{2,1,0:T(8,128)S(1)}, f32[8,64,128]{2,1,0:T(8,128)S(1)}, u32[]{:S(2)}, u32[]{:S(2)}) collective-permute-start(f32[8,64,128]{2,1,0:T(8,128)S(1)} %carry.23), channel_id=1, source_target_pairs={{0,2},{1,0},{2,4},{3,1},{4,6},{5,3},{6,7},{7,5},{8,10},{9,8},{10,1... | collective-permute-start | bytes 786440 | tf_op jit(solution)/shard_map/ppermute | solution.py:305
  78.9 1.1 %collective-permute-done.26.came_ref.rest_1_ = f32[8,64,128]{2,1,0:T(8,128)S(1)} collective-permute-done((f32[8,64,128]{2,1,0:T(8,128)S(1)}, f32[8,64,128]{2,1,0:T(8,128)S(1)}, u32[]{:S(2)}, u32[]{:S(2)}) %collective-permute-start.26) | collective-permute-done | bytes 262176 | tf_op jit(solution)/shard_map/ppermute | solution.py:305
  80.0 2.7 %collective-permute-done.32.came_ref.rest_4_ = f32[8,64,128]{2,1,0:T(8,128)S(1)} collective-permute-done((f32[8,64,128]{2,1,0:T(8,128)S(1)}, f32[8,64,128]{2,1,0:T(8,128)S(1)}, u32[]{:S(2)}, u32[]{:S(2)}) %collective-permute-start.32) | collective-permute-done | bytes 262176 | tf_op jit(solution)/shard_map/ppermute | solution.py:305
  82.9 1.3 %collective-permute-done.33.rest_5_ = f32[4,64,128]{2,1,0:T(8,128)S(1)} collective-permute-done((f32[4,64,128]{2,1,0:T(8,128)S(1)}, f32[4,64,128]{2,1,0:T(8,128)S(1)}, u32[]{:S(2)}, u32[]{:S(2)}) %collective-permute-start.33) | collective-permute-done | bytes 131104 | tf_op jit(solution)/shard_map/ppermute | solution.py:315
  84.2 0.8 finish.5
  (66 shorter events, 5.5 us)
Async XLA Ops:
  0.0 10.8 %collective-permute-start = (f32[8,64,128]{2,1,0:T(8,128)}, f32[8,64,128]{2,1,0:T(8,128)S(1)}, u32[]{:S(2)}, u32[]{:S(2)}) collective-permute-start(f32[8,64,128]{2,1,0:T(8,128)} %source_ref.5), channel_id=1, source_target_pairs={{8,0},{0,8},{24,16},{16,24},{9,1},{1,9},{25,17},{17,25},{10,2},{2,... | collective-permute-start | bytes 786440 | tf_op jit(solution)/shard_map/ppermute | solution.py:265
  2.9 8.0 %collective-permute-start.1 = (f32[8,64,128]{2,1,0:T(8,128)}, f32[8,64,128]{2,1,0:T(8,128)S(1)}, u32[]{:S(2)}, u32[]{:S(2)}) collective-permute-start(f32[8,64,128]{2,1,0:T(8,128)} %source_ref.5), channel_id=1, source_target_pairs={{16,0},{24,8},{0,16},{8,24},{17,1},{25,9},{1,17},{9,25},{18,2},{26... | collective-permute-start | bytes 786440 | tf_op jit(solution)/shard_map/ppermute | solution.py:265
  10.9 5.1 %collective-permute-start.2 = (f32[4,64,128]{2,1,0:T(8,128)S(1)}, f32[4,64,128]{2,1,0:T(8,128)S(1)}, u32[]{:S(2)}, u32[]{:S(2)}) collective-permute-start(f32[4,64,128]{2,1,0:T(8,128)S(1)} %cut.8), channel_id=1, source_target_pairs={{16,0},{24,8},{0,16},{8,24},{17,1},{25,9},{1,17},{9,25},{18,2},{26... | collective-permute-start | bytes 393224 | tf_op jit(solution)/shard_map/ppermute | solution.py:265
  12.5 1.4 %copy-start = (f32[8,64,128]{2,1,0:T(8,128)S(1)}, f32[8,64,128]{2,1,0:T(8,128)}, u32[]{:S(2)}) copy-start(f32[8,64,128]{2,1,0:T(8,128)} %source_ref.5) | copy-start | bytes 786436
  12.6 5.0 %collective-permute-start.3 = (f32[4,64,128]{2,1,0:T(8,128)S(1)}, f32[4,64,128]{2,1,0:T(8,128)S(1)}, u32[]{:S(2)}, u32[]{:S(2)}) collective-permute-start(f32[4,64,128]{2,1,0:T(8,128)S(1)} %cut.9), channel_id=1, source_target_pairs={{8,0},{0,8},{24,16},{16,24},{9,1},{1,9},{25,17},{17,25},{10,2},{2,... | collective-permute-start | bytes 393224 | tf_op jit(solution)/shard_map/ppermute | solution.py:265
  18.6 1.6 %collective-permute-start.4 = (f32[8,64,128]{2,1,0:T(8,128)S(1)}, f32[8,64,128]{2,1,0:T(8,128)S(1)}, u32[]{:S(2)}, u32[]{:S(2)}) collective-permute-start(f32[8,64,128]{2,1,0:T(8,128)S(1)} %get-tuple-element.15), channel_id=1, source_target_pairs={{0,1},{1,0},{2,3},{3,2},{4,5},{5,4},{6,7},{7,6},{8,9},{9,8},{10,11... | collective-permute-start | bytes 786440 | tf_op jit(solution)/shard_map/ppermute | solution.py:288
  18.7 1.9 %collective-permute-start.12 = (f32[8,64,128]{2,1,0:T(8,128)S(1)}, f32[8,64,128]{2,1,0:T(8,128)S(1)}, u32[]{:S(2)}, u32[]{:S(2)}) collective-permute-start(f32[8,64,128]{2,1,0:T(8,128)S(1)} %get-tuple-element.14), channel_id=1, source_target_pairs={{0,1},{1,0},{2,3},{3,2},{4,5},{5,4},{6,7},{7,6},{8,9},{9,8},{10,11... | collective-permute-start | bytes 786440 | tf_op jit(solution)/shard_map/ppermute | solution.py:288
  20.3 6.2 %collective-permute-start.5 = (f32[24,64,128]{2,1,0:T(8,128)S(1)}, f32[24,64,128]{2,1,0:T(8,128)S(1)}, u32[]{:S(2)}, u32[]{:S(2)}) collective-permute-start(f32[24,64,128]{2,1,0:T(8,128)S(1)} %cut.10), channel_id=1, source_target_pairs={{0,1},{1,0},{2,3},{3,2},{4,5},{5,4},{6,7},{7,6},{8,9},{9,8},{10,11... | collective-permute-start | bytes 2359304 | tf_op jit(solution)/shard_map/ppermute | solution.py:292
  20.7 8.7 %collective-permute-start.13 = (f32[24,64,128]{2,1,0:T(8,128)S(1)}, f32[24,64,128]{2,1,0:T(8,128)S(1)}, u32[]{:S(2)}, u32[]{:S(2)}) collective-permute-start(f32[24,64,128]{2,1,0:T(8,128)S(1)} %cut.11), channel_id=1, source_target_pairs={{0,1},{1,0},{2,3},{3,2},{4,5},{5,4},{6,7},{7,6},{8,9},{9,8},{10,11... | collective-permute-start | bytes 2359304 | tf_op jit(solution)/shard_map/ppermute | solution.py:292
  21.0 5.5 %collective-permute-start.6 = (f32[8,64,128]{2,1,0:T(8,128)S(1)}, f32[8,64,128]{2,1,0:T(8,128)S(1)}, u32[]{:S(2)}, u32[]{:S(2)}) collective-permute-start(f32[8,64,128]{2,1,0:T(8,128)S(1)} %carry.12.rest_0_), channel_id=1, source_target_pairs={{0,2},{1,0},{2,4},{3,1},{4,6},{5,3},{6,7},{7,5},{8,10},{9,8},{10,1... | collective-permute-start | bytes 786440 | tf_op jit(solution)/shard_map/ppermute | solution.py:303
  22.6 6.7 %collective-permute-start.14 = (f32[8,64,128]{2,1,0:T(8,128)S(1)}, f32[8,64,128]{2,1,0:T(8,128)S(1)}, u32[]{:S(2)}, u32[]{:S(2)}) collective-permute-start(f32[8,64,128]{2,1,0:T(8,128)S(1)} %carry.15.rest_0_), channel_id=1, source_target_pairs={{0,2},{1,0},{2,4},{3,1},{4,6},{5,3},{6,7},{7,5},{8,10},{9,8},{10,1... | collective-permute-start | bytes 786440 | tf_op jit(solution)/shard_map/ppermute | solution.py:303
  26.6 6.4 %collective-permute-start.7 = (f32[8,64,128]{2,1,0:T(8,128)S(1)}, f32[8,64,128]{2,1,0:T(8,128)S(1)}, u32[]{:S(2)}, u32[]{:S(2)}) collective-permute-start(f32[8,64,128]{2,1,0:T(8,128)S(1)} %carry.13), channel_id=1, source_target_pairs={{0,2},{1,0},{2,4},{3,1},{4,6},{5,3},{6,7},{7,5},{8,10},{9,8},{10,1... | collective-permute-start | bytes 786440 | tf_op jit(solution)/shard_map/ppermute | solution.py:305
  29.4 6.4 %collective-permute-start.15 = (f32[8,64,128]{2,1,0:T(8,128)S(1)}, f32[8,64,128]{2,1,0:T(8,128)S(1)}, u32[]{:S(2)}, u32[]{:S(2)}) collective-permute-start(f32[8,64,128]{2,1,0:T(8,128)S(1)} %carry.16), channel_id=1, source_target_pairs={{0,2},{1,0},{2,4},{3,1},{4,6},{5,3},{6,7},{7,5},{8,10},{9,8},{10,1... | collective-permute-start | bytes 786440 | tf_op jit(solution)/shard_map/ppermute | solution.py:305
  33.0 6.4 %collective-permute-start.8 = (f32[8,64,128]{2,1,0:T(8,128)S(1)}, f32[8,64,128]{2,1,0:T(8,128)S(1)}, u32[]{:S(2)}, u32[]{:S(2)}) collective-permute-start(f32[8,64,128]{2,1,0:T(8,128)S(1)} %carry.14), channel_id=1, source_target_pairs={{0,2},{1,0},{2,4},{3,1},{4,6},{5,3},{6,7},{7,5},{8,10},{9,8},{10,1... | collective-permute-start | bytes 786440 | tf_op jit(solution)/shard_map/ppermute | solution.py:305
  35.8 6.4 %collective-permute-start.16 = (f32[8,64,128]{2,1,0:T(8,128)S(1)}, f32[8,64,128]{2,1,0:T(8,128)S(1)}, u32[]{:S(2)}, u32[]{:S(2)}) collective-permute-start(f32[8,64,128]{2,1,0:T(8,128)S(1)} %carry.17), channel_id=1, source_target_pairs={{0,2},{1,0},{2,4},{3,1},{4,6},{5,3},{6,7},{7,5},{8,10},{9,8},{10,1... | collective-permute-start | bytes 786440 | tf_op jit(solution)/shard_map/ppermute | solution.py:305
  39.4 1.4 %collective-permute-start.9 = (f32[4,64,128]{2,1,0:T(8,128)S(1)}, f32[4,64,128]{2,1,0:T(8,128)S(1)}, u32[]{:S(2)}, u32[]{:S(2)}) collective-permute-start(f32[4,64,128]{2,1,0:T(8,128)S(1)} %cross.4), channel_id=1, source_target_pairs={{0,1},{1,0},{2,3},{3,2},{4,5},{5,4},{6,7},{7,6},{8,9},{9,8},{10,11... | collective-permute-start | bytes 393224 | tf_op jit(solution)/shard_map/ppermute | solution.py:315
  42.2 1.4 %collective-permute-start.17 = (f32[4,64,128]{2,1,0:T(8,128)S(1)}, f32[4,64,128]{2,1,0:T(8,128)S(1)}, u32[]{:S(2)}, u32[]{:S(2)}) collective-permute-start(f32[4,64,128]{2,1,0:T(8,128)S(1)} %cross.5), channel_id=1, source_target_pairs={{0,1},{1,0},{2,3},{3,2},{4,5},{5,4},{6,7},{7,6},{8,9},{9,8},{10,11... | collective-permute-start | bytes 393224 | tf_op jit(solution)/shard_map/ppermute | solution.py:315
  42.3 6.4 %collective-permute-start.10 = (f32[4,64,128]{2,1,0:T(8,128)S(1)}, f32[4,64,128]{2,1,0:T(8,128)S(1)}, u32[]{:S(2)}, u32[]{:S(2)}) collective-permute-start(f32[4,64,128]{2,1,0:T(8,128)S(1)} %finish.3.rest_0_), channel_id=1, source_target_pairs={{8,0},{0,8},{24,16},{16,24},{9,1},{1,9},{25,17},{17,25},{10,2},{2,... | collective-permute-start | bytes 393224 | tf_op jit(solution)/shard_map/ppermute | solution.py:265
  43.0 6.3 %collective-permute-start.11 = (f32[4,64,128]{2,1,0:T(8,128)S(1)}, f32[4,64,128]{2,1,0:T(8,128)S(1)}, u32[]{:S(2)}, u32[]{:S(2)}) collective-permute-start(f32[4,64,128]{2,1,0:T(8,128)S(1)} %finish.3.rest_0_), channel_id=1, source_target_pairs={{16,0},{24,8},{0,16},{8,24},{17,1},{25,9},{1,17},{9,25},{18,2},{26... | collective-permute-start | bytes 393224 | tf_op jit(solution)/shard_map/ppermute | solution.py:265
  43.7 8.5 %collective-permute-start.19 = (f32[4,64,128]{2,1,0:T(8,128)S(1)}, f32[4,64,128]{2,1,0:T(8,128)S(1)}, u32[]{:S(2)}, u32[]{:S(2)}) collective-permute-start(f32[4,64,128]{2,1,0:T(8,128)S(1)} %finish.4.rest_1_), channel_id=1, source_target_pairs={{16,0},{24,8},{0,16},{8,24},{17,1},{25,9},{1,17},{9,25},{18,2},{26... | collective-permute-start | bytes 393224 | tf_op jit(solution)/shard_map/ppermute | solution.py:265
  45.2 7.0 %collective-permute-start.20 = (f32[4,64,128]{2,1,0:T(8,128)S(1)}, f32[4,64,128]{2,1,0:T(8,128)S(1)}, u32[]{:S(2)}, u32[]{:S(2)}) collective-permute-start(f32[4,64,128]{2,1,0:T(8,128)S(1)} %finish.4.rest_1_), channel_id=1, source_target_pairs={{8,0},{0,8},{24,16},{16,24},{9,1},{1,9},{25,17},{17,25},{10,2},{2,... | collective-permute-start | bytes 393224 | tf_op jit(solution)/shard_map/ppermute | solution.py:265
  49.4 5.6 %collective-permute-start.18 = (f32[4,64,128]{2,1,0:T(8,128)S(1)}, f32[4,64,128]{2,1,0:T(8,128)S(1)}, u32[]{:S(2)}, u32[]{:S(2)}) collective-permute-start(f32[4,64,128]{2,1,0:T(8,128)S(1)} %cut.12), channel_id=1, source_target_pairs={{16,0},{24,8},{0,16},{8,24},{17,1},{25,9},{1,17},{9,25},{18,2},{26... | collective-permute-start | bytes 393224 | tf_op jit(solution)/shard_map/ppermute | solution.py:265
  52.2 5.0 %collective-permute-start.21 = (f32[4,64,128]{2,1,0:T(8,128)S(1)}, f32[4,64,128]{2,1,0:T(8,128)S(1)}, u32[]{:S(2)}, u32[]{:S(2)}) collective-permute-start(f32[4,64,128]{2,1,0:T(8,128)S(1)} %cut.13), channel_id=1, source_target_pairs={{8,0},{0,8},{24,16},{16,24},{9,1},{1,9},{25,17},{17,25},{10,2},{2,... | collective-permute-start | bytes 393224 | tf_op jit(solution)/shard_map/ppermute | solution.py:265
  58.2 1.6 %collective-permute-start.22 = (f32[8,64,128]{2,1,0:T(8,128)S(1)}, f32[8,64,128]{2,1,0:T(8,128)S(1)}, u32[]{:S(2)}, u32[]{:S(2)}) collective-permute-start(f32[8,64,128]{2,1,0:T(8,128)S(1)} %get-tuple-element.13), channel_id=1, source_target_pairs={{0,1},{1,0},{2,3},{3,2},{4,5},{5,4},{6,7},{7,6},{8,9},{9,8},{10,11... | collective-permute-start | bytes 786440 | tf_op jit(solution)/shard_map/ppermute | solution.py:288
  58.3 1.9 %collective-permute-start.28 = (f32[8,64,128]{2,1,0:T(8,128)S(1)}, f32[8,64,128]{2,1,0:T(8,128)S(1)}, u32[]{:S(2)}, u32[]{:S(2)}) collective-permute-start(f32[8,64,128]{2,1,0:T(8,128)S(1)} %get-tuple-element.12), channel_id=1, source_target_pairs={{0,1},{1,0},{2,3},{3,2},{4,5},{5,4},{6,7},{7,6},{8,9},{9,8},{10,11... | collective-permute-start | bytes 786440 | tf_op jit(solution)/shard_map/ppermute | solution.py:288
  59.9 7.1 %collective-permute-start.23 = (f32[24,64,128]{2,1,0:T(8,128)S(1)}, f32[24,64,128]{2,1,0:T(8,128)S(1)}, u32[]{:S(2)}, u32[]{:S(2)}) collective-permute-start(f32[24,64,128]{2,1,0:T(8,128)S(1)} %cut.14), channel_id=1, source_target_pairs={{0,1},{1,0},{2,3},{3,2},{4,5},{5,4},{6,7},{7,6},{8,9},{9,8},{10,11... | collective-permute-start | bytes 2359304 | tf_op jit(solution)/shard_map/ppermute | solution.py:292
  60.3 9.5 %collective-permute-start.29 = (f32[24,64,128]{2,1,0:T(8,128)S(1)}, f32[24,64,128]{2,1,0:T(8,128)S(1)}, u32[]{:S(2)}, u32[]{:S(2)}) collective-permute-start(f32[24,64,128]{2,1,0:T(8,128)S(1)} %cut.15), channel_id=1, source_target_pairs={{0,1},{1,0},{2,3},{3,2},{4,5},{5,4},{6,7},{7,6},{8,9},{9,8},{10,11... | collective-permute-start | bytes 2359304 | tf_op jit(solution)/shard_map/ppermute | solution.py:292
  60.7 6.4 %collective-permute-start.24 = (f32[8,64,128]{2,1,0:T(8,128)S(1)}, f32[8,64,128]{2,1,0:T(8,128)S(1)}, u32[]{:S(2)}, u32[]{:S(2)}) collective-permute-start(f32[8,64,128]{2,1,0:T(8,128)S(1)} %carry.18.rest_0_), channel_id=1, source_target_pairs={{0,2},{1,0},{2,4},{3,1},{4,6},{5,3},{6,7},{7,5},{8,10},{9,8},{10,1... | collective-permute-start | bytes 786440 | tf_op jit(solution)/shard_map/ppermute | solution.py:303
  63.1 6.7 %collective-permute-start.30 = (f32[8,64,128]{2,1,0:T(8,128)S(1)}, f32[8,64,128]{2,1,0:T(8,128)S(1)}, u32[]{:S(2)}, u32[]{:S(2)}) collective-permute-start(f32[8,64,128]{2,1,0:T(8,128)S(1)} %carry.21.rest_0_), channel_id=1, source_target_pairs={{0,2},{1,0},{2,4},{3,1},{4,6},{5,3},{6,7},{7,5},{8,10},{9,8},{10,1... | collective-permute-start | bytes 786440 | tf_op jit(solution)/shard_map/ppermute | solution.py:303
  67.1 6.4 %collective-permute-start.25 = (f32[8,64,128]{2,1,0:T(8,128)S(1)}, f32[8,64,128]{2,1,0:T(8,128)S(1)}, u32[]{:S(2)}, u32[]{:S(2)}) collective-permute-start(f32[8,64,128]{2,1,0:T(8,128)S(1)} %carry.19), channel_id=1, source_target_pairs={{0,2},{1,0},{2,4},{3,1},{4,6},{5,3},{6,7},{7,5},{8,10},{9,8},{10,1... | collective-permute-start | bytes 786440 | tf_op jit(solution)/shard_map/ppermute | solution.py:305
  69.9 6.4 %collective-permute-start.31 = (f32[8,64,128]{2,1,0:T(8,128)S(1)}, f32[8,64,128]{2,1,0:T(8,128)S(1)}, u32[]{:S(2)}, u32[]{:S(2)}) collective-permute-start(f32[8,64,128]{2,1,0:T(8,128)S(1)} %carry.22), channel_id=1, source_target_pairs={{0,2},{1,0},{2,4},{3,1},{4,6},{5,3},{6,7},{7,5},{8,10},{9,8},{10,1... | collective-permute-start | bytes 786440 | tf_op jit(solution)/shard_map/ppermute | solution.py:305
  73.5 6.4 %collective-permute-start.26 = (f32[8,64,128]{2,1,0:T(8,128)S(1)}, f32[8,64,128]{2,1,0:T(8,128)S(1)}, u32[]{:S(2)}, u32[]{:S(2)}) collective-permute-start(f32[8,64,128]{2,1,0:T(8,128)S(1)} %carry.20), channel_id=1, source_target_pairs={{0,2},{1,0},{2,4},{3,1},{4,6},{5,3},{6,7},{7,5},{8,10},{9,8},{10,1... | collective-permute-start | bytes 786440 | tf_op jit(solution)/shard_map/ppermute | solution.py:305
  76.4 6.4 %collective-permute-start.32 = (f32[8,64,128]{2,1,0:T(8,128)S(1)}, f32[8,64,128]{2,1,0:T(8,128)S(1)}, u32[]{:S(2)}, u32[]{:S(2)}) collective-permute-start(f32[8,64,128]{2,1,0:T(8,128)S(1)} %carry.23), channel_id=1, source_target_pairs={{0,2},{1,0},{2,4},{3,1},{4,6},{5,3},{6,7},{7,5},{8,10},{9,8},{10,1... | collective-permute-start | bytes 786440 | tf_op jit(solution)/shard_map/ppermute | solution.py:305
  80.0 2.9 %collective-permute-start.27 = (f32[4,64,128]{2,1,0:T(8,128)S(1)}, f32[4,64,128]{2,1,0:T(8,128)S(1)}, u32[]{:S(2)}, u32[]{:S(2)}) collective-permute-start(f32[4,64,128]{2,1,0:T(8,128)S(1)} %cross.6), channel_id=1, source_target_pairs={{0,1},{1,0},{2,3},{3,2},{4,5},{5,4},{6,7},{7,6},{8,9},{9,8},{10,11... | collective-permute-start | bytes 393224 | tf_op jit(solution)/shard_map/ppermute | solution.py:315
  82.8 1.4 %collective-permute-start.33 = (f32[4,64,128]{2,1,0:T(8,128)S(1)}, f32[4,64,128]{2,1,0:T(8,128)S(1)}, u32[]{:S(2)}, u32[]{:S(2)}) collective-permute-start(f32[4,64,128]{2,1,0:T(8,128)S(1)} %cross.7), channel_id=1, source_target_pairs={{0,1},{1,0},{2,3},{3,2},{4,5},{5,4},{6,7},{7,6},{8,9},{9,8},{10,11... | collective-permute-start | bytes 393224 | tf_op jit(solution)/shard_map/ppermute | solution.py:315

commit v5 on v4

--- a/solution.py
+++ b/solution.py
@@ -9,7 +9,7 @@
 
 ITERS = 2
 HALVES = 2
-STAGES = 3
+STAGES = 4
 GROUP = 32
 CHUNK = 16
 PLAN_HEAD = 8
@@ -180,10 +180,6 @@
     )(*args, *after)
 
 
-def block_of(distance):
-    return {0: 1, 1: 0}.get(distance, distance)
-
-
 def carry_kernel(mine, other, sums_ref, got_ref, *rest):
     came_refs, out_ref = rest[:-1], rest[-1]
     first = first_of_line()
@@ -194,15 +190,15 @@
         out_ref[c] = total
 
 
-def finish_kernel(n_halves, half_at, owns, source_ref, sums_ref, *rest):
+def finish_kernel(half_at, owns, skipped, source_ref, sums_ref, *rest):
     out_ref = rest[-1]
     first = first_of_line()
-    per = (len(rest) - 1) // n_halves
-    for h in range(n_halves):
+    per = (len(rest) - 1) // len(owns)
+    for h, own in enumerate(owns):
         got_ref, *ends = rest[h * per : (h + 1) * per]
-        half = out_ref.shape[0] // n_halves
+        half = out_ref.shape[0] // len(owns)
         for c in range(half):
-            total = source_ref[(half_at + h) * half + c] + (sums_ref[owns[half_at + h] + c] + got_ref[half + c])
+            total = source_ref[(half_at + h) * half + c] + (sums_ref[own + c] + got_ref[own - skipped + half + c])
             if ends:
                 total += jnp.where(first, 0.0, ends[0][c]) + ends[1][c]
             out_ref[h * half + c] = total
@@ -218,6 +214,12 @@
 def cut_kernel(at, value_ref, *rest):
     out_ref = rest[-1]
     out_ref[...] = value_ref[at : at + out_ref.shape[0]]
+
+
+def sums_at(h, distance, pairs, half):
+    order = (distance + pairs - 1) % pairs if pairs > 1 else distance
+    size = 2 * half
+    return jnp.where(order == 0, h * size, (HALVES + h * (pairs - 1) + order - 1) * size)
 
 
 def make_plan(row_index, col_index, live, bricks, n_row, n_col, flips):
@@ -227,9 +229,8 @@
     column, brick = row_index // bricks, row_index % bricks
     pair, side = column // 2, column % 2
     ahead = jnp.where(my_side == 0, pair - my_pair, my_pair - pair) % pairs
-    ahead = jnp.where(ahead < 2, 1 - ahead, ahead) if pairs > 1 else ahead
     carrier = jnp.where(pair > my_pair, 0, jnp.where(pair < my_pair, 1, my_side))
-    place = ((brick // half * pairs + ahead) * 2 + (side ^ carrier)) * half + brick % half
+    place = sums_at(brick // half, ahead, pairs, half) + (side ^ carrier) * half + brick % half
 
     from_row, from_brick = col_index // bricks, col_index % bricks
     turn = from_row ^ my_row if flips else (from_row - my_row) % n_row
@@ -237,7 +238,7 @@
 
     n = row_index.shape[0]
     slots = jnp.arange(n, dtype=jnp.int32)
-    part = jnp.where(turn == 0, 0, jnp.where(turn < n_row - 1, 1, 2))
+    part = jnp.where(turn == 0, 0, jnp.where(turn < n_row - 1, 1, jnp.where(place < HALVES * 2 * half, 2, 3)))
     part = jnp.where(slots < live, part, STAGES)
     key = part * n + slots
     rank = jnp.sum(key[None, :] < key[:, None], axis=1, dtype=jnp.int32)
@@ -278,32 +279,30 @@
         at = [k * bricks + i * (bricks // len(pieces)) for k, pieces in turns.items() for i in range(len(pieces))]
         return transfer(plan, matrix, fields, at, n_row * bricks, first, end, before, bricks * n_col)
 
-    in_half = half * n_col
-    owns = [h * in_half + (block if pairs > 1 else 0) for h in range(HALVES)]
-
-    def begin(sums, h):
-        base = h * in_half
+    leading = HALVES * block
+
+    def at(h, distance):
+        order = (distance + pairs - 1) % pairs
+        return h * block if order == 0 else leading + (h * (pairs - 1) + order - 1) * block
+
+    def scatter(lead, sums):
+        first = lax.ppermute(lead[:leading], "col", swap)
         if pairs == 1:
-            return base, None, lax.ppermute(sums[base : base + in_half], "col", swap)
-        lead = lax.ppermute(sums[base : base + block], "col", swap)
-        mine = base + block_of(pairs - 1) * block
-        total = small_call(functools.partial(carry_kernel, mine, 0), (block,), "carry", sums, lead)[0]
-        later = cut(sums, base + block, in_half - block, (total,))
-        return base, total, lax.ppermute(later, "col", swap)
-
-    def total_for(sums, base, rest, distance, came):
-        mine, other = base + block_of(distance) * block, (block_of(pairs - distance) - 1) * block
-        return small_call(functools.partial(carry_kernel, mine, other), (block,), "carry", sums, rest, came)[0]
-
-    def scatter(sums):
+            return [[first]] * HALVES
+        far = pairs - 1
+        totals = []
+        for h in range(HALVES):
+            kernel = functools.partial(carry_kernel, at(h, far), h * block)
+            totals += small_call(kernel, (block,), "carry", sums, first)
+        rest = lax.ppermute(cut(sums, leading, sums.shape[0] - leading, totals), "col", swap)
         parts = []
-        for base, total, rest in [begin(sums, h) for h in range(HALVES)]:
-            parts.append([rest])
-            if pairs > 1:
+        for h in range(HALVES):
+            came = lax.ppermute(totals[h], "col", ring)
+            for distance in range(far - 1, 0, -1):
+                kernel = functools.partial(carry_kernel, at(h, distance), at(h, pairs - distance) - leading)
+                total = small_call(kernel, (block,), "carry", sums, rest, came)[0]
                 came = lax.ppermute(total, "col", ring)
-                for distance in range(pairs - 2, 0, -1):
-                    came = lax.ppermute(total_for(sums, base, rest, distance, came), "col", ring)
-                parts[-1].append(came)
+            parts.append([rest, came])
         return parts
 
     def finish(sums, parts, half_at, after=()):
@@ -313,32 +312,38 @@
             if came:
                 crossing = small_call(cross_kernel, (half,), "cross", *came, after=after)[0]
                 args.append(lax.ppermute(crossing, "col", swap))
-        kernel = functools.partial(finish_kernel, len(parts), half_at, owns)
+        owns = [at(half_at + h, 0) for h in range(len(parts))]
+        kernel = functools.partial(finish_kernel, half_at, owns, leading if pairs > 1 else 0)
         return small_call(kernel, (len(parts) * half,), "finish", source, sums, *args)[0]
 
     plan = in_scalar_memory(make_plan(row_index, col_index, live_count[0], bricks, n_row, n_col, flips))
     matrix = prepare(blocks)
 
+    def by_row(field):
+        return dict(enumerate([field, *gather(field, True)]))
+
+    def last_row(last, sums):
+        lead = apply({3: last}, 2, 3, sums)
+        return lead, apply({3: last}, 3, STAGES, lead)
+
     if n_row == 4:
         one, two = gather([source], False)
-        last = [forward(one[0][:half], 2, two[0], matrix), forward(two[0][half:], 1, one[0], matrix)]
-        sums = apply({0: [source], 1: one, 2: two}, 0, 2)
-        sums = apply({3: last}, 2, STAGES, sums)
+        last = [forward(one[0][:half], 2, matrix), forward(two[0][half:], 1, matrix)]
+        lead, sums = last_row(last, apply({0: [source], 1: one, 2: two}, 0, 2))
     else:
-        sums = apply(dict(enumerate([[source], *gather([source], True)])), 0, STAGES)
+        lead = sums = apply(by_row([source]), 0, STAGES)
     for _ in range(ITERS - 1):
         field = []
-        for h, part in enumerate(scatter(sums)):
+        for h, part in enumerate(scatter(lead, sums)):
             field.append(finish(sums, [part], h, field))
-        sums = apply({0: field}, 0, 1)
         if n_row == 4:
             one, two = gather(field, False)
-            last = [forward(one[0], 2, two[0], sums), forward(two[1], 1, one[1])]
-            sums = apply({1: one, 2: two}, 1, 2, sums)
-            sums = apply({3: last}, 2, STAGES, sums)
+            sums = apply({0: field}, 0, 1)
+            last = [forward(one[0], 2), forward(two[1], 1, sums)]
+            lead, sums = last_row(last, apply({1: one, 2: two}, 1, 2, sums))
         else:
-            sums = apply(dict(enumerate(gather(field, True), 1)), 1, STAGES, sums)
-    return finish(sums, scatter(sums), 0)
+            lead = sums = apply(by_row(field), 0, STAGES)
+    return finish(sums, scatter(lead, sums), 0)
 
 
 def solution(mesh):

time: 84.9 us -> 81.6 us (0.961)
  waiting for transfers between devices: 27.9 us -> 21.8 us
  Pallas kernels: 13 us -> 15.9 us
  starting transfers between devices: 41.5 us -> 40.5 us
    ppermute x16 -> x8, starting transfers between devices: 22.2 us -> 7.76 us  [the longest x4 7.21 us: scatter(): came = lax.ppermute(totals[h], 'col', ring)]
    ppermute x4 -> x8, starting transfers between devices: 6.56 us -> 20 us  [scatter(): came = lax.ppermute(total, 'col', ring)]
    ppermute x10, waiting for transfers between devices: 8.15 us -> 3.08 us  [from_turn(): lax.ppermute(value, 'row', [(i ^ k if flips else (i + k) % n_row, i) for...]
    ppermute x16 -> x8, waiting for transfers between devices: 11.1 us -> 6.8 us  [the longest x4 5.21 us: scatter(): came = lax.ppermute(totals[h], 'col', ring)]
    ppermute x4 -> x8, waiting for transfers between devices: 5.78 us -> 8.88 us  [scatter(): came = lax.ppermute(total, 'col', ring)]
    pallas_call x5 -> x7, Pallas kernels: 6.23 us -> 9.19 us  [transfer(): pl.pallas_call(functools.partial(transfer_kernel, fields_at, begin, end,...]
  transfers between devices with their start and end apart: 34 -> 30, of which waited for: 25 -> 23; matrix products, arithmetic and copies ran while one was open for 2% -> 3% of each run, Pallas kernels for 12% -> 17%
where the time goes in v5:
time: 81.6 us; the launch traced here: 81.4 us
  starting transfers between devices  40.5 us (50%)
  waiting for transfers between devices  21.8 us (27%)
  Pallas kernels  15.9 us (19%)
  other arithmetic  2.08 us (3%)
  between operations  1.02 us (1%)
    ppermute x8, starting transfers between devices, scatter(): came = lax.ppermute(total, 'col', ring)  20 us
    ppermute x10, starting transfers between devices, from_turn(): lax.ppermute(value, 'row', [(i ^ k if flips else (i + k) % n_row, i) for...  12.5 us
    pallas_call x7, Pallas kernels, transfer(): pl.pallas_call(functools.partial(transfer_kernel, fields_at, begin, end,...  9.19 us
    ppermute x8, waiting for transfers between devices, scatter(): came = lax.ppermute(total, 'col', ring)  8.88 us
    ppermute x4, starting transfers between devices, scatter(): came = lax.ppermute(totals[h], 'col', ring)  7.21 us
    ppermute x4, waiting for transfers between devices, scatter(): came = lax.ppermute(totals[h], 'col', ring)  5.21 us
    pallas_call x1, Pallas kernels, prepare(): pl.pallas_call(prepare_kernel, in_specs=[pl.BlockSpec(memory_space=pltpu....  4.48 us
    ppermute x10, waiting for transfers between devices, from_turn(): lax.ppermute(value, 'row', [(i ^ k if flips else (i + k) % n_row, i) for...  3.08 us
  transfers between devices with their start and end apart: 30, of which 23 were waited for; matrix products, arithmetic and copies ran while one was open for 3% of the time, Pallas kernels for 17%

profile of v5, /device:TPU:0, one launch (start us, length us, event | category | flops | bytes accessed | tf_op | source)
XLA Modules:
  0.0 81.4 jit_solution(4810826375522352497)
XLA Ops:
  0.0 3.0 %collective-permute-start.2 = (f32[8,64,128]{2,1,0:T(8,128)}, f32[8,64,128]{2,1,0:T(8,128)S(1)}, u32[]{:S(2)}, u32[]{:S(2)}) collective-permute-start(f32[8,64,128]{2,1,0:T(8,128)} %source_ref.5), channel_id=1, source_target_pairs={{16,0},{24,8},{0,16},{8,24},{17,1},{25,9},{1,17},{9,25},{18,2},{26... | collective-permute-start | bytes 786440 | tf_op jit(solution)/shard_map/ppermute | solution.py:266
  3.0 1.5 %collective-permute-start = (f32[8,64,128]{2,1,0:T(8,128)}, f32[8,64,128]{2,1,0:T(8,128)S(1)}, u32[]{:S(2)}, u32[]{:S(2)}) collective-permute-start(f32[8,64,128]{2,1,0:T(8,128)} %source_ref.5), channel_id=1, source_target_pairs={{8,0},{0,8},{24,16},{16,24},{9,1},{1,9},{25,17},{17,25},{10,2},{2,... | collective-permute-start | bytes 786440 | tf_op jit(solution)/shard_map/ppermute | solution.py:266
  5.1 0.7 fusion.4
  5.8 0.7 iota_add_fusion
  6.5 4.5 %prepare.1.rest_0_.a_ref = bf16[257,64,128]{2,1,0:T(8,128)(2,1)S(1)} custom-call(f32[64,64,256]{2,1,0:T(8,128)} %bitcast.3), custom_call_target="tpu_custom_call" | custom-call | bytes 25165824 | tf_op jit(solution)/shard_map/prepare/pallas_call | solution.py:68
  11.6 0.6 collective-permute-start.1
  12.2 0.9 %collective-permute-start.3 = (f32[4,64,128]{2,1,0:T(8,128)S(1)}, f32[4,64,128]{2,1,0:T(8,128)S(1)}, u32[]{:S(2)}, u32[]{:S(2)}) collective-permute-start(f32[4,64,128]{2,1,0:T(8,128)S(1)} %cut.7), channel_id=1, source_target_pairs={{8,0},{0,8},{24,16},{16,24},{9,1},{1,9},{25,17},{17,25},{10,2},{2,... | collective-permute-start | bytes 393224 | tf_op jit(solution)/shard_map/ppermute | solution.py:266
  13.2 0.6 keep.1.plan_ref
  13.9 2.7 %transfer.7.rest_2_ = f32[64,64,128]{2,1,0:T(8,128)S(1)} custom-call(s32[872]{0:T(1024)S(4)} %keep.1.plan_ref, bf16[257,64,128]{2,1,0:T(8,128)(2,1)S(1)} %prepare.1.rest_0_.a_ref, f32[8,64,128]{2,1,0:T(8,128)S(1)} %copy-done, f32[8,64,128]{2,1,0:T(8,128)S(1)} %collective-permute-done.rest_1_, f32[8,64,128]{2,1,0:T(8,128)S(1)} %collective-permute-done.2.rest_2_), custom_call_target="tpu_custom_call" | custom-call | tf_op jit(solution)/shard_map/transfer/pallas_call | solution.py:134
  16.6 0.5 collective-permute-done.3.rest_1_
  17.1 0.5 transfer.8.rest_2_
  17.8 1.1 %transfer.9.sums_ref.value_ref = f32[64,64,128]{2,1,0:T(8,128)S(1)} custom-call(s32[872]{0:T(1024)S(4)} %keep.1.plan_ref, bf16[257,64,128]{2,1,0:T(8,128)(2,1)S(1)} %prepare.1.rest_0_.a_ref, f32[4,64,128]{2,1,0:T(8,128)S(1)} %collective-permute-done.1.rest_0_, f32[4,64,128]{2,1,0:T(8,128)S(1)} %collective-permute-done.3.rest_1_, ...), custom_call_target="tpu_custom_call" | custom-call | tf_op jit(solution)/shard_map/transfer/pallas_call | solution.py:134
  18.9 0.8 collective-permute-done.4.got_ref
  20.1 1.6 %collective-permute-start.6 = (f32[8,64,128]{2,1,0:T(8,128)S(1)}, f32[8,64,128]{2,1,0:T(8,128)S(1)}, u32[]{:S(2)}, u32[]{:S(2)}) collective-permute-start(f32[8,64,128]{2,1,0:T(8,128)S(1)} %carry.12.rest_0_), channel_id=1, source_target_pairs={{0,2},{1,0},{2,4},{3,1},{4,6},{5,3},{6,7},{7,5},{8,10},{9,8},{10,1... | collective-permute-start | bytes 786440 | tf_op jit(solution)/shard_map/ppermute | solution.py:300
  21.6 1.6 %collective-permute-start.12 = (f32[8,64,128]{2,1,0:T(8,128)S(1)}, f32[8,64,128]{2,1,0:T(8,128)S(1)}, u32[]{:S(2)}, u32[]{:S(2)}) collective-permute-start(f32[8,64,128]{2,1,0:T(8,128)S(1)} %carry.13.rest_1_), channel_id=1, source_target_pairs={{0,2},{1,0},{2,4},{3,1},{4,6},{5,3},{6,7},{7,5},{8,10},{9,8},{10,1... | collective-permute-start | bytes 786440 | tf_op jit(solution)/shard_map/ppermute | solution.py:300
  23.2 2.3 %collective-permute-done.6.rest_0_ = f32[8,64,128]{2,1,0:T(8,128)S(1)} collective-permute-done((f32[8,64,128]{2,1,0:T(8,128)S(1)}, f32[8,64,128]{2,1,0:T(8,128)S(1)}, u32[]{:S(2)}, u32[]{:S(2)}) %collective-permute-start.6) | collective-permute-done | bytes 262176 | tf_op jit(solution)/shard_map/ppermute | solution.py:300
  25.6 2.5 %collective-permute-start.7 = (f32[8,64,128]{2,1,0:T(8,128)S(1)}, f32[8,64,128]{2,1,0:T(8,128)S(1)}, u32[]{:S(2)}, u32[]{:S(2)}) collective-permute-start(f32[8,64,128]{2,1,0:T(8,128)S(1)} %carry.14), channel_id=1, source_target_pairs={{0,2},{1,0},{2,4},{3,1},{4,6},{5,3},{6,7},{7,5},{8,10},{9,8},{10,1... | collective-permute-start | bytes 786440 | tf_op jit(solution)/shard_map/ppermute | solution.py:304
  28.4 2.5 %collective-permute-start.13 = (f32[8,64,128]{2,1,0:T(8,128)S(1)}, f32[8,64,128]{2,1,0:T(8,128)S(1)}, u32[]{:S(2)}, u32[]{:S(2)}) collective-permute-start(f32[8,64,128]{2,1,0:T(8,128)S(1)} %carry.16), channel_id=1, source_target_pairs={{0,2},{1,0},{2,4},{3,1},{4,6},{5,3},{6,7},{7,5},{8,10},{9,8},{10,1... | collective-permute-start | bytes 786440 | tf_op jit(solution)/shard_map/ppermute | solution.py:304
  30.9 1.1 %collective-permute-done.7.rest_0_ = f32[8,64,128]{2,1,0:T(8,128)S(1)} collective-permute-done((f32[8,64,128]{2,1,0:T(8,128)S(1)}, f32[8,64,128]{2,1,0:T(8,128)S(1)}, u32[]{:S(2)}, u32[]{:S(2)}) %collective-permute-start.7) | collective-permute-done | bytes 262176 | tf_op jit(solution)/shard_map/ppermute | solution.py:304
  32.0 2.5 %collective-permute-start.8 = (f32[8,64,128]{2,1,0:T(8,128)S(1)}, f32[8,64,128]{2,1,0:T(8,128)S(1)}, u32[]{:S(2)}, u32[]{:S(2)}) collective-permute-start(f32[8,64,128]{2,1,0:T(8,128)S(1)} %carry.15), channel_id=1, source_target_pairs={{0,2},{1,0},{2,4},{3,1},{4,6},{5,3},{6,7},{7,5},{8,10},{9,8},{10,1... | collective-permute-start | bytes 786440 | tf_op jit(solution)/shard_map/ppermute | solution.py:304
  34.8 2.5 %collective-permute-start.14 = (f32[8,64,128]{2,1,0:T(8,128)S(1)}, f32[8,64,128]{2,1,0:T(8,128)S(1)}, u32[]{:S(2)}, u32[]{:S(2)}) collective-permute-start(f32[8,64,128]{2,1,0:T(8,128)S(1)} %carry.17), channel_id=1, source_target_pairs={{0,2},{1,0},{2,4},{3,1},{4,6},{5,3},{6,7},{7,5},{8,10},{9,8},{10,1... | collective-permute-start | bytes 786440 | tf_op jit(solution)/shard_map/ppermute | solution.py:304
  37.3 1.1 %collective-permute-done.8.came_ref.rest_1_ = f32[8,64,128]{2,1,0:T(8,128)S(1)} collective-permute-done((f32[8,64,128]{2,1,0:T(8,128)S(1)}, f32[8,64,128]{2,1,0:T(8,128)S(1)}, u32[]{:S(2)}, u32[]{:S(2)}) %collective-permute-start.8) | collective-permute-done | bytes 262176 | tf_op jit(solution)/shard_map/ppermute | solution.py:304
  38.5 1.3 %collective-permute-done.9.rest_2_ = f32[4,64,128]{2,1,0:T(8,128)S(1)} collective-permute-done((f32[4,64,128]{2,1,0:T(8,128)S(1)}, f32[4,64,128]{2,1,0:T(8,128)S(1)}, u32[]{:S(2)}, u32[]{:S(2)}) %collective-permute-start.9) | collective-permute-done | bytes 131104 | tf_op jit(solution)/shard_map/ppermute | solution.py:314
  39.9 1.3 %collective-permute-done.14.came_ref.rest_1_ = f32[8,64,128]{2,1,0:T(8,128)S(1)} collective-permute-done((f32[8,64,128]{2,1,0:T(8,128)S(1)}, f32[8,64,128]{2,1,0:T(8,128)S(1)}, u32[]{:S(2)}, u32[]{:S(2)}) %collective-permute-start.14) | collective-permute-done | bytes 262176 | tf_op jit(solution)/shard_map/ppermute | solution.py:304
  41.3 1.0 %collective-permute-start.10 = (f32[4,64,128]{2,1,0:T(8,128)S(1)}, f32[4,64,128]{2,1,0:T(8,128)S(1)}, u32[]{:S(2)}, u32[]{:S(2)}) collective-permute-start(f32[4,64,128]{2,1,0:T(8,128)S(1)} %finish.3.rest_0_), channel_id=1, source_target_pairs={{8,0},{0,8},{24,16},{16,24},{9,1},{1,9},{25,17},{17,25},{10,2},{2,... | collective-permute-start | bytes 393224 | tf_op jit(solution)/shard_map/ppermute | solution.py:266
  42.7 1.6 %collective-permute-start.16 = (f32[4,64,128]{2,1,0:T(8,128)S(1)}, f32[4,64,128]{2,1,0:T(8,128)S(1)}, u32[]{:S(2)}, u32[]{:S(2)}) collective-permute-start(f32[4,64,128]{2,1,0:T(8,128)S(1)} %finish.4.rest_1_), channel_id=1, source_target_pairs={{16,0},{24,8},{0,16},{8,24},{17,1},{25,9},{1,17},{9,25},{18,2},{26... | collective-permute-start | bytes 393224 | tf_op jit(solution)/shard_map/ppermute | solution.py:266
  44.3 0.5 collective-permute-start.19
  44.8 0.9 %collective-permute-start.18 = (f32[4,64,128]{2,1,0:T(8,128)S(1)}, f32[4,64,128]{2,1,0:T(8,128)S(1)}, u32[]{:S(2)}, u32[]{:S(2)}) collective-permute-start(f32[4,64,128]{2,1,0:T(8,128)S(1)} %finish.4.rest_1_), channel_id=1, source_target_pairs={{8,0},{0,8},{24,16},{16,24},{9,1},{1,9},{25,17},{17,25},{10,2},{2,... | collective-permute-start | bytes 393224 | tf_op jit(solution)/shard_map/ppermute | solution.py:266
  45.7 1.4 %transfer.10.rest_0_.rest_4_ = f32[64,64,128]{2,1,0:T(8,128)S(1)} custom-call(s32[872]{0:T(1024)S(4)} %keep.1.plan_ref, bf16[257,64,128]{2,1,0:T(8,128)(2,1)S(1)} %prepare.1.rest_0_.a_ref, f32[4,64,128]{2,1,0:T(8,128)S(1)} %finish.3.rest_0_, f32[4,64,128]{2,1,0:T(8,128)S(1)} %finish.4.rest_1_), custom_call_target="tpu_custom_call" | custom-call | tf_op jit(solution)/shard_map/transfer/pallas_call | solution.py:134
  47.4 1.6 %collective-permute-start.11 = (f32[4,64,128]{2,1,0:T(8,128)S(1)}, f32[4,64,128]{2,1,0:T(8,128)S(1)}, u32[]{:S(2)}, u32[]{:S(2)}) collective-permute-start(f32[4,64,128]{2,1,0:T(8,128)S(1)} %cut.9), channel_id=1, source_target_pairs={{16,0},{24,8},{0,16},{8,24},{17,1},{25,9},{1,17},{9,25},{18,2},{26... | collective-permute-start | bytes 393224 | tf_op jit(solution)/shard_map/ppermute | solution.py:266
  49.1 1.0 %collective-permute-start.17 = (f32[4,64,128]{2,1,0:T(8,128)S(1)}, f32[4,64,128]{2,1,0:T(8,128)S(1)}, u32[]{:S(2)}, u32[]{:S(2)}) collective-permute-start(f32[4,64,128]{2,1,0:T(8,128)S(1)} %cut.10), channel_id=1, source_target_pairs={{8,0},{0,8},{24,16},{16,24},{9,1},{1,9},{25,17},{17,25},{10,2},{2,... | collective-permute-start | bytes 393224 | tf_op jit(solution)/shard_map/ppermute | solution.py:266
  50.1 1.8 %collective-permute-done.19.rest_2_ = f32[4,64,128]{2,1,0:T(8,128)S(1)} collective-permute-done((f32[4,64,128]{2,1,0:T(8,128)S(1)}, f32[4,64,128]{2,1,0:T(8,128)S(1)}, u32[]{:S(2)}, u32[]{:S(2)}) %collective-permute-start.19) | collective-permute-done | bytes 131104 | tf_op jit(solution)/shard_map/ppermute | solution.py:266
  51.9 1.9 %transfer.11.rest_2_ = f32[64,64,128]{2,1,0:T(8,128)S(1)} custom-call(s32[872]{0:T(1024)S(4)} %keep.1.plan_ref, bf16[257,64,128]{2,1,0:T(8,128)(2,1)S(1)} %prepare.1.rest_0_.a_ref, f32[4,64,128]{2,1,0:T(8,128)S(1)} %collective-permute-done.10.value_ref.rest_0_, f32[4,64,128]{2,1,0:T(8,128)S(1)} %collective-permute-done.18.rest_1_, ...), custom_call_target="tpu_custom_call" | custom-call | tf_op jit(solution)/shard_map/transfer/pallas_call | solution.py:134
  54.2 0.5 transfer.12.rest_2_
  54.8 1.1 %transfer.13.sums_ref.value_ref = f32[64,64,128]{2,1,0:T(8,128)S(1)} custom-call(s32[872]{0:T(1024)S(4)} %keep.1.plan_ref, bf16[257,64,128]{2,1,0:T(8,128)(2,1)S(1)} %prepare.1.rest_0_.a_ref, f32[4,64,128]{2,1,0:T(8,128)S(1)} %collective-permute-done.11.rest_0_, f32[4,64,128]{2,1,0:T(8,128)S(1)} %collective-permute-done.17.rest_1_, ...), custom_call_target="tpu_custom_call" | custom-call | tf_op jit(solution)/shard_map/transfer/pallas_call | solution.py:134
  55.9 0.8 collective-permute-done.20.got_ref
  57.1 2.6 %collective-permute-start.22 = (f32[8,64,128]{2,1,0:T(8,128)S(1)}, f32[8,64,128]{2,1,0:T(8,128)S(1)}, u32[]{:S(2)}, u32[]{:S(2)}) collective-permute-start(f32[8,64,128]{2,1,0:T(8,128)S(1)} %carry.18.rest_0_), channel_id=1, source_target_pairs={{0,2},{1,0},{2,4},{3,1},{4,6},{5,3},{6,7},{7,5},{8,10},{9,8},{10,1... | collective-permute-start | bytes 786440 | tf_op jit(solution)/shard_map/ppermute | solution.py:300
  59.7 1.5 %collective-permute-start.26 = (f32[8,64,128]{2,1,0:T(8,128)S(1)}, f32[8,64,128]{2,1,0:T(8,128)S(1)}, u32[]{:S(2)}, u32[]{:S(2)}) collective-permute-start(f32[8,64,128]{2,1,0:T(8,128)S(1)} %carry.19.rest_1_), channel_id=1, source_target_pairs={{0,2},{1,0},{2,4},{3,1},{4,6},{5,3},{6,7},{7,5},{8,10},{9,8},{10,1... | collective-permute-start | bytes 786440 | tf_op jit(solution)/shard_map/ppermute | solution.py:300
  61.1 2.4 %collective-permute-done.22.rest_0_ = f32[8,64,128]{2,1,0:T(8,128)S(1)} collective-permute-done((f32[8,64,128]{2,1,0:T(8,128)S(1)}, f32[8,64,128]{2,1,0:T(8,128)S(1)}, u32[]{:S(2)}, u32[]{:S(2)}) %collective-permute-start.22) | collective-permute-done | bytes 262176 | tf_op jit(solution)/shard_map/ppermute | solution.py:300
  63.6 2.5 %collective-permute-start.23 = (f32[8,64,128]{2,1,0:T(8,128)S(1)}, f32[8,64,128]{2,1,0:T(8,128)S(1)}, u32[]{:S(2)}, u32[]{:S(2)}) collective-permute-start(f32[8,64,128]{2,1,0:T(8,128)S(1)} %carry.20), channel_id=1, source_target_pairs={{0,2},{1,0},{2,4},{3,1},{4,6},{5,3},{6,7},{7,5},{8,10},{9,8},{10,1... | collective-permute-start | bytes 786440 | tf_op jit(solution)/shard_map/ppermute | solution.py:304
  66.4 2.5 %collective-permute-start.27 = (f32[8,64,128]{2,1,0:T(8,128)S(1)}, f32[8,64,128]{2,1,0:T(8,128)S(1)}, u32[]{:S(2)}, u32[]{:S(2)}) collective-permute-start(f32[8,64,128]{2,1,0:T(8,128)S(1)} %carry.22), channel_id=1, source_target_pairs={{0,2},{1,0},{2,4},{3,1},{4,6},{5,3},{6,7},{7,5},{8,10},{9,8},{10,1... | collective-permute-start | bytes 786440 | tf_op jit(solution)/shard_map/ppermute | solution.py:304
  68.9 1.1 %collective-permute-done.23.rest_0_ = f32[8,64,128]{2,1,0:T(8,128)S(1)} collective-permute-done((f32[8,64,128]{2,1,0:T(8,128)S(1)}, f32[8,64,128]{2,1,0:T(8,128)S(1)}, u32[]{:S(2)}, u32[]{:S(2)}) %collective-permute-start.23) | collective-permute-done | bytes 262176 | tf_op jit(solution)/shard_map/ppermute | solution.py:304
  70.0 2.5 %collective-permute-start.24 = (f32[8,64,128]{2,1,0:T(8,128)S(1)}, f32[8,64,128]{2,1,0:T(8,128)S(1)}, u32[]{:S(2)}, u32[]{:S(2)}) collective-permute-start(f32[8,64,128]{2,1,0:T(8,128)S(1)} %carry.21), channel_id=1, source_target_pairs={{0,2},{1,0},{2,4},{3,1},{4,6},{5,3},{6,7},{7,5},{8,10},{9,8},{10,1... | collective-permute-start | bytes 786440 | tf_op jit(solution)/shard_map/ppermute | solution.py:304
  72.9 2.5 %collective-permute-start.28 = (f32[8,64,128]{2,1,0:T(8,128)S(1)}, f32[8,64,128]{2,1,0:T(8,128)S(1)}, u32[]{:S(2)}, u32[]{:S(2)}) collective-permute-start(f32[8,64,128]{2,1,0:T(8,128)S(1)} %carry.23), channel_id=1, source_target_pairs={{0,2},{1,0},{2,4},{3,1},{4,6},{5,3},{6,7},{7,5},{8,10},{9,8},{10,1... | collective-permute-start | bytes 786440 | tf_op jit(solution)/shard_map/ppermute | solution.py:304
  75.4 1.1 %collective-permute-done.24.came_ref.rest_1_ = f32[8,64,128]{2,1,0:T(8,128)S(1)} collective-permute-done((f32[8,64,128]{2,1,0:T(8,128)S(1)}, f32[8,64,128]{2,1,0:T(8,128)S(1)}, u32[]{:S(2)}, u32[]{:S(2)}) %collective-permute-start.24) | collective-permute-done | bytes 262176 | tf_op jit(solution)/shard_map/ppermute | solution.py:304
  76.5 2.7 %collective-permute-done.28.came_ref.rest_4_ = f32[8,64,128]{2,1,0:T(8,128)S(1)} collective-permute-done((f32[8,64,128]{2,1,0:T(8,128)S(1)}, f32[8,64,128]{2,1,0:T(8,128)S(1)}, u32[]{:S(2)}, u32[]{:S(2)}) %collective-permute-start.28) | collective-permute-done | bytes 262176 | tf_op jit(solution)/shard_map/ppermute | solution.py:304
  79.4 1.3 %collective-permute-done.29.rest_5_ = f32[4,64,128]{2,1,0:T(8,128)S(1)} collective-permute-done((f32[4,64,128]{2,1,0:T(8,128)S(1)}, f32[4,64,128]{2,1,0:T(8,128)S(1)}, u32[]{:S(2)}, u32[]{:S(2)}) %collective-permute-start.29) | collective-permute-done | bytes 131104 | tf_op jit(solution)/shard_map/ppermute | solution.py:314
  80.7 0.8 finish.5
  (58 shorter events, 4.7 us)
Async XLA Ops:
  0.0 11.5 %collective-permute-start.2 = (f32[8,64,128]{2,1,0:T(8,128)}, f32[8,64,128]{2,1,0:T(8,128)S(1)}, u32[]{:S(2)}, u32[]{:S(2)}) collective-permute-start(f32[8,64,128]{2,1,0:T(8,128)} %source_ref.5), channel_id=1, source_target_pairs={{16,0},{24,8},{0,16},{8,24},{17,1},{25,9},{1,17},{9,25},{18,2},{26... | collective-permute-start | bytes 786440 | tf_op jit(solution)/shard_map/ppermute | solution.py:266
  3.0 8.6 %collective-permute-start = (f32[8,64,128]{2,1,0:T(8,128)}, f32[8,64,128]{2,1,0:T(8,128)S(1)}, u32[]{:S(2)}, u32[]{:S(2)}) collective-permute-start(f32[8,64,128]{2,1,0:T(8,128)} %source_ref.5), channel_id=1, source_target_pairs={{8,0},{0,8},{24,16},{16,24},{9,1},{1,9},{25,17},{17,25},{10,2},{2,... | collective-permute-start | bytes 786440 | tf_op jit(solution)/shard_map/ppermute | solution.py:266
  11.6 2.3 %copy-start = (f32[8,64,128]{2,1,0:T(8,128)S(1)}, f32[8,64,128]{2,1,0:T(8,128)}, u32[]{:S(2)}) copy-start(f32[8,64,128]{2,1,0:T(8,128)} %source_ref.5) | copy-start | bytes 786436
  11.6 5.0 %collective-permute-start.1 = (f32[4,64,128]{2,1,0:T(8,128)S(1)}, f32[4,64,128]{2,1,0:T(8,128)S(1)}, u32[]{:S(2)}, u32[]{:S(2)}) collective-permute-start(f32[4,64,128]{2,1,0:T(8,128)S(1)} %cut.6), channel_id=1, source_target_pairs={{16,0},{24,8},{0,16},{8,24},{17,1},{25,9},{1,17},{9,25},{18,2},{26... | collective-permute-start | bytes 393224 | tf_op jit(solution)/shard_map/ppermute | solution.py:266
  12.2 5.0 %collective-permute-start.3 = (f32[4,64,128]{2,1,0:T(8,128)S(1)}, f32[4,64,128]{2,1,0:T(8,128)S(1)}, u32[]{:S(2)}, u32[]{:S(2)}) collective-permute-start(f32[4,64,128]{2,1,0:T(8,128)S(1)} %cut.7), channel_id=1, source_target_pairs={{8,0},{0,8},{24,16},{16,24},{9,1},{1,9},{25,17},{17,25},{10,2},{2,... | collective-permute-start | bytes 393224 | tf_op jit(solution)/shard_map/ppermute | solution.py:266
  17.7 2.0 %collective-permute-start.4 = (f32[16,64,128]{2,1,0:T(8,128)S(1)}, f32[16,64,128]{2,1,0:T(8,128)S(1)}, u32[]{:S(2)}, u32[]{:S(2)}) collective-permute-start(f32[16,64,128]{2,1,0:T(8,128)S(1)} %slice.18), channel_id=1, source_target_pairs={{0,1},{1,0},{2,3},{3,2},{4,5},{5,4},{6,7},{7,6},{8,9},{9,8},{10,11... | collective-permute-start | bytes 1572872 | tf_op jit(solution)/shard_map/ppermute | solution.py:289
  19.9 5.7 %collective-permute-start.5 = (f32[48,64,128]{2,1,0:T(8,128)S(1)}, f32[48,64,128]{2,1,0:T(8,128)S(1)}, u32[]{:S(2)}, u32[]{:S(2)}) collective-permute-start(f32[48,64,128]{2,1,0:T(8,128)S(1)} %cut.8), channel_id=1, source_target_pairs={{0,1},{1,0},{2,3},{3,2},{4,5},{5,4},{6,7},{7,6},{8,9},{9,8},{10,11... | collective-permute-start | bytes 4718600 | tf_op jit(solution)/shard_map/ppermute | solution.py:297
  20.1 5.5 %collective-permute-start.6 = (f32[8,64,128]{2,1,0:T(8,128)S(1)}, f32[8,64,128]{2,1,0:T(8,128)S(1)}, u32[]{:S(2)}, u32[]{:S(2)}) collective-permute-start(f32[8,64,128]{2,1,0:T(8,128)S(1)} %carry.12.rest_0_), channel_id=1, source_target_pairs={{0,2},{1,0},{2,4},{3,1},{4,6},{5,3},{6,7},{7,5},{8,10},{9,8},{10,1... | collective-permute-start | bytes 786440 | tf_op jit(solution)/shard_map/ppermute | solution.py:300
  21.6 6.7 %collective-permute-start.12 = (f32[8,64,128]{2,1,0:T(8,128)S(1)}, f32[8,64,128]{2,1,0:T(8,128)S(1)}, u32[]{:S(2)}, u32[]{:S(2)}) collective-permute-start(f32[8,64,128]{2,1,0:T(8,128)S(1)} %carry.13.rest_1_), channel_id=1, source_target_pairs={{0,2},{1,0},{2,4},{3,1},{4,6},{5,3},{6,7},{7,5},{8,10},{9,8},{10,1... | collective-permute-start | bytes 786440 | tf_op jit(solution)/shard_map/ppermute | solution.py:300
  25.6 6.4 %collective-permute-start.7 = (f32[8,64,128]{2,1,0:T(8,128)S(1)}, f32[8,64,128]{2,1,0:T(8,128)S(1)}, u32[]{:S(2)}, u32[]{:S(2)}) collective-permute-start(f32[8,64,128]{2,1,0:T(8,128)S(1)} %carry.14), channel_id=1, source_target_pairs={{0,2},{1,0},{2,4},{3,1},{4,6},{5,3},{6,7},{7,5},{8,10},{9,8},{10,1... | collective-permute-start | bytes 786440 | tf_op jit(solution)/shard_map/ppermute | solution.py:304
  28.4 6.4 %collective-permute-start.13 = (f32[8,64,128]{2,1,0:T(8,128)S(1)}, f32[8,64,128]{2,1,0:T(8,128)S(1)}, u32[]{:S(2)}, u32[]{:S(2)}) collective-permute-start(f32[8,64,128]{2,1,0:T(8,128)S(1)} %carry.16), channel_id=1, source_target_pairs={{0,2},{1,0},{2,4},{3,1},{4,6},{5,3},{6,7},{7,5},{8,10},{9,8},{10,1... | collective-permute-start | bytes 786440 | tf_op jit(solution)/shard_map/ppermute | solution.py:304
  32.0 6.4 %collective-permute-start.8 = (f32[8,64,128]{2,1,0:T(8,128)S(1)}, f32[8,64,128]{2,1,0:T(8,128)S(1)}, u32[]{:S(2)}, u32[]{:S(2)}) collective-permute-start(f32[8,64,128]{2,1,0:T(8,128)S(1)} %carry.15), channel_id=1, source_target_pairs={{0,2},{1,0},{2,4},{3,1},{4,6},{5,3},{6,7},{7,5},{8,10},{9,8},{10,1... | collective-permute-start | bytes 786440 | tf_op jit(solution)/shard_map/ppermute | solution.py:304
  34.8 6.4 %collective-permute-start.14 = (f32[8,64,128]{2,1,0:T(8,128)S(1)}, f32[8,64,128]{2,1,0:T(8,128)S(1)}, u32[]{:S(2)}, u32[]{:S(2)}) collective-permute-start(f32[8,64,128]{2,1,0:T(8,128)S(1)} %carry.17), channel_id=1, source_target_pairs={{0,2},{1,0},{2,4},{3,1},{4,6},{5,3},{6,7},{7,5},{8,10},{9,8},{10,1... | collective-permute-start | bytes 786440 | tf_op jit(solution)/shard_map/ppermute | solution.py:304
  38.4 1.4 %collective-permute-start.9 = (f32[4,64,128]{2,1,0:T(8,128)S(1)}, f32[4,64,128]{2,1,0:T(8,128)S(1)}, u32[]{:S(2)}, u32[]{:S(2)}) collective-permute-start(f32[4,64,128]{2,1,0:T(8,128)S(1)} %cross.4), channel_id=1, source_target_pairs={{0,1},{1,0},{2,3},{3,2},{4,5},{5,4},{6,7},{7,6},{8,9},{9,8},{10,11... | collective-permute-start | bytes 393224 | tf_op jit(solution)/shard_map/ppermute | solution.py:314
  41.2 1.4 %collective-permute-start.15 = (f32[4,64,128]{2,1,0:T(8,128)S(1)}, f32[4,64,128]{2,1,0:T(8,128)S(1)}, u32[]{:S(2)}, u32[]{:S(2)}) collective-permute-start(f32[4,64,128]{2,1,0:T(8,128)S(1)} %cross.5), channel_id=1, source_target_pairs={{0,1},{1,0},{2,3},{3,2},{4,5},{5,4},{6,7},{7,6},{8,9},{9,8},{10,11... | collective-permute-start | bytes 393224 | tf_op jit(solution)/shard_map/ppermute | solution.py:314
  41.3 6.1 %collective-permute-start.10 = (f32[4,64,128]{2,1,0:T(8,128)S(1)}, f32[4,64,128]{2,1,0:T(8,128)S(1)}, u32[]{:S(2)}, u32[]{:S(2)}) collective-permute-start(f32[4,64,128]{2,1,0:T(8,128)S(1)} %finish.3.rest_0_), channel_id=1, source_target_pairs={{8,0},{0,8},{24,16},{16,24},{9,1},{1,9},{25,17},{17,25},{10,2},{2,... | collective-permute-start | bytes 393224 | tf_op jit(solution)/shard_map/ppermute | solution.py:266
  42.7 6.4 %collective-permute-start.16 = (f32[4,64,128]{2,1,0:T(8,128)S(1)}, f32[4,64,128]{2,1,0:T(8,128)S(1)}, u32[]{:S(2)}, u32[]{:S(2)}) collective-permute-start(f32[4,64,128]{2,1,0:T(8,128)S(1)} %finish.4.rest_1_), channel_id=1, source_target_pairs={{16,0},{24,8},{0,16},{8,24},{17,1},{25,9},{1,17},{9,25},{18,2},{26... | collective-permute-start | bytes 393224 | tf_op jit(solution)/shard_map/ppermute | solution.py:266
  44.3 7.6 %collective-permute-start.19 = (f32[4,64,128]{2,1,0:T(8,128)S(1)}, f32[4,64,128]{2,1,0:T(8,128)S(1)}, u32[]{:S(2)}, u32[]{:S(2)}) collective-permute-start(f32[4,64,128]{2,1,0:T(8,128)S(1)} %finish.3.rest_0_), channel_id=1, source_target_pairs={{16,0},{24,8},{0,16},{8,24},{17,1},{25,9},{1,17},{9,25},{18,2},{26... | collective-permute-start | bytes 393224 | tf_op jit(solution)/shard_map/ppermute | solution.py:266
  44.8 7.1 %collective-permute-start.18 = (f32[4,64,128]{2,1,0:T(8,128)S(1)}, f32[4,64,128]{2,1,0:T(8,128)S(1)}, u32[]{:S(2)}, u32[]{:S(2)}) collective-permute-start(f32[4,64,128]{2,1,0:T(8,128)S(1)} %finish.4.rest_1_), channel_id=1, source_target_pairs={{8,0},{0,8},{24,16},{16,24},{9,1},{1,9},{25,17},{17,25},{10,2},{2,... | collective-permute-start | bytes 393224 | tf_op jit(solution)/shard_map/ppermute | solution.py:266
  47.4 6.5 %collective-permute-start.11 = (f32[4,64,128]{2,1,0:T(8,128)S(1)}, f32[4,64,128]{2,1,0:T(8,128)S(1)}, u32[]{:S(2)}, u32[]{:S(2)}) collective-permute-start(f32[4,64,128]{2,1,0:T(8,128)S(1)} %cut.9), channel_id=1, source_target_pairs={{16,0},{24,8},{0,16},{8,24},{17,1},{25,9},{1,17},{9,25},{18,2},{26... | collective-permute-start | bytes 393224 | tf_op jit(solution)/shard_map/ppermute | solution.py:266
  49.1 5.0 %collective-permute-start.17 = (f32[4,64,128]{2,1,0:T(8,128)S(1)}, f32[4,64,128]{2,1,0:T(8,128)S(1)}, u32[]{:S(2)}, u32[]{:S(2)}) collective-permute-start(f32[4,64,128]{2,1,0:T(8,128)S(1)} %cut.10), channel_id=1, source_target_pairs={{8,0},{0,8},{24,16},{16,24},{9,1},{1,9},{25,17},{17,25},{10,2},{2,... | collective-permute-start | bytes 393224 | tf_op jit(solution)/shard_map/ppermute | solution.py:266
  54.7 2.0 %collective-permute-start.20 = (f32[16,64,128]{2,1,0:T(8,128)S(1)}, f32[16,64,128]{2,1,0:T(8,128)S(1)}, u32[]{:S(2)}, u32[]{:S(2)}) collective-permute-start(f32[16,64,128]{2,1,0:T(8,128)S(1)} %slice.19), channel_id=1, source_target_pairs={{0,1},{1,0},{2,3},{3,2},{4,5},{5,4},{6,7},{7,6},{8,9},{9,8},{10,11... | collective-permute-start | bytes 1572872 | tf_op jit(solution)/shard_map/ppermute | solution.py:289
  56.9 6.7 %collective-permute-start.21 = (f32[48,64,128]{2,1,0:T(8,128)S(1)}, f32[48,64,128]{2,1,0:T(8,128)S(1)}, u32[]{:S(2)}, u32[]{:S(2)}) collective-permute-start(f32[48,64,128]{2,1,0:T(8,128)S(1)} %cut.11), channel_id=1, source_target_pairs={{0,1},{1,0},{2,3},{3,2},{4,5},{5,4},{6,7},{7,6},{8,9},{9,8},{10,11... | collective-permute-start | bytes 4718600 | tf_op jit(solution)/shard_map/ppermute | solution.py:297
  57.1 6.5 %collective-permute-start.22 = (f32[8,64,128]{2,1,0:T(8,128)S(1)}, f32[8,64,128]{2,1,0:T(8,128)S(1)}, u32[]{:S(2)}, u32[]{:S(2)}) collective-permute-start(f32[8,64,128]{2,1,0:T(8,128)S(1)} %carry.18.rest_0_), channel_id=1, source_target_pairs={{0,2},{1,0},{2,4},{3,1},{4,6},{5,3},{6,7},{7,5},{8,10},{9,8},{10,1... | collective-permute-start | bytes 786440 | tf_op jit(solution)/shard_map/ppermute | solution.py:300
  59.7 6.7 %collective-permute-start.26 = (f32[8,64,128]{2,1,0:T(8,128)S(1)}, f32[8,64,128]{2,1,0:T(8,128)S(1)}, u32[]{:S(2)}, u32[]{:S(2)}) collective-permute-start(f32[8,64,128]{2,1,0:T(8,128)S(1)} %carry.19.rest_1_), channel_id=1, source_target_pairs={{0,2},{1,0},{2,4},{3,1},{4,6},{5,3},{6,7},{7,5},{8,10},{9,8},{10,1... | collective-permute-start | bytes 786440 | tf_op jit(solution)/shard_map/ppermute | solution.py:300
  63.6 6.4 %collective-permute-start.23 = (f32[8,64,128]{2,1,0:T(8,128)S(1)}, f32[8,64,128]{2,1,0:T(8,128)S(1)}, u32[]{:S(2)}, u32[]{:S(2)}) collective-permute-start(f32[8,64,128]{2,1,0:T(8,128)S(1)} %carry.20), channel_id=1, source_target_pairs={{0,2},{1,0},{2,4},{3,1},{4,6},{5,3},{6,7},{7,5},{8,10},{9,8},{10,1... | collective-permute-start | bytes 786440 | tf_op jit(solution)/shard_map/ppermute | solution.py:304
  66.4 6.4 %collective-permute-start.27 = (f32[8,64,128]{2,1,0:T(8,128)S(1)}, f32[8,64,128]{2,1,0:T(8,128)S(1)}, u32[]{:S(2)}, u32[]{:S(2)}) collective-permute-start(f32[8,64,128]{2,1,0:T(8,128)S(1)} %carry.22), channel_id=1, source_target_pairs={{0,2},{1,0},{2,4},{3,1},{4,6},{5,3},{6,7},{7,5},{8,10},{9,8},{10,1... | collective-permute-start | bytes 786440 | tf_op jit(solution)/shard_map/ppermute | solution.py:304
  70.0 6.4 %collective-permute-start.24 = (f32[8,64,128]{2,1,0:T(8,128)S(1)}, f32[8,64,128]{2,1,0:T(8,128)S(1)}, u32[]{:S(2)}, u32[]{:S(2)}) collective-permute-start(f32[8,64,128]{2,1,0:T(8,128)S(1)} %carry.21), channel_id=1, source_target_pairs={{0,2},{1,0},{2,4},{3,1},{4,6},{5,3},{6,7},{7,5},{8,10},{9,8},{10,1... | collective-permute-start | bytes 786440 | tf_op jit(solution)/shard_map/ppermute | solution.py:304
  72.9 6.4 %collective-permute-start.28 = (f32[8,64,128]{2,1,0:T(8,128)S(1)}, f32[8,64,128]{2,1,0:T(8,128)S(1)}, u32[]{:S(2)}, u32[]{:S(2)}) collective-permute-start(f32[8,64,128]{2,1,0:T(8,128)S(1)} %carry.23), channel_id=1, source_target_pairs={{0,2},{1,0},{2,4},{3,1},{4,6},{5,3},{6,7},{7,5},{8,10},{9,8},{10,1... | collective-permute-start | bytes 786440 | tf_op jit(solution)/shard_map/ppermute | solution.py:304
  76.5 2.9 %collective-permute-start.25 = (f32[4,64,128]{2,1,0:T(8,128)S(1)}, f32[4,64,128]{2,1,0:T(8,128)S(1)}, u32[]{:S(2)}, u32[]{:S(2)}) collective-permute-start(f32[4,64,128]{2,1,0:T(8,128)S(1)} %cross.6), channel_id=1, source_target_pairs={{0,1},{1,0},{2,3},{3,2},{4,5},{5,4},{6,7},{7,6},{8,9},{9,8},{10,11... | collective-permute-start | bytes 393224 | tf_op jit(solution)/shard_map/ppermute | solution.py:314
  79.3 1.4 %collective-permute-start.29 = (f32[4,64,128]{2,1,0:T(8,128)S(1)}, f32[4,64,128]{2,1,0:T(8,128)S(1)}, u32[]{:S(2)}, u32[]{:S(2)}) collective-permute-start(f32[4,64,128]{2,1,0:T(8,128)S(1)} %cross.7), channel_id=1, source_target_pairs={{0,1},{1,0},{2,3},{3,2},{4,5},{5,4},{6,7},{7,6},{8,9},{9,8},{10,11... | collective-permute-start | bytes 393224 | tf_op jit(solution)/shard_map/ppermute | solution.py:314

commit v6 on v5

--- a/solution.py
+++ b/solution.py
@@ -8,7 +8,8 @@
 from jax.sharding import PartitionSpec as P
 
 ITERS = 2
-HALVES = 2
+PARTS = 4
+GROUPS = (0, 2), (2, 4)
 STAGES = 4
 GROUP = 32
 CHUNK = 16
@@ -219,11 +220,11 @@
 def sums_at(h, distance, pairs, half):
     order = (distance + pairs - 1) % pairs if pairs > 1 else distance
     size = 2 * half
-    return jnp.where(order == 0, h * size, (HALVES + h * (pairs - 1) + order - 1) * size)
+    return jnp.where(order == 0, h * size, (PARTS + h * (pairs - 1) + order - 1) * size)
 
 
 def make_plan(row_index, col_index, live, bricks, n_row, n_col, flips):
-    pairs, half = n_col // 2, bricks // HALVES
+    pairs, half = n_col // 2, bricks // PARTS
     my_row, me = lax.axis_index("row"), lax.axis_index("col")
     my_pair, my_side = me // 2, me % 2
     column, brick = row_index // bricks, row_index % bricks
@@ -238,7 +239,7 @@
 
     n = row_index.shape[0]
     slots = jnp.arange(n, dtype=jnp.int32)
-    part = jnp.where(turn == 0, 0, jnp.where(turn < n_row - 1, 1, jnp.where(place < HALVES * 2 * half, 2, 3)))
+    part = jnp.where(turn == 0, 0, jnp.where(turn < n_row - 1, 1, jnp.where(place < PARTS * 2 * half, 2, 3)))
     part = jnp.where(slots < live, part, STAGES)
     key = part * n + slots
     rank = jnp.sum(key[None, :] < key[:, None], axis=1, dtype=jnp.int32)
@@ -255,7 +256,7 @@
 def body(source, blocks, row_index, col_index, live_count):
     bricks = source.shape[0]
     n_row, n_col = lax.axis_size("row"), lax.axis_size("col")
-    pairs, half = n_col // 2, bricks // HALVES
+    pairs, half = n_col // 2, bricks // PARTS
     block = 2 * half
     flips = n_row & (n_row - 1) == 0
 
@@ -276,10 +277,10 @@
 
     def apply(turns, first, end, *before):
         fields = [f for pieces in turns.values() for f in pieces]
-        at = [k * bricks + i * (bricks // len(pieces)) for k, pieces in turns.items() for i in range(len(pieces))]
+        at = [k * bricks + sum(f.shape[0] for f in pieces[:i]) for k, pieces in turns.items() for i in range(len(pieces))]
         return transfer(plan, matrix, fields, at, n_row * bricks, first, end, before, bricks * n_col)
 
-    leading = HALVES * block
+    leading = PARTS * block
 
     def at(h, distance):
         order = (distance + pairs - 1) % pairs
@@ -288,15 +289,15 @@
     def scatter(lead, sums):
         first = lax.ppermute(lead[:leading], "col", swap)
         if pairs == 1:
-            return [[first]] * HALVES
+            return [[first]] * PARTS
         far = pairs - 1
         totals = []
-        for h in range(HALVES):
+        for h in range(PARTS):
             kernel = functools.partial(carry_kernel, at(h, far), h * block)
             totals += small_call(kernel, (block,), "carry", sums, first)
         rest = lax.ppermute(cut(sums, leading, sums.shape[0] - leading, totals), "col", swap)
         parts = []
-        for h in range(HALVES):
+        for h in range(PARTS):
             came = lax.ppermute(totals[h], "col", ring)
             for distance in range(far - 1, 0, -1):
                 kernel = functools.partial(carry_kernel, at(h, distance), at(h, pairs - distance) - leading)
@@ -328,14 +329,15 @@
 
     if n_row == 4:
         one, two = gather([source], False)
-        last = [forward(one[0][:half], 2, matrix), forward(two[0][half:], 1, matrix)]
+        last = [forward(one[0][: bricks // 2], 2, matrix), forward(two[0][bricks // 2 :], 1, matrix)]
         lead, sums = last_row(last, apply({0: [source], 1: one, 2: two}, 0, 2))
     else:
         lead = sums = apply(by_row([source]), 0, STAGES)
     for _ in range(ITERS - 1):
         field = []
-        for h, part in enumerate(scatter(lead, sums)):
-            field.append(finish(sums, [part], h, field))
+        parts = scatter(lead, sums)
+        for begin, end in GROUPS:
+            field.append(finish(sums, parts[begin:end], begin, field))
         if n_row == 4:
             one, two = gather(field, False)
             sums = apply({0: field}, 0, 1)

time: 81.6 us -> 78.5 us (0.962)
  waiting for transfers between devices: 21.8 us -> 10.7 us
  starting transfers between devices: 40.5 us -> 48.5 us
    ppermute x8 -> x16, waiting for transfers between devices: 8.88 us -> 3.27 us  [scatter(): came = lax.ppermute(total, 'col', ring)]
    ppermute x4 -> x8, waiting for transfers between devices: 5.21 us -> 0.02 us  [scatter(): came = lax.ppermute(totals[h], 'col', ring)]
    ppermute x4 -> x8, starting transfers between devices: 7.21 us -> 10.8 us  [scatter(): came = lax.ppermute(totals[h], 'col', ring)]
    ppermute x8 -> x16, starting transfers between devices: 20 us -> 22.9 us  [scatter(): came = lax.ppermute(total, 'col', ring)]
    ppermute x4 -> x8, starting transfers between devices: 0.28 us -> 1.77 us  [finish(): args.append(lax.ppermute(crossing, 'col', swap))]
    ppermute x4 -> x8, waiting for transfers between devices: 3.04 us -> 2.4 us  [finish(): args.append(lax.ppermute(crossing, 'col', swap))]
    pallas_call x25 -> x41, Pallas kernels: 1.67 us -> 1.75 us  [small_call(): pl.pallas_call(kernel, in_specs=[whole] * len(args) + [anywhere] * len(af...]
  transfers between devices with their start and end apart: 30 -> 46, of which waited for: 23 -> 15; matrix products, arithmetic and copies ran while one was open for 3% -> 3% of each run, Pallas kernels for 17% -> 17%
where the time goes in v6:
time: 78.5 us; the launch traced here: 78.3 us
  starting transfers between devices  48.5 us (62%)
  Pallas kernels  15.7 us (20%)
  waiting for transfers between devices  10.7 us (14%)
  other arithmetic  2.08 us (3%)
  between operations  1.19 us (2%)
    ppermute x16, starting transfers between devices, scatter(): came = lax.ppermute(total, 'col', ring)  22.9 us
    ppermute x10, starting transfers between devices, from_turn(): lax.ppermute(value, 'row', [(i ^ k if flips else (i + k) % n_row, i) for...  12.5 us
    ppermute x8, starting transfers between devices, scatter(): came = lax.ppermute(totals[h], 'col', ring)  10.8 us
    pallas_call x7, Pallas kernels, transfer(): pl.pallas_call(functools.partial(transfer_kernel, fields_at, begin, end,...  8.89 us
    pallas_call x1, Pallas kernels, prepare(): pl.pallas_call(prepare_kernel, in_specs=[pl.BlockSpec(memory_space=pltpu....  4.48 us
    ppermute x16, waiting for transfers between devices, scatter(): came = lax.ppermute(total, 'col', ring)  3.27 us
    ppermute x10, waiting for transfers between devices, from_turn(): lax.ppermute(value, 'row', [(i ^ k if flips else (i + k) % n_row, i) for...  3.13 us
    ppermute x8, waiting for transfers between devices, finish(): args.append(lax.ppermute(crossing, 'col', swap))  2.4 us
  transfers between devices with their start and end apart: 46, of which 15 were waited for; matrix products, arithmetic and copies ran while one was open for 3% of the time, Pallas kernels for 17%

profile of v6, /device:TPU:0, one launch (start us, length us, event | category | flops | bytes accessed | tf_op | source)
XLA Modules:
  0.0 78.3 jit_solution(4263460577238154532)
XLA Ops:
  0.0 3.0 %collective-permute-start.2 = (f32[8,64,128]{2,1,0:T(8,128)}, f32[8,64,128]{2,1,0:T(8,128)S(1)}, u32[]{:S(2)}, u32[]{:S(2)}) collective-permute-start(f32[8,64,128]{2,1,0:T(8,128)} %source_ref.5), channel_id=1, source_target_pairs={{16,0},{24,8},{0,16},{8,24},{17,1},{25,9},{1,17},{9,25},{18,2},{26... | collective-permute-start | bytes 786440 | tf_op jit(solution)/shard_map/ppermute | solution.py:267
  3.0 1.5 %collective-permute-start = (f32[8,64,128]{2,1,0:T(8,128)}, f32[8,64,128]{2,1,0:T(8,128)S(1)}, u32[]{:S(2)}, u32[]{:S(2)}) collective-permute-start(f32[8,64,128]{2,1,0:T(8,128)} %source_ref.5), channel_id=1, source_target_pairs={{8,0},{0,8},{24,16},{16,24},{9,1},{1,9},{25,17},{17,25},{10,2},{2,... | collective-permute-start | bytes 786440 | tf_op jit(solution)/shard_map/ppermute | solution.py:267
  5.1 0.7 fusion.4
  5.8 0.7 iota_add_fusion
  6.5 4.5 %prepare.1.rest_0_.a_ref = bf16[257,64,128]{2,1,0:T(8,128)(2,1)S(1)} custom-call(f32[64,64,256]{2,1,0:T(8,128)} %bitcast.3), custom_call_target="tpu_custom_call" | custom-call | bytes 25165824 | tf_op jit(solution)/shard_map/prepare/pallas_call | solution.py:69
  12.2 0.9 %collective-permute-start.3 = (f32[4,64,128]{2,1,0:T(8,128)S(1)}, f32[4,64,128]{2,1,0:T(8,128)S(1)}, u32[]{:S(2)}, u32[]{:S(2)}) collective-permute-start(f32[4,64,128]{2,1,0:T(8,128)S(1)} %cut.7), channel_id=1, source_target_pairs={{8,0},{0,8},{24,16},{16,24},{9,1},{1,9},{25,17},{17,25},{10,2},{2,... | collective-permute-start | bytes 393224 | tf_op jit(solution)/shard_map/ppermute | solution.py:267
  13.9 2.9 %transfer.7.rest_2_ = f32[64,64,128]{2,1,0:T(8,128)S(1)} custom-call(s32[872]{0:T(1024)S(4)} %keep.1.plan_ref, bf16[257,64,128]{2,1,0:T(8,128)(2,1)S(1)} %prepare.1.rest_0_.a_ref, f32[8,64,128]{2,1,0:T(8,128)S(1)} %copy-done, f32[8,64,128]{2,1,0:T(8,128)S(1)} %collective-permute-done.rest_1_, f32[8,64,128]{2,1,0:T(8,128)S(1)} %collective-permute-done.2.rest_2_), custom_call_target="tpu_custom_call" | custom-call | tf_op jit(solution)/shard_map/transfer/pallas_call | solution.py:135
  17.8 1.0 %transfer.9.sums_ref.value_ref = f32[64,64,128]{2,1,0:T(8,128)S(1)} custom-call(s32[872]{0:T(1024)S(4)} %keep.1.plan_ref, bf16[257,64,128]{2,1,0:T(8,128)(2,1)S(1)} %prepare.1.rest_0_.a_ref, f32[4,64,128]{2,1,0:T(8,128)S(1)} %collective-permute-done.1.rest_0_, f32[4,64,128]{2,1,0:T(8,128)S(1)} %collective-permute-done.3.rest_1_, ...), custom_call_target="tpu_custom_call" | custom-call | tf_op jit(solution)/shard_map/transfer/pallas_call | solution.py:135
  18.7 0.9 %collective-permute-done.4.got_ref = f32[16,64,128]{2,1,0:T(8,128)S(1)} collective-permute-done((f32[16,64,128]{2,1,0:T(8,128)S(1)}, f32[16,64,128]{2,1,0:T(8,128)S(1)}, u32[]{:S(2)}, u32[]{:S(2)}) %collective-permute-start.4) | collective-permute-done | bytes 524320 | tf_op jit(solution)/shard_map/ppermute | solution.py:290
  20.1 1.6 %collective-permute-start.6 = (f32[4,64,128]{2,1,0:T(8,128)S(1)}, f32[4,64,128]{2,1,0:T(8,128)S(1)}, u32[]{:S(2)}, u32[]{:S(2)}) collective-permute-start(f32[4,64,128]{2,1,0:T(8,128)S(1)} %carry.24.rest_0_), channel_id=1, source_target_pairs={{0,2},{1,0},{2,4},{3,1},{4,6},{5,3},{6,7},{7,5},{8,10},{9,8},{10,1... | collective-permute-start | bytes 393224 | tf_op jit(solution)/shard_map/ppermute | solution.py:301
  21.6 1.6 %collective-permute-start.10 = (f32[4,64,128]{2,1,0:T(8,128)S(1)}, f32[4,64,128]{2,1,0:T(8,128)S(1)}, u32[]{:S(2)}, u32[]{:S(2)}) collective-permute-start(f32[4,64,128]{2,1,0:T(8,128)S(1)} %carry.25.rest_1_), channel_id=1, source_target_pairs={{0,2},{1,0},{2,4},{3,1},{4,6},{5,3},{6,7},{7,5},{8,10},{9,8},{10,1... | collective-permute-start | bytes 393224 | tf_op jit(solution)/shard_map/ppermute | solution.py:301
  23.2 1.6 %collective-permute-start.16 = (f32[4,64,128]{2,1,0:T(8,128)S(1)}, f32[4,64,128]{2,1,0:T(8,128)S(1)}, u32[]{:S(2)}, u32[]{:S(2)}) collective-permute-start(f32[4,64,128]{2,1,0:T(8,128)S(1)} %carry.26.rest_2_), channel_id=1, source_target_pairs={{0,2},{1,0},{2,4},{3,1},{4,6},{5,3},{6,7},{7,5},{8,10},{9,8},{10,1... | collective-permute-start | bytes 393224 | tf_op jit(solution)/shard_map/ppermute | solution.py:301
  25.2 1.4 %collective-permute-start.7 = (f32[4,64,128]{2,1,0:T(8,128)S(1)}, f32[4,64,128]{2,1,0:T(8,128)S(1)}, u32[]{:S(2)}, u32[]{:S(2)}) collective-permute-start(f32[4,64,128]{2,1,0:T(8,128)S(1)} %carry.28), channel_id=1, source_target_pairs={{0,2},{1,0},{2,4},{3,1},{4,6},{5,3},{6,7},{7,5},{8,10},{9,8},{10,1... | collective-permute-start | bytes 393224 | tf_op jit(solution)/shard_map/ppermute | solution.py:305
  26.7 1.6 %collective-permute-start.11 = (f32[4,64,128]{2,1,0:T(8,128)S(1)}, f32[4,64,128]{2,1,0:T(8,128)S(1)}, u32[]{:S(2)}, u32[]{:S(2)}) collective-permute-start(f32[4,64,128]{2,1,0:T(8,128)S(1)} %carry.30), channel_id=1, source_target_pairs={{0,2},{1,0},{2,4},{3,1},{4,6},{5,3},{6,7},{7,5},{8,10},{9,8},{10,1... | collective-permute-start | bytes 393224 | tf_op jit(solution)/shard_map/ppermute | solution.py:305
  28.3 1.6 %collective-permute-start.17 = (f32[4,64,128]{2,1,0:T(8,128)S(1)}, f32[4,64,128]{2,1,0:T(8,128)S(1)}, u32[]{:S(2)}, u32[]{:S(2)}) collective-permute-start(f32[4,64,128]{2,1,0:T(8,128)S(1)} %carry.32), channel_id=1, source_target_pairs={{0,2},{1,0},{2,4},{3,1},{4,6},{5,3},{6,7},{7,5},{8,10},{9,8},{10,1... | collective-permute-start | bytes 393224 | tf_op jit(solution)/shard_map/ppermute | solution.py:305
  30.0 1.4 %collective-permute-start.21 = (f32[4,64,128]{2,1,0:T(8,128)S(1)}, f32[4,64,128]{2,1,0:T(8,128)S(1)}, u32[]{:S(2)}, u32[]{:S(2)}) collective-permute-start(f32[4,64,128]{2,1,0:T(8,128)S(1)} %carry.34), channel_id=1, source_target_pairs={{0,2},{1,0},{2,4},{3,1},{4,6},{5,3},{6,7},{7,5},{8,10},{9,8},{10,1... | collective-permute-start | bytes 393224 | tf_op jit(solution)/shard_map/ppermute | solution.py:305
  31.4 1.4 %collective-permute-start.8 = (f32[4,64,128]{2,1,0:T(8,128)S(1)}, f32[4,64,128]{2,1,0:T(8,128)S(1)}, u32[]{:S(2)}, u32[]{:S(2)}) collective-permute-start(f32[4,64,128]{2,1,0:T(8,128)S(1)} %carry.29), channel_id=1, source_target_pairs={{0,2},{1,0},{2,4},{3,1},{4,6},{5,3},{6,7},{7,5},{8,10},{9,8},{10,1... | collective-permute-start | bytes 393224 | tf_op jit(solution)/shard_map/ppermute | solution.py:305
  32.8 1.4 %collective-permute-start.12 = (f32[4,64,128]{2,1,0:T(8,128)S(1)}, f32[4,64,128]{2,1,0:T(8,128)S(1)}, u32[]{:S(2)}, u32[]{:S(2)}) collective-permute-start(f32[4,64,128]{2,1,0:T(8,128)S(1)} %carry.31), channel_id=1, source_target_pairs={{0,2},{1,0},{2,4},{3,1},{4,6},{5,3},{6,7},{7,5},{8,10},{9,8},{10,1... | collective-permute-start | bytes 393224 | tf_op jit(solution)/shard_map/ppermute | solution.py:305
  34.2 1.4 %collective-permute-start.18 = (f32[4,64,128]{2,1,0:T(8,128)S(1)}, f32[4,64,128]{2,1,0:T(8,128)S(1)}, u32[]{:S(2)}, u32[]{:S(2)}) collective-permute-start(f32[4,64,128]{2,1,0:T(8,128)S(1)} %carry.33), channel_id=1, source_target_pairs={{0,2},{1,0},{2,4},{3,1},{4,6},{5,3},{6,7},{7,5},{8,10},{9,8},{10,1... | collective-permute-start | bytes 393224 | tf_op jit(solution)/shard_map/ppermute | solution.py:305
  35.6 1.4 %collective-permute-start.22 = (f32[4,64,128]{2,1,0:T(8,128)S(1)}, f32[4,64,128]{2,1,0:T(8,128)S(1)}, u32[]{:S(2)}, u32[]{:S(2)}) collective-permute-start(f32[4,64,128]{2,1,0:T(8,128)S(1)} %carry.35), channel_id=1, source_target_pairs={{0,2},{1,0},{2,4},{3,1},{4,6},{5,3},{6,7},{7,5},{8,10},{9,8},{10,1... | collective-permute-start | bytes 393224 | tf_op jit(solution)/shard_map/ppermute | solution.py:305
  37.6 0.7 collective-permute-done.9.rest_2_
  39.0 0.9 %collective-permute-done.22.came_ref.rest_4_ = f32[4,64,128]{2,1,0:T(8,128)S(1)} collective-permute-done((f32[4,64,128]{2,1,0:T(8,128)S(1)}, f32[4,64,128]{2,1,0:T(8,128)S(1)}, u32[]{:S(2)}, u32[]{:S(2)}) %collective-permute-start.22) | collective-permute-done | bytes 131104 | tf_op jit(solution)/shard_map/ppermute | solution.py:305
  40.0 1.0 %collective-permute-start.14 = (f32[4,64,128]{2,1,0:T(8,128)S(1)}, f32[4,64,128]{2,1,0:T(8,128)S(1)}, u32[]{:S(2)}, u32[]{:S(2)}) collective-permute-start(f32[4,64,128]{2,1,0:T(8,128)S(1)} %finish.3.rest_0_), channel_id=1, source_target_pairs={{8,0},{0,8},{24,16},{16,24},{9,1},{1,9},{25,17},{17,25},{10,2},{2,... | collective-permute-start | bytes 393224 | tf_op jit(solution)/shard_map/ppermute | solution.py:267
  41.3 1.6 %collective-permute-start.24 = (f32[4,64,128]{2,1,0:T(8,128)S(1)}, f32[4,64,128]{2,1,0:T(8,128)S(1)}, u32[]{:S(2)}, u32[]{:S(2)}) collective-permute-start(f32[4,64,128]{2,1,0:T(8,128)S(1)} %finish.4.rest_1_), channel_id=1, source_target_pairs={{16,0},{24,8},{0,16},{8,24},{17,1},{25,9},{1,17},{9,25},{18,2},{26... | collective-permute-start | bytes 393224 | tf_op jit(solution)/shard_map/ppermute | solution.py:267
  43.4 0.9 %collective-permute-start.26 = (f32[4,64,128]{2,1,0:T(8,128)S(1)}, f32[4,64,128]{2,1,0:T(8,128)S(1)}, u32[]{:S(2)}, u32[]{:S(2)}) collective-permute-start(f32[4,64,128]{2,1,0:T(8,128)S(1)} %finish.4.rest_1_), channel_id=1, source_target_pairs={{8,0},{0,8},{24,16},{16,24},{9,1},{1,9},{25,17},{17,25},{10,2},{2,... | collective-permute-start | bytes 393224 | tf_op jit(solution)/shard_map/ppermute | solution.py:267
  44.3 1.1 %transfer.10.rest_0_.rest_4_ = f32[64,64,128]{2,1,0:T(8,128)S(1)} custom-call(s32[872]{0:T(1024)S(4)} %keep.1.plan_ref, bf16[257,64,128]{2,1,0:T(8,128)(2,1)S(1)} %prepare.1.rest_0_.a_ref, f32[4,64,128]{2,1,0:T(8,128)S(1)} %finish.3.rest_0_, f32[4,64,128]{2,1,0:T(8,128)S(1)} %finish.4.rest_1_), custom_call_target="tpu_custom_call" | custom-call | tf_op jit(solution)/shard_map/transfer/pallas_call | solution.py:135
  45.4 0.8 %collective-permute-done.14.value_ref.rest_0_ = f32[4,64,128]{2,1,0:T(8,128)S(1)} collective-permute-done((f32[4,64,128]{2,1,0:T(8,128)S(1)}, f32[4,64,128]{2,1,0:T(8,128)S(1)}, u32[]{:S(2)}, u32[]{:S(2)}) %collective-permute-start.14) | collective-permute-done | bytes 131104 | tf_op jit(solution)/shard_map/ppermute | solution.py:267
  46.2 1.6 %collective-permute-start.15 = (f32[4,64,128]{2,1,0:T(8,128)S(1)}, f32[4,64,128]{2,1,0:T(8,128)S(1)}, u32[]{:S(2)}, u32[]{:S(2)}) collective-permute-start(f32[4,64,128]{2,1,0:T(8,128)S(1)} %cut.9), channel_id=1, source_target_pairs={{16,0},{24,8},{0,16},{8,24},{17,1},{25,9},{1,17},{9,25},{18,2},{26... | collective-permute-start | bytes 393224 | tf_op jit(solution)/shard_map/ppermute | solution.py:267
  47.8 1.1 %collective-permute-start.25 = (f32[4,64,128]{2,1,0:T(8,128)S(1)}, f32[4,64,128]{2,1,0:T(8,128)S(1)}, u32[]{:S(2)}, u32[]{:S(2)}) collective-permute-start(f32[4,64,128]{2,1,0:T(8,128)S(1)} %cut.10), channel_id=1, source_target_pairs={{8,0},{0,8},{24,16},{16,24},{9,1},{1,9},{25,17},{17,25},{10,2},{2,... | collective-permute-start | bytes 393224 | tf_op jit(solution)/shard_map/ppermute | solution.py:267
  48.9 1.6 %collective-permute-done.27.rest_2_ = f32[4,64,128]{2,1,0:T(8,128)S(1)} collective-permute-done((f32[4,64,128]{2,1,0:T(8,128)S(1)}, f32[4,64,128]{2,1,0:T(8,128)S(1)}, u32[]{:S(2)}, u32[]{:S(2)}) %collective-permute-start.27) | collective-permute-done | bytes 131104 | tf_op jit(solution)/shard_map/ppermute | solution.py:267
  50.5 2.0 %transfer.11.rest_2_ = f32[64,64,128]{2,1,0:T(8,128)S(1)} custom-call(s32[872]{0:T(1024)S(4)} %keep.1.plan_ref, bf16[257,64,128]{2,1,0:T(8,128)(2,1)S(1)} %prepare.1.rest_0_.a_ref, f32[4,64,128]{2,1,0:T(8,128)S(1)} %collective-permute-done.14.value_ref.rest_0_, f32[4,64,128]{2,1,0:T(8,128)S(1)} %collective-permute-done.26.rest_1_, ...), custom_call_target="tpu_custom_call" | custom-call | tf_op jit(solution)/shard_map/transfer/pallas_call | solution.py:135
  53.5 1.0 %transfer.13.sums_ref.value_ref = f32[64,64,128]{2,1,0:T(8,128)S(1)} custom-call(s32[872]{0:T(1024)S(4)} %keep.1.plan_ref, bf16[257,64,128]{2,1,0:T(8,128)(2,1)S(1)} %prepare.1.rest_0_.a_ref, f32[4,64,128]{2,1,0:T(8,128)S(1)} %collective-permute-done.15.rest_0_, f32[4,64,128]{2,1,0:T(8,128)S(1)} %collective-permute-done.25.rest_1_, ...), custom_call_target="tpu_custom_call" | custom-call | tf_op jit(solution)/shard_map/transfer/pallas_call | solution.py:135
  54.5 0.9 %collective-permute-done.28.got_ref = f32[16,64,128]{2,1,0:T(8,128)S(1)} collective-permute-done((f32[16,64,128]{2,1,0:T(8,128)S(1)}, f32[16,64,128]{2,1,0:T(8,128)S(1)}, u32[]{:S(2)}, u32[]{:S(2)}) %collective-permute-start.28) | collective-permute-done | bytes 524320 | tf_op jit(solution)/shard_map/ppermute | solution.py:290
  55.8 2.5 %collective-permute-start.30 = (f32[4,64,128]{2,1,0:T(8,128)S(1)}, f32[4,64,128]{2,1,0:T(8,128)S(1)}, u32[]{:S(2)}, u32[]{:S(2)}) collective-permute-start(f32[4,64,128]{2,1,0:T(8,128)S(1)} %carry.36.rest_0_), channel_id=1, source_target_pairs={{0,2},{1,0},{2,4},{3,1},{4,6},{5,3},{6,7},{7,5},{8,10},{9,8},{10,1... | collective-permute-start | bytes 393224 | tf_op jit(solution)/shard_map/ppermute | solution.py:301
  58.3 1.4 %collective-permute-start.34 = (f32[4,64,128]{2,1,0:T(8,128)S(1)}, f32[4,64,128]{2,1,0:T(8,128)S(1)}, u32[]{:S(2)}, u32[]{:S(2)}) collective-permute-start(f32[4,64,128]{2,1,0:T(8,128)S(1)} %carry.37.rest_1_), channel_id=1, source_target_pairs={{0,2},{1,0},{2,4},{3,1},{4,6},{5,3},{6,7},{7,5},{8,10},{9,8},{10,1... | collective-permute-start | bytes 393224 | tf_op jit(solution)/shard_map/ppermute | solution.py:301
  59.7 1.4 %collective-permute-start.38 = (f32[4,64,128]{2,1,0:T(8,128)S(1)}, f32[4,64,128]{2,1,0:T(8,128)S(1)}, u32[]{:S(2)}, u32[]{:S(2)}) collective-permute-start(f32[4,64,128]{2,1,0:T(8,128)S(1)} %carry.38.rest_2_), channel_id=1, source_target_pairs={{0,2},{1,0},{2,4},{3,1},{4,6},{5,3},{6,7},{7,5},{8,10},{9,8},{10,1... | collective-permute-start | bytes 393224 | tf_op jit(solution)/shard_map/ppermute | solution.py:301
  61.5 1.8 %collective-permute-start.31 = (f32[4,64,128]{2,1,0:T(8,128)S(1)}, f32[4,64,128]{2,1,0:T(8,128)S(1)}, u32[]{:S(2)}, u32[]{:S(2)}) collective-permute-start(f32[4,64,128]{2,1,0:T(8,128)S(1)} %carry.40), channel_id=1, source_target_pairs={{0,2},{1,0},{2,4},{3,1},{4,6},{5,3},{6,7},{7,5},{8,10},{9,8},{10,1... | collective-permute-start | bytes 393224 | tf_op jit(solution)/shard_map/ppermute | solution.py:305
  63.4 1.4 %collective-permute-start.35 = (f32[4,64,128]{2,1,0:T(8,128)S(1)}, f32[4,64,128]{2,1,0:T(8,128)S(1)}, u32[]{:S(2)}, u32[]{:S(2)}) collective-permute-start(f32[4,64,128]{2,1,0:T(8,128)S(1)} %carry.42), channel_id=1, source_target_pairs={{0,2},{1,0},{2,4},{3,1},{4,6},{5,3},{6,7},{7,5},{8,10},{9,8},{10,1... | collective-permute-start | bytes 393224 | tf_op jit(solution)/shard_map/ppermute | solution.py:305
  64.8 1.4 %collective-permute-start.39 = (f32[4,64,128]{2,1,0:T(8,128)S(1)}, f32[4,64,128]{2,1,0:T(8,128)S(1)}, u32[]{:S(2)}, u32[]{:S(2)}) collective-permute-start(f32[4,64,128]{2,1,0:T(8,128)S(1)} %carry.44), channel_id=1, source_target_pairs={{0,2},{1,0},{2,4},{3,1},{4,6},{5,3},{6,7},{7,5},{8,10},{9,8},{10,1... | collective-permute-start | bytes 393224 | tf_op jit(solution)/shard_map/ppermute | solution.py:305
  66.3 1.4 %collective-permute-start.43 = (f32[4,64,128]{2,1,0:T(8,128)S(1)}, f32[4,64,128]{2,1,0:T(8,128)S(1)}, u32[]{:S(2)}, u32[]{:S(2)}) collective-permute-start(f32[4,64,128]{2,1,0:T(8,128)S(1)} %carry.46), channel_id=1, source_target_pairs={{0,2},{1,0},{2,4},{3,1},{4,6},{5,3},{6,7},{7,5},{8,10},{9,8},{10,1... | collective-permute-start | bytes 393224 | tf_op jit(solution)/shard_map/ppermute | solution.py:305
  67.7 1.4 %collective-permute-start.32 = (f32[4,64,128]{2,1,0:T(8,128)S(1)}, f32[4,64,128]{2,1,0:T(8,128)S(1)}, u32[]{:S(2)}, u32[]{:S(2)}) collective-permute-start(f32[4,64,128]{2,1,0:T(8,128)S(1)} %carry.41), channel_id=1, source_target_pairs={{0,2},{1,0},{2,4},{3,1},{4,6},{5,3},{6,7},{7,5},{8,10},{9,8},{10,1... | collective-permute-start | bytes 393224 | tf_op jit(solution)/shard_map/ppermute | solution.py:305
  69.1 1.4 %collective-permute-start.36 = (f32[4,64,128]{2,1,0:T(8,128)S(1)}, f32[4,64,128]{2,1,0:T(8,128)S(1)}, u32[]{:S(2)}, u32[]{:S(2)}) collective-permute-start(f32[4,64,128]{2,1,0:T(8,128)S(1)} %carry.43), channel_id=1, source_target_pairs={{0,2},{1,0},{2,4},{3,1},{4,6},{5,3},{6,7},{7,5},{8,10},{9,8},{10,1... | collective-permute-start | bytes 393224 | tf_op jit(solution)/shard_map/ppermute | solution.py:305
  70.5 1.4 %collective-permute-start.40 = (f32[4,64,128]{2,1,0:T(8,128)S(1)}, f32[4,64,128]{2,1,0:T(8,128)S(1)}, u32[]{:S(2)}, u32[]{:S(2)}) collective-permute-start(f32[4,64,128]{2,1,0:T(8,128)S(1)} %carry.45), channel_id=1, source_target_pairs={{0,2},{1,0},{2,4},{3,1},{4,6},{5,3},{6,7},{7,5},{8,10},{9,8},{10,1... | collective-permute-start | bytes 393224 | tf_op jit(solution)/shard_map/ppermute | solution.py:305
  71.9 1.4 %collective-permute-start.44 = (f32[4,64,128]{2,1,0:T(8,128)S(1)}, f32[4,64,128]{2,1,0:T(8,128)S(1)}, u32[]{:S(2)}, u32[]{:S(2)}) collective-permute-start(f32[4,64,128]{2,1,0:T(8,128)S(1)} %carry.47), channel_id=1, source_target_pairs={{0,2},{1,0},{2,4},{3,1},{4,6},{5,3},{6,7},{7,5},{8,10},{9,8},{10,1... | collective-permute-start | bytes 393224 | tf_op jit(solution)/shard_map/ppermute | solution.py:305
  73.9 0.9 %collective-permute-done.40.came_ref.rest_7_ = f32[4,64,128]{2,1,0:T(8,128)S(1)} collective-permute-done((f32[4,64,128]{2,1,0:T(8,128)S(1)}, f32[4,64,128]{2,1,0:T(8,128)S(1)}, u32[]{:S(2)}, u32[]{:S(2)}) %collective-permute-start.40) | collective-permute-done | bytes 131104 | tf_op jit(solution)/shard_map/ppermute | solution.py:305
  74.9 1.3 %collective-permute-done.44.came_ref.rest_10_ = f32[4,64,128]{2,1,0:T(8,128)S(1)} collective-permute-done((f32[4,64,128]{2,1,0:T(8,128)S(1)}, f32[4,64,128]{2,1,0:T(8,128)S(1)}, u32[]{:S(2)}, u32[]{:S(2)}) %collective-permute-start.44) | collective-permute-done | bytes 131104 | tf_op jit(solution)/shard_map/ppermute | solution.py:305
  76.4 1.2 %collective-permute-done.45.rest_11_ = f32[2,64,128]{2,1,0:T(8,128)S(1)} collective-permute-done((f32[2,64,128]{2,1,0:T(8,128)S(1)}, f32[2,64,128]{2,1,0:T(8,128)S(1)}, u32[]{:S(2)}, u32[]{:S(2)}) %collective-permute-start.45) | collective-permute-done | bytes 65568 | tf_op jit(solution)/shard_map/ppermute | solution.py:315
  77.6 0.8 finish.5
  (106 shorter events, 8.9 us)
Async XLA Ops:
  0.0 11.5 %collective-permute-start.2 = (f32[8,64,128]{2,1,0:T(8,128)}, f32[8,64,128]{2,1,0:T(8,128)S(1)}, u32[]{:S(2)}, u32[]{:S(2)}) collective-permute-start(f32[8,64,128]{2,1,0:T(8,128)} %source_ref.5), channel_id=1, source_target_pairs={{16,0},{24,8},{0,16},{8,24},{17,1},{25,9},{1,17},{9,25},{18,2},{26... | collective-permute-start | bytes 786440 | tf_op jit(solution)/shard_map/ppermute | solution.py:267
  3.0 8.6 %collective-permute-start = (f32[8,64,128]{2,1,0:T(8,128)}, f32[8,64,128]{2,1,0:T(8,128)S(1)}, u32[]{:S(2)}, u32[]{:S(2)}) collective-permute-start(f32[8,64,128]{2,1,0:T(8,128)} %source_ref.5), channel_id=1, source_target_pairs={{8,0},{0,8},{24,16},{16,24},{9,1},{1,9},{25,17},{17,25},{10,2},{2,... | collective-permute-start | bytes 786440 | tf_op jit(solution)/shard_map/ppermute | solution.py:267
  11.6 2.3 %copy-start = (f32[8,64,128]{2,1,0:T(8,128)S(1)}, f32[8,64,128]{2,1,0:T(8,128)}, u32[]{:S(2)}) copy-start(f32[8,64,128]{2,1,0:T(8,128)} %source_ref.5) | copy-start | bytes 786436
  11.6 5.2 %collective-permute-start.1 = (f32[4,64,128]{2,1,0:T(8,128)S(1)}, f32[4,64,128]{2,1,0:T(8,128)S(1)}, u32[]{:S(2)}, u32[]{:S(2)}) collective-permute-start(f32[4,64,128]{2,1,0:T(8,128)S(1)} %cut.6), channel_id=1, source_target_pairs={{16,0},{24,8},{0,16},{8,24},{17,1},{25,9},{1,17},{9,25},{18,2},{26... | collective-permute-start | bytes 393224 | tf_op jit(solution)/shard_map/ppermute | solution.py:267
  12.2 5.0 %collective-permute-start.3 = (f32[4,64,128]{2,1,0:T(8,128)S(1)}, f32[4,64,128]{2,1,0:T(8,128)S(1)}, u32[]{:S(2)}, u32[]{:S(2)}) collective-permute-start(f32[4,64,128]{2,1,0:T(8,128)S(1)} %cut.7), channel_id=1, source_target_pairs={{8,0},{0,8},{24,16},{16,24},{9,1},{1,9},{25,17},{17,25},{10,2},{2,... | collective-permute-start | bytes 393224 | tf_op jit(solution)/shard_map/ppermute | solution.py:267
  17.7 2.0 %collective-permute-start.4 = (f32[16,64,128]{2,1,0:T(8,128)S(1)}, f32[16,64,128]{2,1,0:T(8,128)S(1)}, u32[]{:S(2)}, u32[]{:S(2)}) collective-permute-start(f32[16,64,128]{2,1,0:T(8,128)S(1)} %slice.18), channel_id=1, source_target_pairs={{0,1},{1,0},{2,3},{3,2},{4,5},{5,4},{6,7},{7,6},{8,9},{9,8},{10,11... | collective-permute-start | bytes 1572872 | tf_op jit(solution)/shard_map/ppermute | solution.py:290
  19.9 5.3 %collective-permute-start.5 = (f32[48,64,128]{2,1,0:T(8,128)S(1)}, f32[48,64,128]{2,1,0:T(8,128)S(1)}, u32[]{:S(2)}, u32[]{:S(2)}) collective-permute-start(f32[48,64,128]{2,1,0:T(8,128)S(1)} %cut.8), channel_id=1, source_target_pairs={{0,1},{1,0},{2,3},{3,2},{4,5},{5,4},{6,7},{7,6},{8,9},{9,8},{10,11... | collective-permute-start | bytes 4718600 | tf_op jit(solution)/shard_map/ppermute | solution.py:298
  20.1 5.1 %collective-permute-start.6 = (f32[4,64,128]{2,1,0:T(8,128)S(1)}, f32[4,64,128]{2,1,0:T(8,128)S(1)}, u32[]{:S(2)}, u32[]{:S(2)}) collective-permute-start(f32[4,64,128]{2,1,0:T(8,128)S(1)} %carry.24.rest_0_), channel_id=1, source_target_pairs={{0,2},{1,0},{2,4},{3,1},{4,6},{5,3},{6,7},{7,5},{8,10},{9,8},{10,1... | collective-permute-start | bytes 393224 | tf_op jit(solution)/shard_map/ppermute | solution.py:301
  21.6 5.0 %collective-permute-start.10 = (f32[4,64,128]{2,1,0:T(8,128)S(1)}, f32[4,64,128]{2,1,0:T(8,128)S(1)}, u32[]{:S(2)}, u32[]{:S(2)}) collective-permute-start(f32[4,64,128]{2,1,0:T(8,128)S(1)} %carry.25.rest_1_), channel_id=1, source_target_pairs={{0,2},{1,0},{2,4},{3,1},{4,6},{5,3},{6,7},{7,5},{8,10},{9,8},{10,1... | collective-permute-start | bytes 393224 | tf_op jit(solution)/shard_map/ppermute | solution.py:301
  23.2 5.1 %collective-permute-start.16 = (f32[4,64,128]{2,1,0:T(8,128)S(1)}, f32[4,64,128]{2,1,0:T(8,128)S(1)}, u32[]{:S(2)}, u32[]{:S(2)}) collective-permute-start(f32[4,64,128]{2,1,0:T(8,128)S(1)} %carry.26.rest_2_), channel_id=1, source_target_pairs={{0,2},{1,0},{2,4},{3,1},{4,6},{5,3},{6,7},{7,5},{8,10},{9,8},{10,1... | collective-permute-start | bytes 393224 | tf_op jit(solution)/shard_map/ppermute | solution.py:301
  24.8 5.1 %collective-permute-start.20 = (f32[4,64,128]{2,1,0:T(8,128)S(1)}, f32[4,64,128]{2,1,0:T(8,128)S(1)}, u32[]{:S(2)}, u32[]{:S(2)}) collective-permute-start(f32[4,64,128]{2,1,0:T(8,128)S(1)} %carry.27.rest_3_), channel_id=1, source_target_pairs={{0,2},{1,0},{2,4},{3,1},{4,6},{5,3},{6,7},{7,5},{8,10},{9,8},{10,1... | collective-permute-start | bytes 393224 | tf_op jit(solution)/shard_map/ppermute | solution.py:301
  25.2 6.1 %collective-permute-start.7 = (f32[4,64,128]{2,1,0:T(8,128)S(1)}, f32[4,64,128]{2,1,0:T(8,128)S(1)}, u32[]{:S(2)}, u32[]{:S(2)}) collective-permute-start(f32[4,64,128]{2,1,0:T(8,128)S(1)} %carry.28), channel_id=1, source_target_pairs={{0,2},{1,0},{2,4},{3,1},{4,6},{5,3},{6,7},{7,5},{8,10},{9,8},{10,1... | collective-permute-start | bytes 393224 | tf_op jit(solution)/shard_map/ppermute | solution.py:305
  26.7 6.0 %collective-permute-start.11 = (f32[4,64,128]{2,1,0:T(8,128)S(1)}, f32[4,64,128]{2,1,0:T(8,128)S(1)}, u32[]{:S(2)}, u32[]{:S(2)}) collective-permute-start(f32[4,64,128]{2,1,0:T(8,128)S(1)} %carry.30), channel_id=1, source_target_pairs={{0,2},{1,0},{2,4},{3,1},{4,6},{5,3},{6,7},{7,5},{8,10},{9,8},{10,1... | collective-permute-start | bytes 393224 | tf_op jit(solution)/shard_map/ppermute | solution.py:305
  28.3 5.8 %collective-permute-start.17 = (f32[4,64,128]{2,1,0:T(8,128)S(1)}, f32[4,64,128]{2,1,0:T(8,128)S(1)}, u32[]{:S(2)}, u32[]{:S(2)}) collective-permute-start(f32[4,64,128]{2,1,0:T(8,128)S(1)} %carry.32), channel_id=1, source_target_pairs={{0,2},{1,0},{2,4},{3,1},{4,6},{5,3},{6,7},{7,5},{8,10},{9,8},{10,1... | collective-permute-start | bytes 393224 | tf_op jit(solution)/shard_map/ppermute | solution.py:305
  30.0 5.6 %collective-permute-start.21 = (f32[4,64,128]{2,1,0:T(8,128)S(1)}, f32[4,64,128]{2,1,0:T(8,128)S(1)}, u32[]{:S(2)}, u32[]{:S(2)}) collective-permute-start(f32[4,64,128]{2,1,0:T(8,128)S(1)} %carry.34), channel_id=1, source_target_pairs={{0,2},{1,0},{2,4},{3,1},{4,6},{5,3},{6,7},{7,5},{8,10},{9,8},{10,1... | collective-permute-start | bytes 393224 | tf_op jit(solution)/shard_map/ppermute | solution.py:305
  31.4 5.6 %collective-permute-start.8 = (f32[4,64,128]{2,1,0:T(8,128)S(1)}, f32[4,64,128]{2,1,0:T(8,128)S(1)}, u32[]{:S(2)}, u32[]{:S(2)}) collective-permute-start(f32[4,64,128]{2,1,0:T(8,128)S(1)} %carry.29), channel_id=1, source_target_pairs={{0,2},{1,0},{2,4},{3,1},{4,6},{5,3},{6,7},{7,5},{8,10},{9,8},{10,1... | collective-permute-start | bytes 393224 | tf_op jit(solution)/shard_map/ppermute | solution.py:305
  32.8 4.3 %collective-permute-start.12 = (f32[4,64,128]{2,1,0:T(8,128)S(1)}, f32[4,64,128]{2,1,0:T(8,128)S(1)}, u32[]{:S(2)}, u32[]{:S(2)}) collective-permute-start(f32[4,64,128]{2,1,0:T(8,128)S(1)} %carry.31), channel_id=1, source_target_pairs={{0,2},{1,0},{2,4},{3,1},{4,6},{5,3},{6,7},{7,5},{8,10},{9,8},{10,1... | collective-permute-start | bytes 393224 | tf_op jit(solution)/shard_map/ppermute | solution.py:305
  34.2 4.4 %collective-permute-start.18 = (f32[4,64,128]{2,1,0:T(8,128)S(1)}, f32[4,64,128]{2,1,0:T(8,128)S(1)}, u32[]{:S(2)}, u32[]{:S(2)}) collective-permute-start(f32[4,64,128]{2,1,0:T(8,128)S(1)} %carry.33), channel_id=1, source_target_pairs={{0,2},{1,0},{2,4},{3,1},{4,6},{5,3},{6,7},{7,5},{8,10},{9,8},{10,1... | collective-permute-start | bytes 393224 | tf_op jit(solution)/shard_map/ppermute | solution.py:305
  35.6 4.3 %collective-permute-start.22 = (f32[4,64,128]{2,1,0:T(8,128)S(1)}, f32[4,64,128]{2,1,0:T(8,128)S(1)}, u32[]{:S(2)}, u32[]{:S(2)}) collective-permute-start(f32[4,64,128]{2,1,0:T(8,128)S(1)} %carry.35), channel_id=1, source_target_pairs={{0,2},{1,0},{2,4},{3,1},{4,6},{5,3},{6,7},{7,5},{8,10},{9,8},{10,1... | collective-permute-start | bytes 393224 | tf_op jit(solution)/shard_map/ppermute | solution.py:305
  37.0 1.3 %collective-permute-start.9 = (f32[2,64,128]{2,1,0:T(8,128)S(1)}, f32[2,64,128]{2,1,0:T(8,128)S(1)}, u32[]{:S(2)}, u32[]{:S(2)}) collective-permute-start(f32[2,64,128]{2,1,0:T(8,128)S(1)} %cross.8), channel_id=1, source_target_pairs={{0,1},{1,0},{2,3},{3,2},{4,5},{5,4},{6,7},{7,6},{8,9},{9,8},{10,11... | collective-permute-start | bytes 196616 | tf_op jit(solution)/shard_map/ppermute | solution.py:315
  37.1 1.4 %collective-permute-start.13 = (f32[2,64,128]{2,1,0:T(8,128)S(1)}, f32[2,64,128]{2,1,0:T(8,128)S(1)}, u32[]{:S(2)}, u32[]{:S(2)}) collective-permute-start(f32[2,64,128]{2,1,0:T(8,128)S(1)} %cross.9), channel_id=1, source_target_pairs={{0,1},{1,0},{2,3},{3,2},{4,5},{5,4},{6,7},{7,6},{8,9},{9,8},{10,11... | collective-permute-start | bytes 196616 | tf_op jit(solution)/shard_map/ppermute | solution.py:315
  38.6 2.4 %collective-permute-start.19 = (f32[2,64,128]{2,1,0:T(8,128)S(1)}, f32[2,64,128]{2,1,0:T(8,128)S(1)}, u32[]{:S(2)}, u32[]{:S(2)}) collective-permute-start(f32[2,64,128]{2,1,0:T(8,128)S(1)} %cross.10), channel_id=1, source_target_pairs={{0,1},{1,0},{2,3},{3,2},{4,5},{5,4},{6,7},{7,6},{8,9},{9,8},{10,11... | collective-permute-start | bytes 196616 | tf_op jit(solution)/shard_map/ppermute | solution.py:315
  39.9 1.3 %collective-permute-start.23 = (f32[2,64,128]{2,1,0:T(8,128)S(1)}, f32[2,64,128]{2,1,0:T(8,128)S(1)}, u32[]{:S(2)}, u32[]{:S(2)}) collective-permute-start(f32[2,64,128]{2,1,0:T(8,128)S(1)} %cross.11), channel_id=1, source_target_pairs={{0,1},{1,0},{2,3},{3,2},{4,5},{5,4},{6,7},{7,6},{8,9},{9,8},{10,11... | collective-permute-start | bytes 196616 | tf_op jit(solution)/shard_map/ppermute | solution.py:315
  40.0 6.2 %collective-permute-start.14 = (f32[4,64,128]{2,1,0:T(8,128)S(1)}, f32[4,64,128]{2,1,0:T(8,128)S(1)}, u32[]{:S(2)}, u32[]{:S(2)}) collective-permute-start(f32[4,64,128]{2,1,0:T(8,128)S(1)} %finish.3.rest_0_), channel_id=1, source_target_pairs={{8,0},{0,8},{24,16},{16,24},{9,1},{1,9},{25,17},{17,25},{10,2},{2,... | collective-permute-start | bytes 393224 | tf_op jit(solution)/shard_map/ppermute | solution.py:267
  41.3 6.5 %collective-permute-start.24 = (f32[4,64,128]{2,1,0:T(8,128)S(1)}, f32[4,64,128]{2,1,0:T(8,128)S(1)}, u32[]{:S(2)}, u32[]{:S(2)}) collective-permute-start(f32[4,64,128]{2,1,0:T(8,128)S(1)} %finish.4.rest_1_), channel_id=1, source_target_pairs={{16,0},{24,8},{0,16},{8,24},{17,1},{25,9},{1,17},{9,25},{18,2},{26... | collective-permute-start | bytes 393224 | tf_op jit(solution)/shard_map/ppermute | solution.py:267
  42.9 7.6 %collective-permute-start.27 = (f32[4,64,128]{2,1,0:T(8,128)S(1)}, f32[4,64,128]{2,1,0:T(8,128)S(1)}, u32[]{:S(2)}, u32[]{:S(2)}) collective-permute-start(f32[4,64,128]{2,1,0:T(8,128)S(1)} %finish.3.rest_0_), channel_id=1, source_target_pairs={{16,0},{24,8},{0,16},{8,24},{17,1},{25,9},{1,17},{9,25},{18,2},{26... | collective-permute-start | bytes 393224 | tf_op jit(solution)/shard_map/ppermute | solution.py:267
  43.4 7.1 %collective-permute-start.26 = (f32[4,64,128]{2,1,0:T(8,128)S(1)}, f32[4,64,128]{2,1,0:T(8,128)S(1)}, u32[]{:S(2)}, u32[]{:S(2)}) collective-permute-start(f32[4,64,128]{2,1,0:T(8,128)S(1)} %finish.4.rest_1_), channel_id=1, source_target_pairs={{8,0},{0,8},{24,16},{16,24},{9,1},{1,9},{25,17},{17,25},{10,2},{2,... | collective-permute-start | bytes 393224 | tf_op jit(solution)/shard_map/ppermute | solution.py:267
  46.2 6.3 %collective-permute-start.15 = (f32[4,64,128]{2,1,0:T(8,128)S(1)}, f32[4,64,128]{2,1,0:T(8,128)S(1)}, u32[]{:S(2)}, u32[]{:S(2)}) collective-permute-start(f32[4,64,128]{2,1,0:T(8,128)S(1)} %cut.9), channel_id=1, source_target_pairs={{16,0},{24,8},{0,16},{8,24},{17,1},{25,9},{1,17},{9,25},{18,2},{26... | collective-permute-start | bytes 393224 | tf_op jit(solution)/shard_map/ppermute | solution.py:267
  47.8 5.0 %collective-permute-start.25 = (f32[4,64,128]{2,1,0:T(8,128)S(1)}, f32[4,64,128]{2,1,0:T(8,128)S(1)}, u32[]{:S(2)}, u32[]{:S(2)}) collective-permute-start(f32[4,64,128]{2,1,0:T(8,128)S(1)} %cut.10), channel_id=1, source_target_pairs={{8,0},{0,8},{24,16},{16,24},{9,1},{1,9},{25,17},{17,25},{10,2},{2,... | collective-permute-start | bytes 393224 | tf_op jit(solution)/shard_map/ppermute | solution.py:267
  53.4 2.0 %collective-permute-start.28 = (f32[16,64,128]{2,1,0:T(8,128)S(1)}, f32[16,64,128]{2,1,0:T(8,128)S(1)}, u32[]{:S(2)}, u32[]{:S(2)}) collective-permute-start(f32[16,64,128]{2,1,0:T(8,128)S(1)} %slice.19), channel_id=1, source_target_pairs={{0,1},{1,0},{2,3},{3,2},{4,5},{5,4},{6,7},{7,6},{8,9},{9,8},{10,11... | collective-permute-start | bytes 1572872 | tf_op jit(solution)/shard_map/ppermute | solution.py:290
  55.6 5.9 %collective-permute-start.29 = (f32[48,64,128]{2,1,0:T(8,128)S(1)}, f32[48,64,128]{2,1,0:T(8,128)S(1)}, u32[]{:S(2)}, u32[]{:S(2)}) collective-permute-start(f32[48,64,128]{2,1,0:T(8,128)S(1)} %cut.11), channel_id=1, source_target_pairs={{0,1},{1,0},{2,3},{3,2},{4,5},{5,4},{6,7},{7,6},{8,9},{9,8},{10,11... | collective-permute-start | bytes 4718600 | tf_op jit(solution)/shard_map/ppermute | solution.py:298
  55.8 5.7 %collective-permute-start.30 = (f32[4,64,128]{2,1,0:T(8,128)S(1)}, f32[4,64,128]{2,1,0:T(8,128)S(1)}, u32[]{:S(2)}, u32[]{:S(2)}) collective-permute-start(f32[4,64,128]{2,1,0:T(8,128)S(1)} %carry.36.rest_0_), channel_id=1, source_target_pairs={{0,2},{1,0},{2,4},{3,1},{4,6},{5,3},{6,7},{7,5},{8,10},{9,8},{10,1... | collective-permute-start | bytes 393224 | tf_op jit(solution)/shard_map/ppermute | solution.py:301
  58.3 5.0 %collective-permute-start.34 = (f32[4,64,128]{2,1,0:T(8,128)S(1)}, f32[4,64,128]{2,1,0:T(8,128)S(1)}, u32[]{:S(2)}, u32[]{:S(2)}) collective-permute-start(f32[4,64,128]{2,1,0:T(8,128)S(1)} %carry.37.rest_1_), channel_id=1, source_target_pairs={{0,2},{1,0},{2,4},{3,1},{4,6},{5,3},{6,7},{7,5},{8,10},{9,8},{10,1... | collective-permute-start | bytes 393224 | tf_op jit(solution)/shard_map/ppermute | solution.py:301
  59.7 5.1 %collective-permute-start.38 = (f32[4,64,128]{2,1,0:T(8,128)S(1)}, f32[4,64,128]{2,1,0:T(8,128)S(1)}, u32[]{:S(2)}, u32[]{:S(2)}) collective-permute-start(f32[4,64,128]{2,1,0:T(8,128)S(1)} %carry.38.rest_2_), channel_id=1, source_target_pairs={{0,2},{1,0},{2,4},{3,1},{4,6},{5,3},{6,7},{7,5},{8,10},{9,8},{10,1... | collective-permute-start | bytes 393224 | tf_op jit(solution)/shard_map/ppermute | solution.py:301
  61.1 5.1 %collective-permute-start.42 = (f32[4,64,128]{2,1,0:T(8,128)S(1)}, f32[4,64,128]{2,1,0:T(8,128)S(1)}, u32[]{:S(2)}, u32[]{:S(2)}) collective-permute-start(f32[4,64,128]{2,1,0:T(8,128)S(1)} %carry.39.rest_3_), channel_id=1, source_target_pairs={{0,2},{1,0},{2,4},{3,1},{4,6},{5,3},{6,7},{7,5},{8,10},{9,8},{10,1... | collective-permute-start | bytes 393224 | tf_op jit(solution)/shard_map/ppermute | solution.py:301
  61.5 6.1 %collective-permute-start.31 = (f32[4,64,128]{2,1,0:T(8,128)S(1)}, f32[4,64,128]{2,1,0:T(8,128)S(1)}, u32[]{:S(2)}, u32[]{:S(2)}) collective-permute-start(f32[4,64,128]{2,1,0:T(8,128)S(1)} %carry.40), channel_id=1, source_target_pairs={{0,2},{1,0},{2,4},{3,1},{4,6},{5,3},{6,7},{7,5},{8,10},{9,8},{10,1... | collective-permute-start | bytes 393224 | tf_op jit(solution)/shard_map/ppermute | solution.py:305
  63.4 5.7 %collective-permute-start.35 = (f32[4,64,128]{2,1,0:T(8,128)S(1)}, f32[4,64,128]{2,1,0:T(8,128)S(1)}, u32[]{:S(2)}, u32[]{:S(2)}) collective-permute-start(f32[4,64,128]{2,1,0:T(8,128)S(1)} %carry.42), channel_id=1, source_target_pairs={{0,2},{1,0},{2,4},{3,1},{4,6},{5,3},{6,7},{7,5},{8,10},{9,8},{10,1... | collective-permute-start | bytes 393224 | tf_op jit(solution)/shard_map/ppermute | solution.py:305
  64.8 5.6 %collective-permute-start.39 = (f32[4,64,128]{2,1,0:T(8,128)S(1)}, f32[4,64,128]{2,1,0:T(8,128)S(1)}, u32[]{:S(2)}, u32[]{:S(2)}) collective-permute-start(f32[4,64,128]{2,1,0:T(8,128)S(1)} %carry.44), channel_id=1, source_target_pairs={{0,2},{1,0},{2,4},{3,1},{4,6},{5,3},{6,7},{7,5},{8,10},{9,8},{10,1... | collective-permute-start | bytes 393224 | tf_op jit(solution)/shard_map/ppermute | solution.py:305
  66.3 5.6 %collective-permute-start.43 = (f32[4,64,128]{2,1,0:T(8,128)S(1)}, f32[4,64,128]{2,1,0:T(8,128)S(1)}, u32[]{:S(2)}, u32[]{:S(2)}) collective-permute-start(f32[4,64,128]{2,1,0:T(8,128)S(1)} %carry.46), channel_id=1, source_target_pairs={{0,2},{1,0},{2,4},{3,1},{4,6},{5,3},{6,7},{7,5},{8,10},{9,8},{10,1... | collective-permute-start | bytes 393224 | tf_op jit(solution)/shard_map/ppermute | solution.py:305
  67.7 5.6 %collective-permute-start.32 = (f32[4,64,128]{2,1,0:T(8,128)S(1)}, f32[4,64,128]{2,1,0:T(8,128)S(1)}, u32[]{:S(2)}, u32[]{:S(2)}) collective-permute-start(f32[4,64,128]{2,1,0:T(8,128)S(1)} %carry.41), channel_id=1, source_target_pairs={{0,2},{1,0},{2,4},{3,1},{4,6},{5,3},{6,7},{7,5},{8,10},{9,8},{10,1... | collective-permute-start | bytes 393224 | tf_op jit(solution)/shard_map/ppermute | solution.py:305
  69.1 4.3 %collective-permute-start.36 = (f32[4,64,128]{2,1,0:T(8,128)S(1)}, f32[4,64,128]{2,1,0:T(8,128)S(1)}, u32[]{:S(2)}, u32[]{:S(2)}) collective-permute-start(f32[4,64,128]{2,1,0:T(8,128)S(1)} %carry.43), channel_id=1, source_target_pairs={{0,2},{1,0},{2,4},{3,1},{4,6},{5,3},{6,7},{7,5},{8,10},{9,8},{10,1... | collective-permute-start | bytes 393224 | tf_op jit(solution)/shard_map/ppermute | solution.py:305
  70.5 4.3 %collective-permute-start.40 = (f32[4,64,128]{2,1,0:T(8,128)S(1)}, f32[4,64,128]{2,1,0:T(8,128)S(1)}, u32[]{:S(2)}, u32[]{:S(2)}) collective-permute-start(f32[4,64,128]{2,1,0:T(8,128)S(1)} %carry.45), channel_id=1, source_target_pairs={{0,2},{1,0},{2,4},{3,1},{4,6},{5,3},{6,7},{7,5},{8,10},{9,8},{10,1... | collective-permute-start | bytes 393224 | tf_op jit(solution)/shard_map/ppermute | solution.py:305
  71.9 4.3 %collective-permute-start.44 = (f32[4,64,128]{2,1,0:T(8,128)S(1)}, f32[4,64,128]{2,1,0:T(8,128)S(1)}, u32[]{:S(2)}, u32[]{:S(2)}) collective-permute-start(f32[4,64,128]{2,1,0:T(8,128)S(1)} %carry.47), channel_id=1, source_target_pairs={{0,2},{1,0},{2,4},{3,1},{4,6},{5,3},{6,7},{7,5},{8,10},{9,8},{10,1... | collective-permute-start | bytes 393224 | tf_op jit(solution)/shard_map/ppermute | solution.py:305
  73.3 3.1 %collective-permute-start.33 = (f32[2,64,128]{2,1,0:T(8,128)S(1)}, f32[2,64,128]{2,1,0:T(8,128)S(1)}, u32[]{:S(2)}, u32[]{:S(2)}) collective-permute-start(f32[2,64,128]{2,1,0:T(8,128)S(1)} %cross.12), channel_id=1, source_target_pairs={{0,1},{1,0},{2,3},{3,2},{4,5},{5,4},{6,7},{7,6},{8,9},{9,8},{10,11... | collective-permute-start | bytes 196616 | tf_op jit(solution)/shard_map/ppermute | solution.py:315
  73.4 2.9 %collective-permute-start.37 = (f32[2,64,128]{2,1,0:T(8,128)S(1)}, f32[2,64,128]{2,1,0:T(8,128)S(1)}, u32[]{:S(2)}, u32[]{:S(2)}) collective-permute-start(f32[2,64,128]{2,1,0:T(8,128)S(1)} %cross.13), channel_id=1, source_target_pairs={{0,1},{1,0},{2,3},{3,2},{4,5},{5,4},{6,7},{7,6},{8,9},{9,8},{10,11... | collective-permute-start | bytes 196616 | tf_op jit(solution)/shard_map/ppermute | solution.py:315
  74.8 1.5 %collective-permute-start.41 = (f32[2,64,128]{2,1,0:T(8,128)S(1)}, f32[2,64,128]{2,1,0:T(8,128)S(1)}, u32[]{:S(2)}, u32[]{:S(2)}) collective-permute-start(f32[2,64,128]{2,1,0:T(8,128)S(1)} %cross.14), channel_id=1, source_target_pairs={{0,1},{1,0},{2,3},{3,2},{4,5},{5,4},{6,7},{7,6},{8,9},{9,8},{10,11... | collective-permute-start | bytes 196616 | tf_op jit(solution)/shard_map/ppermute | solution.py:315
  76.2 1.3 %collective-permute-start.45 = (f32[2,64,128]{2,1,0:T(8,128)S(1)}, f32[2,64,128]{2,1,0:T(8,128)S(1)}, u32[]{:S(2)}, u32[]{:S(2)}) collective-permute-start(f32[2,64,128]{2,1,0:T(8,128)S(1)} %cross.15), channel_id=1, source_target_pairs={{0,1},{1,0},{2,3},{3,2},{4,5},{5,4},{6,7},{7,6},{8,9},{9,8},{10,11... | collective-permute-start | bytes 196616 | tf_op jit(solution)/shard_map/ppermute | solution.py:315

commit v7 on v6

--- a/solution.py
+++ b/solution.py
@@ -263,6 +263,8 @@
     swap = [(i, i ^ 1) for i in range(n_col)]
     ring = [(i, (i + 2 if i + 2 < n_col else n_col - 1) if i % 2 == 0 else (i - 2 if i > 2 else 0)) for i in range(n_col)]
 
+    squares = [(i, (i ^ 2) if (i // 2 + i) % 2 == 0 else i ^ 1) for i in range(n_col)] if pairs % 2 == 0 else ring
+
     def from_turn(value, k):
         return lax.ppermute(value, "row", [(i ^ k if flips else (i + k) % n_row, i) for i in range(n_row)])
 
@@ -298,7 +300,7 @@
         rest = lax.ppermute(cut(sums, leading, sums.shape[0] - leading, totals), "col", swap)
         parts = []
         for h in range(PARTS):
-            came = lax.ppermute(totals[h], "col", ring)
+            came = lax.ppermute(totals[h], "col", squares)
             for distance in range(far - 1, 0, -1):
                 kernel = functools.partial(carry_kernel, at(h, distance), at(h, pairs - distance) - leading)
                 total = small_call(kernel, (block,), "carry", sums, rest, came)[0]

time: 78.5 us -> 78.1 us (level)
  waiting for transfers between devices: 10.7 us -> 14.8 us
  starting transfers between devices: 48.5 us -> 45 us
  Pallas kernels: 15.7 us -> 14.7 us
    ppermute x8, starting transfers between devices: 10.8 us -> 5.18 us  [scatter(): came = lax.ppermute(totals[h], 'col', squares)]
    ppermute x8, waiting for transfers between devices: 0.02 us -> 3.94 us  [scatter(): came = lax.ppermute(totals[h], 'col', squares)]
    ppermute x16, starting transfers between devices: 22.9 us -> 24.9 us  [scatter(): came = lax.ppermute(total, 'col', ring)]
    ppermute x10, waiting for transfers between devices: 3.13 us -> 4.26 us  [from_turn(): lax.ppermute(value, 'row', [(i ^ k if flips else (i + k) % n_row, i) for...]
    pallas_call x7, Pallas kernels: 8.89 us -> 7.85 us  [transfer(): pl.pallas_call(functools.partial(transfer_kernel, fields_at, begin, end,...]
    ppermute x16, waiting for transfers between devices: 3.27 us -> 2.43 us  [scatter(): came = lax.ppermute(total, 'col', ring)]
  transfers between devices with their start and end apart: 46 -> 46, of which waited for: 15 -> 17; matrix products, arithmetic and copies ran while one was open for 3% -> 3% of each run, Pallas kernels for 17% -> 16%
where the time goes in v7:
time: 78.1 us; the launch traced here: 78 us
  starting transfers between devices  45 us (58%)
  waiting for transfers between devices  14.8 us (19%)
  Pallas kernels  14.7 us (19%)
  other arithmetic  2.08 us (3%)
  between operations  1.2 us (2%)
    ppermute x16, starting transfers between devices, scatter(): came = lax.ppermute(total, 'col', ring)  24.9 us
    ppermute x10, starting transfers between devices, from_turn(): lax.ppermute(value, 'row', [(i ^ k if flips else (i + k) % n_row, i) for...  12.4 us
    pallas_call x7, Pallas kernels, transfer(): pl.pallas_call(functools.partial(transfer_kernel, fields_at, begin, end,...  7.85 us
    ppermute x8, starting transfers between devices, scatter(): came = lax.ppermute(totals[h], 'col', squares)  5.18 us
    pallas_call x1, Pallas kernels, prepare(): pl.pallas_call(prepare_kernel, in_specs=[pl.BlockSpec(memory_space=pltpu....  4.48 us
    ppermute x10, waiting for transfers between devices, from_turn(): lax.ppermute(value, 'row', [(i ^ k if flips else (i + k) % n_row, i) for...  4.26 us
    ppermute x8, waiting for transfers between devices, scatter(): came = lax.ppermute(totals[h], 'col', squares)  3.94 us
    ppermute x16, waiting for transfers between devices, scatter(): came = lax.ppermute(total, 'col', ring)  2.43 us
  transfers between devices with their start and end apart: 46, of which 17 were waited for; matrix products, arithmetic and copies ran while one was open for 3% of the time, Pallas kernels for 16%

profile of v7, /device:TPU:0, one launch (start us, length us, event | category | flops | bytes accessed | tf_op | source)
XLA Modules:
  0.0 78.0 jit_solution(960707366567678561)
XLA Ops:
  0.0 3.0 %collective-permute-start.2 = (f32[8,64,128]{2,1,0:T(8,128)}, f32[8,64,128]{2,1,0:T(8,128)S(1)}, u32[]{:S(2)}, u32[]{:S(2)}) collective-permute-start(f32[8,64,128]{2,1,0:T(8,128)} %source_ref.5), channel_id=1, source_target_pairs={{16,0},{24,8},{0,16},{8,24},{17,1},{25,9},{1,17},{9,25},{18,2},{26... | collective-permute-start | bytes 786440 | tf_op jit(solution)/shard_map/ppermute | solution.py:269
  3.0 1.5 %collective-permute-start = (f32[8,64,128]{2,1,0:T(8,128)}, f32[8,64,128]{2,1,0:T(8,128)S(1)}, u32[]{:S(2)}, u32[]{:S(2)}) collective-permute-start(f32[8,64,128]{2,1,0:T(8,128)} %source_ref.5), channel_id=1, source_target_pairs={{8,0},{0,8},{24,16},{16,24},{9,1},{1,9},{25,17},{17,25},{10,2},{2,... | collective-permute-start | bytes 786440 | tf_op jit(solution)/shard_map/ppermute | solution.py:269
  5.1 0.7 fusion.4
  5.8 0.7 iota_add_fusion
  6.5 4.5 %prepare.1.rest_0_.a_ref = bf16[257,64,128]{2,1,0:T(8,128)(2,1)S(1)} custom-call(f32[64,64,256]{2,1,0:T(8,128)} %bitcast.3), custom_call_target="tpu_custom_call" | custom-call | bytes 25165824 | tf_op jit(solution)/shard_map/prepare/pallas_call | solution.py:69
  11.6 0.6 collective-permute-start.1
  12.2 0.9 %collective-permute-start.3 = (f32[4,64,128]{2,1,0:T(8,128)S(1)}, f32[4,64,128]{2,1,0:T(8,128)S(1)}, u32[]{:S(2)}, u32[]{:S(2)}) collective-permute-start(f32[4,64,128]{2,1,0:T(8,128)S(1)} %cut.7), channel_id=1, source_target_pairs={{8,0},{0,8},{24,16},{16,24},{9,1},{1,9},{25,17},{17,25},{10,2},{2,... | collective-permute-start | bytes 393224 | tf_op jit(solution)/shard_map/ppermute | solution.py:269
  13.2 0.6 keep.1.plan_ref
  13.9 2.3 %transfer.7.rest_2_ = f32[64,64,128]{2,1,0:T(8,128)S(1)} custom-call(s32[872]{0:T(1024)S(4)} %keep.1.plan_ref, bf16[257,64,128]{2,1,0:T(8,128)(2,1)S(1)} %prepare.1.rest_0_.a_ref, f32[8,64,128]{2,1,0:T(8,128)S(1)} %copy-done, f32[8,64,128]{2,1,0:T(8,128)S(1)} %collective-permute-done.rest_1_, f32[8,64,128]{2,1,0:T(8,128)S(1)} %collective-permute-done.2.rest_2_), custom_call_target="tpu_custom_call" | custom-call | tf_op jit(solution)/shard_map/transfer/pallas_call | solution.py:135
  17.8 1.0 %transfer.9.sums_ref.value_ref = f32[64,64,128]{2,1,0:T(8,128)S(1)} custom-call(s32[872]{0:T(1024)S(4)} %keep.1.plan_ref, bf16[257,64,128]{2,1,0:T(8,128)(2,1)S(1)} %prepare.1.rest_0_.a_ref, f32[4,64,128]{2,1,0:T(8,128)S(1)} %collective-permute-done.1.rest_0_, f32[4,64,128]{2,1,0:T(8,128)S(1)} %collective-permute-done.3.rest_1_, ...), custom_call_target="tpu_custom_call" | custom-call | tf_op jit(solution)/shard_map/transfer/pallas_call | solution.py:135
  18.7 0.9 %collective-permute-done.4.got_ref = f32[16,64,128]{2,1,0:T(8,128)S(1)} collective-permute-done((f32[16,64,128]{2,1,0:T(8,128)S(1)}, f32[16,64,128]{2,1,0:T(8,128)S(1)}, u32[]{:S(2)}, u32[]{:S(2)}) %collective-permute-start.4) | collective-permute-done | bytes 524320 | tf_op jit(solution)/shard_map/ppermute | solution.py:292
  20.1 1.6 %collective-permute-start.6 = (f32[4,64,128]{2,1,0:T(8,128)S(1)}, f32[4,64,128]{2,1,0:T(8,128)S(1)}, u32[]{:S(2)}, u32[]{:S(2)}) collective-permute-start(f32[4,64,128]{2,1,0:T(8,128)S(1)} %carry.24.rest_0_), channel_id=1, source_target_pairs={{0,2},{1,0},{2,3},{3,1},{4,6},{5,4},{6,7},{7,5},{8,10},{9,8},{10,1... | collective-permute-start | bytes 393224 | tf_op jit(solution)/shard_map/ppermute | solution.py:303
  22.3 1.8 %collective-permute-done.6.rest_0_ = f32[4,64,128]{2,1,0:T(8,128)S(1)} collective-permute-done((f32[4,64,128]{2,1,0:T(8,128)S(1)}, f32[4,64,128]{2,1,0:T(8,128)S(1)}, u32[]{:S(2)}, u32[]{:S(2)}) %collective-permute-start.6) | collective-permute-done | bytes 131104 | tf_op jit(solution)/shard_map/ppermute | solution.py:303
  24.2 2.5 %collective-permute-start.7 = (f32[4,64,128]{2,1,0:T(8,128)S(1)}, f32[4,64,128]{2,1,0:T(8,128)S(1)}, u32[]{:S(2)}, u32[]{:S(2)}) collective-permute-start(f32[4,64,128]{2,1,0:T(8,128)S(1)} %carry.28), channel_id=1, source_target_pairs={{0,2},{1,0},{2,4},{3,1},{4,6},{5,3},{6,7},{7,5},{8,10},{9,8},{10,1... | collective-permute-start | bytes 393224 | tf_op jit(solution)/shard_map/ppermute | solution.py:307
  26.7 1.4 %collective-permute-start.11 = (f32[4,64,128]{2,1,0:T(8,128)S(1)}, f32[4,64,128]{2,1,0:T(8,128)S(1)}, u32[]{:S(2)}, u32[]{:S(2)}) collective-permute-start(f32[4,64,128]{2,1,0:T(8,128)S(1)} %carry.30), channel_id=1, source_target_pairs={{0,2},{1,0},{2,4},{3,1},{4,6},{5,3},{6,7},{7,5},{8,10},{9,8},{10,1... | collective-permute-start | bytes 393224 | tf_op jit(solution)/shard_map/ppermute | solution.py:307
  28.1 1.8 %collective-permute-start.17 = (f32[4,64,128]{2,1,0:T(8,128)S(1)}, f32[4,64,128]{2,1,0:T(8,128)S(1)}, u32[]{:S(2)}, u32[]{:S(2)}) collective-permute-start(f32[4,64,128]{2,1,0:T(8,128)S(1)} %carry.32), channel_id=1, source_target_pairs={{0,2},{1,0},{2,4},{3,1},{4,6},{5,3},{6,7},{7,5},{8,10},{9,8},{10,1... | collective-permute-start | bytes 393224 | tf_op jit(solution)/shard_map/ppermute | solution.py:307
  30.0 1.4 %collective-permute-start.21 = (f32[4,64,128]{2,1,0:T(8,128)S(1)}, f32[4,64,128]{2,1,0:T(8,128)S(1)}, u32[]{:S(2)}, u32[]{:S(2)}) collective-permute-start(f32[4,64,128]{2,1,0:T(8,128)S(1)} %carry.34), channel_id=1, source_target_pairs={{0,2},{1,0},{2,4},{3,1},{4,6},{5,3},{6,7},{7,5},{8,10},{9,8},{10,1... | collective-permute-start | bytes 393224 | tf_op jit(solution)/shard_map/ppermute | solution.py:307
  31.4 1.4 %collective-permute-start.8 = (f32[4,64,128]{2,1,0:T(8,128)S(1)}, f32[4,64,128]{2,1,0:T(8,128)S(1)}, u32[]{:S(2)}, u32[]{:S(2)}) collective-permute-start(f32[4,64,128]{2,1,0:T(8,128)S(1)} %carry.29), channel_id=1, source_target_pairs={{0,2},{1,0},{2,4},{3,1},{4,6},{5,3},{6,7},{7,5},{8,10},{9,8},{10,1... | collective-permute-start | bytes 393224 | tf_op jit(solution)/shard_map/ppermute | solution.py:307
  32.8 1.4 %collective-permute-start.12 = (f32[4,64,128]{2,1,0:T(8,128)S(1)}, f32[4,64,128]{2,1,0:T(8,128)S(1)}, u32[]{:S(2)}, u32[]{:S(2)}) collective-permute-start(f32[4,64,128]{2,1,0:T(8,128)S(1)} %carry.31), channel_id=1, source_target_pairs={{0,2},{1,0},{2,4},{3,1},{4,6},{5,3},{6,7},{7,5},{8,10},{9,8},{10,1... | collective-permute-start | bytes 393224 | tf_op jit(solution)/shard_map/ppermute | solution.py:307
  34.2 1.4 %collective-permute-start.18 = (f32[4,64,128]{2,1,0:T(8,128)S(1)}, f32[4,64,128]{2,1,0:T(8,128)S(1)}, u32[]{:S(2)}, u32[]{:S(2)}) collective-permute-start(f32[4,64,128]{2,1,0:T(8,128)S(1)} %carry.33), channel_id=1, source_target_pairs={{0,2},{1,0},{2,4},{3,1},{4,6},{5,3},{6,7},{7,5},{8,10},{9,8},{10,1... | collective-permute-start | bytes 393224 | tf_op jit(solution)/shard_map/ppermute | solution.py:307
  35.6 1.4 %collective-permute-start.22 = (f32[4,64,128]{2,1,0:T(8,128)S(1)}, f32[4,64,128]{2,1,0:T(8,128)S(1)}, u32[]{:S(2)}, u32[]{:S(2)}) collective-permute-start(f32[4,64,128]{2,1,0:T(8,128)S(1)} %carry.35), channel_id=1, source_target_pairs={{0,2},{1,0},{2,4},{3,1},{4,6},{5,3},{6,7},{7,5},{8,10},{9,8},{10,1... | collective-permute-start | bytes 393224 | tf_op jit(solution)/shard_map/ppermute | solution.py:307
  37.6 0.7 collective-permute-done.9.rest_2_
  39.0 0.5 collective-permute-done.22.came_ref.rest_4_
  39.8 0.9 %collective-permute-start.14 = (f32[4,64,128]{2,1,0:T(8,128)S(1)}, f32[4,64,128]{2,1,0:T(8,128)S(1)}, u32[]{:S(2)}, u32[]{:S(2)}) collective-permute-start(f32[4,64,128]{2,1,0:T(8,128)S(1)} %finish.3.rest_0_), channel_id=1, source_target_pairs={{8,0},{0,8},{24,16},{16,24},{9,1},{1,9},{25,17},{17,25},{10,2},{2,... | collective-permute-start | bytes 393224 | tf_op jit(solution)/shard_map/ppermute | solution.py:269
  41.0 1.6 %collective-permute-start.24 = (f32[4,64,128]{2,1,0:T(8,128)S(1)}, f32[4,64,128]{2,1,0:T(8,128)S(1)}, u32[]{:S(2)}, u32[]{:S(2)}) collective-permute-start(f32[4,64,128]{2,1,0:T(8,128)S(1)} %finish.4.rest_1_), channel_id=1, source_target_pairs={{16,0},{24,8},{0,16},{8,24},{17,1},{25,9},{1,17},{9,25},{18,2},{26... | collective-permute-start | bytes 393224 | tf_op jit(solution)/shard_map/ppermute | solution.py:269
  43.1 0.9 %collective-permute-start.26 = (f32[4,64,128]{2,1,0:T(8,128)S(1)}, f32[4,64,128]{2,1,0:T(8,128)S(1)}, u32[]{:S(2)}, u32[]{:S(2)}) collective-permute-start(f32[4,64,128]{2,1,0:T(8,128)S(1)} %finish.4.rest_1_), channel_id=1, source_target_pairs={{8,0},{0,8},{24,16},{16,24},{9,1},{1,9},{25,17},{17,25},{10,2},{2,... | collective-permute-start | bytes 393224 | tf_op jit(solution)/shard_map/ppermute | solution.py:269
  44.0 1.1 %transfer.10.rest_0_.rest_4_ = f32[64,64,128]{2,1,0:T(8,128)S(1)} custom-call(s32[872]{0:T(1024)S(4)} %keep.1.plan_ref, bf16[257,64,128]{2,1,0:T(8,128)(2,1)S(1)} %prepare.1.rest_0_.a_ref, f32[4,64,128]{2,1,0:T(8,128)S(1)} %finish.3.rest_0_, f32[4,64,128]{2,1,0:T(8,128)S(1)} %finish.4.rest_1_), custom_call_target="tpu_custom_call" | custom-call | tf_op jit(solution)/shard_map/transfer/pallas_call | solution.py:135
  45.1 0.8 collective-permute-done.14.value_ref.rest_0_
  45.9 1.6 %collective-permute-start.15 = (f32[4,64,128]{2,1,0:T(8,128)S(1)}, f32[4,64,128]{2,1,0:T(8,128)S(1)}, u32[]{:S(2)}, u32[]{:S(2)}) collective-permute-start(f32[4,64,128]{2,1,0:T(8,128)S(1)} %cut.9), channel_id=1, source_target_pairs={{16,0},{24,8},{0,16},{8,24},{17,1},{25,9},{1,17},{9,25},{18,2},{26... | collective-permute-start | bytes 393224 | tf_op jit(solution)/shard_map/ppermute | solution.py:269
  47.5 0.9 %collective-permute-start.25 = (f32[4,64,128]{2,1,0:T(8,128)S(1)}, f32[4,64,128]{2,1,0:T(8,128)S(1)}, u32[]{:S(2)}, u32[]{:S(2)}) collective-permute-start(f32[4,64,128]{2,1,0:T(8,128)S(1)} %cut.10), channel_id=1, source_target_pairs={{8,0},{0,8},{24,16},{16,24},{9,1},{1,9},{25,17},{17,25},{10,2},{2,... | collective-permute-start | bytes 393224 | tf_op jit(solution)/shard_map/ppermute | solution.py:269
  48.4 1.8 %collective-permute-done.27.rest_2_ = f32[4,64,128]{2,1,0:T(8,128)S(1)} collective-permute-done((f32[4,64,128]{2,1,0:T(8,128)S(1)}, f32[4,64,128]{2,1,0:T(8,128)S(1)}, u32[]{:S(2)}, u32[]{:S(2)}) %collective-permute-start.27) | collective-permute-done | bytes 131104 | tf_op jit(solution)/shard_map/ppermute | solution.py:269
  50.2 1.6 %transfer.11.rest_2_ = f32[64,64,128]{2,1,0:T(8,128)S(1)} custom-call(s32[872]{0:T(1024)S(4)} %keep.1.plan_ref, bf16[257,64,128]{2,1,0:T(8,128)(2,1)S(1)} %prepare.1.rest_0_.a_ref, f32[4,64,128]{2,1,0:T(8,128)S(1)} %collective-permute-done.14.value_ref.rest_0_, f32[4,64,128]{2,1,0:T(8,128)S(1)} %collective-permute-done.26.rest_1_, ...), custom_call_target="tpu_custom_call" | custom-call | tf_op jit(solution)/shard_map/transfer/pallas_call | solution.py:135
  53.1 1.0 %transfer.13.sums_ref.value_ref = f32[64,64,128]{2,1,0:T(8,128)S(1)} custom-call(s32[872]{0:T(1024)S(4)} %keep.1.plan_ref, bf16[257,64,128]{2,1,0:T(8,128)(2,1)S(1)} %prepare.1.rest_0_.a_ref, f32[4,64,128]{2,1,0:T(8,128)S(1)} %collective-permute-done.15.rest_0_, f32[4,64,128]{2,1,0:T(8,128)S(1)} %collective-permute-done.25.rest_1_, ...), custom_call_target="tpu_custom_call" | custom-call | tf_op jit(solution)/shard_map/transfer/pallas_call | solution.py:135
  54.1 0.9 %collective-permute-done.28.got_ref = f32[16,64,128]{2,1,0:T(8,128)S(1)} collective-permute-done((f32[16,64,128]{2,1,0:T(8,128)S(1)}, f32[16,64,128]{2,1,0:T(8,128)S(1)}, u32[]{:S(2)}, u32[]{:S(2)}) %collective-permute-start.28) | collective-permute-done | bytes 524320 | tf_op jit(solution)/shard_map/ppermute | solution.py:292
  55.4 2.5 %collective-permute-start.30 = (f32[4,64,128]{2,1,0:T(8,128)S(1)}, f32[4,64,128]{2,1,0:T(8,128)S(1)}, u32[]{:S(2)}, u32[]{:S(2)}) collective-permute-start(f32[4,64,128]{2,1,0:T(8,128)S(1)} %carry.36.rest_0_), channel_id=1, source_target_pairs={{0,2},{1,0},{2,3},{3,1},{4,6},{5,4},{6,7},{7,5},{8,10},{9,8},{10,1... | collective-permute-start | bytes 393224 | tf_op jit(solution)/shard_map/ppermute | solution.py:303
  58.4 2.1 %collective-permute-done.30.rest_0_ = f32[4,64,128]{2,1,0:T(8,128)S(1)} collective-permute-done((f32[4,64,128]{2,1,0:T(8,128)S(1)}, f32[4,64,128]{2,1,0:T(8,128)S(1)}, u32[]{:S(2)}, u32[]{:S(2)}) %collective-permute-start.30) | collective-permute-done | bytes 131104 | tf_op jit(solution)/shard_map/ppermute | solution.py:303
  60.5 2.5 %collective-permute-start.31 = (f32[4,64,128]{2,1,0:T(8,128)S(1)}, f32[4,64,128]{2,1,0:T(8,128)S(1)}, u32[]{:S(2)}, u32[]{:S(2)}) collective-permute-start(f32[4,64,128]{2,1,0:T(8,128)S(1)} %carry.40), channel_id=1, source_target_pairs={{0,2},{1,0},{2,4},{3,1},{4,6},{5,3},{6,7},{7,5},{8,10},{9,8},{10,1... | collective-permute-start | bytes 393224 | tf_op jit(solution)/shard_map/ppermute | solution.py:307
  63.0 1.4 %collective-permute-start.35 = (f32[4,64,128]{2,1,0:T(8,128)S(1)}, f32[4,64,128]{2,1,0:T(8,128)S(1)}, u32[]{:S(2)}, u32[]{:S(2)}) collective-permute-start(f32[4,64,128]{2,1,0:T(8,128)S(1)} %carry.42), channel_id=1, source_target_pairs={{0,2},{1,0},{2,4},{3,1},{4,6},{5,3},{6,7},{7,5},{8,10},{9,8},{10,1... | collective-permute-start | bytes 393224 | tf_op jit(solution)/shard_map/ppermute | solution.py:307
  64.4 1.8 %collective-permute-start.39 = (f32[4,64,128]{2,1,0:T(8,128)S(1)}, f32[4,64,128]{2,1,0:T(8,128)S(1)}, u32[]{:S(2)}, u32[]{:S(2)}) collective-permute-start(f32[4,64,128]{2,1,0:T(8,128)S(1)} %carry.44), channel_id=1, source_target_pairs={{0,2},{1,0},{2,4},{3,1},{4,6},{5,3},{6,7},{7,5},{8,10},{9,8},{10,1... | collective-permute-start | bytes 393224 | tf_op jit(solution)/shard_map/ppermute | solution.py:307
  66.3 1.4 %collective-permute-start.43 = (f32[4,64,128]{2,1,0:T(8,128)S(1)}, f32[4,64,128]{2,1,0:T(8,128)S(1)}, u32[]{:S(2)}, u32[]{:S(2)}) collective-permute-start(f32[4,64,128]{2,1,0:T(8,128)S(1)} %carry.46), channel_id=1, source_target_pairs={{0,2},{1,0},{2,4},{3,1},{4,6},{5,3},{6,7},{7,5},{8,10},{9,8},{10,1... | collective-permute-start | bytes 393224 | tf_op jit(solution)/shard_map/ppermute | solution.py:307
  67.7 1.4 %collective-permute-start.32 = (f32[4,64,128]{2,1,0:T(8,128)S(1)}, f32[4,64,128]{2,1,0:T(8,128)S(1)}, u32[]{:S(2)}, u32[]{:S(2)}) collective-permute-start(f32[4,64,128]{2,1,0:T(8,128)S(1)} %carry.41), channel_id=1, source_target_pairs={{0,2},{1,0},{2,4},{3,1},{4,6},{5,3},{6,7},{7,5},{8,10},{9,8},{10,1... | collective-permute-start | bytes 393224 | tf_op jit(solution)/shard_map/ppermute | solution.py:307
  69.1 1.4 %collective-permute-start.36 = (f32[4,64,128]{2,1,0:T(8,128)S(1)}, f32[4,64,128]{2,1,0:T(8,128)S(1)}, u32[]{:S(2)}, u32[]{:S(2)}) collective-permute-start(f32[4,64,128]{2,1,0:T(8,128)S(1)} %carry.43), channel_id=1, source_target_pairs={{0,2},{1,0},{2,4},{3,1},{4,6},{5,3},{6,7},{7,5},{8,10},{9,8},{10,1... | collective-permute-start | bytes 393224 | tf_op jit(solution)/shard_map/ppermute | solution.py:307
  70.5 1.4 %collective-permute-start.40 = (f32[4,64,128]{2,1,0:T(8,128)S(1)}, f32[4,64,128]{2,1,0:T(8,128)S(1)}, u32[]{:S(2)}, u32[]{:S(2)}) collective-permute-start(f32[4,64,128]{2,1,0:T(8,128)S(1)} %carry.45), channel_id=1, source_target_pairs={{0,2},{1,0},{2,4},{3,1},{4,6},{5,3},{6,7},{7,5},{8,10},{9,8},{10,1... | collective-permute-start | bytes 393224 | tf_op jit(solution)/shard_map/ppermute | solution.py:307
  71.9 1.4 %collective-permute-start.44 = (f32[4,64,128]{2,1,0:T(8,128)S(1)}, f32[4,64,128]{2,1,0:T(8,128)S(1)}, u32[]{:S(2)}, u32[]{:S(2)}) collective-permute-start(f32[4,64,128]{2,1,0:T(8,128)S(1)} %carry.47), channel_id=1, source_target_pairs={{0,2},{1,0},{2,4},{3,1},{4,6},{5,3},{6,7},{7,5},{8,10},{9,8},{10,1... | collective-permute-start | bytes 393224 | tf_op jit(solution)/shard_map/ppermute | solution.py:307
  73.9 0.5 collective-permute-done.40.came_ref.rest_7_
  74.6 1.3 %collective-permute-done.44.came_ref.rest_10_ = f32[4,64,128]{2,1,0:T(8,128)S(1)} collective-permute-done((f32[4,64,128]{2,1,0:T(8,128)S(1)}, f32[4,64,128]{2,1,0:T(8,128)S(1)}, u32[]{:S(2)}, u32[]{:S(2)}) %collective-permute-start.44) | collective-permute-done | bytes 131104 | tf_op jit(solution)/shard_map/ppermute | solution.py:307
  76.0 1.2 %collective-permute-done.45.rest_11_ = f32[2,64,128]{2,1,0:T(8,128)S(1)} collective-permute-done((f32[2,64,128]{2,1,0:T(8,128)S(1)}, f32[2,64,128]{2,1,0:T(8,128)S(1)}, u32[]{:S(2)}, u32[]{:S(2)}) %collective-permute-start.45) | collective-permute-done | bytes 65568 | tf_op jit(solution)/shard_map/ppermute | solution.py:317
  77.2 0.8 finish.5
  (106 shorter events, 9.2 us)
Async XLA Ops:
  0.0 11.5 %collective-permute-start.2 = (f32[8,64,128]{2,1,0:T(8,128)}, f32[8,64,128]{2,1,0:T(8,128)S(1)}, u32[]{:S(2)}, u32[]{:S(2)}) collective-permute-start(f32[8,64,128]{2,1,0:T(8,128)} %source_ref.5), channel_id=1, source_target_pairs={{16,0},{24,8},{0,16},{8,24},{17,1},{25,9},{1,17},{9,25},{18,2},{26... | collective-permute-start | bytes 786440 | tf_op jit(solution)/shard_map/ppermute | solution.py:269
  3.0 8.6 %collective-permute-start = (f32[8,64,128]{2,1,0:T(8,128)}, f32[8,64,128]{2,1,0:T(8,128)S(1)}, u32[]{:S(2)}, u32[]{:S(2)}) collective-permute-start(f32[8,64,128]{2,1,0:T(8,128)} %source_ref.5), channel_id=1, source_target_pairs={{8,0},{0,8},{24,16},{16,24},{9,1},{1,9},{25,17},{17,25},{10,2},{2,... | collective-permute-start | bytes 786440 | tf_op jit(solution)/shard_map/ppermute | solution.py:269
  11.6 2.3 %copy-start = (f32[8,64,128]{2,1,0:T(8,128)S(1)}, f32[8,64,128]{2,1,0:T(8,128)}, u32[]{:S(2)}) copy-start(f32[8,64,128]{2,1,0:T(8,128)} %source_ref.5) | copy-start | bytes 786436
  11.6 5.0 %collective-permute-start.1 = (f32[4,64,128]{2,1,0:T(8,128)S(1)}, f32[4,64,128]{2,1,0:T(8,128)S(1)}, u32[]{:S(2)}, u32[]{:S(2)}) collective-permute-start(f32[4,64,128]{2,1,0:T(8,128)S(1)} %cut.6), channel_id=1, source_target_pairs={{16,0},{24,8},{0,16},{8,24},{17,1},{25,9},{1,17},{9,25},{18,2},{26... | collective-permute-start | bytes 393224 | tf_op jit(solution)/shard_map/ppermute | solution.py:269
  12.2 5.0 %collective-permute-start.3 = (f32[4,64,128]{2,1,0:T(8,128)S(1)}, f32[4,64,128]{2,1,0:T(8,128)S(1)}, u32[]{:S(2)}, u32[]{:S(2)}) collective-permute-start(f32[4,64,128]{2,1,0:T(8,128)S(1)} %cut.7), channel_id=1, source_target_pairs={{8,0},{0,8},{24,16},{16,24},{9,1},{1,9},{25,17},{17,25},{10,2},{2,... | collective-permute-start | bytes 393224 | tf_op jit(solution)/shard_map/ppermute | solution.py:269
  17.7 2.0 %collective-permute-start.4 = (f32[16,64,128]{2,1,0:T(8,128)S(1)}, f32[16,64,128]{2,1,0:T(8,128)S(1)}, u32[]{:S(2)}, u32[]{:S(2)}) collective-permute-start(f32[16,64,128]{2,1,0:T(8,128)S(1)} %slice.18), channel_id=1, source_target_pairs={{0,1},{1,0},{2,3},{3,2},{4,5},{5,4},{6,7},{7,6},{8,9},{9,8},{10,11... | collective-permute-start | bytes 1572872 | tf_op jit(solution)/shard_map/ppermute | solution.py:292
  19.9 4.3 %collective-permute-start.5 = (f32[48,64,128]{2,1,0:T(8,128)S(1)}, f32[48,64,128]{2,1,0:T(8,128)S(1)}, u32[]{:S(2)}, u32[]{:S(2)}) collective-permute-start(f32[48,64,128]{2,1,0:T(8,128)S(1)} %cut.8), channel_id=1, source_target_pairs={{0,1},{1,0},{2,3},{3,2},{4,5},{5,4},{6,7},{7,6},{8,9},{9,8},{10,11... | collective-permute-start | bytes 4718600 | tf_op jit(solution)/shard_map/ppermute | solution.py:300
  20.1 4.1 %collective-permute-start.6 = (f32[4,64,128]{2,1,0:T(8,128)S(1)}, f32[4,64,128]{2,1,0:T(8,128)S(1)}, u32[]{:S(2)}, u32[]{:S(2)}) collective-permute-start(f32[4,64,128]{2,1,0:T(8,128)S(1)} %carry.24.rest_0_), channel_id=1, source_target_pairs={{0,2},{1,0},{2,3},{3,1},{4,6},{5,4},{6,7},{7,5},{8,10},{9,8},{10,1... | collective-permute-start | bytes 393224 | tf_op jit(solution)/shard_map/ppermute | solution.py:303
  21.6 5.0 %collective-permute-start.10 = (f32[4,64,128]{2,1,0:T(8,128)S(1)}, f32[4,64,128]{2,1,0:T(8,128)S(1)}, u32[]{:S(2)}, u32[]{:S(2)}) collective-permute-start(f32[4,64,128]{2,1,0:T(8,128)S(1)} %carry.25.rest_1_), channel_id=1, source_target_pairs={{0,2},{1,0},{2,3},{3,1},{4,6},{5,4},{6,7},{7,5},{8,10},{9,8},{10,1... | collective-permute-start | bytes 393224 | tf_op jit(solution)/shard_map/ppermute | solution.py:303
  22.0 6.1 %collective-permute-start.16 = (f32[4,64,128]{2,1,0:T(8,128)S(1)}, f32[4,64,128]{2,1,0:T(8,128)S(1)}, u32[]{:S(2)}, u32[]{:S(2)}) collective-permute-start(f32[4,64,128]{2,1,0:T(8,128)S(1)} %carry.26.rest_2_), channel_id=1, source_target_pairs={{0,2},{1,0},{2,3},{3,1},{4,6},{5,4},{6,7},{7,5},{8,10},{9,8},{10,1... | collective-permute-start | bytes 393224 | tf_op jit(solution)/shard_map/ppermute | solution.py:303
  22.2 7.7 %collective-permute-start.20 = (f32[4,64,128]{2,1,0:T(8,128)S(1)}, f32[4,64,128]{2,1,0:T(8,128)S(1)}, u32[]{:S(2)}, u32[]{:S(2)}) collective-permute-start(f32[4,64,128]{2,1,0:T(8,128)S(1)} %carry.27.rest_3_), channel_id=1, source_target_pairs={{0,2},{1,0},{2,3},{3,1},{4,6},{5,4},{6,7},{7,5},{8,10},{9,8},{10,1... | collective-permute-start | bytes 393224 | tf_op jit(solution)/shard_map/ppermute | solution.py:303
  24.2 7.1 %collective-permute-start.7 = (f32[4,64,128]{2,1,0:T(8,128)S(1)}, f32[4,64,128]{2,1,0:T(8,128)S(1)}, u32[]{:S(2)}, u32[]{:S(2)}) collective-permute-start(f32[4,64,128]{2,1,0:T(8,128)S(1)} %carry.28), channel_id=1, source_target_pairs={{0,2},{1,0},{2,4},{3,1},{4,6},{5,3},{6,7},{7,5},{8,10},{9,8},{10,1... | collective-permute-start | bytes 393224 | tf_op jit(solution)/shard_map/ppermute | solution.py:307
  26.7 6.0 %collective-permute-start.11 = (f32[4,64,128]{2,1,0:T(8,128)S(1)}, f32[4,64,128]{2,1,0:T(8,128)S(1)}, u32[]{:S(2)}, u32[]{:S(2)}) collective-permute-start(f32[4,64,128]{2,1,0:T(8,128)S(1)} %carry.30), channel_id=1, source_target_pairs={{0,2},{1,0},{2,4},{3,1},{4,6},{5,3},{6,7},{7,5},{8,10},{9,8},{10,1... | collective-permute-start | bytes 393224 | tf_op jit(solution)/shard_map/ppermute | solution.py:307
  28.1 6.0 %collective-permute-start.17 = (f32[4,64,128]{2,1,0:T(8,128)S(1)}, f32[4,64,128]{2,1,0:T(8,128)S(1)}, u32[]{:S(2)}, u32[]{:S(2)}) collective-permute-start(f32[4,64,128]{2,1,0:T(8,128)S(1)} %carry.32), channel_id=1, source_target_pairs={{0,2},{1,0},{2,4},{3,1},{4,6},{5,3},{6,7},{7,5},{8,10},{9,8},{10,1... | collective-permute-start | bytes 393224 | tf_op jit(solution)/shard_map/ppermute | solution.py:307
  30.0 5.6 %collective-permute-start.21 = (f32[4,64,128]{2,1,0:T(8,128)S(1)}, f32[4,64,128]{2,1,0:T(8,128)S(1)}, u32[]{:S(2)}, u32[]{:S(2)}) collective-permute-start(f32[4,64,128]{2,1,0:T(8,128)S(1)} %carry.34), channel_id=1, source_target_pairs={{0,2},{1,0},{2,4},{3,1},{4,6},{5,3},{6,7},{7,5},{8,10},{9,8},{10,1... | collective-permute-start | bytes 393224 | tf_op jit(solution)/shard_map/ppermute | solution.py:307
  31.4 5.6 %collective-permute-start.8 = (f32[4,64,128]{2,1,0:T(8,128)S(1)}, f32[4,64,128]{2,1,0:T(8,128)S(1)}, u32[]{:S(2)}, u32[]{:S(2)}) collective-permute-start(f32[4,64,128]{2,1,0:T(8,128)S(1)} %carry.29), channel_id=1, source_target_pairs={{0,2},{1,0},{2,4},{3,1},{4,6},{5,3},{6,7},{7,5},{8,10},{9,8},{10,1... | collective-permute-start | bytes 393224 | tf_op jit(solution)/shard_map/ppermute | solution.py:307
  32.8 4.3 %collective-permute-start.12 = (f32[4,64,128]{2,1,0:T(8,128)S(1)}, f32[4,64,128]{2,1,0:T(8,128)S(1)}, u32[]{:S(2)}, u32[]{:S(2)}) collective-permute-start(f32[4,64,128]{2,1,0:T(8,128)S(1)} %carry.31), channel_id=1, source_target_pairs={{0,2},{1,0},{2,4},{3,1},{4,6},{5,3},{6,7},{7,5},{8,10},{9,8},{10,1... | collective-permute-start | bytes 393224 | tf_op jit(solution)/shard_map/ppermute | solution.py:307
  34.2 4.4 %collective-permute-start.18 = (f32[4,64,128]{2,1,0:T(8,128)S(1)}, f32[4,64,128]{2,1,0:T(8,128)S(1)}, u32[]{:S(2)}, u32[]{:S(2)}) collective-permute-start(f32[4,64,128]{2,1,0:T(8,128)S(1)} %carry.33), channel_id=1, source_target_pairs={{0,2},{1,0},{2,4},{3,1},{4,6},{5,3},{6,7},{7,5},{8,10},{9,8},{10,1... | collective-permute-start | bytes 393224 | tf_op jit(solution)/shard_map/ppermute | solution.py:307
  35.6 4.0 %collective-permute-start.22 = (f32[4,64,128]{2,1,0:T(8,128)S(1)}, f32[4,64,128]{2,1,0:T(8,128)S(1)}, u32[]{:S(2)}, u32[]{:S(2)}) collective-permute-start(f32[4,64,128]{2,1,0:T(8,128)S(1)} %carry.35), channel_id=1, source_target_pairs={{0,2},{1,0},{2,4},{3,1},{4,6},{5,3},{6,7},{7,5},{8,10},{9,8},{10,1... | collective-permute-start | bytes 393224 | tf_op jit(solution)/shard_map/ppermute | solution.py:307
  37.0 1.3 %collective-permute-start.9 = (f32[2,64,128]{2,1,0:T(8,128)S(1)}, f32[2,64,128]{2,1,0:T(8,128)S(1)}, u32[]{:S(2)}, u32[]{:S(2)}) collective-permute-start(f32[2,64,128]{2,1,0:T(8,128)S(1)} %cross.8), channel_id=1, source_target_pairs={{0,1},{1,0},{2,3},{3,2},{4,5},{5,4},{6,7},{7,6},{8,9},{9,8},{10,11... | collective-permute-start | bytes 196616 | tf_op jit(solution)/shard_map/ppermute | solution.py:317
  37.1 1.4 %collective-permute-start.13 = (f32[2,64,128]{2,1,0:T(8,128)S(1)}, f32[2,64,128]{2,1,0:T(8,128)S(1)}, u32[]{:S(2)}, u32[]{:S(2)}) collective-permute-start(f32[2,64,128]{2,1,0:T(8,128)S(1)} %cross.9), channel_id=1, source_target_pairs={{0,1},{1,0},{2,3},{3,2},{4,5},{5,4},{6,7},{7,6},{8,9},{9,8},{10,11... | collective-permute-start | bytes 196616 | tf_op jit(solution)/shard_map/ppermute | solution.py:317
  38.6 2.1 %collective-permute-start.19 = (f32[2,64,128]{2,1,0:T(8,128)S(1)}, f32[2,64,128]{2,1,0:T(8,128)S(1)}, u32[]{:S(2)}, u32[]{:S(2)}) collective-permute-start(f32[2,64,128]{2,1,0:T(8,128)S(1)} %cross.10), channel_id=1, source_target_pairs={{0,1},{1,0},{2,3},{3,2},{4,5},{5,4},{6,7},{7,6},{8,9},{9,8},{10,11... | collective-permute-start | bytes 196616 | tf_op jit(solution)/shard_map/ppermute | solution.py:317
  39.6 1.3 %collective-permute-start.23 = (f32[2,64,128]{2,1,0:T(8,128)S(1)}, f32[2,64,128]{2,1,0:T(8,128)S(1)}, u32[]{:S(2)}, u32[]{:S(2)}) collective-permute-start(f32[2,64,128]{2,1,0:T(8,128)S(1)} %cross.11), channel_id=1, source_target_pairs={{0,1},{1,0},{2,3},{3,2},{4,5},{5,4},{6,7},{7,6},{8,9},{9,8},{10,11... | collective-permute-start | bytes 196616 | tf_op jit(solution)/shard_map/ppermute | solution.py:317
  39.8 6.0 %collective-permute-start.14 = (f32[4,64,128]{2,1,0:T(8,128)S(1)}, f32[4,64,128]{2,1,0:T(8,128)S(1)}, u32[]{:S(2)}, u32[]{:S(2)}) collective-permute-start(f32[4,64,128]{2,1,0:T(8,128)S(1)} %finish.3.rest_0_), channel_id=1, source_target_pairs={{8,0},{0,8},{24,16},{16,24},{9,1},{1,9},{25,17},{17,25},{10,2},{2,... | collective-permute-start | bytes 393224 | tf_op jit(solution)/shard_map/ppermute | solution.py:269
  41.0 6.5 %collective-permute-start.24 = (f32[4,64,128]{2,1,0:T(8,128)S(1)}, f32[4,64,128]{2,1,0:T(8,128)S(1)}, u32[]{:S(2)}, u32[]{:S(2)}) collective-permute-start(f32[4,64,128]{2,1,0:T(8,128)S(1)} %finish.4.rest_1_), channel_id=1, source_target_pairs={{16,0},{24,8},{0,16},{8,24},{17,1},{25,9},{1,17},{9,25},{18,2},{26... | collective-permute-start | bytes 393224 | tf_op jit(solution)/shard_map/ppermute | solution.py:269
  42.6 7.6 %collective-permute-start.27 = (f32[4,64,128]{2,1,0:T(8,128)S(1)}, f32[4,64,128]{2,1,0:T(8,128)S(1)}, u32[]{:S(2)}, u32[]{:S(2)}) collective-permute-start(f32[4,64,128]{2,1,0:T(8,128)S(1)} %finish.3.rest_0_), channel_id=1, source_target_pairs={{16,0},{24,8},{0,16},{8,24},{17,1},{25,9},{1,17},{9,25},{18,2},{26... | collective-permute-start | bytes 393224 | tf_op jit(solution)/shard_map/ppermute | solution.py:269
  43.1 7.1 %collective-permute-start.26 = (f32[4,64,128]{2,1,0:T(8,128)S(1)}, f32[4,64,128]{2,1,0:T(8,128)S(1)}, u32[]{:S(2)}, u32[]{:S(2)}) collective-permute-start(f32[4,64,128]{2,1,0:T(8,128)S(1)} %finish.4.rest_1_), channel_id=1, source_target_pairs={{8,0},{0,8},{24,16},{16,24},{9,1},{1,9},{25,17},{17,25},{10,2},{2,... | collective-permute-start | bytes 393224 | tf_op jit(solution)/shard_map/ppermute | solution.py:269
  45.9 6.4 %collective-permute-start.15 = (f32[4,64,128]{2,1,0:T(8,128)S(1)}, f32[4,64,128]{2,1,0:T(8,128)S(1)}, u32[]{:S(2)}, u32[]{:S(2)}) collective-permute-start(f32[4,64,128]{2,1,0:T(8,128)S(1)} %cut.9), channel_id=1, source_target_pairs={{16,0},{24,8},{0,16},{8,24},{17,1},{25,9},{1,17},{9,25},{18,2},{26... | collective-permute-start | bytes 393224 | tf_op jit(solution)/shard_map/ppermute | solution.py:269
  47.5 5.0 %collective-permute-start.25 = (f32[4,64,128]{2,1,0:T(8,128)S(1)}, f32[4,64,128]{2,1,0:T(8,128)S(1)}, u32[]{:S(2)}, u32[]{:S(2)}) collective-permute-start(f32[4,64,128]{2,1,0:T(8,128)S(1)} %cut.10), channel_id=1, source_target_pairs={{8,0},{0,8},{24,16},{16,24},{9,1},{1,9},{25,17},{17,25},{10,2},{2,... | collective-permute-start | bytes 393224 | tf_op jit(solution)/shard_map/ppermute | solution.py:269
  53.1 2.0 %collective-permute-start.28 = (f32[16,64,128]{2,1,0:T(8,128)S(1)}, f32[16,64,128]{2,1,0:T(8,128)S(1)}, u32[]{:S(2)}, u32[]{:S(2)}) collective-permute-start(f32[16,64,128]{2,1,0:T(8,128)S(1)} %slice.19), channel_id=1, source_target_pairs={{0,1},{1,0},{2,3},{3,2},{4,5},{5,4},{6,7},{7,6},{8,9},{9,8},{10,11... | collective-permute-start | bytes 1572872 | tf_op jit(solution)/shard_map/ppermute | solution.py:292
  55.2 5.2 %collective-permute-start.29 = (f32[48,64,128]{2,1,0:T(8,128)S(1)}, f32[48,64,128]{2,1,0:T(8,128)S(1)}, u32[]{:S(2)}, u32[]{:S(2)}) collective-permute-start(f32[48,64,128]{2,1,0:T(8,128)S(1)} %cut.11), channel_id=1, source_target_pairs={{0,1},{1,0},{2,3},{3,2},{4,5},{5,4},{6,7},{7,6},{8,9},{9,8},{10,11... | collective-permute-start | bytes 4718600 | tf_op jit(solution)/shard_map/ppermute | solution.py:300
  55.4 5.0 %collective-permute-start.30 = (f32[4,64,128]{2,1,0:T(8,128)S(1)}, f32[4,64,128]{2,1,0:T(8,128)S(1)}, u32[]{:S(2)}, u32[]{:S(2)}) collective-permute-start(f32[4,64,128]{2,1,0:T(8,128)S(1)} %carry.36.rest_0_), channel_id=1, source_target_pairs={{0,2},{1,0},{2,3},{3,1},{4,6},{5,4},{6,7},{7,5},{8,10},{9,8},{10,1... | collective-permute-start | bytes 393224 | tf_op jit(solution)/shard_map/ppermute | solution.py:303
  57.9 5.0 %collective-permute-start.34 = (f32[4,64,128]{2,1,0:T(8,128)S(1)}, f32[4,64,128]{2,1,0:T(8,128)S(1)}, u32[]{:S(2)}, u32[]{:S(2)}) collective-permute-start(f32[4,64,128]{2,1,0:T(8,128)S(1)} %carry.37.rest_1_), channel_id=1, source_target_pairs={{0,2},{1,0},{2,3},{3,1},{4,6},{5,4},{6,7},{7,5},{8,10},{9,8},{10,1... | collective-permute-start | bytes 393224 | tf_op jit(solution)/shard_map/ppermute | solution.py:303
  58.3 6.1 %collective-permute-start.38 = (f32[4,64,128]{2,1,0:T(8,128)S(1)}, f32[4,64,128]{2,1,0:T(8,128)S(1)}, u32[]{:S(2)}, u32[]{:S(2)}) collective-permute-start(f32[4,64,128]{2,1,0:T(8,128)S(1)} %carry.38.rest_2_), channel_id=1, source_target_pairs={{0,2},{1,0},{2,3},{3,1},{4,6},{5,4},{6,7},{7,5},{8,10},{9,8},{10,1... | collective-permute-start | bytes 393224 | tf_op jit(solution)/shard_map/ppermute | solution.py:303
  58.4 7.9 %collective-permute-start.42 = (f32[4,64,128]{2,1,0:T(8,128)S(1)}, f32[4,64,128]{2,1,0:T(8,128)S(1)}, u32[]{:S(2)}, u32[]{:S(2)}) collective-permute-start(f32[4,64,128]{2,1,0:T(8,128)S(1)} %carry.39.rest_3_), channel_id=1, source_target_pairs={{0,2},{1,0},{2,3},{3,1},{4,6},{5,4},{6,7},{7,5},{8,10},{9,8},{10,1... | collective-permute-start | bytes 393224 | tf_op jit(solution)/shard_map/ppermute | solution.py:303
  60.5 7.1 %collective-permute-start.31 = (f32[4,64,128]{2,1,0:T(8,128)S(1)}, f32[4,64,128]{2,1,0:T(8,128)S(1)}, u32[]{:S(2)}, u32[]{:S(2)}) collective-permute-start(f32[4,64,128]{2,1,0:T(8,128)S(1)} %carry.40), channel_id=1, source_target_pairs={{0,2},{1,0},{2,4},{3,1},{4,6},{5,3},{6,7},{7,5},{8,10},{9,8},{10,1... | collective-permute-start | bytes 393224 | tf_op jit(solution)/shard_map/ppermute | solution.py:307
  63.0 6.0 %collective-permute-start.35 = (f32[4,64,128]{2,1,0:T(8,128)S(1)}, f32[4,64,128]{2,1,0:T(8,128)S(1)}, u32[]{:S(2)}, u32[]{:S(2)}) collective-permute-start(f32[4,64,128]{2,1,0:T(8,128)S(1)} %carry.42), channel_id=1, source_target_pairs={{0,2},{1,0},{2,4},{3,1},{4,6},{5,3},{6,7},{7,5},{8,10},{9,8},{10,1... | collective-permute-start | bytes 393224 | tf_op jit(solution)/shard_map/ppermute | solution.py:307
  64.4 6.0 %collective-permute-start.39 = (f32[4,64,128]{2,1,0:T(8,128)S(1)}, f32[4,64,128]{2,1,0:T(8,128)S(1)}, u32[]{:S(2)}, u32[]{:S(2)}) collective-permute-start(f32[4,64,128]{2,1,0:T(8,128)S(1)} %carry.44), channel_id=1, source_target_pairs={{0,2},{1,0},{2,4},{3,1},{4,6},{5,3},{6,7},{7,5},{8,10},{9,8},{10,1... | collective-permute-start | bytes 393224 | tf_op jit(solution)/shard_map/ppermute | solution.py:307
  66.3 5.6 %collective-permute-start.43 = (f32[4,64,128]{2,1,0:T(8,128)S(1)}, f32[4,64,128]{2,1,0:T(8,128)S(1)}, u32[]{:S(2)}, u32[]{:S(2)}) collective-permute-start(f32[4,64,128]{2,1,0:T(8,128)S(1)} %carry.46), channel_id=1, source_target_pairs={{0,2},{1,0},{2,4},{3,1},{4,6},{5,3},{6,7},{7,5},{8,10},{9,8},{10,1... | collective-permute-start | bytes 393224 | tf_op jit(solution)/shard_map/ppermute | solution.py:307
  67.7 5.6 %collective-permute-start.32 = (f32[4,64,128]{2,1,0:T(8,128)S(1)}, f32[4,64,128]{2,1,0:T(8,128)S(1)}, u32[]{:S(2)}, u32[]{:S(2)}) collective-permute-start(f32[4,64,128]{2,1,0:T(8,128)S(1)} %carry.41), channel_id=1, source_target_pairs={{0,2},{1,0},{2,4},{3,1},{4,6},{5,3},{6,7},{7,5},{8,10},{9,8},{10,1... | collective-permute-start | bytes 393224 | tf_op jit(solution)/shard_map/ppermute | solution.py:307
  69.1 4.3 %collective-permute-start.36 = (f32[4,64,128]{2,1,0:T(8,128)S(1)}, f32[4,64,128]{2,1,0:T(8,128)S(1)}, u32[]{:S(2)}, u32[]{:S(2)}) collective-permute-start(f32[4,64,128]{2,1,0:T(8,128)S(1)} %carry.43), channel_id=1, source_target_pairs={{0,2},{1,0},{2,4},{3,1},{4,6},{5,3},{6,7},{7,5},{8,10},{9,8},{10,1... | collective-permute-start | bytes 393224 | tf_op jit(solution)/shard_map/ppermute | solution.py:307
  70.5 4.0 %collective-permute-start.40 = (f32[4,64,128]{2,1,0:T(8,128)S(1)}, f32[4,64,128]{2,1,0:T(8,128)S(1)}, u32[]{:S(2)}, u32[]{:S(2)}) collective-permute-start(f32[4,64,128]{2,1,0:T(8,128)S(1)} %carry.45), channel_id=1, source_target_pairs={{0,2},{1,0},{2,4},{3,1},{4,6},{5,3},{6,7},{7,5},{8,10},{9,8},{10,1... | collective-permute-start | bytes 393224 | tf_op jit(solution)/shard_map/ppermute | solution.py:307
  71.9 4.0 %collective-permute-start.44 = (f32[4,64,128]{2,1,0:T(8,128)S(1)}, f32[4,64,128]{2,1,0:T(8,128)S(1)}, u32[]{:S(2)}, u32[]{:S(2)}) collective-permute-start(f32[4,64,128]{2,1,0:T(8,128)S(1)} %carry.47), channel_id=1, source_target_pairs={{0,2},{1,0},{2,4},{3,1},{4,6},{5,3},{6,7},{7,5},{8,10},{9,8},{10,1... | collective-permute-start | bytes 393224 | tf_op jit(solution)/shard_map/ppermute | solution.py:307
  73.3 2.7 %collective-permute-start.33 = (f32[2,64,128]{2,1,0:T(8,128)S(1)}, f32[2,64,128]{2,1,0:T(8,128)S(1)}, u32[]{:S(2)}, u32[]{:S(2)}) collective-permute-start(f32[2,64,128]{2,1,0:T(8,128)S(1)} %cross.12), channel_id=1, source_target_pairs={{0,1},{1,0},{2,3},{3,2},{4,5},{5,4},{6,7},{7,6},{8,9},{9,8},{10,11... | collective-permute-start | bytes 196616 | tf_op jit(solution)/shard_map/ppermute | solution.py:317
  73.4 2.6 %collective-permute-start.37 = (f32[2,64,128]{2,1,0:T(8,128)S(1)}, f32[2,64,128]{2,1,0:T(8,128)S(1)}, u32[]{:S(2)}, u32[]{:S(2)}) collective-permute-start(f32[2,64,128]{2,1,0:T(8,128)S(1)} %cross.13), channel_id=1, source_target_pairs={{0,1},{1,0},{2,3},{3,2},{4,5},{5,4},{6,7},{7,6},{8,9},{9,8},{10,11... | collective-permute-start | bytes 196616 | tf_op jit(solution)/shard_map/ppermute | solution.py:317
  74.5 1.5 %collective-permute-start.41 = (f32[2,64,128]{2,1,0:T(8,128)S(1)}, f32[2,64,128]{2,1,0:T(8,128)S(1)}, u32[]{:S(2)}, u32[]{:S(2)}) collective-permute-start(f32[2,64,128]{2,1,0:T(8,128)S(1)} %cross.14), channel_id=1, source_target_pairs={{0,1},{1,0},{2,3},{3,2},{4,5},{5,4},{6,7},{7,6},{8,9},{9,8},{10,11... | collective-permute-start | bytes 196616 | tf_op jit(solution)/shard_map/ppermute | solution.py:317
  75.9 1.3 %collective-permute-start.45 = (f32[2,64,128]{2,1,0:T(8,128)S(1)}, f32[2,64,128]{2,1,0:T(8,128)S(1)}, u32[]{:S(2)}, u32[]{:S(2)}) collective-permute-start(f32[2,64,128]{2,1,0:T(8,128)S(1)} %cross.15), channel_id=1, source_target_pairs={{0,1},{1,0},{2,3},{3,2},{4,5},{5,4},{6,7},{7,6},{8,9},{9,8},{10,11... | collective-permute-start | bytes 196616 | tf_op jit(solution)/shard_map/ppermute | solution.py:317

commit v8 on v7

--- a/solution.py
+++ b/solution.py
@@ -120,6 +120,9 @@
             out_ref[targets[u]] += results[u]
         return carry
 
+    huge = (last - first) // (2 * GROUP)
+    lax.fori_loop(0, huge, functools.partial(step, size=2 * GROUP, first=first), 0)
+    first += huge * 2 * GROUP
     large = (last - first + GROUP // 2 - 1) // GROUP
     lax.fori_loop(0, large, functools.partial(step, size=GROUP, first=first), 0)
     rest_first = first + large * GROUP
@@ -164,7 +167,7 @@
 
 def first_of_line():
     me, n = lax.axis_index("col"), lax.axis_size("col")
-    return jnp.where(me % 2 == 0, me == 0, me == n - 1)
+    return jnp.where(me & 1 == 0, me == 0, me == n - 1)
 
 
 def small_call(kernel, out_bricks, name, *args, after=()):
@@ -218,7 +221,7 @@
 
 
 def sums_at(h, distance, pairs, half):
-    order = (distance + pairs - 1) % pairs if pairs > 1 else distance
+    order = lax.rem(distance + pairs - 1, pairs) if pairs > 1 else distance
     size = 2 * half
     return jnp.where(order == 0, h * size, (PARTS + h * (pairs - 1) + order - 1) * size)
 
@@ -226,15 +229,15 @@
 def make_plan(row_index, col_index, live, bricks, n_row, n_col, flips):
     pairs, half = n_col // 2, bricks // PARTS
     my_row, me = lax.axis_index("row"), lax.axis_index("col")
-    my_pair, my_side = me // 2, me % 2
-    column, brick = row_index // bricks, row_index % bricks
-    pair, side = column // 2, column % 2
-    ahead = jnp.where(my_side == 0, pair - my_pair, my_pair - pair) % pairs
+    my_pair, my_side = me >> 1, me & 1
+    column, brick = lax.div(row_index, bricks), lax.rem(row_index, bricks)
+    pair, side = column >> 1, column & 1
+    ahead = lax.rem(jnp.where(my_side == 0, pair - my_pair, my_pair - pair) + pairs, pairs)
     carrier = jnp.where(pair > my_pair, 0, jnp.where(pair < my_pair, 1, my_side))
-    place = sums_at(brick // half, ahead, pairs, half) + (side ^ carrier) * half + brick % half
-
-    from_row, from_brick = col_index // bricks, col_index % bricks
-    turn = from_row ^ my_row if flips else (from_row - my_row) % n_row
+    place = sums_at(lax.div(brick, half), ahead, pairs, half) + (side ^ carrier) * half + lax.rem(brick, half)
+
+    from_row, from_brick = lax.div(col_index, bricks), lax.rem(col_index, bricks)
+    turn = from_row ^ my_row if flips else lax.rem(from_row - my_row + n_row, n_row)
     sender = turn * bricks + from_brick
 
     n = row_index.shape[0]

time: 78.1 us -> 77.9 us (level)
  Pallas kernels: 14.7 us -> 11.9 us
  waiting for transfers between devices: 14.8 us -> 16.5 us
  starting transfers between devices: 45 us -> 46.6 us
    pallas_call x7, Pallas kernels: 7.85 us -> 5.08 us  [transfer(): pl.pallas_call(functools.partial(transfer_kernel, fields_at, begin, end,...]
    ppermute x10, starting transfers between devices: 12.4 us -> 14.1 us  [from_turn(): lax.ppermute(value, 'row', [(i ^ k if flips else (i + k) % n_row, i) for...]
    ppermute x10, waiting for transfers between devices: 4.26 us -> 5.13 us  [from_turn(): lax.ppermute(value, 'row', [(i ^ k if flips else (i + k) % n_row, i) for...]
    ppermute x2, waiting for transfers between devices: 1.87 us -> 2.71 us  [scatter(): first = lax.ppermute(lead[:leading], 'col', swap)]
  transfers between devices with their start and end apart: 46 -> 46, of which waited for: 17 -> 18; matrix products, arithmetic and copies ran while one was open for 3% -> 2% of each run, Pallas kernels for 16% -> 13%
where the time goes in v8:
time: 77.9 us; the launch traced here: 77.6 us
  starting transfers between devices  46.6 us (60%)
  waiting for transfers between devices  16.5 us (21%)
  Pallas kernels  11.9 us (15%)
  other arithmetic  1.39 us (2%)
  between operations  1.15 us (1%)
    ppermute x16, starting transfers between devices, scatter(): came = lax.ppermute(total, 'col', ring)  25 us
    ppermute x10, starting transfers between devices, from_turn(): lax.ppermute(value, 'row', [(i ^ k if flips else (i + k) % n_row, i) for...  14.1 us
    ppermute x10, waiting for transfers between devices, from_turn(): lax.ppermute(value, 'row', [(i ^ k if flips else (i + k) % n_row, i) for...  5.13 us
    ppermute x8, starting transfers between devices, scatter(): came = lax.ppermute(totals[h], 'col', squares)  5.08 us
    pallas_call x7, Pallas kernels, transfer(): pl.pallas_call(functools.partial(transfer_kernel, fields_at, begin, end,...  5.08 us
    pallas_call x1, Pallas kernels, prepare(): pl.pallas_call(prepare_kernel, in_specs=[pl.BlockSpec(memory_space=pltpu....  4.48 us
    ppermute x8, waiting for transfers between devices, scatter(): came = lax.ppermute(totals[h], 'col', squares)  4.05 us
    ppermute x2, waiting for transfers between devices, scatter(): first = lax.ppermute(lead[:leading], 'col', swap)  2.71 us
  transfers between devices with their start and end apart: 46, of which 18 were waited for; matrix products, arithmetic and copies ran while one was open for 2% of the time, Pallas kernels for 13%

profile of v8, /device:TPU:0, one launch (start us, length us, event | category | flops | bytes accessed | tf_op | source)
XLA Modules:
  0.0 77.6 jit_solution(8068638169411411332)
XLA Ops:
  0.0 3.0 %collective-permute-start.2 = (f32[8,64,128]{2,1,0:T(8,128)}, f32[8,64,128]{2,1,0:T(8,128)S(1)}, u32[]{:S(2)}, u32[]{:S(2)}) collective-permute-start(f32[8,64,128]{2,1,0:T(8,128)} %source_ref.5), channel_id=1, source_target_pairs={{16,0},{24,8},{0,16},{8,24},{17,1},{25,9},{1,17},{9,25},{18,2},{26... | collective-permute-start | bytes 786440 | tf_op jit(solution)/shard_map/ppermute | solution.py:272
  3.0 1.5 %collective-permute-start = (f32[8,64,128]{2,1,0:T(8,128)}, f32[8,64,128]{2,1,0:T(8,128)S(1)}, u32[]{:S(2)}, u32[]{:S(2)}) collective-permute-start(f32[8,64,128]{2,1,0:T(8,128)} %source_ref.5), channel_id=1, source_target_pairs={{8,0},{0,8},{24,16},{16,24},{9,1},{1,9},{25,17},{17,25},{10,2},{2,... | collective-permute-start | bytes 786440 | tf_op jit(solution)/shard_map/ppermute | solution.py:272
  5.1 0.7 iota_add_fusion
  5.8 4.5 %prepare.1.rest_0_.a_ref = bf16[257,64,128]{2,1,0:T(8,128)(2,1)S(1)} custom-call(f32[64,64,256]{2,1,0:T(8,128)} %bitcast.3), custom_call_target="tpu_custom_call" | custom-call | bytes 25165824 | tf_op jit(solution)/shard_map/prepare/pallas_call | solution.py:69
  11.5 1.6 %collective-permute-start.3 = (f32[4,64,128]{2,1,0:T(8,128)S(1)}, f32[4,64,128]{2,1,0:T(8,128)S(1)}, u32[]{:S(2)}, u32[]{:S(2)}) collective-permute-start(f32[4,64,128]{2,1,0:T(8,128)S(1)} %cut.7), channel_id=1, source_target_pairs={{8,0},{0,8},{24,16},{16,24},{9,1},{1,9},{25,17},{17,25},{10,2},{2,... | collective-permute-start | bytes 393224 | tf_op jit(solution)/shard_map/ppermute | solution.py:272
  13.2 0.6 keep.1.plan_ref
  13.9 1.2 %transfer.7.rest_2_ = f32[64,64,128]{2,1,0:T(8,128)S(1)} custom-call(s32[872]{0:T(1024)S(4)} %keep.1.plan_ref, bf16[257,64,128]{2,1,0:T(8,128)(2,1)S(1)} %prepare.1.rest_0_.a_ref, f32[8,64,128]{2,1,0:T(8,128)S(1)} %copy-done, f32[8,64,128]{2,1,0:T(8,128)S(1)} %collective-permute-done.rest_1_, f32[8,64,128]{2,1,0:T(8,128)S(1)} %collective-permute-done.2.rest_2_), custom_call_target="tpu_custom_call" | custom-call | tf_op jit(solution)/shard_map/transfer/pallas_call | solution.py:138
  15.0 1.0 %collective-permute-done.1.rest_0_ = f32[4,64,128]{2,1,0:T(8,128)S(1)} collective-permute-done((f32[4,64,128]{2,1,0:T(8,128)S(1)}, f32[4,64,128]{2,1,0:T(8,128)S(1)}, u32[]{:S(2)}, u32[]{:S(2)}) %collective-permute-start.1) | collective-permute-done | bytes 131104 | tf_op jit(solution)/shard_map/ppermute | solution.py:272
  17.6 1.4 %collective-permute-done.4.got_ref = f32[16,64,128]{2,1,0:T(8,128)S(1)} collective-permute-done((f32[16,64,128]{2,1,0:T(8,128)S(1)}, f32[16,64,128]{2,1,0:T(8,128)S(1)}, u32[]{:S(2)}, u32[]{:S(2)}) %collective-permute-start.4) | collective-permute-done | bytes 524320 | tf_op jit(solution)/shard_map/ppermute | solution.py:295
  19.4 1.7 %collective-permute-start.6 = (f32[4,64,128]{2,1,0:T(8,128)S(1)}, f32[4,64,128]{2,1,0:T(8,128)S(1)}, u32[]{:S(2)}, u32[]{:S(2)}) collective-permute-start(f32[4,64,128]{2,1,0:T(8,128)S(1)} %carry.24.rest_0_), channel_id=1, source_target_pairs={{0,2},{1,0},{2,3},{3,1},{4,6},{5,4},{6,7},{7,5},{8,10},{9,8},{10,1... | collective-permute-start | bytes 393224 | tf_op jit(solution)/shard_map/ppermute | solution.py:306
  21.7 1.9 %collective-permute-done.6.rest_0_ = f32[4,64,128]{2,1,0:T(8,128)S(1)} collective-permute-done((f32[4,64,128]{2,1,0:T(8,128)S(1)}, f32[4,64,128]{2,1,0:T(8,128)S(1)}, u32[]{:S(2)}, u32[]{:S(2)}) %collective-permute-start.6) | collective-permute-done | bytes 131104 | tf_op jit(solution)/shard_map/ppermute | solution.py:306
  23.6 2.5 %collective-permute-start.7 = (f32[4,64,128]{2,1,0:T(8,128)S(1)}, f32[4,64,128]{2,1,0:T(8,128)S(1)}, u32[]{:S(2)}, u32[]{:S(2)}) collective-permute-start(f32[4,64,128]{2,1,0:T(8,128)S(1)} %carry.28), channel_id=1, source_target_pairs={{0,2},{1,0},{2,4},{3,1},{4,6},{5,3},{6,7},{7,5},{8,10},{9,8},{10,1... | collective-permute-start | bytes 393224 | tf_op jit(solution)/shard_map/ppermute | solution.py:310
  26.1 1.4 %collective-permute-start.11 = (f32[4,64,128]{2,1,0:T(8,128)S(1)}, f32[4,64,128]{2,1,0:T(8,128)S(1)}, u32[]{:S(2)}, u32[]{:S(2)}) collective-permute-start(f32[4,64,128]{2,1,0:T(8,128)S(1)} %carry.30), channel_id=1, source_target_pairs={{0,2},{1,0},{2,4},{3,1},{4,6},{5,3},{6,7},{7,5},{8,10},{9,8},{10,1... | collective-permute-start | bytes 393224 | tf_op jit(solution)/shard_map/ppermute | solution.py:310
  27.5 1.8 %collective-permute-start.17 = (f32[4,64,128]{2,1,0:T(8,128)S(1)}, f32[4,64,128]{2,1,0:T(8,128)S(1)}, u32[]{:S(2)}, u32[]{:S(2)}) collective-permute-start(f32[4,64,128]{2,1,0:T(8,128)S(1)} %carry.32), channel_id=1, source_target_pairs={{0,2},{1,0},{2,4},{3,1},{4,6},{5,3},{6,7},{7,5},{8,10},{9,8},{10,1... | collective-permute-start | bytes 393224 | tf_op jit(solution)/shard_map/ppermute | solution.py:310
  29.4 1.4 %collective-permute-start.21 = (f32[4,64,128]{2,1,0:T(8,128)S(1)}, f32[4,64,128]{2,1,0:T(8,128)S(1)}, u32[]{:S(2)}, u32[]{:S(2)}) collective-permute-start(f32[4,64,128]{2,1,0:T(8,128)S(1)} %carry.34), channel_id=1, source_target_pairs={{0,2},{1,0},{2,4},{3,1},{4,6},{5,3},{6,7},{7,5},{8,10},{9,8},{10,1... | collective-permute-start | bytes 393224 | tf_op jit(solution)/shard_map/ppermute | solution.py:310
  30.8 1.4 %collective-permute-start.8 = (f32[4,64,128]{2,1,0:T(8,128)S(1)}, f32[4,64,128]{2,1,0:T(8,128)S(1)}, u32[]{:S(2)}, u32[]{:S(2)}) collective-permute-start(f32[4,64,128]{2,1,0:T(8,128)S(1)} %carry.29), channel_id=1, source_target_pairs={{0,2},{1,0},{2,4},{3,1},{4,6},{5,3},{6,7},{7,5},{8,10},{9,8},{10,1... | collective-permute-start | bytes 393224 | tf_op jit(solution)/shard_map/ppermute | solution.py:310
  32.2 1.4 %collective-permute-start.12 = (f32[4,64,128]{2,1,0:T(8,128)S(1)}, f32[4,64,128]{2,1,0:T(8,128)S(1)}, u32[]{:S(2)}, u32[]{:S(2)}) collective-permute-start(f32[4,64,128]{2,1,0:T(8,128)S(1)} %carry.31), channel_id=1, source_target_pairs={{0,2},{1,0},{2,4},{3,1},{4,6},{5,3},{6,7},{7,5},{8,10},{9,8},{10,1... | collective-permute-start | bytes 393224 | tf_op jit(solution)/shard_map/ppermute | solution.py:310
  33.6 1.4 %collective-permute-start.18 = (f32[4,64,128]{2,1,0:T(8,128)S(1)}, f32[4,64,128]{2,1,0:T(8,128)S(1)}, u32[]{:S(2)}, u32[]{:S(2)}) collective-permute-start(f32[4,64,128]{2,1,0:T(8,128)S(1)} %carry.33), channel_id=1, source_target_pairs={{0,2},{1,0},{2,4},{3,1},{4,6},{5,3},{6,7},{7,5},{8,10},{9,8},{10,1... | collective-permute-start | bytes 393224 | tf_op jit(solution)/shard_map/ppermute | solution.py:310
  35.0 1.4 %collective-permute-start.22 = (f32[4,64,128]{2,1,0:T(8,128)S(1)}, f32[4,64,128]{2,1,0:T(8,128)S(1)}, u32[]{:S(2)}, u32[]{:S(2)}) collective-permute-start(f32[4,64,128]{2,1,0:T(8,128)S(1)} %carry.35), channel_id=1, source_target_pairs={{0,2},{1,0},{2,4},{3,1},{4,6},{5,3},{6,7},{7,5},{8,10},{9,8},{10,1... | collective-permute-start | bytes 393224 | tf_op jit(solution)/shard_map/ppermute | solution.py:310
  36.5 0.5 collective-permute-start.13
  37.0 0.7 collective-permute-done.9.rest_2_
  38.4 0.6 collective-permute-done.22.came_ref.rest_4_
  39.1 1.6 %collective-permute-start.14 = (f32[4,64,128]{2,1,0:T(8,128)S(1)}, f32[4,64,128]{2,1,0:T(8,128)S(1)}, u32[]{:S(2)}, u32[]{:S(2)}) collective-permute-start(f32[4,64,128]{2,1,0:T(8,128)S(1)} %finish.3.rest_0_), channel_id=1, source_target_pairs={{8,0},{0,8},{24,16},{16,24},{9,1},{1,9},{25,17},{17,25},{10,2},{2,... | collective-permute-start | bytes 393224 | tf_op jit(solution)/shard_map/ppermute | solution.py:272
  40.8 1.6 %collective-permute-start.24 = (f32[4,64,128]{2,1,0:T(8,128)S(1)}, f32[4,64,128]{2,1,0:T(8,128)S(1)}, u32[]{:S(2)}, u32[]{:S(2)}) collective-permute-start(f32[4,64,128]{2,1,0:T(8,128)S(1)} %finish.4.rest_1_), channel_id=1, source_target_pairs={{16,0},{24,8},{0,16},{8,24},{17,1},{25,9},{1,17},{9,25},{18,2},{26... | collective-permute-start | bytes 393224 | tf_op jit(solution)/shard_map/ppermute | solution.py:272
  42.9 1.1 %collective-permute-start.26 = (f32[4,64,128]{2,1,0:T(8,128)S(1)}, f32[4,64,128]{2,1,0:T(8,128)S(1)}, u32[]{:S(2)}, u32[]{:S(2)}) collective-permute-start(f32[4,64,128]{2,1,0:T(8,128)S(1)} %finish.4.rest_1_), channel_id=1, source_target_pairs={{8,0},{0,8},{24,16},{16,24},{9,1},{1,9},{25,17},{17,25},{10,2},{2,... | collective-permute-start | bytes 393224 | tf_op jit(solution)/shard_map/ppermute | solution.py:272
  44.0 0.8 %transfer.10.rest_0_.rest_4_ = f32[64,64,128]{2,1,0:T(8,128)S(1)} custom-call(s32[872]{0:T(1024)S(4)} %keep.1.plan_ref, bf16[257,64,128]{2,1,0:T(8,128)(2,1)S(1)} %prepare.1.rest_0_.a_ref, f32[4,64,128]{2,1,0:T(8,128)S(1)} %finish.3.rest_0_, f32[4,64,128]{2,1,0:T(8,128)S(1)} %finish.4.rest_1_), custom_call_target="tpu_custom_call" | custom-call | tf_op jit(solution)/shard_map/transfer/pallas_call | solution.py:138
  45.0 1.6 %collective-permute-start.15 = (f32[4,64,128]{2,1,0:T(8,128)S(1)}, f32[4,64,128]{2,1,0:T(8,128)S(1)}, u32[]{:S(2)}, u32[]{:S(2)}) collective-permute-start(f32[4,64,128]{2,1,0:T(8,128)S(1)} %cut.9), channel_id=1, source_target_pairs={{16,0},{24,8},{0,16},{8,24},{17,1},{25,9},{1,17},{9,25},{18,2},{26... | collective-permute-start | bytes 393224 | tf_op jit(solution)/shard_map/ppermute | solution.py:272
  46.6 0.6 collective-permute-done.24.value_ref.rest_3_
  47.2 1.2 %collective-permute-start.25 = (f32[4,64,128]{2,1,0:T(8,128)S(1)}, f32[4,64,128]{2,1,0:T(8,128)S(1)}, u32[]{:S(2)}, u32[]{:S(2)}) collective-permute-start(f32[4,64,128]{2,1,0:T(8,128)S(1)} %cut.10), channel_id=1, source_target_pairs={{8,0},{0,8},{24,16},{16,24},{9,1},{1,9},{25,17},{17,25},{10,2},{2,... | collective-permute-start | bytes 393224 | tf_op jit(solution)/shard_map/ppermute | solution.py:272
  48.4 1.6 %collective-permute-done.27.rest_2_ = f32[4,64,128]{2,1,0:T(8,128)S(1)} collective-permute-done((f32[4,64,128]{2,1,0:T(8,128)S(1)}, f32[4,64,128]{2,1,0:T(8,128)S(1)}, u32[]{:S(2)}, u32[]{:S(2)}) %collective-permute-start.27) | collective-permute-done | bytes 131104 | tf_op jit(solution)/shard_map/ppermute | solution.py:272
  50.0 1.0 %transfer.11.rest_2_ = f32[64,64,128]{2,1,0:T(8,128)S(1)} custom-call(s32[872]{0:T(1024)S(4)} %keep.1.plan_ref, bf16[257,64,128]{2,1,0:T(8,128)(2,1)S(1)} %prepare.1.rest_0_.a_ref, f32[4,64,128]{2,1,0:T(8,128)S(1)} %collective-permute-done.14.value_ref.rest_0_, f32[4,64,128]{2,1,0:T(8,128)S(1)} %collective-permute-done.26.rest_1_, ...), custom_call_target="tpu_custom_call" | custom-call | tf_op jit(solution)/shard_map/transfer/pallas_call | solution.py:138
  51.0 1.0 %collective-permute-done.15.rest_0_ = f32[4,64,128]{2,1,0:T(8,128)S(1)} collective-permute-done((f32[4,64,128]{2,1,0:T(8,128)S(1)}, f32[4,64,128]{2,1,0:T(8,128)S(1)}, u32[]{:S(2)}, u32[]{:S(2)}) %collective-permute-start.15) | collective-permute-done | bytes 131104 | tf_op jit(solution)/shard_map/ppermute | solution.py:272
  53.4 1.4 %collective-permute-done.28.got_ref = f32[16,64,128]{2,1,0:T(8,128)S(1)} collective-permute-done((f32[16,64,128]{2,1,0:T(8,128)S(1)}, f32[16,64,128]{2,1,0:T(8,128)S(1)}, u32[]{:S(2)}, u32[]{:S(2)}) %collective-permute-start.28) | collective-permute-done | bytes 524320 | tf_op jit(solution)/shard_map/ppermute | solution.py:295
  55.2 2.4 %collective-permute-start.30 = (f32[4,64,128]{2,1,0:T(8,128)S(1)}, f32[4,64,128]{2,1,0:T(8,128)S(1)}, u32[]{:S(2)}, u32[]{:S(2)}) collective-permute-start(f32[4,64,128]{2,1,0:T(8,128)S(1)} %carry.36.rest_0_), channel_id=1, source_target_pairs={{0,2},{1,0},{2,3},{3,1},{4,6},{5,4},{6,7},{7,5},{8,10},{9,8},{10,1... | collective-permute-start | bytes 393224 | tf_op jit(solution)/shard_map/ppermute | solution.py:306
  58.0 2.1 %collective-permute-done.30.rest_0_ = f32[4,64,128]{2,1,0:T(8,128)S(1)} collective-permute-done((f32[4,64,128]{2,1,0:T(8,128)S(1)}, f32[4,64,128]{2,1,0:T(8,128)S(1)}, u32[]{:S(2)}, u32[]{:S(2)}) %collective-permute-start.30) | collective-permute-done | bytes 131104 | tf_op jit(solution)/shard_map/ppermute | solution.py:306
  60.2 2.5 %collective-permute-start.31 = (f32[4,64,128]{2,1,0:T(8,128)S(1)}, f32[4,64,128]{2,1,0:T(8,128)S(1)}, u32[]{:S(2)}, u32[]{:S(2)}) collective-permute-start(f32[4,64,128]{2,1,0:T(8,128)S(1)} %carry.40), channel_id=1, source_target_pairs={{0,2},{1,0},{2,4},{3,1},{4,6},{5,3},{6,7},{7,5},{8,10},{9,8},{10,1... | collective-permute-start | bytes 393224 | tf_op jit(solution)/shard_map/ppermute | solution.py:310
  62.7 1.4 %collective-permute-start.35 = (f32[4,64,128]{2,1,0:T(8,128)S(1)}, f32[4,64,128]{2,1,0:T(8,128)S(1)}, u32[]{:S(2)}, u32[]{:S(2)}) collective-permute-start(f32[4,64,128]{2,1,0:T(8,128)S(1)} %carry.42), channel_id=1, source_target_pairs={{0,2},{1,0},{2,4},{3,1},{4,6},{5,3},{6,7},{7,5},{8,10},{9,8},{10,1... | collective-permute-start | bytes 393224 | tf_op jit(solution)/shard_map/ppermute | solution.py:310
  64.1 1.8 %collective-permute-start.39 = (f32[4,64,128]{2,1,0:T(8,128)S(1)}, f32[4,64,128]{2,1,0:T(8,128)S(1)}, u32[]{:S(2)}, u32[]{:S(2)}) collective-permute-start(f32[4,64,128]{2,1,0:T(8,128)S(1)} %carry.44), channel_id=1, source_target_pairs={{0,2},{1,0},{2,4},{3,1},{4,6},{5,3},{6,7},{7,5},{8,10},{9,8},{10,1... | collective-permute-start | bytes 393224 | tf_op jit(solution)/shard_map/ppermute | solution.py:310
  65.9 1.4 %collective-permute-start.43 = (f32[4,64,128]{2,1,0:T(8,128)S(1)}, f32[4,64,128]{2,1,0:T(8,128)S(1)}, u32[]{:S(2)}, u32[]{:S(2)}) collective-permute-start(f32[4,64,128]{2,1,0:T(8,128)S(1)} %carry.46), channel_id=1, source_target_pairs={{0,2},{1,0},{2,4},{3,1},{4,6},{5,3},{6,7},{7,5},{8,10},{9,8},{10,1... | collective-permute-start | bytes 393224 | tf_op jit(solution)/shard_map/ppermute | solution.py:310
  67.3 1.4 %collective-permute-start.32 = (f32[4,64,128]{2,1,0:T(8,128)S(1)}, f32[4,64,128]{2,1,0:T(8,128)S(1)}, u32[]{:S(2)}, u32[]{:S(2)}) collective-permute-start(f32[4,64,128]{2,1,0:T(8,128)S(1)} %carry.41), channel_id=1, source_target_pairs={{0,2},{1,0},{2,4},{3,1},{4,6},{5,3},{6,7},{7,5},{8,10},{9,8},{10,1... | collective-permute-start | bytes 393224 | tf_op jit(solution)/shard_map/ppermute | solution.py:310
  68.7 1.4 %collective-permute-start.36 = (f32[4,64,128]{2,1,0:T(8,128)S(1)}, f32[4,64,128]{2,1,0:T(8,128)S(1)}, u32[]{:S(2)}, u32[]{:S(2)}) collective-permute-start(f32[4,64,128]{2,1,0:T(8,128)S(1)} %carry.43), channel_id=1, source_target_pairs={{0,2},{1,0},{2,4},{3,1},{4,6},{5,3},{6,7},{7,5},{8,10},{9,8},{10,1... | collective-permute-start | bytes 393224 | tf_op jit(solution)/shard_map/ppermute | solution.py:310
  70.1 1.4 %collective-permute-start.40 = (f32[4,64,128]{2,1,0:T(8,128)S(1)}, f32[4,64,128]{2,1,0:T(8,128)S(1)}, u32[]{:S(2)}, u32[]{:S(2)}) collective-permute-start(f32[4,64,128]{2,1,0:T(8,128)S(1)} %carry.45), channel_id=1, source_target_pairs={{0,2},{1,0},{2,4},{3,1},{4,6},{5,3},{6,7},{7,5},{8,10},{9,8},{10,1... | collective-permute-start | bytes 393224 | tf_op jit(solution)/shard_map/ppermute | solution.py:310
  71.5 1.4 %collective-permute-start.44 = (f32[4,64,128]{2,1,0:T(8,128)S(1)}, f32[4,64,128]{2,1,0:T(8,128)S(1)}, u32[]{:S(2)}, u32[]{:S(2)}) collective-permute-start(f32[4,64,128]{2,1,0:T(8,128)S(1)} %carry.47), channel_id=1, source_target_pairs={{0,2},{1,0},{2,4},{3,1},{4,6},{5,3},{6,7},{7,5},{8,10},{9,8},{10,1... | collective-permute-start | bytes 393224 | tf_op jit(solution)/shard_map/ppermute | solution.py:310
  73.0 0.5 collective-permute-start.37
  73.6 0.6 collective-permute-done.40.came_ref.rest_7_
  74.2 1.3 %collective-permute-done.44.came_ref.rest_10_ = f32[4,64,128]{2,1,0:T(8,128)S(1)} collective-permute-done((f32[4,64,128]{2,1,0:T(8,128)S(1)}, f32[4,64,128]{2,1,0:T(8,128)S(1)}, u32[]{:S(2)}, u32[]{:S(2)}) %collective-permute-start.44) | collective-permute-done | bytes 131104 | tf_op jit(solution)/shard_map/ppermute | solution.py:310
  75.7 1.2 %collective-permute-done.45.rest_11_ = f32[2,64,128]{2,1,0:T(8,128)S(1)} collective-permute-done((f32[2,64,128]{2,1,0:T(8,128)S(1)}, f32[2,64,128]{2,1,0:T(8,128)S(1)}, u32[]{:S(2)}, u32[]{:S(2)}) %collective-permute-start.45) | collective-permute-done | bytes 65568 | tf_op jit(solution)/shard_map/ppermute | solution.py:320
  76.9 0.8 finish.5
  (105 shorter events, 8.5 us)
Async XLA Ops:
  0.0 10.8 %collective-permute-start.2 = (f32[8,64,128]{2,1,0:T(8,128)}, f32[8,64,128]{2,1,0:T(8,128)S(1)}, u32[]{:S(2)}, u32[]{:S(2)}) collective-permute-start(f32[8,64,128]{2,1,0:T(8,128)} %source_ref.5), channel_id=1, source_target_pairs={{16,0},{24,8},{0,16},{8,24},{17,1},{25,9},{1,17},{9,25},{18,2},{26... | collective-permute-start | bytes 786440 | tf_op jit(solution)/shard_map/ppermute | solution.py:272
  3.0 8.0 %collective-permute-start = (f32[8,64,128]{2,1,0:T(8,128)}, f32[8,64,128]{2,1,0:T(8,128)S(1)}, u32[]{:S(2)}, u32[]{:S(2)}) collective-permute-start(f32[8,64,128]{2,1,0:T(8,128)} %source_ref.5), channel_id=1, source_target_pairs={{8,0},{0,8},{24,16},{16,24},{9,1},{1,9},{25,17},{17,25},{10,2},{2,... | collective-permute-start | bytes 786440 | tf_op jit(solution)/shard_map/ppermute | solution.py:272
  11.0 2.9 %copy-start = (f32[8,64,128]{2,1,0:T(8,128)S(1)}, f32[8,64,128]{2,1,0:T(8,128)}, u32[]{:S(2)}) copy-start(f32[8,64,128]{2,1,0:T(8,128)} %source_ref.5) | copy-start | bytes 786436
  11.0 5.0 %collective-permute-start.1 = (f32[4,64,128]{2,1,0:T(8,128)S(1)}, f32[4,64,128]{2,1,0:T(8,128)S(1)}, u32[]{:S(2)}, u32[]{:S(2)}) collective-permute-start(f32[4,64,128]{2,1,0:T(8,128)S(1)} %cut.6), channel_id=1, source_target_pairs={{16,0},{24,8},{0,16},{8,24},{17,1},{25,9},{1,17},{9,25},{18,2},{26... | collective-permute-start | bytes 393224 | tf_op jit(solution)/shard_map/ppermute | solution.py:272
  11.5 5.0 %collective-permute-start.3 = (f32[4,64,128]{2,1,0:T(8,128)S(1)}, f32[4,64,128]{2,1,0:T(8,128)S(1)}, u32[]{:S(2)}, u32[]{:S(2)}) collective-permute-start(f32[4,64,128]{2,1,0:T(8,128)S(1)} %cut.7), channel_id=1, source_target_pairs={{8,0},{0,8},{24,16},{16,24},{9,1},{1,9},{25,17},{17,25},{10,2},{2,... | collective-permute-start | bytes 393224 | tf_op jit(solution)/shard_map/ppermute | solution.py:272
  17.0 2.0 %collective-permute-start.4 = (f32[16,64,128]{2,1,0:T(8,128)S(1)}, f32[16,64,128]{2,1,0:T(8,128)S(1)}, u32[]{:S(2)}, u32[]{:S(2)}) collective-permute-start(f32[16,64,128]{2,1,0:T(8,128)S(1)} %slice.18), channel_id=1, source_target_pairs={{0,1},{1,0},{2,3},{3,2},{4,5},{5,4},{6,7},{7,6},{8,9},{9,8},{10,11... | collective-permute-start | bytes 1572872 | tf_op jit(solution)/shard_map/ppermute | solution.py:295
  19.2 4.4 %collective-permute-start.5 = (f32[48,64,128]{2,1,0:T(8,128)S(1)}, f32[48,64,128]{2,1,0:T(8,128)S(1)}, u32[]{:S(2)}, u32[]{:S(2)}) collective-permute-start(f32[48,64,128]{2,1,0:T(8,128)S(1)} %cut.8), channel_id=1, source_target_pairs={{0,1},{1,0},{2,3},{3,2},{4,5},{5,4},{6,7},{7,6},{8,9},{9,8},{10,11... | collective-permute-start | bytes 4718600 | tf_op jit(solution)/shard_map/ppermute | solution.py:303
  19.4 4.2 %collective-permute-start.6 = (f32[4,64,128]{2,1,0:T(8,128)S(1)}, f32[4,64,128]{2,1,0:T(8,128)S(1)}, u32[]{:S(2)}, u32[]{:S(2)}) collective-permute-start(f32[4,64,128]{2,1,0:T(8,128)S(1)} %carry.24.rest_0_), channel_id=1, source_target_pairs={{0,2},{1,0},{2,3},{3,1},{4,6},{5,4},{6,7},{7,5},{8,10},{9,8},{10,1... | collective-permute-start | bytes 393224 | tf_op jit(solution)/shard_map/ppermute | solution.py:306
  21.1 5.0 %collective-permute-start.10 = (f32[4,64,128]{2,1,0:T(8,128)S(1)}, f32[4,64,128]{2,1,0:T(8,128)S(1)}, u32[]{:S(2)}, u32[]{:S(2)}) collective-permute-start(f32[4,64,128]{2,1,0:T(8,128)S(1)} %carry.25.rest_1_), channel_id=1, source_target_pairs={{0,2},{1,0},{2,3},{3,1},{4,6},{5,4},{6,7},{7,5},{8,10},{9,8},{10,1... | collective-permute-start | bytes 393224 | tf_op jit(solution)/shard_map/ppermute | solution.py:306
  21.4 6.0 %collective-permute-start.16 = (f32[4,64,128]{2,1,0:T(8,128)S(1)}, f32[4,64,128]{2,1,0:T(8,128)S(1)}, u32[]{:S(2)}, u32[]{:S(2)}) collective-permute-start(f32[4,64,128]{2,1,0:T(8,128)S(1)} %carry.26.rest_2_), channel_id=1, source_target_pairs={{0,2},{1,0},{2,3},{3,1},{4,6},{5,4},{6,7},{7,5},{8,10},{9,8},{10,1... | collective-permute-start | bytes 393224 | tf_op jit(solution)/shard_map/ppermute | solution.py:306
  21.5 7.8 %collective-permute-start.20 = (f32[4,64,128]{2,1,0:T(8,128)S(1)}, f32[4,64,128]{2,1,0:T(8,128)S(1)}, u32[]{:S(2)}, u32[]{:S(2)}) collective-permute-start(f32[4,64,128]{2,1,0:T(8,128)S(1)} %carry.27.rest_3_), channel_id=1, source_target_pairs={{0,2},{1,0},{2,3},{3,1},{4,6},{5,4},{6,7},{7,5},{8,10},{9,8},{10,1... | collective-permute-start | bytes 393224 | tf_op jit(solution)/shard_map/ppermute | solution.py:306
  23.6 7.1 %collective-permute-start.7 = (f32[4,64,128]{2,1,0:T(8,128)S(1)}, f32[4,64,128]{2,1,0:T(8,128)S(1)}, u32[]{:S(2)}, u32[]{:S(2)}) collective-permute-start(f32[4,64,128]{2,1,0:T(8,128)S(1)} %carry.28), channel_id=1, source_target_pairs={{0,2},{1,0},{2,4},{3,1},{4,6},{5,3},{6,7},{7,5},{8,10},{9,8},{10,1... | collective-permute-start | bytes 393224 | tf_op jit(solution)/shard_map/ppermute | solution.py:310
  26.1 6.0 %collective-permute-start.11 = (f32[4,64,128]{2,1,0:T(8,128)S(1)}, f32[4,64,128]{2,1,0:T(8,128)S(1)}, u32[]{:S(2)}, u32[]{:S(2)}) collective-permute-start(f32[4,64,128]{2,1,0:T(8,128)S(1)} %carry.30), channel_id=1, source_target_pairs={{0,2},{1,0},{2,4},{3,1},{4,6},{5,3},{6,7},{7,5},{8,10},{9,8},{10,1... | collective-permute-start | bytes 393224 | tf_op jit(solution)/shard_map/ppermute | solution.py:310
  27.5 6.0 %collective-permute-start.17 = (f32[4,64,128]{2,1,0:T(8,128)S(1)}, f32[4,64,128]{2,1,0:T(8,128)S(1)}, u32[]{:S(2)}, u32[]{:S(2)}) collective-permute-start(f32[4,64,128]{2,1,0:T(8,128)S(1)} %carry.32), channel_id=1, source_target_pairs={{0,2},{1,0},{2,4},{3,1},{4,6},{5,3},{6,7},{7,5},{8,10},{9,8},{10,1... | collective-permute-start | bytes 393224 | tf_op jit(solution)/shard_map/ppermute | solution.py:310
  29.4 5.6 %collective-permute-start.21 = (f32[4,64,128]{2,1,0:T(8,128)S(1)}, f32[4,64,128]{2,1,0:T(8,128)S(1)}, u32[]{:S(2)}, u32[]{:S(2)}) collective-permute-start(f32[4,64,128]{2,1,0:T(8,128)S(1)} %carry.34), channel_id=1, source_target_pairs={{0,2},{1,0},{2,4},{3,1},{4,6},{5,3},{6,7},{7,5},{8,10},{9,8},{10,1... | collective-permute-start | bytes 393224 | tf_op jit(solution)/shard_map/ppermute | solution.py:310
  30.8 5.6 %collective-permute-start.8 = (f32[4,64,128]{2,1,0:T(8,128)S(1)}, f32[4,64,128]{2,1,0:T(8,128)S(1)}, u32[]{:S(2)}, u32[]{:S(2)}) collective-permute-start(f32[4,64,128]{2,1,0:T(8,128)S(1)} %carry.29), channel_id=1, source_target_pairs={{0,2},{1,0},{2,4},{3,1},{4,6},{5,3},{6,7},{7,5},{8,10},{9,8},{10,1... | collective-permute-start | bytes 393224 | tf_op jit(solution)/shard_map/ppermute | solution.py:310
  32.2 4.3 %collective-permute-start.12 = (f32[4,64,128]{2,1,0:T(8,128)S(1)}, f32[4,64,128]{2,1,0:T(8,128)S(1)}, u32[]{:S(2)}, u32[]{:S(2)}) collective-permute-start(f32[4,64,128]{2,1,0:T(8,128)S(1)} %carry.31), channel_id=1, source_target_pairs={{0,2},{1,0},{2,4},{3,1},{4,6},{5,3},{6,7},{7,5},{8,10},{9,8},{10,1... | collective-permute-start | bytes 393224 | tf_op jit(solution)/shard_map/ppermute | solution.py:310
  33.6 4.4 %collective-permute-start.18 = (f32[4,64,128]{2,1,0:T(8,128)S(1)}, f32[4,64,128]{2,1,0:T(8,128)S(1)}, u32[]{:S(2)}, u32[]{:S(2)}) collective-permute-start(f32[4,64,128]{2,1,0:T(8,128)S(1)} %carry.33), channel_id=1, source_target_pairs={{0,2},{1,0},{2,4},{3,1},{4,6},{5,3},{6,7},{7,5},{8,10},{9,8},{10,1... | collective-permute-start | bytes 393224 | tf_op jit(solution)/shard_map/ppermute | solution.py:310
  35.0 4.0 %collective-permute-start.22 = (f32[4,64,128]{2,1,0:T(8,128)S(1)}, f32[4,64,128]{2,1,0:T(8,128)S(1)}, u32[]{:S(2)}, u32[]{:S(2)}) collective-permute-start(f32[4,64,128]{2,1,0:T(8,128)S(1)} %carry.35), channel_id=1, source_target_pairs={{0,2},{1,0},{2,4},{3,1},{4,6},{5,3},{6,7},{7,5},{8,10},{9,8},{10,1... | collective-permute-start | bytes 393224 | tf_op jit(solution)/shard_map/ppermute | solution.py:310
  36.4 1.3 %collective-permute-start.9 = (f32[2,64,128]{2,1,0:T(8,128)S(1)}, f32[2,64,128]{2,1,0:T(8,128)S(1)}, u32[]{:S(2)}, u32[]{:S(2)}) collective-permute-start(f32[2,64,128]{2,1,0:T(8,128)S(1)} %cross.8), channel_id=1, source_target_pairs={{0,1},{1,0},{2,3},{3,2},{4,5},{5,4},{6,7},{7,6},{8,9},{9,8},{10,11... | collective-permute-start | bytes 196616 | tf_op jit(solution)/shard_map/ppermute | solution.py:320
  36.5 1.4 %collective-permute-start.13 = (f32[2,64,128]{2,1,0:T(8,128)S(1)}, f32[2,64,128]{2,1,0:T(8,128)S(1)}, u32[]{:S(2)}, u32[]{:S(2)}) collective-permute-start(f32[2,64,128]{2,1,0:T(8,128)S(1)} %cross.9), channel_id=1, source_target_pairs={{0,1},{1,0},{2,3},{3,2},{4,5},{5,4},{6,7},{7,6},{8,9},{9,8},{10,11... | collective-permute-start | bytes 196616 | tf_op jit(solution)/shard_map/ppermute | solution.py:320
  38.0 2.7 %collective-permute-start.19 = (f32[2,64,128]{2,1,0:T(8,128)S(1)}, f32[2,64,128]{2,1,0:T(8,128)S(1)}, u32[]{:S(2)}, u32[]{:S(2)}) collective-permute-start(f32[2,64,128]{2,1,0:T(8,128)S(1)} %cross.10), channel_id=1, source_target_pairs={{0,1},{1,0},{2,3},{3,2},{4,5},{5,4},{6,7},{7,6},{8,9},{9,8},{10,11... | collective-permute-start | bytes 196616 | tf_op jit(solution)/shard_map/ppermute | solution.py:320
  39.0 1.7 %collective-permute-start.23 = (f32[2,64,128]{2,1,0:T(8,128)S(1)}, f32[2,64,128]{2,1,0:T(8,128)S(1)}, u32[]{:S(2)}, u32[]{:S(2)}) collective-permute-start(f32[2,64,128]{2,1,0:T(8,128)S(1)} %cross.11), channel_id=1, source_target_pairs={{0,1},{1,0},{2,3},{3,2},{4,5},{5,4},{6,7},{7,6},{8,9},{9,8},{10,11... | collective-permute-start | bytes 196616 | tf_op jit(solution)/shard_map/ppermute | solution.py:320
  39.1 5.9 %collective-permute-start.14 = (f32[4,64,128]{2,1,0:T(8,128)S(1)}, f32[4,64,128]{2,1,0:T(8,128)S(1)}, u32[]{:S(2)}, u32[]{:S(2)}) collective-permute-start(f32[4,64,128]{2,1,0:T(8,128)S(1)} %finish.3.rest_0_), channel_id=1, source_target_pairs={{8,0},{0,8},{24,16},{16,24},{9,1},{1,9},{25,17},{17,25},{10,2},{2,... | collective-permute-start | bytes 393224 | tf_op jit(solution)/shard_map/ppermute | solution.py:272
  40.8 6.4 %collective-permute-start.24 = (f32[4,64,128]{2,1,0:T(8,128)S(1)}, f32[4,64,128]{2,1,0:T(8,128)S(1)}, u32[]{:S(2)}, u32[]{:S(2)}) collective-permute-start(f32[4,64,128]{2,1,0:T(8,128)S(1)} %finish.4.rest_1_), channel_id=1, source_target_pairs={{16,0},{24,8},{0,16},{8,24},{17,1},{25,9},{1,17},{9,25},{18,2},{26... | collective-permute-start | bytes 393224 | tf_op jit(solution)/shard_map/ppermute | solution.py:272
  42.4 7.6 %collective-permute-start.27 = (f32[4,64,128]{2,1,0:T(8,128)S(1)}, f32[4,64,128]{2,1,0:T(8,128)S(1)}, u32[]{:S(2)}, u32[]{:S(2)}) collective-permute-start(f32[4,64,128]{2,1,0:T(8,128)S(1)} %finish.3.rest_0_), channel_id=1, source_target_pairs={{16,0},{24,8},{0,16},{8,24},{17,1},{25,9},{1,17},{9,25},{18,2},{26... | collective-permute-start | bytes 393224 | tf_op jit(solution)/shard_map/ppermute | solution.py:272
  42.9 7.1 %collective-permute-start.26 = (f32[4,64,128]{2,1,0:T(8,128)S(1)}, f32[4,64,128]{2,1,0:T(8,128)S(1)}, u32[]{:S(2)}, u32[]{:S(2)}) collective-permute-start(f32[4,64,128]{2,1,0:T(8,128)S(1)} %finish.4.rest_1_), channel_id=1, source_target_pairs={{8,0},{0,8},{24,16},{16,24},{9,1},{1,9},{25,17},{17,25},{10,2},{2,... | collective-permute-start | bytes 393224 | tf_op jit(solution)/shard_map/ppermute | solution.py:272
  45.0 6.9 %collective-permute-start.15 = (f32[4,64,128]{2,1,0:T(8,128)S(1)}, f32[4,64,128]{2,1,0:T(8,128)S(1)}, u32[]{:S(2)}, u32[]{:S(2)}) collective-permute-start(f32[4,64,128]{2,1,0:T(8,128)S(1)} %cut.9), channel_id=1, source_target_pairs={{16,0},{24,8},{0,16},{8,24},{17,1},{25,9},{1,17},{9,25},{18,2},{26... | collective-permute-start | bytes 393224 | tf_op jit(solution)/shard_map/ppermute | solution.py:272
  47.2 5.0 %collective-permute-start.25 = (f32[4,64,128]{2,1,0:T(8,128)S(1)}, f32[4,64,128]{2,1,0:T(8,128)S(1)}, u32[]{:S(2)}, u32[]{:S(2)}) collective-permute-start(f32[4,64,128]{2,1,0:T(8,128)S(1)} %cut.10), channel_id=1, source_target_pairs={{8,0},{0,8},{24,16},{16,24},{9,1},{1,9},{25,17},{17,25},{10,2},{2,... | collective-permute-start | bytes 393224 | tf_op jit(solution)/shard_map/ppermute | solution.py:272
  52.8 2.0 %collective-permute-start.28 = (f32[16,64,128]{2,1,0:T(8,128)S(1)}, f32[16,64,128]{2,1,0:T(8,128)S(1)}, u32[]{:S(2)}, u32[]{:S(2)}) collective-permute-start(f32[16,64,128]{2,1,0:T(8,128)S(1)} %slice.19), channel_id=1, source_target_pairs={{0,1},{1,0},{2,3},{3,2},{4,5},{5,4},{6,7},{7,6},{8,9},{9,8},{10,11... | collective-permute-start | bytes 1572872 | tf_op jit(solution)/shard_map/ppermute | solution.py:295
  55.0 5.1 %collective-permute-start.29 = (f32[48,64,128]{2,1,0:T(8,128)S(1)}, f32[48,64,128]{2,1,0:T(8,128)S(1)}, u32[]{:S(2)}, u32[]{:S(2)}) collective-permute-start(f32[48,64,128]{2,1,0:T(8,128)S(1)} %cut.11), channel_id=1, source_target_pairs={{0,1},{1,0},{2,3},{3,2},{4,5},{5,4},{6,7},{7,6},{8,9},{9,8},{10,11... | collective-permute-start | bytes 4718600 | tf_op jit(solution)/shard_map/ppermute | solution.py:303
  55.2 4.9 %collective-permute-start.30 = (f32[4,64,128]{2,1,0:T(8,128)S(1)}, f32[4,64,128]{2,1,0:T(8,128)S(1)}, u32[]{:S(2)}, u32[]{:S(2)}) collective-permute-start(f32[4,64,128]{2,1,0:T(8,128)S(1)} %carry.36.rest_0_), channel_id=1, source_target_pairs={{0,2},{1,0},{2,3},{3,1},{4,6},{5,4},{6,7},{7,5},{8,10},{9,8},{10,1... | collective-permute-start | bytes 393224 | tf_op jit(solution)/shard_map/ppermute | solution.py:306
  57.6 5.0 %collective-permute-start.34 = (f32[4,64,128]{2,1,0:T(8,128)S(1)}, f32[4,64,128]{2,1,0:T(8,128)S(1)}, u32[]{:S(2)}, u32[]{:S(2)}) collective-permute-start(f32[4,64,128]{2,1,0:T(8,128)S(1)} %carry.37.rest_1_), channel_id=1, source_target_pairs={{0,2},{1,0},{2,3},{3,1},{4,6},{5,4},{6,7},{7,5},{8,10},{9,8},{10,1... | collective-permute-start | bytes 393224 | tf_op jit(solution)/shard_map/ppermute | solution.py:306
  58.0 6.0 %collective-permute-start.38 = (f32[4,64,128]{2,1,0:T(8,128)S(1)}, f32[4,64,128]{2,1,0:T(8,128)S(1)}, u32[]{:S(2)}, u32[]{:S(2)}) collective-permute-start(f32[4,64,128]{2,1,0:T(8,128)S(1)} %carry.38.rest_2_), channel_id=1, source_target_pairs={{0,2},{1,0},{2,3},{3,1},{4,6},{5,4},{6,7},{7,5},{8,10},{9,8},{10,1... | collective-permute-start | bytes 393224 | tf_op jit(solution)/shard_map/ppermute | solution.py:306
  58.0 7.9 %collective-permute-start.42 = (f32[4,64,128]{2,1,0:T(8,128)S(1)}, f32[4,64,128]{2,1,0:T(8,128)S(1)}, u32[]{:S(2)}, u32[]{:S(2)}) collective-permute-start(f32[4,64,128]{2,1,0:T(8,128)S(1)} %carry.39.rest_3_), channel_id=1, source_target_pairs={{0,2},{1,0},{2,3},{3,1},{4,6},{5,4},{6,7},{7,5},{8,10},{9,8},{10,1... | collective-permute-start | bytes 393224 | tf_op jit(solution)/shard_map/ppermute | solution.py:306
  60.2 7.1 %collective-permute-start.31 = (f32[4,64,128]{2,1,0:T(8,128)S(1)}, f32[4,64,128]{2,1,0:T(8,128)S(1)}, u32[]{:S(2)}, u32[]{:S(2)}) collective-permute-start(f32[4,64,128]{2,1,0:T(8,128)S(1)} %carry.40), channel_id=1, source_target_pairs={{0,2},{1,0},{2,4},{3,1},{4,6},{5,3},{6,7},{7,5},{8,10},{9,8},{10,1... | collective-permute-start | bytes 393224 | tf_op jit(solution)/shard_map/ppermute | solution.py:310
  62.7 6.0 %collective-permute-start.35 = (f32[4,64,128]{2,1,0:T(8,128)S(1)}, f32[4,64,128]{2,1,0:T(8,128)S(1)}, u32[]{:S(2)}, u32[]{:S(2)}) collective-permute-start(f32[4,64,128]{2,1,0:T(8,128)S(1)} %carry.42), channel_id=1, source_target_pairs={{0,2},{1,0},{2,4},{3,1},{4,6},{5,3},{6,7},{7,5},{8,10},{9,8},{10,1... | collective-permute-start | bytes 393224 | tf_op jit(solution)/shard_map/ppermute | solution.py:310
  64.1 6.0 %collective-permute-start.39 = (f32[4,64,128]{2,1,0:T(8,128)S(1)}, f32[4,64,128]{2,1,0:T(8,128)S(1)}, u32[]{:S(2)}, u32[]{:S(2)}) collective-permute-start(f32[4,64,128]{2,1,0:T(8,128)S(1)} %carry.44), channel_id=1, source_target_pairs={{0,2},{1,0},{2,4},{3,1},{4,6},{5,3},{6,7},{7,5},{8,10},{9,8},{10,1... | collective-permute-start | bytes 393224 | tf_op jit(solution)/shard_map/ppermute | solution.py:310
  65.9 5.6 %collective-permute-start.43 = (f32[4,64,128]{2,1,0:T(8,128)S(1)}, f32[4,64,128]{2,1,0:T(8,128)S(1)}, u32[]{:S(2)}, u32[]{:S(2)}) collective-permute-start(f32[4,64,128]{2,1,0:T(8,128)S(1)} %carry.46), channel_id=1, source_target_pairs={{0,2},{1,0},{2,4},{3,1},{4,6},{5,3},{6,7},{7,5},{8,10},{9,8},{10,1... | collective-permute-start | bytes 393224 | tf_op jit(solution)/shard_map/ppermute | solution.py:310
  67.3 5.6 %collective-permute-start.32 = (f32[4,64,128]{2,1,0:T(8,128)S(1)}, f32[4,64,128]{2,1,0:T(8,128)S(1)}, u32[]{:S(2)}, u32[]{:S(2)}) collective-permute-start(f32[4,64,128]{2,1,0:T(8,128)S(1)} %carry.41), channel_id=1, source_target_pairs={{0,2},{1,0},{2,4},{3,1},{4,6},{5,3},{6,7},{7,5},{8,10},{9,8},{10,1... | collective-permute-start | bytes 393224 | tf_op jit(solution)/shard_map/ppermute | solution.py:310
  68.7 4.3 %collective-permute-start.36 = (f32[4,64,128]{2,1,0:T(8,128)S(1)}, f32[4,64,128]{2,1,0:T(8,128)S(1)}, u32[]{:S(2)}, u32[]{:S(2)}) collective-permute-start(f32[4,64,128]{2,1,0:T(8,128)S(1)} %carry.43), channel_id=1, source_target_pairs={{0,2},{1,0},{2,4},{3,1},{4,6},{5,3},{6,7},{7,5},{8,10},{9,8},{10,1... | collective-permute-start | bytes 393224 | tf_op jit(solution)/shard_map/ppermute | solution.py:310
  70.1 4.0 %collective-permute-start.40 = (f32[4,64,128]{2,1,0:T(8,128)S(1)}, f32[4,64,128]{2,1,0:T(8,128)S(1)}, u32[]{:S(2)}, u32[]{:S(2)}) collective-permute-start(f32[4,64,128]{2,1,0:T(8,128)S(1)} %carry.45), channel_id=1, source_target_pairs={{0,2},{1,0},{2,4},{3,1},{4,6},{5,3},{6,7},{7,5},{8,10},{9,8},{10,1... | collective-permute-start | bytes 393224 | tf_op jit(solution)/shard_map/ppermute | solution.py:310
  71.5 4.0 %collective-permute-start.44 = (f32[4,64,128]{2,1,0:T(8,128)S(1)}, f32[4,64,128]{2,1,0:T(8,128)S(1)}, u32[]{:S(2)}, u32[]{:S(2)}) collective-permute-start(f32[4,64,128]{2,1,0:T(8,128)S(1)} %carry.47), channel_id=1, source_target_pairs={{0,2},{1,0},{2,4},{3,1},{4,6},{5,3},{6,7},{7,5},{8,10},{9,8},{10,1... | collective-permute-start | bytes 393224 | tf_op jit(solution)/shard_map/ppermute | solution.py:310
  72.9 2.7 %collective-permute-start.33 = (f32[2,64,128]{2,1,0:T(8,128)S(1)}, f32[2,64,128]{2,1,0:T(8,128)S(1)}, u32[]{:S(2)}, u32[]{:S(2)}) collective-permute-start(f32[2,64,128]{2,1,0:T(8,128)S(1)} %cross.12), channel_id=1, source_target_pairs={{0,1},{1,0},{2,3},{3,2},{4,5},{5,4},{6,7},{7,6},{8,9},{9,8},{10,11... | collective-permute-start | bytes 196616 | tf_op jit(solution)/shard_map/ppermute | solution.py:320
  73.0 2.6 %collective-permute-start.37 = (f32[2,64,128]{2,1,0:T(8,128)S(1)}, f32[2,64,128]{2,1,0:T(8,128)S(1)}, u32[]{:S(2)}, u32[]{:S(2)}) collective-permute-start(f32[2,64,128]{2,1,0:T(8,128)S(1)} %cross.13), channel_id=1, source_target_pairs={{0,1},{1,0},{2,3},{3,2},{4,5},{5,4},{6,7},{7,6},{8,9},{9,8},{10,11... | collective-permute-start | bytes 196616 | tf_op jit(solution)/shard_map/ppermute | solution.py:320
  74.2 1.5 %collective-permute-start.41 = (f32[2,64,128]{2,1,0:T(8,128)S(1)}, f32[2,64,128]{2,1,0:T(8,128)S(1)}, u32[]{:S(2)}, u32[]{:S(2)}) collective-permute-start(f32[2,64,128]{2,1,0:T(8,128)S(1)} %cross.14), channel_id=1, source_target_pairs={{0,1},{1,0},{2,3},{3,2},{4,5},{5,4},{6,7},{7,6},{8,9},{9,8},{10,11... | collective-permute-start | bytes 196616 | tf_op jit(solution)/shard_map/ppermute | solution.py:320
  75.6 1.3 %collective-permute-start.45 = (f32[2,64,128]{2,1,0:T(8,128)S(1)}, f32[2,64,128]{2,1,0:T(8,128)S(1)}, u32[]{:S(2)}, u32[]{:S(2)}) collective-permute-start(f32[2,64,128]{2,1,0:T(8,128)S(1)} %cross.15), channel_id=1, source_target_pairs={{0,1},{1,0},{2,3},{3,2},{4,5},{5,4},{6,7},{7,6},{8,9},{9,8},{10,11... | collective-permute-start | bytes 196616 | tf_op jit(solution)/shard_map/ppermute | solution.py:320

commit v9 on v8

--- a/solution.py
+++ b/solution.py
@@ -11,6 +11,7 @@
 PARTS = 4
 GROUPS = (0, 2), (2, 4)
 STAGES = 4
+LEADS = 2
 GROUP = 32
 CHUNK = 16
 PLAN_HEAD = 8
@@ -292,14 +293,15 @@
         return h * block if order == 0 else leading + (h * (pairs - 1) + order - 1) * block
 
     def scatter(lead, sums):
-        first = lax.ppermute(lead[:leading], "col", swap)
         if pairs == 1:
-            return [[first]] * PARTS
+            return [[lax.ppermute(lead[:leading], "col", swap)]] * PARTS
+        few = leading // LEADS
+        first = [lax.ppermute(lead[i * few : (i + 1) * few], "col", swap) for i in range(LEADS)]
         far = pairs - 1
         totals = []
         for h in range(PARTS):
-            kernel = functools.partial(carry_kernel, at(h, far), h * block)
-            totals += small_call(kernel, (block,), "carry", sums, first)
+            kernel = functools.partial(carry_kernel, at(h, far), h * block % few)
+            totals += small_call(kernel, (block,), "carry", sums, first[h * block // few])
         rest = lax.ppermute(cut(sums, leading, sums.shape[0] - leading, totals), "col", swap)
         parts = []
         for h in range(PARTS):

time: 77.9 us -> 77.7 us (level)
  waiting for transfers between devices: 16.5 us -> 15.3 us
  starting transfers between devices: 46.6 us -> 47.8 us
    ppermute x2 -> x4, waiting for transfers between devices: 2.71 us -> 1.65 us  [scatter(): lax.ppermute(lead[i * few:(i + 1) * few], 'col', swap)]
    ppermute x2 -> x4, starting transfers between devices: 0.14 us -> 1.14 us  [scatter(): lax.ppermute(lead[i * few:(i + 1) * few], 'col', swap)]
  transfers between devices with their start and end apart: 46 -> 48, of which waited for: 18 -> 20; matrix products, arithmetic and copies ran while one was open for 2% -> 2% of each run, Pallas kernels for 13% -> 13%
where the time goes in v9:
time: 77.7 us; the launch traced here: 77.5 us
  starting transfers between devices  47.8 us (62%)
  waiting for transfers between devices  15.3 us (20%)
  Pallas kernels  11.9 us (15%)
  other arithmetic  1.39 us (2%)
  between operations  1.15 us (1%)
    ppermute x16, starting transfers between devices, scatter(): came = lax.ppermute(total, 'col', ring)  25 us
    ppermute x10, starting transfers between devices, from_turn(): lax.ppermute(value, 'row', [(i ^ k if flips else (i + k) % n_row, i) for...  14.3 us
    ppermute x8, starting transfers between devices, scatter(): came = lax.ppermute(totals[h], 'col', squares)  5.08 us
    pallas_call x7, Pallas kernels, transfer(): pl.pallas_call(functools.partial(transfer_kernel, fields_at, begin, end,...  5.07 us
    ppermute x10, waiting for transfers between devices, from_turn(): lax.ppermute(value, 'row', [(i ^ k if flips else (i + k) % n_row, i) for...  4.95 us
    pallas_call x1, Pallas kernels, prepare(): pl.pallas_call(prepare_kernel, in_specs=[pl.BlockSpec(memory_space=pltpu....  4.48 us
    ppermute x8, waiting for transfers between devices, scatter(): came = lax.ppermute(totals[h], 'col', squares)  4.05 us
    ppermute x16, waiting for transfers between devices, scatter(): came = lax.ppermute(total, 'col', ring)  2.48 us
  transfers between devices with their start and end apart: 48, of which 20 were waited for; matrix products, arithmetic and copies ran while one was open for 2% of the time, Pallas kernels for 13%

profile of v9, /device:TPU:0, one launch (start us, length us, event | category | flops | bytes accessed | tf_op | source)
XLA Modules:
  0.0 77.5 jit_solution(14287979918585640973)
XLA Ops:
  0.0 3.0 %collective-permute-start.2 = (f32[8,64,128]{2,1,0:T(8,128)}, f32[8,64,128]{2,1,0:T(8,128)S(1)}, u32[]{:S(2)}, u32[]{:S(2)}) collective-permute-start(f32[8,64,128]{2,1,0:T(8,128)} %source_ref.5), channel_id=1, source_target_pairs={{16,0},{24,8},{0,16},{8,24},{17,1},{25,9},{1,17},{9,25},{18,2},{26... | collective-permute-start | bytes 786440 | tf_op jit(solution)/shard_map/ppermute | solution.py:273
  3.0 1.5 %collective-permute-start = (f32[8,64,128]{2,1,0:T(8,128)}, f32[8,64,128]{2,1,0:T(8,128)S(1)}, u32[]{:S(2)}, u32[]{:S(2)}) collective-permute-start(f32[8,64,128]{2,1,0:T(8,128)} %source_ref.5), channel_id=1, source_target_pairs={{8,0},{0,8},{24,16},{16,24},{9,1},{1,9},{25,17},{17,25},{10,2},{2,... | collective-permute-start | bytes 786440 | tf_op jit(solution)/shard_map/ppermute | solution.py:273
  5.1 0.7 iota_add_fusion
  5.8 4.5 %prepare.1.rest_0_.a_ref = bf16[257,64,128]{2,1,0:T(8,128)(2,1)S(1)} custom-call(f32[64,64,256]{2,1,0:T(8,128)} %bitcast.3), custom_call_target="tpu_custom_call" | custom-call | bytes 25165824 | tf_op jit(solution)/shard_map/prepare/pallas_call | solution.py:70
  11.5 1.6 %collective-permute-start.3 = (f32[4,64,128]{2,1,0:T(8,128)S(1)}, f32[4,64,128]{2,1,0:T(8,128)S(1)}, u32[]{:S(2)}, u32[]{:S(2)}) collective-permute-start(f32[4,64,128]{2,1,0:T(8,128)S(1)} %cut.7), channel_id=1, source_target_pairs={{8,0},{0,8},{24,16},{16,24},{9,1},{1,9},{25,17},{17,25},{10,2},{2,... | collective-permute-start | bytes 393224 | tf_op jit(solution)/shard_map/ppermute | solution.py:273
  13.2 0.6 keep.1.plan_ref
  13.9 1.1 %transfer.7.rest_2_ = f32[64,64,128]{2,1,0:T(8,128)S(1)} custom-call(s32[872]{0:T(1024)S(4)} %keep.1.plan_ref, bf16[257,64,128]{2,1,0:T(8,128)(2,1)S(1)} %prepare.1.rest_0_.a_ref, f32[8,64,128]{2,1,0:T(8,128)S(1)} %copy-done, f32[8,64,128]{2,1,0:T(8,128)S(1)} %collective-permute-done.rest_1_, f32[8,64,128]{2,1,0:T(8,128)S(1)} %collective-permute-done.2.rest_2_), custom_call_target="tpu_custom_call" | custom-call | tf_op jit(solution)/shard_map/transfer/pallas_call | solution.py:139
  15.0 1.0 %collective-permute-done.1.rest_0_ = f32[4,64,128]{2,1,0:T(8,128)S(1)} collective-permute-done((f32[4,64,128]{2,1,0:T(8,128)S(1)}, f32[4,64,128]{2,1,0:T(8,128)S(1)}, u32[]{:S(2)}, u32[]{:S(2)}) %collective-permute-start.1) | collective-permute-done | bytes 131104 | tf_op jit(solution)/shard_map/ppermute | solution.py:273
  17.6 0.5 transfer.9.sums_ref.value_ref
  19.3 1.7 %collective-permute-start.7 = (f32[4,64,128]{2,1,0:T(8,128)S(1)}, f32[4,64,128]{2,1,0:T(8,128)S(1)}, u32[]{:S(2)}, u32[]{:S(2)}) collective-permute-start(f32[4,64,128]{2,1,0:T(8,128)S(1)} %carry.24.rest_0_), channel_id=1, source_target_pairs={{0,2},{1,0},{2,3},{3,1},{4,6},{5,4},{6,7},{7,5},{8,10},{9,8},{10,1... | collective-permute-start | bytes 393224 | tf_op jit(solution)/shard_map/ppermute | solution.py:308
  21.6 1.9 %collective-permute-done.7.rest_0_ = f32[4,64,128]{2,1,0:T(8,128)S(1)} collective-permute-done((f32[4,64,128]{2,1,0:T(8,128)S(1)}, f32[4,64,128]{2,1,0:T(8,128)S(1)}, u32[]{:S(2)}, u32[]{:S(2)}) %collective-permute-start.7) | collective-permute-done | bytes 131104 | tf_op jit(solution)/shard_map/ppermute | solution.py:308
  23.6 2.5 %collective-permute-start.8 = (f32[4,64,128]{2,1,0:T(8,128)S(1)}, f32[4,64,128]{2,1,0:T(8,128)S(1)}, u32[]{:S(2)}, u32[]{:S(2)}) collective-permute-start(f32[4,64,128]{2,1,0:T(8,128)S(1)} %carry.28), channel_id=1, source_target_pairs={{0,2},{1,0},{2,4},{3,1},{4,6},{5,3},{6,7},{7,5},{8,10},{9,8},{10,1... | collective-permute-start | bytes 393224 | tf_op jit(solution)/shard_map/ppermute | solution.py:312
  26.1 1.4 %collective-permute-start.12 = (f32[4,64,128]{2,1,0:T(8,128)S(1)}, f32[4,64,128]{2,1,0:T(8,128)S(1)}, u32[]{:S(2)}, u32[]{:S(2)}) collective-permute-start(f32[4,64,128]{2,1,0:T(8,128)S(1)} %carry.30), channel_id=1, source_target_pairs={{0,2},{1,0},{2,4},{3,1},{4,6},{5,3},{6,7},{7,5},{8,10},{9,8},{10,1... | collective-permute-start | bytes 393224 | tf_op jit(solution)/shard_map/ppermute | solution.py:312
  27.5 1.8 %collective-permute-start.18 = (f32[4,64,128]{2,1,0:T(8,128)S(1)}, f32[4,64,128]{2,1,0:T(8,128)S(1)}, u32[]{:S(2)}, u32[]{:S(2)}) collective-permute-start(f32[4,64,128]{2,1,0:T(8,128)S(1)} %carry.32), channel_id=1, source_target_pairs={{0,2},{1,0},{2,4},{3,1},{4,6},{5,3},{6,7},{7,5},{8,10},{9,8},{10,1... | collective-permute-start | bytes 393224 | tf_op jit(solution)/shard_map/ppermute | solution.py:312
  29.3 1.4 %collective-permute-start.22 = (f32[4,64,128]{2,1,0:T(8,128)S(1)}, f32[4,64,128]{2,1,0:T(8,128)S(1)}, u32[]{:S(2)}, u32[]{:S(2)}) collective-permute-start(f32[4,64,128]{2,1,0:T(8,128)S(1)} %carry.34), channel_id=1, source_target_pairs={{0,2},{1,0},{2,4},{3,1},{4,6},{5,3},{6,7},{7,5},{8,10},{9,8},{10,1... | collective-permute-start | bytes 393224 | tf_op jit(solution)/shard_map/ppermute | solution.py:312
  30.7 1.4 %collective-permute-start.9 = (f32[4,64,128]{2,1,0:T(8,128)S(1)}, f32[4,64,128]{2,1,0:T(8,128)S(1)}, u32[]{:S(2)}, u32[]{:S(2)}) collective-permute-start(f32[4,64,128]{2,1,0:T(8,128)S(1)} %carry.29), channel_id=1, source_target_pairs={{0,2},{1,0},{2,4},{3,1},{4,6},{5,3},{6,7},{7,5},{8,10},{9,8},{10,1... | collective-permute-start | bytes 393224 | tf_op jit(solution)/shard_map/ppermute | solution.py:312
  32.1 1.4 %collective-permute-start.13 = (f32[4,64,128]{2,1,0:T(8,128)S(1)}, f32[4,64,128]{2,1,0:T(8,128)S(1)}, u32[]{:S(2)}, u32[]{:S(2)}) collective-permute-start(f32[4,64,128]{2,1,0:T(8,128)S(1)} %carry.31), channel_id=1, source_target_pairs={{0,2},{1,0},{2,4},{3,1},{4,6},{5,3},{6,7},{7,5},{8,10},{9,8},{10,1... | collective-permute-start | bytes 393224 | tf_op jit(solution)/shard_map/ppermute | solution.py:312
  33.5 1.4 %collective-permute-start.19 = (f32[4,64,128]{2,1,0:T(8,128)S(1)}, f32[4,64,128]{2,1,0:T(8,128)S(1)}, u32[]{:S(2)}, u32[]{:S(2)}) collective-permute-start(f32[4,64,128]{2,1,0:T(8,128)S(1)} %carry.33), channel_id=1, source_target_pairs={{0,2},{1,0},{2,4},{3,1},{4,6},{5,3},{6,7},{7,5},{8,10},{9,8},{10,1... | collective-permute-start | bytes 393224 | tf_op jit(solution)/shard_map/ppermute | solution.py:312
  34.9 1.4 %collective-permute-start.23 = (f32[4,64,128]{2,1,0:T(8,128)S(1)}, f32[4,64,128]{2,1,0:T(8,128)S(1)}, u32[]{:S(2)}, u32[]{:S(2)}) collective-permute-start(f32[4,64,128]{2,1,0:T(8,128)S(1)} %carry.35), channel_id=1, source_target_pairs={{0,2},{1,0},{2,4},{3,1},{4,6},{5,3},{6,7},{7,5},{8,10},{9,8},{10,1... | collective-permute-start | bytes 393224 | tf_op jit(solution)/shard_map/ppermute | solution.py:312
  36.5 0.5 collective-permute-start.14
  37.0 0.7 collective-permute-done.10.rest_2_
  38.4 0.6 collective-permute-done.23.came_ref.rest_4_
  39.1 1.6 %collective-permute-start.15 = (f32[4,64,128]{2,1,0:T(8,128)S(1)}, f32[4,64,128]{2,1,0:T(8,128)S(1)}, u32[]{:S(2)}, u32[]{:S(2)}) collective-permute-start(f32[4,64,128]{2,1,0:T(8,128)S(1)} %finish.3.rest_0_), channel_id=1, source_target_pairs={{8,0},{0,8},{24,16},{16,24},{9,1},{1,9},{25,17},{17,25},{10,2},{2,... | collective-permute-start | bytes 393224 | tf_op jit(solution)/shard_map/ppermute | solution.py:273
  40.7 1.6 %collective-permute-start.25 = (f32[4,64,128]{2,1,0:T(8,128)S(1)}, f32[4,64,128]{2,1,0:T(8,128)S(1)}, u32[]{:S(2)}, u32[]{:S(2)}) collective-permute-start(f32[4,64,128]{2,1,0:T(8,128)S(1)} %finish.4.rest_1_), channel_id=1, source_target_pairs={{16,0},{24,8},{0,16},{8,24},{17,1},{25,9},{1,17},{9,25},{18,2},{26... | collective-permute-start | bytes 393224 | tf_op jit(solution)/shard_map/ppermute | solution.py:273
  42.8 1.1 %collective-permute-start.27 = (f32[4,64,128]{2,1,0:T(8,128)S(1)}, f32[4,64,128]{2,1,0:T(8,128)S(1)}, u32[]{:S(2)}, u32[]{:S(2)}) collective-permute-start(f32[4,64,128]{2,1,0:T(8,128)S(1)} %finish.4.rest_1_), channel_id=1, source_target_pairs={{8,0},{0,8},{24,16},{16,24},{9,1},{1,9},{25,17},{17,25},{10,2},{2,... | collective-permute-start | bytes 393224 | tf_op jit(solution)/shard_map/ppermute | solution.py:273
  43.9 0.8 %transfer.10.rest_0_.rest_4_ = f32[64,64,128]{2,1,0:T(8,128)S(1)} custom-call(s32[872]{0:T(1024)S(4)} %keep.1.plan_ref, bf16[257,64,128]{2,1,0:T(8,128)(2,1)S(1)} %prepare.1.rest_0_.a_ref, f32[4,64,128]{2,1,0:T(8,128)S(1)} %finish.3.rest_0_, f32[4,64,128]{2,1,0:T(8,128)S(1)} %finish.4.rest_1_), custom_call_target="tpu_custom_call" | custom-call | tf_op jit(solution)/shard_map/transfer/pallas_call | solution.py:139
  45.0 1.7 %collective-permute-start.16 = (f32[4,64,128]{2,1,0:T(8,128)S(1)}, f32[4,64,128]{2,1,0:T(8,128)S(1)}, u32[]{:S(2)}, u32[]{:S(2)}) collective-permute-start(f32[4,64,128]{2,1,0:T(8,128)S(1)} %cut.9), channel_id=1, source_target_pairs={{16,0},{24,8},{0,16},{8,24},{17,1},{25,9},{1,17},{9,25},{18,2},{26... | collective-permute-start | bytes 393224 | tf_op jit(solution)/shard_map/ppermute | solution.py:273
  47.2 1.2 %collective-permute-start.26 = (f32[4,64,128]{2,1,0:T(8,128)S(1)}, f32[4,64,128]{2,1,0:T(8,128)S(1)}, u32[]{:S(2)}, u32[]{:S(2)}) collective-permute-start(f32[4,64,128]{2,1,0:T(8,128)S(1)} %cut.10), channel_id=1, source_target_pairs={{8,0},{0,8},{24,16},{16,24},{9,1},{1,9},{25,17},{17,25},{10,2},{2,... | collective-permute-start | bytes 393224 | tf_op jit(solution)/shard_map/ppermute | solution.py:273
  48.4 1.6 %collective-permute-done.28.rest_2_ = f32[4,64,128]{2,1,0:T(8,128)S(1)} collective-permute-done((f32[4,64,128]{2,1,0:T(8,128)S(1)}, f32[4,64,128]{2,1,0:T(8,128)S(1)}, u32[]{:S(2)}, u32[]{:S(2)}) %collective-permute-start.28) | collective-permute-done | bytes 131104 | tf_op jit(solution)/shard_map/ppermute | solution.py:273
  50.0 1.0 %transfer.11.rest_2_ = f32[64,64,128]{2,1,0:T(8,128)S(1)} custom-call(s32[872]{0:T(1024)S(4)} %keep.1.plan_ref, bf16[257,64,128]{2,1,0:T(8,128)(2,1)S(1)} %prepare.1.rest_0_.a_ref, f32[4,64,128]{2,1,0:T(8,128)S(1)} %collective-permute-done.15.value_ref.rest_0_, f32[4,64,128]{2,1,0:T(8,128)S(1)} %collective-permute-done.27.rest_1_, ...), custom_call_target="tpu_custom_call" | custom-call | tf_op jit(solution)/shard_map/transfer/pallas_call | solution.py:139
  51.0 0.9 %collective-permute-done.16.rest_0_ = f32[4,64,128]{2,1,0:T(8,128)S(1)} collective-permute-done((f32[4,64,128]{2,1,0:T(8,128)S(1)}, f32[4,64,128]{2,1,0:T(8,128)S(1)}, u32[]{:S(2)}, u32[]{:S(2)}) %collective-permute-start.16) | collective-permute-done | bytes 131104 | tf_op jit(solution)/shard_map/ppermute | solution.py:273
  52.2 0.5 transfer.12.rest_2_
  53.4 0.5 transfer.13.sums_ref.value_ref
  55.1 2.4 %collective-permute-start.32 = (f32[4,64,128]{2,1,0:T(8,128)S(1)}, f32[4,64,128]{2,1,0:T(8,128)S(1)}, u32[]{:S(2)}, u32[]{:S(2)}) collective-permute-start(f32[4,64,128]{2,1,0:T(8,128)S(1)} %carry.36.rest_0_), channel_id=1, source_target_pairs={{0,2},{1,0},{2,3},{3,1},{4,6},{5,4},{6,7},{7,5},{8,10},{9,8},{10,1... | collective-permute-start | bytes 393224 | tf_op jit(solution)/shard_map/ppermute | solution.py:308
  57.9 2.1 %collective-permute-done.32.rest_0_ = f32[4,64,128]{2,1,0:T(8,128)S(1)} collective-permute-done((f32[4,64,128]{2,1,0:T(8,128)S(1)}, f32[4,64,128]{2,1,0:T(8,128)S(1)}, u32[]{:S(2)}, u32[]{:S(2)}) %collective-permute-start.32) | collective-permute-done | bytes 131104 | tf_op jit(solution)/shard_map/ppermute | solution.py:308
  60.1 2.5 %collective-permute-start.33 = (f32[4,64,128]{2,1,0:T(8,128)S(1)}, f32[4,64,128]{2,1,0:T(8,128)S(1)}, u32[]{:S(2)}, u32[]{:S(2)}) collective-permute-start(f32[4,64,128]{2,1,0:T(8,128)S(1)} %carry.40), channel_id=1, source_target_pairs={{0,2},{1,0},{2,4},{3,1},{4,6},{5,3},{6,7},{7,5},{8,10},{9,8},{10,1... | collective-permute-start | bytes 393224 | tf_op jit(solution)/shard_map/ppermute | solution.py:312
  62.6 1.4 %collective-permute-start.37 = (f32[4,64,128]{2,1,0:T(8,128)S(1)}, f32[4,64,128]{2,1,0:T(8,128)S(1)}, u32[]{:S(2)}, u32[]{:S(2)}) collective-permute-start(f32[4,64,128]{2,1,0:T(8,128)S(1)} %carry.42), channel_id=1, source_target_pairs={{0,2},{1,0},{2,4},{3,1},{4,6},{5,3},{6,7},{7,5},{8,10},{9,8},{10,1... | collective-permute-start | bytes 393224 | tf_op jit(solution)/shard_map/ppermute | solution.py:312
  64.0 1.8 %collective-permute-start.41 = (f32[4,64,128]{2,1,0:T(8,128)S(1)}, f32[4,64,128]{2,1,0:T(8,128)S(1)}, u32[]{:S(2)}, u32[]{:S(2)}) collective-permute-start(f32[4,64,128]{2,1,0:T(8,128)S(1)} %carry.44), channel_id=1, source_target_pairs={{0,2},{1,0},{2,4},{3,1},{4,6},{5,3},{6,7},{7,5},{8,10},{9,8},{10,1... | collective-permute-start | bytes 393224 | tf_op jit(solution)/shard_map/ppermute | solution.py:312
  65.8 1.4 %collective-permute-start.45 = (f32[4,64,128]{2,1,0:T(8,128)S(1)}, f32[4,64,128]{2,1,0:T(8,128)S(1)}, u32[]{:S(2)}, u32[]{:S(2)}) collective-permute-start(f32[4,64,128]{2,1,0:T(8,128)S(1)} %carry.46), channel_id=1, source_target_pairs={{0,2},{1,0},{2,4},{3,1},{4,6},{5,3},{6,7},{7,5},{8,10},{9,8},{10,1... | collective-permute-start | bytes 393224 | tf_op jit(solution)/shard_map/ppermute | solution.py:312
  67.2 1.4 %collective-permute-start.34 = (f32[4,64,128]{2,1,0:T(8,128)S(1)}, f32[4,64,128]{2,1,0:T(8,128)S(1)}, u32[]{:S(2)}, u32[]{:S(2)}) collective-permute-start(f32[4,64,128]{2,1,0:T(8,128)S(1)} %carry.41), channel_id=1, source_target_pairs={{0,2},{1,0},{2,4},{3,1},{4,6},{5,3},{6,7},{7,5},{8,10},{9,8},{10,1... | collective-permute-start | bytes 393224 | tf_op jit(solution)/shard_map/ppermute | solution.py:312
  68.6 1.4 %collective-permute-start.38 = (f32[4,64,128]{2,1,0:T(8,128)S(1)}, f32[4,64,128]{2,1,0:T(8,128)S(1)}, u32[]{:S(2)}, u32[]{:S(2)}) collective-permute-start(f32[4,64,128]{2,1,0:T(8,128)S(1)} %carry.43), channel_id=1, source_target_pairs={{0,2},{1,0},{2,4},{3,1},{4,6},{5,3},{6,7},{7,5},{8,10},{9,8},{10,1... | collective-permute-start | bytes 393224 | tf_op jit(solution)/shard_map/ppermute | solution.py:312
  70.0 1.4 %collective-permute-start.42 = (f32[4,64,128]{2,1,0:T(8,128)S(1)}, f32[4,64,128]{2,1,0:T(8,128)S(1)}, u32[]{:S(2)}, u32[]{:S(2)}) collective-permute-start(f32[4,64,128]{2,1,0:T(8,128)S(1)} %carry.45), channel_id=1, source_target_pairs={{0,2},{1,0},{2,4},{3,1},{4,6},{5,3},{6,7},{7,5},{8,10},{9,8},{10,1... | collective-permute-start | bytes 393224 | tf_op jit(solution)/shard_map/ppermute | solution.py:312
  71.4 1.4 %collective-permute-start.46 = (f32[4,64,128]{2,1,0:T(8,128)S(1)}, f32[4,64,128]{2,1,0:T(8,128)S(1)}, u32[]{:S(2)}, u32[]{:S(2)}) collective-permute-start(f32[4,64,128]{2,1,0:T(8,128)S(1)} %carry.47), channel_id=1, source_target_pairs={{0,2},{1,0},{2,4},{3,1},{4,6},{5,3},{6,7},{7,5},{8,10},{9,8},{10,1... | collective-permute-start | bytes 393224 | tf_op jit(solution)/shard_map/ppermute | solution.py:312
  72.9 0.5 collective-permute-start.39
  73.5 0.6 collective-permute-done.42.came_ref.rest_7_
  74.1 1.3 %collective-permute-done.46.came_ref.rest_10_ = f32[4,64,128]{2,1,0:T(8,128)S(1)} collective-permute-done((f32[4,64,128]{2,1,0:T(8,128)S(1)}, f32[4,64,128]{2,1,0:T(8,128)S(1)}, u32[]{:S(2)}, u32[]{:S(2)}) %collective-permute-start.46) | collective-permute-done | bytes 131104 | tf_op jit(solution)/shard_map/ppermute | solution.py:312
  75.6 1.2 %collective-permute-done.47.rest_11_ = f32[2,64,128]{2,1,0:T(8,128)S(1)} collective-permute-done((f32[2,64,128]{2,1,0:T(8,128)S(1)}, f32[2,64,128]{2,1,0:T(8,128)S(1)}, u32[]{:S(2)}, u32[]{:S(2)}) %collective-permute-start.47) | collective-permute-done | bytes 65568 | tf_op jit(solution)/shard_map/ppermute | solution.py:322
  76.8 0.8 finish.5
  (109 shorter events, 10.0 us)
Async XLA Ops:
  0.0 10.8 %collective-permute-start.2 = (f32[8,64,128]{2,1,0:T(8,128)}, f32[8,64,128]{2,1,0:T(8,128)S(1)}, u32[]{:S(2)}, u32[]{:S(2)}) collective-permute-start(f32[8,64,128]{2,1,0:T(8,128)} %source_ref.5), channel_id=1, source_target_pairs={{16,0},{24,8},{0,16},{8,24},{17,1},{25,9},{1,17},{9,25},{18,2},{26... | collective-permute-start | bytes 786440 | tf_op jit(solution)/shard_map/ppermute | solution.py:273
  3.0 8.0 %collective-permute-start = (f32[8,64,128]{2,1,0:T(8,128)}, f32[8,64,128]{2,1,0:T(8,128)S(1)}, u32[]{:S(2)}, u32[]{:S(2)}) collective-permute-start(f32[8,64,128]{2,1,0:T(8,128)} %source_ref.5), channel_id=1, source_target_pairs={{8,0},{0,8},{24,16},{16,24},{9,1},{1,9},{25,17},{17,25},{10,2},{2,... | collective-permute-start | bytes 786440 | tf_op jit(solution)/shard_map/ppermute | solution.py:273
  11.0 5.0 %collective-permute-start.1 = (f32[4,64,128]{2,1,0:T(8,128)S(1)}, f32[4,64,128]{2,1,0:T(8,128)S(1)}, u32[]{:S(2)}, u32[]{:S(2)}) collective-permute-start(f32[4,64,128]{2,1,0:T(8,128)S(1)} %cut.6), channel_id=1, source_target_pairs={{16,0},{24,8},{0,16},{8,24},{17,1},{25,9},{1,17},{9,25},{18,2},{26... | collective-permute-start | bytes 393224 | tf_op jit(solution)/shard_map/ppermute | solution.py:273
  11.5 5.0 %collective-permute-start.3 = (f32[4,64,128]{2,1,0:T(8,128)S(1)}, f32[4,64,128]{2,1,0:T(8,128)S(1)}, u32[]{:S(2)}, u32[]{:S(2)}) collective-permute-start(f32[4,64,128]{2,1,0:T(8,128)S(1)} %cut.7), channel_id=1, source_target_pairs={{8,0},{0,8},{24,16},{16,24},{9,1},{1,9},{25,17},{17,25},{10,2},{2,... | collective-permute-start | bytes 393224 | tf_op jit(solution)/shard_map/ppermute | solution.py:273
  17.0 1.6 %collective-permute-start.5 = (f32[8,64,128]{2,1,0:T(8,128)S(1)}, f32[8,64,128]{2,1,0:T(8,128)S(1)}, u32[]{:S(2)}, u32[]{:S(2)}) collective-permute-start(f32[8,64,128]{2,1,0:T(8,128)S(1)} %get-tuple-element.13), channel_id=1, source_target_pairs={{0,1},{1,0},{2,3},{3,2},{4,5},{5,4},{6,7},{7,6},{8,9},{9,8},{10,11... | collective-permute-start | bytes 786440 | tf_op jit(solution)/shard_map/ppermute | solution.py:299
  17.1 1.9 %collective-permute-start.4 = (f32[8,64,128]{2,1,0:T(8,128)S(1)}, f32[8,64,128]{2,1,0:T(8,128)S(1)}, u32[]{:S(2)}, u32[]{:S(2)}) collective-permute-start(f32[8,64,128]{2,1,0:T(8,128)S(1)} %get-tuple-element.14), channel_id=1, source_target_pairs={{0,1},{1,0},{2,3},{3,2},{4,5},{5,4},{6,7},{7,6},{8,9},{9,8},{10,11... | collective-permute-start | bytes 786440 | tf_op jit(solution)/shard_map/ppermute | solution.py:299
  19.1 4.4 %collective-permute-start.6 = (f32[48,64,128]{2,1,0:T(8,128)S(1)}, f32[48,64,128]{2,1,0:T(8,128)S(1)}, u32[]{:S(2)}, u32[]{:S(2)}) collective-permute-start(f32[48,64,128]{2,1,0:T(8,128)S(1)} %cut.8), channel_id=1, source_target_pairs={{0,1},{1,0},{2,3},{3,2},{4,5},{5,4},{6,7},{7,6},{8,9},{9,8},{10,11... | collective-permute-start | bytes 4718600 | tf_op jit(solution)/shard_map/ppermute | solution.py:305
  19.3 4.2 %collective-permute-start.7 = (f32[4,64,128]{2,1,0:T(8,128)S(1)}, f32[4,64,128]{2,1,0:T(8,128)S(1)}, u32[]{:S(2)}, u32[]{:S(2)}) collective-permute-start(f32[4,64,128]{2,1,0:T(8,128)S(1)} %carry.24.rest_0_), channel_id=1, source_target_pairs={{0,2},{1,0},{2,3},{3,1},{4,6},{5,4},{6,7},{7,5},{8,10},{9,8},{10,1... | collective-permute-start | bytes 393224 | tf_op jit(solution)/shard_map/ppermute | solution.py:308
  21.0 5.0 %collective-permute-start.11 = (f32[4,64,128]{2,1,0:T(8,128)S(1)}, f32[4,64,128]{2,1,0:T(8,128)S(1)}, u32[]{:S(2)}, u32[]{:S(2)}) collective-permute-start(f32[4,64,128]{2,1,0:T(8,128)S(1)} %carry.25.rest_1_), channel_id=1, source_target_pairs={{0,2},{1,0},{2,3},{3,1},{4,6},{5,4},{6,7},{7,5},{8,10},{9,8},{10,1... | collective-permute-start | bytes 393224 | tf_op jit(solution)/shard_map/ppermute | solution.py:308
  21.4 6.0 %collective-permute-start.17 = (f32[4,64,128]{2,1,0:T(8,128)S(1)}, f32[4,64,128]{2,1,0:T(8,128)S(1)}, u32[]{:S(2)}, u32[]{:S(2)}) collective-permute-start(f32[4,64,128]{2,1,0:T(8,128)S(1)} %carry.26.rest_2_), channel_id=1, source_target_pairs={{0,2},{1,0},{2,3},{3,1},{4,6},{5,4},{6,7},{7,5},{8,10},{9,8},{10,1... | collective-permute-start | bytes 393224 | tf_op jit(solution)/shard_map/ppermute | solution.py:308
  21.5 7.8 %collective-permute-start.21 = (f32[4,64,128]{2,1,0:T(8,128)S(1)}, f32[4,64,128]{2,1,0:T(8,128)S(1)}, u32[]{:S(2)}, u32[]{:S(2)}) collective-permute-start(f32[4,64,128]{2,1,0:T(8,128)S(1)} %carry.27.rest_3_), channel_id=1, source_target_pairs={{0,2},{1,0},{2,3},{3,1},{4,6},{5,4},{6,7},{7,5},{8,10},{9,8},{10,1... | collective-permute-start | bytes 393224 | tf_op jit(solution)/shard_map/ppermute | solution.py:308
  23.6 7.1 %collective-permute-start.8 = (f32[4,64,128]{2,1,0:T(8,128)S(1)}, f32[4,64,128]{2,1,0:T(8,128)S(1)}, u32[]{:S(2)}, u32[]{:S(2)}) collective-permute-start(f32[4,64,128]{2,1,0:T(8,128)S(1)} %carry.28), channel_id=1, source_target_pairs={{0,2},{1,0},{2,4},{3,1},{4,6},{5,3},{6,7},{7,5},{8,10},{9,8},{10,1... | collective-permute-start | bytes 393224 | tf_op jit(solution)/shard_map/ppermute | solution.py:312
  26.1 6.0 %collective-permute-start.12 = (f32[4,64,128]{2,1,0:T(8,128)S(1)}, f32[4,64,128]{2,1,0:T(8,128)S(1)}, u32[]{:S(2)}, u32[]{:S(2)}) collective-permute-start(f32[4,64,128]{2,1,0:T(8,128)S(1)} %carry.30), channel_id=1, source_target_pairs={{0,2},{1,0},{2,4},{3,1},{4,6},{5,3},{6,7},{7,5},{8,10},{9,8},{10,1... | collective-permute-start | bytes 393224 | tf_op jit(solution)/shard_map/ppermute | solution.py:312
  27.5 6.0 %collective-permute-start.18 = (f32[4,64,128]{2,1,0:T(8,128)S(1)}, f32[4,64,128]{2,1,0:T(8,128)S(1)}, u32[]{:S(2)}, u32[]{:S(2)}) collective-permute-start(f32[4,64,128]{2,1,0:T(8,128)S(1)} %carry.32), channel_id=1, source_target_pairs={{0,2},{1,0},{2,4},{3,1},{4,6},{5,3},{6,7},{7,5},{8,10},{9,8},{10,1... | collective-permute-start | bytes 393224 | tf_op jit(solution)/shard_map/ppermute | solution.py:312
  29.3 5.6 %collective-permute-start.22 = (f32[4,64,128]{2,1,0:T(8,128)S(1)}, f32[4,64,128]{2,1,0:T(8,128)S(1)}, u32[]{:S(2)}, u32[]{:S(2)}) collective-permute-start(f32[4,64,128]{2,1,0:T(8,128)S(1)} %carry.34), channel_id=1, source_target_pairs={{0,2},{1,0},{2,4},{3,1},{4,6},{5,3},{6,7},{7,5},{8,10},{9,8},{10,1... | collective-permute-start | bytes 393224 | tf_op jit(solution)/shard_map/ppermute | solution.py:312
  30.7 5.6 %collective-permute-start.9 = (f32[4,64,128]{2,1,0:T(8,128)S(1)}, f32[4,64,128]{2,1,0:T(8,128)S(1)}, u32[]{:S(2)}, u32[]{:S(2)}) collective-permute-start(f32[4,64,128]{2,1,0:T(8,128)S(1)} %carry.29), channel_id=1, source_target_pairs={{0,2},{1,0},{2,4},{3,1},{4,6},{5,3},{6,7},{7,5},{8,10},{9,8},{10,1... | collective-permute-start | bytes 393224 | tf_op jit(solution)/shard_map/ppermute | solution.py:312
  32.1 4.3 %collective-permute-start.13 = (f32[4,64,128]{2,1,0:T(8,128)S(1)}, f32[4,64,128]{2,1,0:T(8,128)S(1)}, u32[]{:S(2)}, u32[]{:S(2)}) collective-permute-start(f32[4,64,128]{2,1,0:T(8,128)S(1)} %carry.31), channel_id=1, source_target_pairs={{0,2},{1,0},{2,4},{3,1},{4,6},{5,3},{6,7},{7,5},{8,10},{9,8},{10,1... | collective-permute-start | bytes 393224 | tf_op jit(solution)/shard_map/ppermute | solution.py:312
  33.5 4.4 %collective-permute-start.19 = (f32[4,64,128]{2,1,0:T(8,128)S(1)}, f32[4,64,128]{2,1,0:T(8,128)S(1)}, u32[]{:S(2)}, u32[]{:S(2)}) collective-permute-start(f32[4,64,128]{2,1,0:T(8,128)S(1)} %carry.33), channel_id=1, source_target_pairs={{0,2},{1,0},{2,4},{3,1},{4,6},{5,3},{6,7},{7,5},{8,10},{9,8},{10,1... | collective-permute-start | bytes 393224 | tf_op jit(solution)/shard_map/ppermute | solution.py:312
  34.9 4.0 %collective-permute-start.23 = (f32[4,64,128]{2,1,0:T(8,128)S(1)}, f32[4,64,128]{2,1,0:T(8,128)S(1)}, u32[]{:S(2)}, u32[]{:S(2)}) collective-permute-start(f32[4,64,128]{2,1,0:T(8,128)S(1)} %carry.35), channel_id=1, source_target_pairs={{0,2},{1,0},{2,4},{3,1},{4,6},{5,3},{6,7},{7,5},{8,10},{9,8},{10,1... | collective-permute-start | bytes 393224 | tf_op jit(solution)/shard_map/ppermute | solution.py:312
  36.3 1.3 %collective-permute-start.10 = (f32[2,64,128]{2,1,0:T(8,128)S(1)}, f32[2,64,128]{2,1,0:T(8,128)S(1)}, u32[]{:S(2)}, u32[]{:S(2)}) collective-permute-start(f32[2,64,128]{2,1,0:T(8,128)S(1)} %cross.8), channel_id=1, source_target_pairs={{0,1},{1,0},{2,3},{3,2},{4,5},{5,4},{6,7},{7,6},{8,9},{9,8},{10,11... | collective-permute-start | bytes 196616 | tf_op jit(solution)/shard_map/ppermute | solution.py:322
  36.5 1.4 %collective-permute-start.14 = (f32[2,64,128]{2,1,0:T(8,128)S(1)}, f32[2,64,128]{2,1,0:T(8,128)S(1)}, u32[]{:S(2)}, u32[]{:S(2)}) collective-permute-start(f32[2,64,128]{2,1,0:T(8,128)S(1)} %cross.9), channel_id=1, source_target_pairs={{0,1},{1,0},{2,3},{3,2},{4,5},{5,4},{6,7},{7,6},{8,9},{9,8},{10,11... | collective-permute-start | bytes 196616 | tf_op jit(solution)/shard_map/ppermute | solution.py:322
  38.0 2.7 %collective-permute-start.20 = (f32[2,64,128]{2,1,0:T(8,128)S(1)}, f32[2,64,128]{2,1,0:T(8,128)S(1)}, u32[]{:S(2)}, u32[]{:S(2)}) collective-permute-start(f32[2,64,128]{2,1,0:T(8,128)S(1)} %cross.10), channel_id=1, source_target_pairs={{0,1},{1,0},{2,3},{3,2},{4,5},{5,4},{6,7},{7,6},{8,9},{9,8},{10,11... | collective-permute-start | bytes 196616 | tf_op jit(solution)/shard_map/ppermute | solution.py:322
  39.0 1.7 %collective-permute-start.24 = (f32[2,64,128]{2,1,0:T(8,128)S(1)}, f32[2,64,128]{2,1,0:T(8,128)S(1)}, u32[]{:S(2)}, u32[]{:S(2)}) collective-permute-start(f32[2,64,128]{2,1,0:T(8,128)S(1)} %cross.11), channel_id=1, source_target_pairs={{0,1},{1,0},{2,3},{3,2},{4,5},{5,4},{6,7},{7,6},{8,9},{9,8},{10,11... | collective-permute-start | bytes 196616 | tf_op jit(solution)/shard_map/ppermute | solution.py:322
  39.1 5.9 %collective-permute-start.15 = (f32[4,64,128]{2,1,0:T(8,128)S(1)}, f32[4,64,128]{2,1,0:T(8,128)S(1)}, u32[]{:S(2)}, u32[]{:S(2)}) collective-permute-start(f32[4,64,128]{2,1,0:T(8,128)S(1)} %finish.3.rest_0_), channel_id=1, source_target_pairs={{8,0},{0,8},{24,16},{16,24},{9,1},{1,9},{25,17},{17,25},{10,2},{2,... | collective-permute-start | bytes 393224 | tf_op jit(solution)/shard_map/ppermute | solution.py:273
  40.7 6.4 %collective-permute-start.25 = (f32[4,64,128]{2,1,0:T(8,128)S(1)}, f32[4,64,128]{2,1,0:T(8,128)S(1)}, u32[]{:S(2)}, u32[]{:S(2)}) collective-permute-start(f32[4,64,128]{2,1,0:T(8,128)S(1)} %finish.4.rest_1_), channel_id=1, source_target_pairs={{16,0},{24,8},{0,16},{8,24},{17,1},{25,9},{1,17},{9,25},{18,2},{26... | collective-permute-start | bytes 393224 | tf_op jit(solution)/shard_map/ppermute | solution.py:273
  42.3 7.6 %collective-permute-start.28 = (f32[4,64,128]{2,1,0:T(8,128)S(1)}, f32[4,64,128]{2,1,0:T(8,128)S(1)}, u32[]{:S(2)}, u32[]{:S(2)}) collective-permute-start(f32[4,64,128]{2,1,0:T(8,128)S(1)} %finish.3.rest_0_), channel_id=1, source_target_pairs={{16,0},{24,8},{0,16},{8,24},{17,1},{25,9},{1,17},{9,25},{18,2},{26... | collective-permute-start | bytes 393224 | tf_op jit(solution)/shard_map/ppermute | solution.py:273
  42.8 7.1 %collective-permute-start.27 = (f32[4,64,128]{2,1,0:T(8,128)S(1)}, f32[4,64,128]{2,1,0:T(8,128)S(1)}, u32[]{:S(2)}, u32[]{:S(2)}) collective-permute-start(f32[4,64,128]{2,1,0:T(8,128)S(1)} %finish.4.rest_1_), channel_id=1, source_target_pairs={{8,0},{0,8},{24,16},{16,24},{9,1},{1,9},{25,17},{17,25},{10,2},{2,... | collective-permute-start | bytes 393224 | tf_op jit(solution)/shard_map/ppermute | solution.py:273
  45.0 6.9 %collective-permute-start.16 = (f32[4,64,128]{2,1,0:T(8,128)S(1)}, f32[4,64,128]{2,1,0:T(8,128)S(1)}, u32[]{:S(2)}, u32[]{:S(2)}) collective-permute-start(f32[4,64,128]{2,1,0:T(8,128)S(1)} %cut.9), channel_id=1, source_target_pairs={{16,0},{24,8},{0,16},{8,24},{17,1},{25,9},{1,17},{9,25},{18,2},{26... | collective-permute-start | bytes 393224 | tf_op jit(solution)/shard_map/ppermute | solution.py:273
  47.2 5.0 %collective-permute-start.26 = (f32[4,64,128]{2,1,0:T(8,128)S(1)}, f32[4,64,128]{2,1,0:T(8,128)S(1)}, u32[]{:S(2)}, u32[]{:S(2)}) collective-permute-start(f32[4,64,128]{2,1,0:T(8,128)S(1)} %cut.10), channel_id=1, source_target_pairs={{8,0},{0,8},{24,16},{16,24},{9,1},{1,9},{25,17},{17,25},{10,2},{2,... | collective-permute-start | bytes 393224 | tf_op jit(solution)/shard_map/ppermute | solution.py:273
  52.8 1.6 %collective-permute-start.30 = (f32[8,64,128]{2,1,0:T(8,128)S(1)}, f32[8,64,128]{2,1,0:T(8,128)S(1)}, u32[]{:S(2)}, u32[]{:S(2)}) collective-permute-start(f32[8,64,128]{2,1,0:T(8,128)S(1)} %get-tuple-element.11), channel_id=1, source_target_pairs={{0,1},{1,0},{2,3},{3,2},{4,5},{5,4},{6,7},{7,6},{8,9},{9,8},{10,11... | collective-permute-start | bytes 786440 | tf_op jit(solution)/shard_map/ppermute | solution.py:299
  52.9 1.9 %collective-permute-start.29 = (f32[8,64,128]{2,1,0:T(8,128)S(1)}, f32[8,64,128]{2,1,0:T(8,128)S(1)}, u32[]{:S(2)}, u32[]{:S(2)}) collective-permute-start(f32[8,64,128]{2,1,0:T(8,128)S(1)} %get-tuple-element.12), channel_id=1, source_target_pairs={{0,1},{1,0},{2,3},{3,2},{4,5},{5,4},{6,7},{7,6},{8,9},{9,8},{10,11... | collective-permute-start | bytes 786440 | tf_op jit(solution)/shard_map/ppermute | solution.py:299
  54.9 5.1 %collective-permute-start.31 = (f32[48,64,128]{2,1,0:T(8,128)S(1)}, f32[48,64,128]{2,1,0:T(8,128)S(1)}, u32[]{:S(2)}, u32[]{:S(2)}) collective-permute-start(f32[48,64,128]{2,1,0:T(8,128)S(1)} %cut.11), channel_id=1, source_target_pairs={{0,1},{1,0},{2,3},{3,2},{4,5},{5,4},{6,7},{7,6},{8,9},{9,8},{10,11... | collective-permute-start | bytes 4718600 | tf_op jit(solution)/shard_map/ppermute | solution.py:305
  55.1 4.9 %collective-permute-start.32 = (f32[4,64,128]{2,1,0:T(8,128)S(1)}, f32[4,64,128]{2,1,0:T(8,128)S(1)}, u32[]{:S(2)}, u32[]{:S(2)}) collective-permute-start(f32[4,64,128]{2,1,0:T(8,128)S(1)} %carry.36.rest_0_), channel_id=1, source_target_pairs={{0,2},{1,0},{2,3},{3,1},{4,6},{5,4},{6,7},{7,5},{8,10},{9,8},{10,1... | collective-permute-start | bytes 393224 | tf_op jit(solution)/shard_map/ppermute | solution.py:308
  57.5 5.0 %collective-permute-start.36 = (f32[4,64,128]{2,1,0:T(8,128)S(1)}, f32[4,64,128]{2,1,0:T(8,128)S(1)}, u32[]{:S(2)}, u32[]{:S(2)}) collective-permute-start(f32[4,64,128]{2,1,0:T(8,128)S(1)} %carry.37.rest_1_), channel_id=1, source_target_pairs={{0,2},{1,0},{2,3},{3,1},{4,6},{5,4},{6,7},{7,5},{8,10},{9,8},{10,1... | collective-permute-start | bytes 393224 | tf_op jit(solution)/shard_map/ppermute | solution.py:308
  57.9 6.0 %collective-permute-start.40 = (f32[4,64,128]{2,1,0:T(8,128)S(1)}, f32[4,64,128]{2,1,0:T(8,128)S(1)}, u32[]{:S(2)}, u32[]{:S(2)}) collective-permute-start(f32[4,64,128]{2,1,0:T(8,128)S(1)} %carry.38.rest_2_), channel_id=1, source_target_pairs={{0,2},{1,0},{2,3},{3,1},{4,6},{5,4},{6,7},{7,5},{8,10},{9,8},{10,1... | collective-permute-start | bytes 393224 | tf_op jit(solution)/shard_map/ppermute | solution.py:308
  57.9 7.9 %collective-permute-start.44 = (f32[4,64,128]{2,1,0:T(8,128)S(1)}, f32[4,64,128]{2,1,0:T(8,128)S(1)}, u32[]{:S(2)}, u32[]{:S(2)}) collective-permute-start(f32[4,64,128]{2,1,0:T(8,128)S(1)} %carry.39.rest_3_), channel_id=1, source_target_pairs={{0,2},{1,0},{2,3},{3,1},{4,6},{5,4},{6,7},{7,5},{8,10},{9,8},{10,1... | collective-permute-start | bytes 393224 | tf_op jit(solution)/shard_map/ppermute | solution.py:308
  60.1 7.1 %collective-permute-start.33 = (f32[4,64,128]{2,1,0:T(8,128)S(1)}, f32[4,64,128]{2,1,0:T(8,128)S(1)}, u32[]{:S(2)}, u32[]{:S(2)}) collective-permute-start(f32[4,64,128]{2,1,0:T(8,128)S(1)} %carry.40), channel_id=1, source_target_pairs={{0,2},{1,0},{2,4},{3,1},{4,6},{5,3},{6,7},{7,5},{8,10},{9,8},{10,1... | collective-permute-start | bytes 393224 | tf_op jit(solution)/shard_map/ppermute | solution.py:312
  62.6 6.0 %collective-permute-start.37 = (f32[4,64,128]{2,1,0:T(8,128)S(1)}, f32[4,64,128]{2,1,0:T(8,128)S(1)}, u32[]{:S(2)}, u32[]{:S(2)}) collective-permute-start(f32[4,64,128]{2,1,0:T(8,128)S(1)} %carry.42), channel_id=1, source_target_pairs={{0,2},{1,0},{2,4},{3,1},{4,6},{5,3},{6,7},{7,5},{8,10},{9,8},{10,1... | collective-permute-start | bytes 393224 | tf_op jit(solution)/shard_map/ppermute | solution.py:312
  64.0 6.0 %collective-permute-start.41 = (f32[4,64,128]{2,1,0:T(8,128)S(1)}, f32[4,64,128]{2,1,0:T(8,128)S(1)}, u32[]{:S(2)}, u32[]{:S(2)}) collective-permute-start(f32[4,64,128]{2,1,0:T(8,128)S(1)} %carry.44), channel_id=1, source_target_pairs={{0,2},{1,0},{2,4},{3,1},{4,6},{5,3},{6,7},{7,5},{8,10},{9,8},{10,1... | collective-permute-start | bytes 393224 | tf_op jit(solution)/shard_map/ppermute | solution.py:312
  65.8 5.6 %collective-permute-start.45 = (f32[4,64,128]{2,1,0:T(8,128)S(1)}, f32[4,64,128]{2,1,0:T(8,128)S(1)}, u32[]{:S(2)}, u32[]{:S(2)}) collective-permute-start(f32[4,64,128]{2,1,0:T(8,128)S(1)} %carry.46), channel_id=1, source_target_pairs={{0,2},{1,0},{2,4},{3,1},{4,6},{5,3},{6,7},{7,5},{8,10},{9,8},{10,1... | collective-permute-start | bytes 393224 | tf_op jit(solution)/shard_map/ppermute | solution.py:312
  67.2 5.6 %collective-permute-start.34 = (f32[4,64,128]{2,1,0:T(8,128)S(1)}, f32[4,64,128]{2,1,0:T(8,128)S(1)}, u32[]{:S(2)}, u32[]{:S(2)}) collective-permute-start(f32[4,64,128]{2,1,0:T(8,128)S(1)} %carry.41), channel_id=1, source_target_pairs={{0,2},{1,0},{2,4},{3,1},{4,6},{5,3},{6,7},{7,5},{8,10},{9,8},{10,1... | collective-permute-start | bytes 393224 | tf_op jit(solution)/shard_map/ppermute | solution.py:312
  68.6 4.3 %collective-permute-start.38 = (f32[4,64,128]{2,1,0:T(8,128)S(1)}, f32[4,64,128]{2,1,0:T(8,128)S(1)}, u32[]{:S(2)}, u32[]{:S(2)}) collective-permute-start(f32[4,64,128]{2,1,0:T(8,128)S(1)} %carry.43), channel_id=1, source_target_pairs={{0,2},{1,0},{2,4},{3,1},{4,6},{5,3},{6,7},{7,5},{8,10},{9,8},{10,1... | collective-permute-start | bytes 393224 | tf_op jit(solution)/shard_map/ppermute | solution.py:312
  70.0 4.0 %collective-permute-start.42 = (f32[4,64,128]{2,1,0:T(8,128)S(1)}, f32[4,64,128]{2,1,0:T(8,128)S(1)}, u32[]{:S(2)}, u32[]{:S(2)}) collective-permute-start(f32[4,64,128]{2,1,0:T(8,128)S(1)} %carry.45), channel_id=1, source_target_pairs={{0,2},{1,0},{2,4},{3,1},{4,6},{5,3},{6,7},{7,5},{8,10},{9,8},{10,1... | collective-permute-start | bytes 393224 | tf_op jit(solution)/shard_map/ppermute | solution.py:312
  71.4 4.0 %collective-permute-start.46 = (f32[4,64,128]{2,1,0:T(8,128)S(1)}, f32[4,64,128]{2,1,0:T(8,128)S(1)}, u32[]{:S(2)}, u32[]{:S(2)}) collective-permute-start(f32[4,64,128]{2,1,0:T(8,128)S(1)} %carry.47), channel_id=1, source_target_pairs={{0,2},{1,0},{2,4},{3,1},{4,6},{5,3},{6,7},{7,5},{8,10},{9,8},{10,1... | collective-permute-start | bytes 393224 | tf_op jit(solution)/shard_map/ppermute | solution.py:312
  72.8 2.7 %collective-permute-start.35 = (f32[2,64,128]{2,1,0:T(8,128)S(1)}, f32[2,64,128]{2,1,0:T(8,128)S(1)}, u32[]{:S(2)}, u32[]{:S(2)}) collective-permute-start(f32[2,64,128]{2,1,0:T(8,128)S(1)} %cross.12), channel_id=1, source_target_pairs={{0,1},{1,0},{2,3},{3,2},{4,5},{5,4},{6,7},{7,6},{8,9},{9,8},{10,11... | collective-permute-start | bytes 196616 | tf_op jit(solution)/shard_map/ppermute | solution.py:322
  72.9 2.6 %collective-permute-start.39 = (f32[2,64,128]{2,1,0:T(8,128)S(1)}, f32[2,64,128]{2,1,0:T(8,128)S(1)}, u32[]{:S(2)}, u32[]{:S(2)}) collective-permute-start(f32[2,64,128]{2,1,0:T(8,128)S(1)} %cross.13), channel_id=1, source_target_pairs={{0,1},{1,0},{2,3},{3,2},{4,5},{5,4},{6,7},{7,6},{8,9},{9,8},{10,11... | collective-permute-start | bytes 196616 | tf_op jit(solution)/shard_map/ppermute | solution.py:322
  74.1 1.5 %collective-permute-start.43 = (f32[2,64,128]{2,1,0:T(8,128)S(1)}, f32[2,64,128]{2,1,0:T(8,128)S(1)}, u32[]{:S(2)}, u32[]{:S(2)}) collective-permute-start(f32[2,64,128]{2,1,0:T(8,128)S(1)} %cross.14), channel_id=1, source_target_pairs={{0,1},{1,0},{2,3},{3,2},{4,5},{5,4},{6,7},{7,6},{8,9},{9,8},{10,11... | collective-permute-start | bytes 196616 | tf_op jit(solution)/shard_map/ppermute | solution.py:322
  75.5 1.3 %collective-permute-start.47 = (f32[2,64,128]{2,1,0:T(8,128)S(1)}, f32[2,64,128]{2,1,0:T(8,128)S(1)}, u32[]{:S(2)}, u32[]{:S(2)}) collective-permute-start(f32[2,64,128]{2,1,0:T(8,128)S(1)} %cross.15), channel_id=1, source_target_pairs={{0,1},{1,0},{2,3},{3,2},{4,5},{5,4},{6,7},{7,6},{8,9},{9,8},{10,11... | collective-permute-start | bytes 196616 | tf_op jit(solution)/shard_map/ppermute | solution.py:322
  (1 other events, 2.9 us)
